TPU v7x, 32 devices: a whole 2x2x4 slice. The times are simulated.
32 devices in a mesh: groups: 1, dp: 32 (over z, y, x, core).
Axes of the slice: x: 2, y: 2, z: 4, core: 2. Of those that a mesh axis runs over, the one named last changes fastest.
Arguments:
- activations: bfloat16 [128, 8192], P(('groups', 'dp')), may hold values from -6 to 6
- cotangent: bfloat16 [128, 8192], P(('groups', 'dp')), may hold values from -6 to 6
- w_gate: bfloat16 [28672, 8192], P('dp'), may hold values from -0.0625 to 0.0625
- w_up: bfloat16 [28672, 8192], P('dp'), may hold values from -0.0625 to 0.0625
- w_down: bfloat16 [28672, 8192], P('dp'), may hold values from -0.03125 to 0.03125
- proj_model: bfloat16 [8192, 192], P('dp'), may hold values from -0.0625 to 0.0625
- proj_hidden: bfloat16 [28672, 192], P('dp'), may hold values from -0.03125 to 0.03125
- seq_ids: int32 [128], P('groups'), may hold values from 0 to 15, never falling along the last dimension, each value on 1 to 16 neighbouring positions
- targets: bfloat16 [256, 3, 64, 64], P(('groups', 'dp')), may hold values from -24 to 24
- target_domain: int32 [256], P(('groups', 'dp')), may hold values from 0 to 31, never falling along the last dimension, each value on 1 to 16 neighbouring positions
Outputs:
- sketches: float32 [16, 3, 64, 64], P('groups')
- scores: float32 [16, 32], P('groups')
Inputs may be any that keep to these rules, and one draw needn't show every extreme that they name: `seq_ids`: never falling along the tokens; each of the 16 sequences has 1 to 16 tokens, one exactly 16. `target_domain`: never falling along the target examples; each of the 32 domains has 1 to 16 examples, one exactly 16.
All inputs are finite; a program needn't handle non-finite values.
Results may differ from a plain program's by a relative error of at most 0.0032.
Values may be sent and summed in bfloat16 or wider, within the bound.
No kernel may reach another device: no remote copies, remote signals or barrier semaphores. Data moves between devices by JAX's collectives and lax.ppermute only.
A program may use at most 128 MiB of HBM per device.

v0:
```python
import jax
import jax.numpy as jnp
from jax import lax
from jax.sharding import PartitionSpec as P

DOMAINS = 32
SEQS = 16


def sequence_sketch(vectors, onehot, rank_size):
    blocks = vectors.reshape(vectors.shape[0], 6, rank_size)
    left_side = jnp.stack((blocks[:, 4], blocks[:, 5], blocks[:, 3]), 1)
    right_side = jnp.stack((blocks[:, 0], blocks[:, 1], blocks[:, 2]), 1)
    return jnp.einsum(
        "ns,nka,nkb->skab", onehot, left_side, right_side, precision=lax.Precision.HIGHEST
    )


def on_device(
    activations,
    cotangent,
    w_gate,
    w_up,
    w_down,
    proj_model,
    proj_hidden,
    seq_ids,
    targets,
    target_domain,
):
    rank_size = proj_model.shape[1] // 3
    model_cols = proj_model.shape[0]
    hidden_units = w_gate.shape[0]
    position = lax.axis_index("dp")
    offset = position * model_cols
    rows_in = lax.all_gather(activations, "dp", axis=0, tiled=True)
    gate_value = jnp.einsum("rd,fd->rf", rows_in, w_gate, preferred_element_type=jnp.float32)
    up_value = jnp.einsum("rd,fd->rf", rows_in, w_up, preferred_element_type=jnp.float32)
    columns = lax.dynamic_slice_in_dim(rows_in, offset, model_cols, 1)
    in_model = jnp.dot(columns, proj_model[:, : 2 * rank_size], preferred_element_type=jnp.float32)
    gate_value, up_value, in_model = (gate_value, up_value, in_model)
    forward_all = jnp.concatenate([gate_value, up_value, in_model], 1)
    gate_all = forward_all[:, :hidden_units]
    up_all = forward_all[:, hidden_units : 2 * hidden_units]
    in_model_all = forward_all[:, 2 * hidden_units :]
    gate_value = gate_all
    up_value = up_all
    rows_grad = lax.all_gather(cotangent, "dp", axis=0, tiled=True)
    sigmoid_gate = jax.nn.sigmoid(gate_value)
    silu_gate = gate_value * sigmoid_gate
    hidden = (silu_gate * up_value).astype(jnp.bfloat16)
    grad_hidden = jnp.einsum("rd,fd->rf", rows_grad, w_down, preferred_element_type=jnp.float32)
    grad_gate = (
        grad_hidden * up_value * sigmoid_gate * (1.0 + gate_value * (1.0 - sigmoid_gate))
    ).astype(jnp.bfloat16)
    grad_up = (grad_hidden * silu_gate).astype(jnp.bfloat16)
    columns = lax.dynamic_slice_in_dim(rows_grad, offset, model_cols, 1)
    out_down = jnp.dot(columns, proj_model[:, 2 * rank_size :], preferred_element_type=jnp.float32)
    in_down = jnp.dot(hidden, proj_hidden[:, :rank_size], preferred_element_type=jnp.float32)
    out_gate = jnp.dot(
        grad_gate, proj_hidden[:, rank_size : 2 * rank_size], preferred_element_type=jnp.float32
    )
    out_up = jnp.dot(grad_up, proj_hidden[:, 2 * rank_size :], preferred_element_type=jnp.float32)
    grads_all = jnp.concatenate([out_down, in_down, out_gate, out_up], 1)
    partials = jnp.concatenate([in_model_all, grads_all], 1)
    sequence_range = jnp.arange(SEQS)
    own_vectors = lax.psum_scatter(partials, "dp", scatter_dimension=0, tiled=True)
    own_count = own_vectors.shape[0]
    own_ids = lax.dynamic_slice_in_dim(seq_ids, position * own_count, own_count, 0)
    own_onehot = (own_ids[:, None] == sequence_range[None, :]).astype(jnp.float32)
    local_sketch = sequence_sketch(own_vectors, own_onehot, rank_size)
    sketches = lax.psum(local_sketch, "dp")
    entries = 3 * rank_size * rank_size
    flat_sketch = sketches.reshape(SEQS, entries)
    inverse_norm = lax.rsqrt(jnp.sum(flat_sketch * flat_sketch, 1) + 1e-06)
    domain_onehot = (target_domain[None, :] == jnp.arange(DOMAINS)[:, None]).astype(jnp.bfloat16)
    local_targets = targets.reshape(targets.shape[0], entries)
    domain_count = jnp.sum(domain_onehot.astype(jnp.float32), 1)
    target_products = jnp.dot(
        flat_sketch, local_targets.astype(jnp.float32).T, precision=lax.Precision.HIGHEST
    )
    folded = jnp.dot(
        target_products, domain_onehot.astype(jnp.float32).T, precision=lax.Precision.HIGHEST
    )
    total_scores, total_count = lax.psum((folded, domain_count), "dp")
    scores = total_scores / total_count[None, :] * inverse_norm[:, None]
    return (sketches, scores)


def solution(mesh):
    in_specs = (
        P(("groups", "dp"), None),
        P(("groups", "dp"), None),
        P("dp", None),
        P("dp", None),
        P("dp", None),
        P("dp", None),
        P("dp", None),
        P("groups"),
        P(("groups", "dp"), None, None, None),
        P(("groups", "dp")),
    )
    out_specs = (P("groups", None, None, None), P("groups", None))
    return jax.shard_map(
        on_device, mesh=mesh, in_specs=in_specs, out_specs=out_specs, check_vma=False
    )
```

profile of v0, /device:TPU:0, one launch (start us, length us, event | category | flops | bytes accessed | tf_op | source)
XLA Modules:
  0.0 477.8 jit_solution(16426818172373653184)
XLA Ops:
  7.2 0.0 copy-start
  7.2 0.0 all-gather.5.cloned.1.call-start
  7.2 0.7 all-gather.5.cloned.1.call-update
  7.9 0.0 all-gather.7.cloned.1.call-start
  8.0 0.7 all-gather.7.cloned.1.call-update
  8.7 0.0 all-reduce.7.cloned.1.call-start
  8.7 0.7 dynamic_slice.11
  9.4 0.0 copy-start.3
  9.4 60.5 %all-gather.5.cloned.1.call-done = bf16[32,4,8192]{2,1,0:T(4,128)(2,1)} async-done(((bf16[1,4,8192]{2,1,0:T(4,128)(2,1)}), bf16[32,4,8192]{2,1,0:T(4,128)(2,1)}) %all-gather.5.cloned.1.call-update) | async-done | bytes 2097168 | tf_op jit(solution)/shard_map/all_gather | solution.py:36
  70.0 2.5 reshape.18
  72.5 0.0 copy-done.3
  72.5 0.1 convolution_dynamic-update-slice_fusion
  72.7 55.4 %all-gather.7.cloned.1.call-done = bf16[32,4,8192]{2,1,0:T(4,128)(2,1)} async-done(((bf16[1,4,8192]{2,1,0:T(4,128)(2,1)}), bf16[32,4,8192]{2,1,0:T(4,128)(2,1)}) %all-gather.7.cloned.1.call-update) | async-done | bytes 2097168 | tf_op jit(solution)/shard_map/all_gather | solution.py:48
  128.1 3.9 reshape.20
  132.0 1.0 convolution_dynamic-update-slice_fusion.4
  133.0 10.6 %fusion.30 = f32[128,896]{1,0:T(8,128)S(1)} fusion(bf16[128,8192]{1,0:T(8,128)(2,1)} %reshape.20, bf16[896,8192]{1,0:T(8,128)(2,1)} %param.14), kind=kOutput, calls=%fused_computation.45 | convolution fusion | flops 1879048192 | bytes 17235968 | tf_op jit(solution)/shard_map/rd,fd->rf/dot_general | solution.py:52
  143.6 9.9 %fusion.28 = f32[128,896]{1,0:T(8,128)S(1)} fusion(bf16[128,8192]{1,0:T(8,128)(2,1)S(1)} %reshape.18, bf16[896,8192]{1,0:T(8,128)(2,1)} %param.12), kind=kOutput, calls=%fused_computation.43 | convolution fusion | flops 1879048192 | bytes 17235968 | tf_op jit(solution)/shard_map/rd,fd->rf/dot_general | solution.py:37
  153.5 0.0 copy-start.4
  153.5 9.9 %fusion.29 = f32[128,896]{1,0:T(8,128)S(1)} fusion(bf16[128,8192]{1,0:T(8,128)(2,1)S(1)} %reshape.18, bf16[896,8192]{1,0:T(8,128)(2,1)} %param.13), kind=kOutput, calls=%fused_computation.44 | convolution fusion | flops 1879048192 | bytes 17235968 | tf_op jit(solution)/shard_map/rd,fd->rf/dot_general | solution.py:38
  163.5 0.0 copy-done.4
  163.5 0.3 convolution_dynamic-update-slice_fusion.3
  163.7 0.3 convolution_dynamic-update-slice_fusion.2
  164.1 0.3 convolution_dynamic-update-slice_fusion.1
  164.4 0.0 copy-start.2
  164.4 0.0 copy-start.5
  164.4 0.7 copy-done.2
  165.0 0.0 all-reduce.7.cloned.1.call-update
  165.1 0.2 all-reduce.5.cloned.1.call-start
  165.3 121.8 %all-reduce.7.cloned.1.call-done = f32[128,384]{0,1:T(8,128)} async-done(((f32[128,384]{0,1:T(8,128)}), f32[128,384]{0,1:T(8,128)}) %all-reduce.7.cloned.1.call-update) | async-done | bytes 196624
  287.1 1.0 constant_dynamic-slice_fusion
  288.1 0.1 copy.37
  288.2 0.1 copy.24
  288.3 3.9 convolution_bitcast_fusion
  292.2 0.0 all-reduce.5.cloned.1.call-update
  292.2 0.0 copy-done.5
  292.2 0.1 convert_reduce_fusion
  292.3 133.4 %all-reduce.5.cloned.1.call-done = f32[16,3,64,64]{3,2,0,1:T(8,128)} async-done(((f32[16,3,64,64]{3,2,0,1:T(8,128)}), f32[16,3,64,64]{3,2,0,1:T(8,128)}) %all-reduce.5.cloned.1.call-update) | async-done | bytes 786448 | tf_op jit(solution)/shard_map/psum | solution.py:72
  425.7 0.0 copy-start.1
  425.7 1.8 multiply_reduce_fusion
  427.5 0.0 copy-done
  427.5 0.1 copy-done.1
  427.5 2.3 fusion.2
  429.9 0.2 fusion.21
  430.1 39.3 %all-reduce.1 = (f32[16,32]{1,0:T(8,128)S(1)}, f32[32]{0:T(128)S(1)}) all-reduce(f32[16,32]{1,0:T(8,128)S(1)} %fusion.21, f32[32]{0:T(128)S(1)} %convert_reduce_fusion), channel_id=1, replica_groups=mesh['groups'=1,'dp'=32] {'dp'}, use_global_device_ids=true, to_apply=%region_2.0 | all-reduce | flops 544 | bytes 4352 | tf_op jit(solution)/shard_map/psum | solution.py:85
  469.3 0.7 divide_multiply_fusion
  470.0 1.2 copy.29
  (5 shorter events, 0.0 us)
Async XLA Ops:
  7.2 420.3 %copy-start = (bf16[8,3,64,64]{3,2,1,0:T(8,128)(2,1)S(1)}, bf16[8,3,64,64]{3,2,1,0:T(8,128)(2,1)}, u32[]{:S(2)}) copy-start(bf16[8,3,64,64]{3,2,1,0:T(8,128)(2,1)} %param.18) | copy-start | bytes 589828
  7.2 62.8 %all-gather.5.cloned.1.call-start = ((), (), s32[]{:S(2)}) async-start(), calls=%async_computation.1 | async-start | bytes 2162688 | tf_op jit(solution)/shard_map/all_gather | solution.py:36
  7.9 120.2 %all-gather.7.cloned.1.call-start = ((), (), s32[]{:S(2)}) async-start(), calls=%async_computation.2 | async-start | bytes 2162688 | tf_op jit(solution)/shard_map/all_gather | solution.py:48
  8.7 278.4 %all-reduce.7.cloned.1.call-start = ((), (), s32[]{:S(2)}) async-start(), calls=%async_computation.3 | async-start | bytes 393216
  9.4 63.1 %copy-start.3 = (bf16[256,192]{0,1:T(8,128)(2,1)S(1)}, bf16[256,192]{0,1:T(8,128)(2,1)}, u32[]{:S(2)}) copy-start(bf16[256,192]{0,1:T(8,128)(2,1)} %param.15) | copy-start | bytes 294916
  153.5 10.0 %copy-start.4 = (bf16[896,192]{0,1:T(8,128)(2,1)S(1)}, bf16[896,192]{0,1:T(8,128)(2,1)}, u32[]{:S(2)}) copy-start(bf16[896,192]{0,1:T(8,128)(2,1)} %param.16) | copy-start | bytes 1032196
  164.4 0.7 copy-start.2
  164.4 127.8 %copy-start.5 = (s32[8]{0:T(128)S(1)}, s32[8]{0:T(128)}, u32[]{:S(2)}) copy-start(s32[8]{0:T(128)} %param.19) | copy-start | bytes 100
  165.1 260.6 %all-reduce.5.cloned.1.call-start = ((), (), s32[]{:S(2)}) async-start(), calls=%async_computation | async-start | bytes 3145728 | tf_op jit(solution)/shard_map/psum | solution.py:72
  425.7 1.9 copy-start.1
Sparse Core Ops, SparseCore 0:
  10.9 59.0 all-gather.4
  72.8 55.2 all-gather.6
  165.2 121.8 all-reduce.6
  292.8 132.8 all-reduce.4
where the time goes:
time: 478 us
  waiting for transfers between devices  373 us (78%)
  blocking collectives  39.3 us (8%)
  matrix products  38.8 us (8%)
  between operations  13.9 us (3%)
  local copies, waits for them, and re-layouts  10.4 us (2%)
    psum x1, waiting for transfers between devices, on_device(): sketches = lax.psum(local_sketch, 'dp')  133 us
    unnamed x5, waiting for transfers between devices  123 us
    all_gather x1, waiting for transfers between devices, on_device(): rows_in = lax.all_gather(activations, 'dp', axis=0, tiled=True)  60.5 us
    all_gather x1, waiting for transfers between devices, on_device(): rows_grad = lax.all_gather(cotangent, 'dp', axis=0, tiled=True)  55.4 us
    psum x1, blocking collectives, on_device(): total_scores, total_count = lax.psum((folded, domain_count), 'dp')  39.3 us
    dot_general x1, matrix products, on_device(): jnp.einsum('rd,fd->rf', rows_grad, w_down, preferred_element_type=jnp.flo...  10.6 us
    dot_general x1, matrix products, on_device(): jnp.einsum('rd,fd->rf', rows_in, w_up, preferred_element_type=jnp.float32)  9.95 us
    dot_general x1, matrix products, on_device(): jnp.einsum('rd,fd->rf', rows_in, w_gate, preferred_element_type=jnp.float32)  9.9 us
  transfers between devices with their start and end apart: 4, of which 4 were waited for; matrix products, arithmetic and copies ran while one was open for 1% of the time, Pallas kernels for 0%

commit v1 on v0

v1 whole, which is shorter than its diff:
```python
import functools

import jax
import jax.numpy as jnp
import numpy as np
from jax import lax
from jax.experimental import pallas as pl
from jax.experimental.pallas import tpu as pltpu
from jax.sharding import PartitionSpec as P

DOMAINS = 32
SEQS = 16
HIGHEST = lax.Precision.HIGHEST
F32 = jnp.float32
BF16 = jnp.bfloat16


def axis_sizes(count):
    if count == 32:
        return (4, 2, 2, 2)
    if count == 128:
        return (8, 8, 2)
    return (count,)


class Ring:
    def __init__(self, count):
        self.count = count
        self.sizes = axis_sizes(count)
        self.strides = [int(np.prod(self.sizes[i + 1 :])) for i in range(len(self.sizes))]
        self.me = lax.axis_index("dp")

    def coord(self, axis):
        return (self.me // self.strides[axis]) % self.sizes[axis]

    def shift(self, value, axis, amount):
        size, stride = self.sizes[axis], self.strides[axis]
        pairs = []
        for source in range(self.count):
            at = (source // stride) % size
            pairs.append((source, source + ((at + amount) % size - at) * stride))
        return lax.ppermute(value, "dp", pairs)

    def gather(self, rows, order):
        size = self.sizes[0]
        received = [rows] + [self.shift(rows, 0, k) for k in range(1, size)]
        at = self.coord(0)
        block = jnp.concatenate(
            [lax.select_n((at + size - j) % size, *received) for j in range(size)], 0
        )
        pieces = [(block, tuple(0 for _ in self.sizes))]
        for axis in order:
            grown = list(pieces)
            for k in range(1, self.sizes[axis]):
                for piece, back in pieces:
                    moved = tuple(k if i == axis else b for i, b in enumerate(back))
                    grown.append((self.shift(piece, axis, k), moved))
            pieces = grown
        slots = []
        for _, back in pieces:
            slot = 0
            for axis in range(1, len(self.sizes)):
                spot = (self.coord(axis) + self.sizes[axis] - back[axis]) % self.sizes[axis]
                slot = slot * self.sizes[axis] + spot
            slots.append(jnp.asarray(slot, jnp.int32))
        return [piece for piece, _ in pieces], jnp.stack(slots)

    def slot_order(self, per_token):
        size = self.sizes[0]
        rest = self.count // size
        return per_token.reshape(size, rest, -1).transpose(1, 0, 2).reshape(-1)


def exchange(blocks):
    return lax.all_to_all(blocks, "dp", split_axis=0, concat_axis=0, tiled=True)


def spread(block, count):
    return exchange(jnp.broadcast_to(block[None], (count,) + block.shape))


def place(slots, pieces, rows, into):
    for i, piece in enumerate(pieces):
        start = pl.multiple_of(slots[i] * rows, rows)
        into[pl.ds(start, rows), :] = piece[...]


def times_transposed(weight, tokens):
    return lax.dot_general(weight, tokens, (((1,), (1,)), ((), ())), preferred_element_type=F32)


def down_kernel(count, rows, slots, *refs):
    pieces, (weight, out, tokens) = refs[:count], refs[count:]
    place(slots, pieces, rows, tokens)
    part = times_transposed(weight[...], tokens[...])

    @pl.when(pl.program_id(0) == 0)
    def _():
        out[...] = part

    @pl.when(pl.program_id(0) > 0)
    def _():
        out[...] += part


def up_kernel(count, rows, slots, *refs):
    pieces = refs[:count]
    w_gate, w_up, grad_hidden, proj, left, tokens, gate, up = refs[count:]
    step = pl.program_id(0)
    place(slots, pieces, rows, tokens)
    gate_part = times_transposed(w_gate[...], tokens[...])
    up_part = times_transposed(w_up[...], tokens[...])

    @pl.when(step == 0)
    def _():
        gate[...] = gate_part
        up[...] = up_part

    @pl.when(step > 0)
    def _():
        gate[...] += gate_part
        up[...] += up_part

    @pl.when(step == pl.num_programs(0) - 1)
    def _():
        rank = left.shape[0] // 3
        gate_value, up_value, grad = gate[...], up[...], grad_hidden[...]
        s = 1.0 / (1.0 + jnp.exp(-gate_value))
        silu = gate_value * s
        hidden = (silu * up_value).astype(BF16)
        grad_gate = (grad * up_value * s * (1.0 + gate_value * (1.0 - s))).astype(BF16)
        grad_up = (grad * silu).astype(BF16)
        left[:rank, :] = jnp.dot(proj[rank : 2 * rank, :], grad_gate, preferred_element_type=F32)
        left[rank : 2 * rank, :] = jnp.dot(proj[2 * rank :, :], grad_up, preferred_element_type=F32)
        left[2 * rank :, :] = jnp.dot(proj[:rank, :], hidden, preferred_element_type=F32)


def chunk_of(width, rows):
    return min(width, 1024 if rows > 256 else 2048)


def piece_specs(pieces, chunk):
    return [pl.BlockSpec((piece.shape[0], chunk), lambda k, s: (0, k)) for piece in pieces]


def down_product(pieces, slots, weight):
    hidden, width = weight.shape
    rows = pieces[0].shape[0]
    tokens = rows * len(pieces)
    chunk = chunk_of(width, hidden)
    return pl.pallas_call(
        functools.partial(down_kernel, len(pieces), rows),
        out_shape=jax.ShapeDtypeStruct((hidden, tokens), F32),
        grid_spec=pltpu.PrefetchScalarGridSpec(
            num_scalar_prefetch=1,
            grid=(width // chunk,),
            in_specs=piece_specs(pieces, chunk)
            + [pl.BlockSpec((hidden, chunk), lambda k, s: (0, k))],
            out_specs=pl.BlockSpec((hidden, tokens), lambda k, s: (0, 0)),
            scratch_shapes=[pltpu.VMEM((tokens, chunk), BF16)],
        ),
        compiler_params=pltpu.CompilerParams(vmem_limit_bytes=40 * 2**20),
        cost_estimate=pl.CostEstimate(
            flops=2 * hidden * width * tokens, bytes_accessed=2 * hidden * width, transcendentals=0
        ),
        name="down_product",
    )(slots, *pieces, weight)


def up_product(pieces, slots, w_gate, w_up, grad_hidden, proj):
    hidden, width = w_gate.shape
    rows = pieces[0].shape[0]
    tokens = rows * len(pieces)
    chunk = chunk_of(width, hidden)
    whole = lambda shape: pl.BlockSpec(shape, lambda k, s: (0, 0))
    return pl.pallas_call(
        functools.partial(up_kernel, len(pieces), rows),
        out_shape=jax.ShapeDtypeStruct((proj.shape[0], tokens), F32),
        grid_spec=pltpu.PrefetchScalarGridSpec(
            num_scalar_prefetch=1,
            grid=(width // chunk,),
            in_specs=piece_specs(pieces, chunk)
            + [pl.BlockSpec((hidden, chunk), lambda k, s: (0, k))] * 2
            + [whole(grad_hidden.shape), whole(proj.shape)],
            out_specs=whole((proj.shape[0], tokens)),
            scratch_shapes=[
                pltpu.VMEM((tokens, chunk), BF16),
                pltpu.VMEM((hidden, tokens), F32),
                pltpu.VMEM((hidden, tokens), F32),
            ],
        ),
        compiler_params=pltpu.CompilerParams(vmem_limit_bytes=48 * 2**20),
        cost_estimate=pl.CostEstimate(
            flops=4 * hidden * width * tokens,
            bytes_accessed=4 * hidden * width,
            transcendentals=hidden * tokens,
        ),
        name="up_product",
    )(slots, *pieces, w_gate, w_up, grad_hidden, proj)


def model_columns(pieces, slots, offset, width):
    cut = jnp.stack([lax.dynamic_slice_in_dim(piece, offset, width, 1) for piece in pieces])
    order = jnp.argmax(slots[None, :] == jnp.arange(len(pieces))[:, None], axis=1)
    picks = [
        lax.dynamic_index_in_dim(cut, order[i], 0, keepdims=False) for i in range(len(pieces))
    ]
    return jnp.concatenate(picks, 0)


def on_device(
    count,
    activations,
    cotangent,
    w_gate,
    w_up,
    w_down,
    proj_model,
    proj_hidden,
    seq_ids,
    targets,
    target_domain,
):
    ring = Ring(count)
    rank = proj_model.shape[1] // 3
    model_cols = proj_model.shape[0]
    offset = ring.me * model_cols
    own_rank = -(-rank // count)
    padded_rank = own_rank * count

    inner = list(range(1, len(ring.sizes)))
    flipped = inner[:-1][::-1] + inner[-1:]
    out_pieces, out_slots = ring.gather(cotangent, inner)
    in_pieces, in_slots = ring.gather(activations, flipped)
    tokens = count * activations.shape[0]

    examples = targets.shape[0]
    cut = jnp.pad(targets, ((0, 0), (0, 0), (0, padded_rank - rank), (0, 0)))
    cut = cut.reshape(examples, 3, count, own_rank, rank).transpose(2, 0, 1, 3, 4)
    cut = cut.reshape(count, examples, 3 * own_rank * rank)
    tags = jnp.broadcast_to(target_domain.astype(BF16)[None, :, None], (count, examples, 128))
    held = exchange(jnp.concatenate([cut, tags], 2)).reshape(count * examples, -1)
    example_domain = held[:, -1].astype(jnp.int32)
    domain_onehot = (example_domain[None, :] == jnp.arange(DOMAINS)[:, None]).astype(BF16)
    domain_sum = jnp.dot(domain_onehot, held[:, :-128], preferred_element_type=F32)
    domain_count = jnp.sum(domain_onehot.astype(F32), 1)
    domain_mean = (domain_sum / domain_count[:, None]).reshape(DOMAINS, 3, own_rank, rank)

    in_columns = model_columns(in_pieces, in_slots, offset, model_cols)
    out_columns = model_columns(out_pieces, out_slots, offset, model_cols)
    proj_t = proj_model.T
    right = jnp.concatenate(
        [
            times_transposed(proj_t[: 2 * rank], in_columns),
            times_transposed(proj_t[2 * rank :], out_columns),
        ],
        0,
    ).reshape(3, rank, tokens)

    def cut_rows(values):
        values = jnp.pad(values, ((0, 0), (0, padded_rank - rank), (0, 0)))
        values = values.reshape(3, count, own_rank, tokens).transpose(1, 0, 2, 3)
        return values.reshape(count, 3 * own_rank, tokens)

    def join_rows(values):
        values = values.reshape(count, 3, own_rank, tokens).transpose(1, 0, 2, 3)
        return values.reshape(3, padded_rank, tokens)[:, :rank]

    own_right = jnp.sum(exchange(cut_rows(right)), 0)
    right = join_rows(spread(own_right, count))

    grad_hidden = down_product(out_pieces, out_slots, w_down)
    left = up_product(in_pieces, in_slots, w_gate, w_up, grad_hidden, proj_hidden.T)
    own_left = jnp.sum(exchange(cut_rows(left.reshape(3, rank, tokens))), 0)

    ids = ring.slot_order(seq_ids)
    onehot = (ids[None, :] == jnp.arange(SEQS)[:, None]).astype(F32)
    own_rows = own_left.reshape(3, 1, own_rank, tokens) * onehot[None, :, None, :]
    own_sketch = jnp.einsum("ksat,kbt->skab", own_rows, right, precision=HIGHEST)
    own_scores = jnp.einsum("skab,dkab->sd", own_sketch, domain_mean, precision=HIGHEST)

    score_rows = own_scores.reshape(-1, tokens)
    shared = spread(jnp.concatenate([own_left, score_rows], 0), count)
    left = join_rows(shared[:, : 3 * own_rank])
    total = jnp.sum(shared[:, 3 * own_rank :], 0).reshape(SEQS, DOMAINS)
    rows = left[:, None] * onehot[None, :, None, :]
    sketches = jnp.einsum("ksat,kbt->skab", rows, right, precision=HIGHEST)
    flat = sketches.reshape(SEQS, -1)
    inverse_norm = lax.rsqrt(jnp.sum(flat * flat, 1) + 1e-06)
    return sketches, total * inverse_norm[:, None]


def solution(mesh):
    in_specs = (
        P(("groups", "dp"), None),
        P(("groups", "dp"), None),
        P("dp", None),
        P("dp", None),
        P("dp", None),
        P("dp", None),
        P("dp", None),
        P("groups"),
        P(("groups", "dp"), None, None, None),
        P(("groups", "dp")),
    )
    out_specs = (P("groups", None, None, None), P("groups", None))
    return jax.shard_map(
        functools.partial(on_device, mesh.shape["dp"]),
        mesh=mesh,
        in_specs=in_specs,
        out_specs=out_specs,
        check_vma=False,
    )
```

time: 478 us -> 162 us (0.34)
  waiting for transfers between devices: 373 us -> 35.1 us
  starting transfers between devices: 0.34 us -> 37.4 us
  matrix products: 38.8 us -> 5.55 us
  blocking collectives: 39.3 us -> 12.3 us
  Pallas kernels: 0 us -> 26.8 us
  between operations: 13.9 us -> 31.2 us
    psum x1 -> x0, waiting for transfers between devices: 133 us -> none  [on_device(): sketches = lax.psum(local_sketch, 'dp')]
    unnamed x5 -> x0, waiting for transfers between devices: 123 us -> none
    all_gather x2 -> x0, waiting for transfers between devices: 116 us -> none  [the longest x1 60.5 us: on_device(): rows_in = lax.all_gather(activations, 'dp', axis=0, tiled=True)]
    psum x1 -> x0, blocking collectives: 39.3 us -> none  [on_device(): total_scores, total_count = lax.psum((folded, domain_count), 'dp')]
    dot_general x11 -> x6, matrix products: 38.8 us -> 5.55 us  [the longest x1 4.72 us: on_device(): sketches = jnp.einsum('ksat,kbt->skab', rows, right, precision=HIGHEST)]
    pallas_call x0 -> x2, Pallas kernels: none -> 26.8 us  [the longest x1 16.1 us: up_product(): pl.pallas_call(functools.partial(up_kernel, len(pieces), rows), out_shape...]
    ppermute x0 -> x20, starting transfers between devices: none -> 21.9 us  [shift(): return lax.ppermute(value, 'dp', pairs)]
    ppermute x0 -> x20, waiting for transfers between devices: none -> 19.3 us  [shift(): return lax.ppermute(value, 'dp', pairs)]
  transfers between devices with their start and end apart: 4 -> 24, of which waited for: 4 -> 9; matrix products, arithmetic and copies ran while one was open for 1% -> 6% of each run, Pallas kernels for 0% -> 17%
where the time goes in v1:
time: 162 us; the launch traced here: 161 us
  starting transfers between devices  37.4 us (23%)
  waiting for transfers between devices  35.1 us (22%)
  between operations  31.2 us (19%)
  Pallas kernels  26.8 us (17%)
  blocking collectives  12.3 us (8%)
  local copies, waits for them, and re-layouts  7.97 us (5%)
  matrix products  5.55 us (3%)
  other arithmetic  4.42 us (3%)
    ppermute x20, starting transfers between devices, shift(): return lax.ppermute(value, 'dp', pairs)  21.9 us
    ppermute x20, waiting for transfers between devices, shift(): return lax.ppermute(value, 'dp', pairs)  19.3 us
    pallas_call x1, Pallas kernels, up_product(): pl.pallas_call(functools.partial(up_kernel, len(pieces), rows), out_shape...  16.1 us
    all_to_all x4, waiting for transfers between devices, exchange(): return lax.all_to_all(blocks, 'dp', split_axis=0, concat_axis=0, tiled=True)  15.8 us
    all_to_all x4, starting transfers between devices, exchange(): return lax.all_to_all(blocks, 'dp', split_axis=0, concat_axis=0, tiled=True)  15.5 us
    all_to_all x1, blocking collectives, exchange(): return lax.all_to_all(blocks, 'dp', split_axis=0, concat_axis=0, tiled=True)  12.3 us
    pallas_call x1, Pallas kernels, down_product(): pl.pallas_call(functools.partial(down_kernel, len(pieces), rows), out_sha...  10.7 us
    dot_general x1, matrix products, on_device(): sketches = jnp.einsum('ksat,kbt->skab', rows, right, precision=HIGHEST)  4.72 us
  transfers between devices with their start and end apart: 24, of which 9 were waited for; matrix products, arithmetic and copies ran while one was open for 6% of the time, Pallas kernels for 17%

profile of v1, /device:TPU:0, one launch (start us, length us, event | category | flops | bytes accessed | tf_op | source)
XLA Modules:
  0.0 160.8 jit_solution(4771471741334343919)
XLA Ops:
  0.6 3.1 %collective-permute-start = (bf16[4,8192]{1,0:T(4,128)(2,1)}, bf16[4,8192]{1,0:T(4,128)(2,1)S(1)}, u32[]{:S(2)}, u32[]{:S(2)}) collective-permute-start(bf16[4,8192]{1,0:T(4,128)(2,1)} %param.10), channel_id=1, source_target_pairs={{0,8},{1,9},{2,10},{3,11},{4,12},{5,13},{6,14},{7,15},{8,16},{9,17... | collective-permute-start | bytes 196616 | tf_op jit(solution)/shard_map/ppermute | solution.py:42
  3.7 2.6 %collective-permute-start.1 = (bf16[4,8192]{1,0:T(4,128)(2,1)}, bf16[4,8192]{1,0:T(4,128)(2,1)S(1)}, u32[]{:S(2)}, u32[]{:S(2)}) collective-permute-start(bf16[4,8192]{1,0:T(4,128)(2,1)} %param.10), channel_id=1, source_target_pairs={{0,16},{1,17},{2,18},{3,19},{4,20},{5,21},{6,22},{7,23},{8,24},{9,... | collective-permute-start | bytes 196616 | tf_op jit(solution)/shard_map/ppermute | solution.py:42
  6.4 1.8 %collective-permute-start.11 = (bf16[4,8192]{1,0:T(4,128)(2,1)}, bf16[4,8192]{1,0:T(4,128)(2,1)S(1)}, u32[]{:S(2)}, u32[]{:S(2)}) collective-permute-start(bf16[4,8192]{1,0:T(4,128)(2,1)} %param.11), channel_id=1, source_target_pairs={{0,16},{1,17},{2,18},{3,19},{4,20},{5,21},{6,22},{7,23},{8,24},{9,... | collective-permute-start | bytes 196616 | tf_op jit(solution)/shard_map/ppermute | solution.py:42
  8.2 1.9 %collective-permute-start.12 = (bf16[4,8192]{1,0:T(4,128)(2,1)}, bf16[4,8192]{1,0:T(4,128)(2,1)S(1)}, u32[]{:S(2)}, u32[]{:S(2)}) collective-permute-start(bf16[4,8192]{1,0:T(4,128)(2,1)} %param.11), channel_id=1, source_target_pairs={{0,24},{1,25},{2,26},{3,27},{4,28},{5,29},{6,30},{7,31},{8,0},{9,1... | collective-permute-start | bytes 196616 | tf_op jit(solution)/shard_map/ppermute | solution.py:42
  10.1 0.7 convert_element_type.27
  10.8 1.3 copy.69
  12.1 0.3 reshape.103
  12.4 0.7 pad_maximum_fusion.2
  13.2 4.3 %all-to-all-start.3 = ((bf16[32,8,512]{2,1,0:T(8,128)(2,1)}), bf16[32,8,512]{2,1,0:T(8,128)(2,1)S(1)}, u32[]{:S(2)}, u32[]{:S(2)}) async-start(bf16[32,8,512]{2,1,0:T(8,128)(2,1)} %pad_maximum_fusion.2), calls=%async_computation.3 | async-start | bytes 524288 | tf_op jit(solution)/shard_map/all_to_all | solution.py:75
  17.9 0.6 iota_reduce_fusion
  18.5 0.7 fusion.18
  29.2 0.7 iota_reduce_fusion.1
  30.1 0.7 fusion.17
  50.7 3.7 %collective-permute-start.2 = (bf16[4,8192]{1,0:T(4,128)(2,1)S(1)}, bf16[4,8192]{1,0:T(4,128)(2,1)S(1)}, u32[]{:S(2)}, u32[]{:S(2)}) collective-permute-start(bf16[4,8192]{1,0:T(4,128)(2,1)S(1)} %copy-done.3), channel_id=1, source_target_pairs={{0,24},{1,25},{2,26},{3,27},{4,28},{5,29},{6,30},{7,31},{8,0},{9,1... | collective-permute-start | bytes 196616 | tf_op jit(solution)/shard_map/ppermute | solution.py:42
  54.4 0.2 select_select_fusion.3
  54.7 1.5 collective-permute-start.14
  56.2 1.5 collective-permute-start.13
  57.7 0.2 select_select_fusion.7
  58.1 0.6 collective-permute-start.3
  58.7 0.5 collective-permute-start.6
  59.2 4.8 %collective-permute-done.13.refs_1_ = bf16[16,8192]{1,0:T(8,128)(2,1)S(1)} collective-permute-done((bf16[16,8192]{1,0:T(8,128)(2,1)S(1)}, bf16[16,8192]{1,0:T(8,128)(2,1)S(1)}, u32[]{:S(2)}, u32[]{:S(2)}) %collective-permute-start.13) | collective-permute-done | bytes 262176 | tf_op jit(solution)/shard_map/ppermute | solution.py:42
  64.0 1.5 collective-permute-start.4
  65.5 0.5 collective-permute-start.15
  66.1 3.5 %collective-permute-done.3.refs_1_ = bf16[16,8192]{1,0:T(8,128)(2,1)S(1)} collective-permute-done((bf16[16,8192]{1,0:T(8,128)(2,1)S(1)}, bf16[16,8192]{1,0:T(8,128)(2,1)S(1)}, u32[]{:S(2)}, u32[]{:S(2)}) %collective-permute-start.3) | collective-permute-done | bytes 262176 | tf_op jit(solution)/shard_map/ppermute | solution.py:42
  69.6 1.4 collective-permute-done.4.refs_2_
  70.9 3.1 %collective-permute-done.15.refs_3_ = bf16[16,8192]{1,0:T(8,128)(2,1)S(1)} collective-permute-done((bf16[16,8192]{1,0:T(8,128)(2,1)S(1)}, bf16[16,8192]{1,0:T(8,128)(2,1)S(1)}, u32[]{:S(2)}, u32[]{:S(2)}) %collective-permute-start.15) | collective-permute-done | bytes 262176 | tf_op jit(solution)/shard_map/ppermute | solution.py:42
  74.1 1.5 collective-permute-start.5
  75.6 0.5 collective-permute-start.7
  76.1 5.2 %collective-permute-done.5.refs_3_ = bf16[16,8192]{1,0:T(8,128)(2,1)S(1)} collective-permute-done((bf16[16,8192]{1,0:T(8,128)(2,1)S(1)}, bf16[16,8192]{1,0:T(8,128)(2,1)S(1)}, u32[]{:S(2)}, u32[]{:S(2)}) %collective-permute-start.5) | collective-permute-done | bytes 262176 | tf_op jit(solution)/shard_map/ppermute | solution.py:42
  81.3 0.5 collective-permute-start.9
  81.9 0.9 collective-permute-done.19.refs_7_
  82.8 0.4 collective-permute-done.9.refs_7_
  83.8 0.7 copy.48
  84.5 10.7 %down_product.1.refs_10_ = f32[896,128]{1,0:T(8,128)S(1)} custom-call(s32[8]{0:T(128)S(1)} %stack.119.slots, bf16[16,8192]{1,0:T(8,128)(2,1)S(1)} %pad_maximum_fusion.1.refs_0_, bf16[16,8192]{1,0:T(8,128)(2,1)S(1)} %collective-permute-done.13.refs_1_, bf16[16,8192]{1,0:T(8,128)(2,1)S(1)} %collective-permute-done.14.refs_2_, ...), custom_call_target="tpu_custom_call" | custom-call | flops 1879048192 | bytes 14680064 | tf_op jit(solution)/shard_map/down_product/pallas_call | solution.py:151
  95.2 2.8 %all-to-all-start = ((f32[32,6,128]{2,1,0:T(8,128)}), f32[32,6,128]{2,1,0:T(8,128)S(1)}, u32[]{:S(2)}, u32[]{:S(2)}) async-start(f32[32,6,128]{2,1,0:T(8,128)} %copy.48), calls=%async_computation | async-start | bytes 262144 | tf_op jit(solution)/shard_map/all_to_all | solution.py:75
  98.1 16.1 %up_product.1 = f32[192,128]{1,0:T(8,128)S(1)} custom-call(s32[8]{0:T(128)S(1)} %stack.109.slots, bf16[16,8192]{1,0:T(8,128)(2,1)S(1)} %pad_maximum_fusion.refs_0_, bf16[16,8192]{1,0:T(8,128)(2,1)S(1)} %collective-permute-done.3.refs_1_, bf16[16,8192]{1,0:T(8,128)(2,1)S(1)} %collective-permute-done.4.refs_2_, ...), custom_call_target="tpu_custom_call" | custom-call | flops 3758096384 | bytes 29360128 | tf_op jit(solution)/shard_map/up_product/pallas_call | solution.py:176
  114.2 0.7 copy.52
  114.9 5.9 %all-to-all-start.2 = ((f32[32,6,128]{2,1,0:T(8,128)}), f32[32,6,128]{2,1,0:T(8,128)S(1)}, u32[]{:S(2)}, u32[]{:S(2)}) async-start(f32[32,6,128]{2,1,0:T(8,128)} %copy.52), calls=%async_computation.2 | async-start | bytes 262144 | tf_op jit(solution)/shard_map/all_to_all | solution.py:75
  121.1 7.9 %all-to-all-done.2 = f32[32,6,128]{2,1,0:T(8,128)S(1)} async-done(((f32[32,6,128]{2,1,0:T(8,128)}), f32[32,6,128]{2,1,0:T(8,128)S(1)}, u32[]{:S(2)}, u32[]{:S(2)}) %all-to-all-start.2) | async-done | bytes 98336 | tf_op jit(solution)/shard_map/all_to_all | solution.py:75
  129.0 0.7 broadcast_in_dim.6
  129.7 2.6 %all-to-all-start.1 = ((f32[32,6,128]{2,1,0:T(8,128)}), f32[32,6,128]{2,1,0:T(8,128)S(1)}, u32[]{:S(2)}, u32[]{:S(2)}) async-start(f32[32,6,128]{2,1,0:T(8,128)} %broadcast_in_dim.6), calls=%async_computation.1 | async-start | bytes 262144 | tf_op jit(solution)/shard_map/all_to_all | solution.py:75
  132.6 7.9 %all-to-all-done.1 = f32[32,6,128]{2,1,0:T(8,128)S(1)} async-done(((f32[32,6,128]{2,1,0:T(8,128)}), f32[32,6,128]{2,1,0:T(8,128)S(1)}, u32[]{:S(2)}, u32[]{:S(2)}) %all-to-all-start.1) | async-done | bytes 98336 | tf_op jit(solution)/shard_map/all_to_all | solution.py:75
  140.6 0.3 convolution_bitcast_fusion.1
  140.9 0.2 convolution_bitcast_fusion.3
  141.2 12.3 %all_to_all.25 = f32[32,10,128]{2,1,0:T(8,128)S(1)} all-to-all(f32[32,10,128]{2,1,0:T(8,128)S(1)} %broadcast_in_dim.8), channel_id=1, replica_groups=mesh['groups'=1,'dp'=32] {'dp'}, dimensions={0} | all-to-all | bytes 327680 | tf_op jit(solution)/shard_map/all_to_all | solution.py:75
  153.8 4.7 %multiply_reduce_fusion = (f32[16]{0:T(128)S(1)}, f32[16,3,64,64]{2,3,0,1:T(8,128)S(1)}) fusion(f32[3,64,128,1]{2,1,3,0:T(8,128)S(1)} %bitcast.138, f32[16,128]{1,0:T(8,128)S(1)} %fusion.16, f32[3,64,128]{2,1,0:T(8,128)S(1)} %bitcast.147), kind=kOutput, calls=%fused_computation | convolution fusion | flops 302776320 | bytes 991296 | tf_op jit(solution)/shard_map/ksat,kbt->skab/dot_general | solution.py:287
  158.5 1.6 %copy.60 = f32[16,3,64,64]{3,2,1,0:T(8,128)} copy(f32[16,3,64,64]{2,3,0,1:T(8,128)S(1)} %get-tuple-element.41) | data formatting | bytes 1572864
  160.1 0.7 broadcast_multiply_fusion
  (96 shorter events, 2.6 us)
Async XLA Ops:
  0.6 29.2 %copy-start.4 = (s32[128]{0:T(128)S(1)}, s32[128]{0:T(128)}, u32[]{:S(2)}) copy-start(s32[128]{0:T(128)} %param.17) | copy-start | bytes 1540
  0.6 57.1 %collective-permute-start = (bf16[4,8192]{1,0:T(4,128)(2,1)}, bf16[4,8192]{1,0:T(4,128)(2,1)S(1)}, u32[]{:S(2)}, u32[]{:S(2)}) collective-permute-start(bf16[4,8192]{1,0:T(4,128)(2,1)} %param.10), channel_id=1, source_target_pairs={{0,8},{1,9},{2,10},{3,11},{4,12},{5,13},{6,14},{7,15},{8,16},{9,17... | collective-permute-start | bytes 196616 | tf_op jit(solution)/shard_map/ppermute | solution.py:42
  3.7 54.0 %collective-permute-start.1 = (bf16[4,8192]{1,0:T(4,128)(2,1)}, bf16[4,8192]{1,0:T(4,128)(2,1)S(1)}, u32[]{:S(2)}, u32[]{:S(2)}) collective-permute-start(bf16[4,8192]{1,0:T(4,128)(2,1)} %param.10), channel_id=1, source_target_pairs={{0,16},{1,17},{2,18},{3,19},{4,20},{5,21},{6,22},{7,23},{8,24},{9,... | collective-permute-start | bytes 196616 | tf_op jit(solution)/shard_map/ppermute | solution.py:42
  6.3 44.3 %collective-permute-start.10 = (bf16[4,8192]{1,0:T(4,128)(2,1)}, bf16[4,8192]{1,0:T(4,128)(2,1)S(1)}, u32[]{:S(2)}, u32[]{:S(2)}) collective-permute-start(bf16[4,8192]{1,0:T(4,128)(2,1)} %param.11), channel_id=1, source_target_pairs={{0,8},{1,9},{2,10},{3,11},{4,12},{5,13},{6,14},{7,15},{8,16},{9,17... | collective-permute-start | bytes 196616 | tf_op jit(solution)/shard_map/ppermute | solution.py:42
  6.4 48.0 %collective-permute-start.11 = (bf16[4,8192]{1,0:T(4,128)(2,1)}, bf16[4,8192]{1,0:T(4,128)(2,1)S(1)}, u32[]{:S(2)}, u32[]{:S(2)}) collective-permute-start(bf16[4,8192]{1,0:T(4,128)(2,1)} %param.11), channel_id=1, source_target_pairs={{0,16},{1,17},{2,18},{3,19},{4,20},{5,21},{6,22},{7,23},{8,24},{9,... | collective-permute-start | bytes 196616 | tf_op jit(solution)/shard_map/ppermute | solution.py:42
  8.2 46.1 %collective-permute-start.12 = (bf16[4,8192]{1,0:T(4,128)(2,1)}, bf16[4,8192]{1,0:T(4,128)(2,1)S(1)}, u32[]{:S(2)}, u32[]{:S(2)}) collective-permute-start(bf16[4,8192]{1,0:T(4,128)(2,1)} %param.11), channel_id=1, source_target_pairs={{0,24},{1,25},{2,26},{3,27},{4,28},{5,29},{6,30},{7,31},{8,0},{9,1... | collective-permute-start | bytes 196616 | tf_op jit(solution)/shard_map/ppermute | solution.py:42
  10.8 39.9 %copy-start.3 = (bf16[4,8192]{1,0:T(4,128)(2,1)S(1)}, bf16[4,8192]{1,0:T(4,128)(2,1)}, u32[]{:S(2)}) copy-start(bf16[4,8192]{1,0:T(4,128)(2,1)} %param.10) | copy-start | bytes 196612
  10.8 43.6 %copy-start.2 = (bf16[4,8192]{1,0:T(4,128)(2,1)S(1)}, bf16[4,8192]{1,0:T(4,128)(2,1)}, u32[]{:S(2)}) copy-start(bf16[4,8192]{1,0:T(4,128)(2,1)} %param.11) | copy-start | bytes 196612
  13.2 82.0 %all-to-all-start.3 = ((bf16[32,8,512]{2,1,0:T(8,128)(2,1)}), bf16[32,8,512]{2,1,0:T(8,128)(2,1)S(1)}, u32[]{:S(2)}, u32[]{:S(2)}) async-start(bf16[32,8,512]{2,1,0:T(8,128)(2,1)} %pad_maximum_fusion.2), calls=%async_computation.3 | async-start | bytes 524288 | tf_op jit(solution)/shard_map/all_to_all | solution.py:75
  17.5 65.8 %copy-start.1 = (bf16[256,192]{0,1:T(8,128)(2,1)S(1)}, bf16[256,192]{0,1:T(8,128)(2,1)}, u32[]{:S(2)}) copy-start(bf16[256,192]{0,1:T(8,128)(2,1)} %param.15) | copy-start | bytes 294916
  50.7 7.1 %collective-permute-start.2 = (bf16[4,8192]{1,0:T(4,128)(2,1)S(1)}, bf16[4,8192]{1,0:T(4,128)(2,1)S(1)}, u32[]{:S(2)}, u32[]{:S(2)}) collective-permute-start(bf16[4,8192]{1,0:T(4,128)(2,1)S(1)} %copy-done.3), channel_id=1, source_target_pairs={{0,24},{1,25},{2,26},{3,27},{4,28},{5,29},{6,30},{7,31},{8,0},{9,1... | collective-permute-start | bytes 196616 | tf_op jit(solution)/shard_map/ppermute | solution.py:42
  54.7 10.8 %collective-permute-start.14 = (bf16[16,8192]{1,0:T(8,128)(2,1)S(1)}, bf16[16,8192]{1,0:T(8,128)(2,1)S(1)}, u32[]{:S(2)}, u32[]{:S(2)}) collective-permute-start(bf16[16,8192]{1,0:T(8,128)(2,1)S(1)} %pad_maximum_fusion.1.refs_0_), channel_id=1, source_target_pairs={{0,2},{1,3},{2,0},{3,1},{4,6},{5,7},{6,4},{7,5},{8,10},{9,11},{10,... | collective-permute-start | bytes 786440 | tf_op jit(solution)/shard_map/ppermute | solution.py:42
  56.2 7.8 %collective-permute-start.13 = (bf16[16,8192]{1,0:T(8,128)(2,1)S(1)}, bf16[16,8192]{1,0:T(8,128)(2,1)S(1)}, u32[]{:S(2)}, u32[]{:S(2)}) collective-permute-start(bf16[16,8192]{1,0:T(8,128)(2,1)S(1)} %pad_maximum_fusion.1.refs_0_), channel_id=1, source_target_pairs={{0,4},{1,5},{2,6},{3,7},{4,0},{5,1},{6,2},{7,3},{8,12},{9,13},{10,... | collective-permute-start | bytes 786440 | tf_op jit(solution)/shard_map/ppermute | solution.py:42
  58.1 11.5 %collective-permute-start.3 = (bf16[16,8192]{1,0:T(8,128)(2,1)S(1)}, bf16[16,8192]{1,0:T(8,128)(2,1)S(1)}, u32[]{:S(2)}, u32[]{:S(2)}) collective-permute-start(bf16[16,8192]{1,0:T(8,128)(2,1)S(1)} %pad_maximum_fusion.refs_0_), channel_id=1, source_target_pairs={{0,2},{1,3},{2,0},{3,1},{4,6},{5,7},{6,4},{7,5},{8,10},{9,11},{10,... | collective-permute-start | bytes 786440 | tf_op jit(solution)/shard_map/ppermute | solution.py:42
  58.7 16.9 %collective-permute-start.16 = (bf16[16,8192]{1,0:T(8,128)(2,1)S(1)}, bf16[16,8192]{1,0:T(8,128)(2,1)S(1)}, u32[]{:S(2)}, u32[]{:S(2)}) collective-permute-start(bf16[16,8192]{1,0:T(8,128)(2,1)S(1)} %pad_maximum_fusion.1.refs_0_), channel_id=1, source_target_pairs={{0,1},{1,0},{2,3},{3,2},{4,5},{5,4},{6,7},{7,6},{8,9},{9,8},{10,11... | collective-permute-start | bytes 786440 | tf_op jit(solution)/shard_map/ppermute | solution.py:42
  58.7 23.1 %collective-permute-start.6 = (bf16[16,8192]{1,0:T(8,128)(2,1)S(1)}, bf16[16,8192]{1,0:T(8,128)(2,1)S(1)}, u32[]{:S(2)}, u32[]{:S(2)}) collective-permute-start(bf16[16,8192]{1,0:T(8,128)(2,1)S(1)} %pad_maximum_fusion.refs_0_), channel_id=1, source_target_pairs={{0,1},{1,0},{2,3},{3,2},{4,5},{5,4},{6,7},{7,6},{8,9},{9,8},{10,11... | collective-permute-start | bytes 786440 | tf_op jit(solution)/shard_map/ppermute | solution.py:42
  64.0 6.9 %collective-permute-start.4 = (bf16[16,8192]{1,0:T(8,128)(2,1)S(1)}, bf16[16,8192]{1,0:T(8,128)(2,1)S(1)}, u32[]{:S(2)}, u32[]{:S(2)}) collective-permute-start(bf16[16,8192]{1,0:T(8,128)(2,1)S(1)} %pad_maximum_fusion.refs_0_), channel_id=1, source_target_pairs={{0,4},{1,5},{2,6},{3,7},{4,0},{5,1},{6,2},{7,3},{8,12},{9,13},{10,... | collective-permute-start | bytes 786440 | tf_op jit(solution)/shard_map/ppermute | solution.py:42
  65.5 8.5 %collective-permute-start.15 = (bf16[16,8192]{1,0:T(8,128)(2,1)S(1)}, bf16[16,8192]{1,0:T(8,128)(2,1)S(1)}, u32[]{:S(2)}, u32[]{:S(2)}) collective-permute-start(bf16[16,8192]{1,0:T(8,128)(2,1)S(1)} %collective-permute-done.13.refs_1_), channel_id=1, source_target_pairs={{0,2},{1,3},{2,0},{3,1},{4,6},{5,7},{6,4},{7,5},{8,10},{9,11},{10,... | collective-permute-start | bytes 786440 | tf_op jit(solution)/shard_map/ppermute | solution.py:42
  69.6 11.7 %collective-permute-start.18 = (bf16[16,8192]{1,0:T(8,128)(2,1)S(1)}, bf16[16,8192]{1,0:T(8,128)(2,1)S(1)}, u32[]{:S(2)}, u32[]{:S(2)}) collective-permute-start(bf16[16,8192]{1,0:T(8,128)(2,1)S(1)} %collective-permute-done.14.refs_2_), channel_id=1, source_target_pairs={{0,1},{1,0},{2,3},{3,2},{4,5},{5,4},{6,7},{7,6},{8,9},{9,8},{10,11... | collective-permute-start | bytes 786440 | tf_op jit(solution)/shard_map/ppermute | solution.py:42
  70.9 4.7 %collective-permute-start.17 = (bf16[16,8192]{1,0:T(8,128)(2,1)S(1)}, bf16[16,8192]{1,0:T(8,128)(2,1)S(1)}, u32[]{:S(2)}, u32[]{:S(2)}) collective-permute-start(bf16[16,8192]{1,0:T(8,128)(2,1)S(1)} %collective-permute-done.13.refs_1_), channel_id=1, source_target_pairs={{0,1},{1,0},{2,3},{3,2},{4,5},{5,4},{6,7},{7,6},{8,9},{9,8},{10,11... | collective-permute-start | bytes 786440 | tf_op jit(solution)/shard_map/ppermute | solution.py:42
  74.1 7.2 %collective-permute-start.5 = (bf16[16,8192]{1,0:T(8,128)(2,1)S(1)}, bf16[16,8192]{1,0:T(8,128)(2,1)S(1)}, u32[]{:S(2)}, u32[]{:S(2)}) collective-permute-start(bf16[16,8192]{1,0:T(8,128)(2,1)S(1)} %collective-permute-done.3.refs_1_), channel_id=1, source_target_pairs={{0,4},{1,5},{2,6},{3,7},{4,0},{5,1},{6,2},{7,3},{8,12},{9,13},{10,... | collective-permute-start | bytes 786440 | tf_op jit(solution)/shard_map/ppermute | solution.py:42
  75.6 6.3 %collective-permute-start.8 = (bf16[16,8192]{1,0:T(8,128)(2,1)S(1)}, bf16[16,8192]{1,0:T(8,128)(2,1)S(1)}, u32[]{:S(2)}, u32[]{:S(2)}) collective-permute-start(bf16[16,8192]{1,0:T(8,128)(2,1)S(1)} %collective-permute-done.4.refs_2_), channel_id=1, source_target_pairs={{0,1},{1,0},{2,3},{3,2},{4,5},{5,4},{6,7},{7,6},{8,9},{9,8},{10,11... | collective-permute-start | bytes 786440 | tf_op jit(solution)/shard_map/ppermute | solution.py:42
  75.6 6.2 %collective-permute-start.7 = (bf16[16,8192]{1,0:T(8,128)(2,1)S(1)}, bf16[16,8192]{1,0:T(8,128)(2,1)S(1)}, u32[]{:S(2)}, u32[]{:S(2)}) collective-permute-start(bf16[16,8192]{1,0:T(8,128)(2,1)S(1)} %collective-permute-done.3.refs_1_), channel_id=1, source_target_pairs={{0,1},{1,0},{2,3},{3,2},{4,5},{5,4},{6,7},{7,6},{8,9},{9,8},{10,11... | collective-permute-start | bytes 786440 | tf_op jit(solution)/shard_map/ppermute | solution.py:42
  81.3 1.5 collective-permute-start.19
  81.3 1.9 %collective-permute-start.9 = (bf16[16,8192]{1,0:T(8,128)(2,1)S(1)}, bf16[16,8192]{1,0:T(8,128)(2,1)S(1)}, u32[]{:S(2)}, u32[]{:S(2)}) collective-permute-start(bf16[16,8192]{1,0:T(8,128)(2,1)S(1)} %collective-permute-done.5.refs_3_), channel_id=1, source_target_pairs={{0,1},{1,0},{2,3},{3,2},{4,5},{5,4},{6,7},{7,6},{8,9},{9,8},{10,11... | collective-permute-start | bytes 786440 | tf_op jit(solution)/shard_map/ppermute | solution.py:42
  84.5 13.5 %copy-start = (bf16[896,192]{0,1:T(8,128)(2,1)S(1)}, bf16[896,192]{0,1:T(8,128)(2,1)}, u32[]{:S(2)}) copy-start(bf16[896,192]{0,1:T(8,128)(2,1)} %param.16) | copy-start | bytes 1032196
  95.2 19.7 %all-to-all-start = ((f32[32,6,128]{2,1,0:T(8,128)}), f32[32,6,128]{2,1,0:T(8,128)S(1)}, u32[]{:S(2)}, u32[]{:S(2)}) async-start(f32[32,6,128]{2,1,0:T(8,128)} %copy.48), calls=%async_computation | async-start | bytes 262144 | tf_op jit(solution)/shard_map/all_to_all | solution.py:75
  114.9 14.1 %all-to-all-start.2 = ((f32[32,6,128]{2,1,0:T(8,128)}), f32[32,6,128]{2,1,0:T(8,128)S(1)}, u32[]{:S(2)}, u32[]{:S(2)}) async-start(f32[32,6,128]{2,1,0:T(8,128)} %copy.52), calls=%async_computation.2 | async-start | bytes 262144 | tf_op jit(solution)/shard_map/all_to_all | solution.py:75
  129.7 10.8 %all-to-all-start.1 = ((f32[32,6,128]{2,1,0:T(8,128)}), f32[32,6,128]{2,1,0:T(8,128)S(1)}, u32[]{:S(2)}, u32[]{:S(2)}) async-start(f32[32,6,128]{2,1,0:T(8,128)} %broadcast_in_dim.6), calls=%async_computation.1 | async-start | bytes 262144 | tf_op jit(solution)/shard_map/all_to_all | solution.py:75

commit v2 on v0

v2 whole, which is shorter than its diff:
```python
import functools

import jax
import jax.numpy as jnp
import numpy as np
from jax import lax
from jax.experimental import pallas as pl
from jax.experimental.pallas import tpu as pltpu
from jax.sharding import PartitionSpec as P

DOMAINS = 32
SEQS = 16
GROUP = 8
HIGHEST = lax.Precision.HIGHEST
F32 = jnp.float32
BF16 = jnp.bfloat16
VMEM = pl.BlockSpec(memory_space=pltpu.VMEM)


def axis_sizes(count):
    if count == 32:
        return (4, 2, 2, 2)
    if count == 128:
        return (8, 8, 2)
    return (count,)


def strides_of(sizes):
    return [int(np.prod(sizes[i + 1 :])) for i in range(len(sizes))]


def shift(value, sizes, axis, amount):
    size, stride = sizes[axis], strides_of(sizes)[axis]
    pairs = []
    for source in range(int(np.prod(sizes))):
        at = (source // stride) % size
        pairs.append((source, source + ((at + amount) % size - at) * stride))
    return lax.ppermute(value, "dp", pairs)


def gather_first(rows, sizes):
    size = sizes[0]
    rest = int(np.prod(sizes)) // size
    groups = [[r + z * rest for z in range(size)] for r in range(rest)]
    copies = jnp.broadcast_to(rows[None], (size,) + rows.shape)
    return lax.all_to_all(
        copies, "dp", split_axis=0, concat_axis=0, axis_index_groups=groups, tiled=True
    )


def gather_rest(block, sizes, order):
    pieces = [(block, tuple(0 for _ in sizes))]
    for axis in order:
        grown = list(pieces)
        for k in range(1, sizes[axis]):
            for piece, back in pieces:
                moved = tuple(k if i == axis else b for i, b in enumerate(back))
                grown.append((shift(piece, sizes, axis, k), moved))
        pieces = grown
    return [piece for piece, _ in pieces], [back for _, back in pieces]


def slot_order(per_token, sizes):
    rest = int(np.prod(sizes)) // sizes[0]
    each = per_token.shape[0] // (sizes[0] * rest)
    split = per_token.reshape((sizes[0], rest, each) + per_token.shape[1:])
    return jnp.swapaxes(split, 0, 1).reshape(per_token.shape)


def exchange(blocks):
    return lax.all_to_all(blocks, "dp", split_axis=0, concat_axis=0, tiled=True)


def transposed_dot(left, right, precision=None):
    return lax.dot_general(
        left, right, (((1,), (1,)), ((), ())), precision=precision, preferred_element_type=F32
    )


def place_pieces(pieces, backs, sizes, into):
    me = lax.axis_index("dp")
    strides = strides_of(sizes)
    rows = pieces[0].shape[0] // 2
    for piece, back in zip(pieces, backs):
        slot = 0
        for axis in range(1, len(sizes)):
            at = lax.rem(lax.div(me, strides[axis]), sizes[axis])
            slot = slot * sizes[axis] + lax.rem(at + sizes[axis] - back[axis], sizes[axis])
        start = pl.multiple_of(slot * rows, rows)
        for side in range(2):
            into[side, pl.ds(start, rows), :] = piece[side * rows : (side + 1) * rows, :]


def stream_products(weights, first, tokens, sums, buffers, arrived):
    chunk = buffers.shape[3]
    steps = tokens.shape[2] // chunk
    sides = (1, 0, 0)

    def copy(step, w):
        slot = lax.rem(step, 2)
        columns = pl.ds(pl.multiple_of(first + step * chunk, chunk), chunk)
        return pltpu.make_async_copy(
            weights[w].at[:, columns], buffers.at[slot, w], arrived.at[slot, w]
        )

    def fetch():
        for step in range(min(2, steps)):
            for w in range(3):
                copy(step, w).start()

    def run():
        @pl.loop(0, steps)
        def _(step):
            columns = pl.ds(pl.multiple_of(step * chunk, chunk), chunk)
            for w in range(3):
                copy(step, w).wait()
                sums[w] += transposed_dot(
                    buffers[lax.rem(step, 2), w], tokens[sides[w], :, columns]
                )

                @pl.when(step + 2 < steps)
                def _():
                    copy(step + 2, w).start()

    return fetch, run


def first_half_kernel(backs, sizes, *refs):
    pieces, refs = refs[: len(backs)], refs[len(backs) :]
    w_down, w_gate, w_up, sums, tokens, buffers, arrived = refs
    fetch, run = stream_products((w_down, w_gate, w_up), 0, tokens, sums, buffers, arrived)
    fetch()
    place_pieces(pieces, backs, sizes, tokens)
    sums[...] = jnp.zeros_like(sums)
    run()


def second_half_kernel(backs, sizes, *refs):
    pieces, refs = refs[: len(backs)], refs[len(backs) :]
    before, proj, w_down, w_gate, w_up, left, sums, tokens, stacked, buffers, arrived = refs
    first = tokens.shape[2]
    fetch, run = stream_products((w_down, w_gate, w_up), first, tokens, sums, buffers, arrived)
    fetch()
    place_pieces(pieces, backs, sizes, tokens)
    sums[...] = before[...]
    run()
    hidden_units = sums.shape[1]
    tile = 128 if hidden_units % 128 == 0 else 32

    @pl.loop(0, hidden_units // tile)
    def _(step):
        rows = pl.ds(pl.multiple_of(step * tile, tile), tile)
        grad, gate_value, up_value = sums[0, rows, :], sums[1, rows, :], sums[2, rows, :]
        s = 1.0 / (1.0 + jnp.exp(-gate_value))
        silu = gate_value * s
        stacked[0, rows, :] = (
            grad * up_value * s * (1.0 + gate_value * (1.0 - s))
        ).astype(BF16)
        stacked[1, rows, :] = (grad * silu).astype(BF16)
        stacked[2, rows, :] = (silu * up_value).astype(BF16)

    left[...] = sum(
        jnp.dot(proj[k], stacked[k], preferred_element_type=F32) for k in range(3)
    ).reshape(left.shape)


def products(pieces, backs, sizes, weights, before=None, proj=None):
    w_down, w_gate, w_up = weights
    hidden, width = w_gate.shape
    rows, half = pieces[0].shape
    tokens = rows // 2 * len(pieces)
    chunk = min(half, 1024)
    any_space = pl.BlockSpec(memory_space=pl.ANY)
    common = dict(
        compiler_params=pltpu.CompilerParams(vmem_limit_bytes=48 * 2**20),
        cost_estimate=pl.CostEstimate(
            flops=6 * hidden * half * tokens,
            bytes_accessed=6 * hidden * half,
            transcendentals=hidden * tokens,
        ),
    )
    scratch = [
        pltpu.VMEM((2, tokens, half), BF16),
        pltpu.VMEM((2, 3, hidden, chunk), BF16),
        pltpu.SemaphoreType.DMA((2, 3)),
    ]
    sums = (3, hidden, tokens)
    if before is None:
        return pl.pallas_call(
            functools.partial(first_half_kernel, backs, sizes),
            out_shape=jax.ShapeDtypeStruct(sums, F32),
            in_specs=[VMEM] * len(pieces) + [any_space] * 3,
            out_specs=VMEM,
            scratch_shapes=scratch,
            name="first_half",
            **common,
        )(*pieces, w_down, w_gate, w_up)
    count = int(np.prod(sizes))
    return pl.pallas_call(
        functools.partial(second_half_kernel, backs, sizes),
        out_shape=jax.ShapeDtypeStruct((count, GROUP, tokens), F32),
        in_specs=[VMEM] * (len(pieces) + 2) + [any_space] * 3,
        out_specs=VMEM,
        scratch_shapes=[pltpu.VMEM(sums, F32), scratch[0], pltpu.VMEM(sums, BF16)] + scratch[1:],
        name="second_half",
        **common,
    )(*pieces, before, proj, w_down, w_gate, w_up)


def score_kernel(left, right, ids, mean, out):
    tokens = ids.shape[1]
    own = jnp.sum(left[...], 0)
    onehot = (ids[...] == lax.broadcasted_iota(jnp.int32, (SEQS, tokens), 0)).astype(F32)
    rows = jnp.concatenate([onehot * own[r : r + 1, :] for r in range(GROUP)], 0)
    sketch = transposed_dot(rows, right[...].reshape(-1, tokens), HIGHEST)
    sketch = jnp.concatenate([sketch[r * SEQS : (r + 1) * SEQS] for r in range(GROUP)], 1)
    scores = transposed_dot(sketch, mean[...], HIGHEST)
    half = SEQS // 2
    tail = jnp.concatenate(
        [scores[:half], scores[half:], jnp.zeros((half, tokens - 2 * DOMAINS), F32)], 1
    )
    out[:, :GROUP, :] = jnp.broadcast_to(own[None], (out.shape[0],) + own.shape)
    out[:, GROUP:, :] = jnp.broadcast_to(tail[None], (out.shape[0],) + tail.shape)


def sketch_kernel(own_rank, rank, shared, right, ids, sketches, scores):
    count, height, tokens = shared.shape
    onehot = ids[...] == lax.broadcasted_iota(jnp.int32, (SEQS, tokens), 0)
    onehot = onehot.astype(F32).astype(BF16)
    norm = jnp.zeros((SEQS, 1), F32)
    for k in range(3):
        split = []
        for source, first in ((shared, 0), (right, 0)):
            rows = jnp.concatenate(
                [source[:, first + k * own_rank + i, :] for i in range(own_rank)], 0
            )[:rank]
            high = rows.astype(BF16)
            low = (rows - high.astype(F32)).astype(BF16)
            split.append((high, low))
        (left_high, left_low), (right_high, right_low) = split
        left = jnp.concatenate([left_high, left_high, left_low], 1)
        right_k = jnp.concatenate([right_high, right_low, right_high], 1)
        masks = jnp.concatenate([onehot] * 3, 1)
        rows = jnp.concatenate([left * masks[s : s + 1, :] for s in range(SEQS)], 0)
        sketch = transposed_dot(rows, right_k).reshape(SEQS, rank, rank)
        sketches[:, k] = sketch
        norm += jnp.sum(jnp.sum(sketch * sketch, 1), 1, keepdims=True)
    tail = jnp.sum(shared[:, GROUP:, :], 0)
    total = jnp.concatenate([tail[:, :DOMAINS], tail[:, DOMAINS : 2 * DOMAINS]], 0)
    scores[...] = total * lax.rsqrt(norm + 1e-06)


def on_device(
    count,
    activations,
    cotangent,
    w_gate,
    w_up,
    w_down,
    proj_model,
    proj_hidden,
    seq_ids,
    targets,
    target_domain,
):
    sizes = axis_sizes(count)
    rank = proj_model.shape[1] // 3
    model_cols, hidden = proj_model.shape[0], proj_hidden.shape[0]
    own_rank = -(-rank // count)
    padded = own_rank * count
    each, width = activations.shape
    tokens = count * each
    half = width // 2
    examples = targets.shape[0]

    both = jnp.concatenate([activations, cotangent], 0)
    blocks = []
    for h in range(2):
        first = gather_first(both[:, h * half : (h + 1) * half], sizes)
        first = first.reshape(sizes[0], 2, each, half).transpose(1, 0, 2, 3)
        blocks.append(first.reshape(2 * sizes[0] * each, half))
    inner = list(range(1, len(sizes)))
    pieces_0, backs_0 = gather_rest(blocks[0], sizes, inner)
    pieces_1, backs_1 = gather_rest(blocks[1], sizes, inner[:-1][::-1] + inner[-1:])

    def scatter_rows(values, k):
        values = jnp.pad(values, ((0, padded - rank), (0, 0)))
        values = values.reshape(own_rank, count, -1).transpose(1, 0, 2)
        low = k * own_rank
        return jnp.pad(values, ((0, 0), (low, GROUP - low - own_rank), (0, 0))).reshape(
            count * GROUP, -1
        )

    columns = both.reshape(2 * each, count, model_cols).transpose(1, 0, 2)
    cut = jnp.pad(targets, ((0, 0), (0, 0), (0, padded - rank), (0, 0)))
    cut = cut.reshape(examples, 3, own_rank, count, rank).transpose(3, 0, 1, 2, 4)
    cut = cut.reshape(count, examples, 3 * own_rank * rank)
    tags = jnp.broadcast_to(target_domain.astype(BF16)[None, :, None], (count, examples, 128))
    tall = max(2 * each, examples)
    sent = [
        jnp.pad(part, ((0, 0), (0, tall - part.shape[1]), (0, 0))) for part in (cut, tags, columns)
    ]
    held = exchange(jnp.concatenate(sent, 2))

    entries = 3 * own_rank * rank
    held_targets = held[:, :examples, : entries + 128].reshape(count * examples, -1)
    domains = held_targets[:, -1].astype(F32)
    domain_onehot = (domains[None, :] == jnp.arange(DOMAINS, dtype=F32)[:, None]).astype(BF16)
    domain_sum = jnp.dot(domain_onehot, held_targets[:, :entries], preferred_element_type=F32)
    domain_count = jnp.sum(domain_onehot.astype(F32), 1)
    mean = (domain_sum / domain_count[:, None]).reshape(DOMAINS, 3, own_rank, rank)
    mean = jnp.pad(mean, ((0, 0), (0, 0), (0, 0), (0, padded - rank)))
    mean = mean.reshape(DOMAINS, 3, own_rank, own_rank, count).transpose(0, 1, 2, 4, 3)
    mean = mean[:, :, :, :, None, :] * jnp.eye(3, dtype=F32)[None, :, None, None, :, None]
    mean = mean.reshape(DOMAINS, 3 * own_rank, count, 3 * own_rank)
    spare = GROUP - 3 * own_rank
    mean = jnp.pad(mean, ((0, 0), (0, spare), (0, 0), (0, spare)))
    mean = mean.reshape(DOMAINS, GROUP * count * GROUP)

    held_columns = held[:, : 2 * each, entries + 128 :].reshape(count, 2, each, model_cols)
    sides = [
        slot_order(held_columns[:, side].reshape(tokens, model_cols), sizes) for side in range(2)
    ]
    proj_t = proj_model.T
    proj_in = scatter_rows(proj_t[:rank], 0) + scatter_rows(proj_t[rank : 2 * rank], 1)
    proj_out = scatter_rows(proj_t[2 * rank :], 2)
    right = transposed_dot(proj_in, sides[0]) + transposed_dot(proj_out, sides[1])
    own_right = jnp.sum(exchange(right.reshape(count, GROUP, tokens)), 0)
    right = exchange(jnp.broadcast_to(own_right[None], (count, GROUP, tokens)))

    proj_h = proj_hidden.T
    proj_left = jnp.stack(
        [
            scatter_rows(proj_h[rank : 2 * rank], 0),
            scatter_rows(proj_h[2 * rank :], 1),
            scatter_rows(proj_h[:rank], 2),
        ]
    )
    ids = slot_order(seq_ids, sizes)[None, :]

    weights = (w_down, w_gate, w_up)
    sums = products(pieces_0, backs_0, sizes, weights)
    left = exchange(products(pieces_1, backs_1, sizes, weights, sums, proj_left))

    shared = exchange(
        pl.pallas_call(
            score_kernel,
            out_shape=jax.ShapeDtypeStruct((count, 2 * GROUP, tokens), F32),
            in_specs=[VMEM] * 4,
            out_specs=VMEM,
            compiler_params=pltpu.CompilerParams(vmem_limit_bytes=32 * 2**20),
            name="own_scores",
        )(left, right, ids, mean)
    )
    return pl.pallas_call(
        functools.partial(sketch_kernel, own_rank, rank),
        out_shape=(
            jax.ShapeDtypeStruct((SEQS, 3, rank, rank), F32),
            jax.ShapeDtypeStruct((SEQS, DOMAINS), F32),
        ),
        in_specs=[VMEM] * 3,
        out_specs=(VMEM, VMEM),
        compiler_params=pltpu.CompilerParams(vmem_limit_bytes=40 * 2**20),
        name="sketches",
    )(shared, right, ids)


def solution(mesh):
    in_specs = (
        P(("groups", "dp"), None),
        P(("groups", "dp"), None),
        P("dp", None),
        P("dp", None),
        P("dp", None),
        P("dp", None),
        P("dp", None),
        P("groups"),
        P(("groups", "dp"), None, None, None),
        P(("groups", "dp")),
    )
    out_specs = (P("groups", None, None, None), P("groups", None))
    return jax.shard_map(
        functools.partial(on_device, mesh.shape["dp"]),
        mesh=mesh,
        in_specs=in_specs,
        out_specs=out_specs,
        check_vma=False,
    )
```

time: 478 us -> 120 us (0.25)
  waiting for transfers between devices: 373 us -> 20.6 us
  matrix products: 38.8 us -> 2.88 us
  starting transfers between devices: 0.34 us -> 29.4 us
  Pallas kernels: 0 us -> 25.1 us
  between operations: 13.9 us -> 1.12 us
  blocking collectives: 39.3 us -> 27.4 us
    psum x1 -> x0, waiting for transfers between devices: 133 us -> none  [on_device(): sketches = lax.psum(local_sketch, 'dp')]
    unnamed x5 -> x0, waiting for transfers between devices: 123 us -> none
    all_gather x2 -> x0, waiting for transfers between devices: 116 us -> none  [the longest x1 60.5 us: on_device(): rows_in = lax.all_gather(activations, 'dp', axis=0, tiled=True)]
    psum x1 -> x0, blocking collectives: 39.3 us -> none  [on_device(): total_scores, total_count = lax.psum((folded, domain_count), 'dp')]
    dot_general x11 -> x3, matrix products: 38.8 us -> 2.88 us  [the longest x2 1.8 us: transposed_dot(): lax.dot_general(left, right, (((1,), (1,)), ((), ())), precision=precisio...]
    all_to_all x0 -> x2, blocking collectives: none -> 27.4 us  [the longest x1 15 us: gather_first(): lax.all_to_all(copies, 'dp', split_axis=0, concat_axis=0, axis_index_grou...]
    pallas_call x0 -> x4, Pallas kernels: none -> 25.1 us  [the longest x1 11.8 us: products(): pl.pallas_call(functools.partial(second_half_kernel, backs, sizes), out_s...]
    all_to_all x0 -> x5, starting transfers between devices: none -> 20.3 us  [the longest x4 16.9 us: exchange(): return lax.all_to_all(blocks, 'dp', split_axis=0, concat_axis=0, tiled=True)]
  transfers between devices with their start and end apart: 4 -> 19, of which waited for: 4 -> 4; matrix products, arithmetic and copies ran while one was open for 1% -> 11% of each run, Pallas kernels for 0% -> 19%
where the time goes in v2:
time: 120 us; the launch traced here: 119 us
  starting transfers between devices  29.4 us (24%)
  blocking collectives  27.4 us (23%)
  Pallas kernels  25.1 us (21%)
  waiting for transfers between devices  20.6 us (17%)
  local copies, waits for them, and re-layouts  10.1 us (8%)
  other arithmetic  2.97 us (2%)
  matrix products  2.88 us (2%)
    all_to_all x4, starting transfers between devices, exchange(): return lax.all_to_all(blocks, 'dp', split_axis=0, concat_axis=0, tiled=True)  16.9 us
    all_to_all x1, blocking collectives, gather_first(): lax.all_to_all(copies, 'dp', split_axis=0, concat_axis=0, axis_index_grou...  15 us
    all_to_all x1, blocking collectives, exchange(): return lax.all_to_all(blocks, 'dp', split_axis=0, concat_axis=0, tiled=True)  12.4 us
    pallas_call x1, Pallas kernels, products(): pl.pallas_call(functools.partial(second_half_kernel, backs, sizes), out_s...  11.8 us
    pallas_call x1, Pallas kernels, products(): pl.pallas_call(functools.partial(first_half_kernel, backs, sizes), out_sh...  10.5 us
    ppermute x14, starting transfers between devices, shift(): return lax.ppermute(value, 'dp', pairs)  9.04 us
    all_to_all x4, waiting for transfers between devices, exchange(): return lax.all_to_all(blocks, 'dp', split_axis=0, concat_axis=0, tiled=True)  8.48 us
    ppermute x14, waiting for transfers between devices, shift(): return lax.ppermute(value, 'dp', pairs)  6.15 us
  transfers between devices with their start and end apart: 19, of which 4 were waited for; matrix products, arithmetic and copies ran while one was open for 11% of the time, Pallas kernels for 19%

profile of v2, /device:TPU:0, one launch (start us, length us, event | category | flops | bytes accessed | tf_op | source)
XLA Modules:
  0.0 119.5 jit_solution(13738534206118803562)
XLA Ops:
  0.7 0.9 fusion.6
  1.6 15.0 %all_to_all.35 = bf16[4,8,4096]{2,1,0:T(8,128)(2,1)S(1)} all-to-all(bf16[4,8,4096]{2,1,0:T(8,128)(2,1)S(1)} %broadcast_in_dim.9), channel_id=1, replica_groups={{0,8,16,24},{1,9,17,25},{2,10,18,26},{3,11,19,27},{4,12,20,28},{5,13,21..., dimensions={0} | all-to-all | bytes 524288 | tf_op jit(solution)/shard_map/all_to_all | solution.py:46
  16.6 0.7 broadcast_in_dim.8
  17.3 3.4 %all-to-all-start = ((bf16[4,8,4096]{2,1,0:T(8,128)(2,1)}), bf16[4,8,4096]{2,1,0:T(8,128)(2,1)S(1)}, u32[]{:S(2)}, u32[]{:S(2)}) async-start(bf16[4,8,4096]{2,1,0:T(8,128)(2,1)} %broadcast_in_dim.8), calls=%async_computation | async-start | bytes 524288 | tf_op jit(solution)/shard_map/all_to_all | solution.py:46
  21.2 0.3 copy.96
  21.5 0.3 reshape.109
  21.9 0.8 pad_maximum_fusion.1
  22.7 6.0 %all-to-all-done = bf16[4,8,4096]{2,1,0:T(8,128)(2,1)S(1)} async-done(((bf16[4,8,4096]{2,1,0:T(8,128)(2,1)}), bf16[4,8,4096]{2,1,0:T(8,128)(2,1)S(1)}, u32[]{:S(2)}, u32[]{:S(2)}) %all-to-all-start) | async-done | bytes 262176 | tf_op jit(solution)/shard_map/all_to_all | solution.py:46
  28.7 3.6 %all-to-all-start.3 = ((bf16[32,8,768]{2,1,0:T(8,128)(2,1)}), bf16[32,8,768]{2,1,0:T(8,128)(2,1)}, u32[]{:S(2)}, u32[]{:S(2)}) async-start(bf16[32,8,768]{2,1,0:T(8,128)(2,1)} %pad_maximum_fusion.1), calls=%async_computation.3 | async-start | bytes 786432 | tf_op jit(solution)/shard_map/all_to_all | solution.py:71
  32.3 0.6 copy.85
  33.4 0.3 pad_bitcast_fusion
  33.7 0.2 copy.66
  33.9 0.2 copy.67
  34.2 1.8 %collective-permute-start.7 = (bf16[32,4096]{1,0:T(8,128)(2,1)S(1)}, bf16[32,4096]{1,0:T(8,128)(2,1)S(1)}, u32[]{:S(2)}, u32[]{:S(2)}) collective-permute-start(bf16[32,4096]{1,0:T(8,128)(2,1)S(1)} %reshape.102.refs_0_), channel_id=1, source_target_pairs={{0,4},{1,5},{2,6},{3,7},{4,0},{5,1},{6,2},{7,3},{8,12},{9,13},{10,... | collective-permute-start | bytes 786440 | tf_op jit(solution)/shard_map/ppermute | solution.py:38
  36.0 0.7 pad_add_fusion
  36.8 1.5 %collective-permute-start.8 = (bf16[32,4096]{1,0:T(8,128)(2,1)S(1)}, bf16[32,4096]{1,0:T(8,128)(2,1)S(1)}, u32[]{:S(2)}, u32[]{:S(2)}) collective-permute-start(bf16[32,4096]{1,0:T(8,128)(2,1)S(1)} %reshape.102.refs_0_), channel_id=1, source_target_pairs={{0,2},{1,3},{2,0},{3,1},{4,6},{5,7},{6,4},{7,5},{8,10},{9,11},{10,... | collective-permute-start | bytes 786440 | tf_op jit(solution)/shard_map/ppermute | solution.py:38
  38.6 0.2 copy.65
  38.9 0.6 collective-permute-start
  39.5 0.3 collective-permute-start.1
  39.8 6.1 %collective-permute-done.7.refs_1_ = bf16[32,4096]{1,0:T(8,128)(2,1)S(1)} collective-permute-done((bf16[32,4096]{1,0:T(8,128)(2,1)S(1)}, bf16[32,4096]{1,0:T(8,128)(2,1)S(1)}, u32[]{:S(2)}, u32[]{:S(2)}) %collective-permute-start.7) | collective-permute-done | bytes 262176 | tf_op jit(solution)/shard_map/ppermute | solution.py:38
  45.9 1.4 %collective-permute-start.9 = (bf16[32,4096]{1,0:T(8,128)(2,1)S(1)}, bf16[32,4096]{1,0:T(8,128)(2,1)}, u32[]{:S(2)}, u32[]{:S(2)}) collective-permute-start(bf16[32,4096]{1,0:T(8,128)(2,1)S(1)} %collective-permute-done.7.refs_1_), channel_id=1, source_target_pairs={{0,2},{1,3},{2,0},{3,1},{4,6},{5,7},{6,4},{7,5},{8,10},{9,11},{10,... | collective-permute-start | bytes 786440 | tf_op jit(solution)/shard_map/ppermute | solution.py:38
  47.3 0.9 slice.65
  48.7 1.6 %fusion = f32[32,8,128]{2,1,0:T(8,128)} fusion(f32[256,128]{1,0:T(8,128)S(1)} %fusion.2, bf16[128,256]{1,0:T(8,128)(2,1)S(1)} %reshape.115, bf16[32,2,256]{2,1,0:T(2,128)(2,1)} %copy.85), kind=kOutput, calls=%fused_computation.2 | convolution fusion | flops 16809984 | bytes 360448 | tf_op jit(solution)/shard_map/dot_general | solution.py:75
  50.3 3.7 %all-to-all-start.4 = ((f32[32,8,128]{2,1,0:T(8,128)}), f32[32,8,128]{2,1,0:T(8,128)S(1)}, u32[]{:S(2)}, u32[]{:S(2)}) async-start(f32[32,8,128]{2,1,0:T(8,128)} %fusion), calls=%async_computation.4 | async-start | bytes 262144 | tf_op jit(solution)/shard_map/all_to_all | solution.py:71
  53.9 1.0 slice_bitcast_fusion
  54.9 0.7 copy-done.1
  55.8 0.3 collective-permute-start.11
  56.1 0.3 collective-permute-start.12
  56.3 1.8 %collective-permute-start.2 = (bf16[32,4096]{1,0:T(8,128)(2,1)S(1)}, bf16[32,4096]{1,0:T(8,128)(2,1)}, u32[]{:S(2)}, u32[]{:S(2)}) collective-permute-start(bf16[32,4096]{1,0:T(8,128)(2,1)S(1)} %collective-permute-done.refs_1_), channel_id=1, source_target_pairs={{0,4},{1,5},{2,6},{3,7},{4,0},{5,1},{6,2},{7,3},{8,12},{9,13},{10,... | collective-permute-start | bytes 786440 | tf_op jit(solution)/shard_map/ppermute | solution.py:38
  58.2 1.1 convolution_divide_fusion
  59.3 0.9 reshape.119
  60.2 0.9 copy.80
  61.1 1.1 all-to-all-done.4
  62.3 0.7 broadcast_in_dim.11
  63.0 3.8 %all-to-all-start.5 = ((f32[32,8,128]{2,1,0:T(8,128)}), f32[32,8,128]{2,1,0:T(8,128)S(1)}, u32[]{:S(2)}, u32[]{:S(2)}) async-start(f32[32,8,128]{2,1,0:T(8,128)} %broadcast_in_dim.11), calls=%async_computation.5 | async-start | bytes 262144 | tf_op jit(solution)/shard_map/all_to_all | solution.py:71
  66.8 0.3 collective-permute-start.3
  67.1 0.3 collective-permute-start.4
  67.4 0.3 collective-permute-start.5
  67.6 0.3 collective-permute-start.6
  67.9 10.5 %first_half.1.refs_8_ = f32[3,896,128]{2,1,0:T(8,128)S(1)} custom-call(bf16[32,4096]{1,0:T(8,128)(2,1)S(1)} %reshape.102.refs_0_, bf16[32,4096]{1,0:T(8,128)(2,1)S(1)} %collective-permute-done.7.refs_1_, bf16[32,4096]{1,0:T(8,128)(2,1)S(1)} %collective-permute-done.8.refs_2_, bf16[32,4096]{1,0:T(8,128)(2,1)} %collective-permute-done.9.refs_3_, ...), custom_call_target="tpu_custom_call" | custom-call | flops 2818572288 | bytes 22020096 | tf_op jit(solution)/shard_map/first_half/pallas_call | solution.py:189
  78.5 11.8 %second_half.1 = f32[32,8,128]{2,1,0:T(8,128)} custom-call(bf16[32,4096]{1,0:T(8,128)(2,1)S(1)} %reshape.100.refs_0_, bf16[32,4096]{1,0:T(8,128)(2,1)S(1)} %collective-permute-done.refs_1_, bf16[32,4096]{1,0:T(8,128)(2,1)S(1)} %collective-permute-done.1.refs_2_, bf16[32,4096]{1,0:T(8,128)(2,1)} %collective-permute-done.2.refs_3_, ...), custom_call_target="tpu_custom_call" | custom-call | flops 2818572288 | bytes 22020096 | tf_op jit(solution)/shard_map/second_half/pallas_call | solution.py:199
  90.3 5.8 %all-to-all-start.2 = ((f32[32,8,128]{2,1,0:T(8,128)}), f32[32,8,128]{2,1,0:T(8,128)S(1)}, u32[]{:S(2)}, u32[]{:S(2)}) async-start(f32[32,8,128]{2,1,0:T(8,128)} %second_half.1), calls=%async_computation.2 | async-start | bytes 262144 | tf_op jit(solution)/shard_map/all_to_all | solution.py:71
  96.3 0.3 copy.86
  96.7 0.3 copy.82.mean
  97.0 7.4 %all-to-all-done.2.left = f32[32,8,128]{2,1,0:T(8,128)S(1)} async-done(((f32[32,8,128]{2,1,0:T(8,128)}), f32[32,8,128]{2,1,0:T(8,128)S(1)}, u32[]{:S(2)}, u32[]{:S(2)}) %all-to-all-start.2) | async-done | bytes 131104 | tf_op jit(solution)/shard_map/all_to_all | solution.py:71
  104.3 0.8 own_scores.1
  105.2 12.4 %all_to_all.36.shared = f32[32,16,128]{2,1,0:T(8,128)S(1)} all-to-all(f32[32,16,128]{2,1,0:T(8,128)S(1)} %own_scores.1), channel_id=1, replica_groups=mesh['groups'=1,'dp'=32] {'dp'}, dimensions={0} | all-to-all | bytes 524288 | tf_op jit(solution)/shard_map/all_to_all | solution.py:71
  117.6 1.9 %sketches.1 = (f32[16,3,64,64]{3,2,1,0:T(8,128)}, f32[16,32]{1,0:T(8,128)}) custom-call(f32[32,16,128]{2,1,0:T(8,128)S(1)} %all_to_all.36.shared, f32[32,8,128]{2,1,0:T(8,128)S(1)} %all-to-all-done.5.right, s32[1,128]{1,0:T(1,128)S(1)} %broadcast_in_dim_reshape.3.ids), custom_call_target="tpu_custom_call" | custom-call | tf_op jit(solution)/shard_map/sketches/pallas_call | solution.py:355
  (68 shorter events, 2.5 us)
Async XLA Ops:
  0.6 20.1 %copy-start.4 = (bf16[4,8192]{1,0:T(4,128)(2,1)S(1)}, bf16[4,8192]{1,0:T(4,128)(2,1)}, u32[]{:S(2)}) copy-start(bf16[4,8192]{1,0:T(4,128)(2,1)} %param.10) | copy-start | bytes 196612
  0.6 20.1 %copy-start.5 = (bf16[4,8192]{1,0:T(4,128)(2,1)S(1)}, bf16[4,8192]{1,0:T(4,128)(2,1)}, u32[]{:S(2)}) copy-start(bf16[4,8192]{1,0:T(4,128)(2,1)} %param.11) | copy-start | bytes 196612
  0.6 20.2 %copy-start.3 = (bf16[896,192]{0,1:T(8,128)(2,1)S(1)}, bf16[896,192]{0,1:T(8,128)(2,1)}, u32[]{:S(2)}) copy-start(bf16[896,192]{0,1:T(8,128)(2,1)} %param.16) | copy-start | bytes 1032196
  16.6 4.6 %copy-start.2 = (bf16[8,3,64,64]{3,2,1,0:T(8,128)(2,1)S(1)}, bf16[8,3,64,64]{3,2,1,0:T(8,128)(2,1)}, u32[]{:S(2)}) copy-start(bf16[8,3,64,64]{3,2,1,0:T(8,128)(2,1)} %param.18) | copy-start | bytes 589828
  17.3 11.3 %all-to-all-start = ((bf16[4,8,4096]{2,1,0:T(8,128)(2,1)}), bf16[4,8,4096]{2,1,0:T(8,128)(2,1)S(1)}, u32[]{:S(2)}, u32[]{:S(2)}) async-start(bf16[4,8,4096]{2,1,0:T(8,128)(2,1)} %broadcast_in_dim.8), calls=%async_computation | async-start | bytes 524288 | tf_op jit(solution)/shard_map/all_to_all | solution.py:46
  20.8 1.0 copy-start.8
  21.2 11.1 %copy-start.6 = (bf16[256,192]{0,1:T(8,128)(2,1)S(1)}, bf16[256,192]{0,1:T(8,128)(2,1)}, u32[]{:S(2)}) copy-start(bf16[256,192]{0,1:T(8,128)(2,1)} %param.15) | copy-start | bytes 294916
  21.5 11.6 %copy-start.7 = (s32[128]{0:T(128)S(1)}, s32[128]{0:T(128)}, u32[]{:S(2)}) copy-start(s32[128]{0:T(128)} %param.17) | copy-start | bytes 1540
  28.7 18.7 %all-to-all-start.3 = ((bf16[32,8,768]{2,1,0:T(8,128)(2,1)}), bf16[32,8,768]{2,1,0:T(8,128)(2,1)}, u32[]{:S(2)}, u32[]{:S(2)}) async-start(bf16[32,8,768]{2,1,0:T(8,128)(2,1)} %pad_maximum_fusion.1), calls=%async_computation.3 | async-start | bytes 786432 | tf_op jit(solution)/shard_map/all_to_all | solution.py:71
  34.2 11.7 %collective-permute-start.7 = (bf16[32,4096]{1,0:T(8,128)(2,1)S(1)}, bf16[32,4096]{1,0:T(8,128)(2,1)S(1)}, u32[]{:S(2)}, u32[]{:S(2)}) collective-permute-start(bf16[32,4096]{1,0:T(8,128)(2,1)S(1)} %reshape.102.refs_0_), channel_id=1, source_target_pairs={{0,4},{1,5},{2,6},{3,7},{4,0},{5,1},{6,2},{7,3},{8,12},{9,13},{10,... | collective-permute-start | bytes 786440 | tf_op jit(solution)/shard_map/ppermute | solution.py:38
  36.8 11.6 %copy-start = (bf16[32,8,256]{2,0,1:T(8,128)(2,1)S(1)}, bf16[32,8,256]{2,0,1:T(8,128)(2,1)}, u32[]{:S(2)}) copy-start(bf16[32,8,256]{2,0,1:T(8,128)(2,1)} %pad_add_fusion) | copy-start | bytes 393220
  36.8 18.9 %collective-permute-start.8 = (bf16[32,4096]{1,0:T(8,128)(2,1)S(1)}, bf16[32,4096]{1,0:T(8,128)(2,1)S(1)}, u32[]{:S(2)}, u32[]{:S(2)}) collective-permute-start(bf16[32,4096]{1,0:T(8,128)(2,1)S(1)} %reshape.102.refs_0_), channel_id=1, source_target_pairs={{0,2},{1,3},{2,0},{3,1},{4,6},{5,7},{6,4},{7,5},{8,10},{9,11},{10,... | collective-permute-start | bytes 786440 | tf_op jit(solution)/shard_map/ppermute | solution.py:38
  38.4 17.7 %collective-permute-start.10 = (bf16[32,4096]{1,0:T(8,128)(2,1)S(1)}, bf16[32,4096]{1,0:T(8,128)(2,1)S(1)}, u32[]{:S(2)}, u32[]{:S(2)}) collective-permute-start(bf16[32,4096]{1,0:T(8,128)(2,1)S(1)} %reshape.102.refs_0_), channel_id=1, source_target_pairs={{0,1},{1,0},{2,3},{3,2},{4,5},{5,4},{6,7},{7,6},{8,9},{9,8},{10,11... | collective-permute-start | bytes 786440 | tf_op jit(solution)/shard_map/ppermute | solution.py:38
  38.9 17.5 %collective-permute-start = (bf16[32,4096]{1,0:T(8,128)(2,1)S(1)}, bf16[32,4096]{1,0:T(8,128)(2,1)S(1)}, u32[]{:S(2)}, u32[]{:S(2)}) collective-permute-start(bf16[32,4096]{1,0:T(8,128)(2,1)S(1)} %reshape.100.refs_0_), channel_id=1, source_target_pairs={{0,2},{1,3},{2,0},{3,1},{4,6},{5,7},{6,4},{7,5},{8,10},{9,11},{10,... | collective-permute-start | bytes 786440 | tf_op jit(solution)/shard_map/ppermute | solution.py:38
  39.5 27.3 %collective-permute-start.1 = (bf16[32,4096]{1,0:T(8,128)(2,1)S(1)}, bf16[32,4096]{1,0:T(8,128)(2,1)S(1)}, u32[]{:S(2)}, u32[]{:S(2)}) collective-permute-start(bf16[32,4096]{1,0:T(8,128)(2,1)S(1)} %reshape.100.refs_0_), channel_id=1, source_target_pairs={{0,4},{1,5},{2,6},{3,7},{4,0},{5,1},{6,2},{7,3},{8,12},{9,13},{10,... | collective-permute-start | bytes 786440 | tf_op jit(solution)/shard_map/ppermute | solution.py:38
  45.9 12.2 %collective-permute-start.9 = (bf16[32,4096]{1,0:T(8,128)(2,1)S(1)}, bf16[32,4096]{1,0:T(8,128)(2,1)}, u32[]{:S(2)}, u32[]{:S(2)}) collective-permute-start(bf16[32,4096]{1,0:T(8,128)(2,1)S(1)} %collective-permute-done.7.refs_1_), channel_id=1, source_target_pairs={{0,2},{1,3},{2,0},{3,1},{4,6},{5,7},{6,4},{7,5},{8,10},{9,11},{10,... | collective-permute-start | bytes 786440 | tf_op jit(solution)/shard_map/ppermute | solution.py:38
  50.3 12.0 %all-to-all-start.4 = ((f32[32,8,128]{2,1,0:T(8,128)}), f32[32,8,128]{2,1,0:T(8,128)S(1)}, u32[]{:S(2)}, u32[]{:S(2)}) async-start(f32[32,8,128]{2,1,0:T(8,128)} %fusion), calls=%async_computation.4 | async-start | bytes 262144 | tf_op jit(solution)/shard_map/all_to_all | solution.py:71
  54.9 0.7 copy-start.1
  55.8 11.3 %collective-permute-start.11 = (bf16[32,4096]{1,0:T(8,128)(2,1)S(1)}, bf16[32,4096]{1,0:T(8,128)(2,1)}, u32[]{:S(2)}, u32[]{:S(2)}) collective-permute-start(bf16[32,4096]{1,0:T(8,128)(2,1)S(1)} %collective-permute-done.7.refs_1_), channel_id=1, source_target_pairs={{0,1},{1,0},{2,3},{3,2},{4,5},{5,4},{6,7},{7,6},{8,9},{9,8},{10,11... | collective-permute-start | bytes 786440 | tf_op jit(solution)/shard_map/ppermute | solution.py:38
  56.1 11.3 %collective-permute-start.12 = (bf16[32,4096]{1,0:T(8,128)(2,1)S(1)}, bf16[32,4096]{1,0:T(8,128)(2,1)}, u32[]{:S(2)}, u32[]{:S(2)}) collective-permute-start(bf16[32,4096]{1,0:T(8,128)(2,1)S(1)} %collective-permute-done.8.refs_2_), channel_id=1, source_target_pairs={{0,1},{1,0},{2,3},{3,2},{4,5},{5,4},{6,7},{7,6},{8,9},{9,8},{10,11... | collective-permute-start | bytes 786440 | tf_op jit(solution)/shard_map/ppermute | solution.py:38
  56.3 11.3 %collective-permute-start.2 = (bf16[32,4096]{1,0:T(8,128)(2,1)S(1)}, bf16[32,4096]{1,0:T(8,128)(2,1)}, u32[]{:S(2)}, u32[]{:S(2)}) collective-permute-start(bf16[32,4096]{1,0:T(8,128)(2,1)S(1)} %collective-permute-done.refs_1_), channel_id=1, source_target_pairs={{0,4},{1,5},{2,6},{3,7},{4,0},{5,1},{6,2},{7,3},{8,12},{9,13},{10,... | collective-permute-start | bytes 786440 | tf_op jit(solution)/shard_map/ppermute | solution.py:38
  58.1 9.8 %collective-permute-start.13 = (bf16[32,4096]{1,0:T(8,128)(2,1)}, bf16[32,4096]{1,0:T(8,128)(2,1)}, u32[]{:S(2)}, u32[]{:S(2)}) collective-permute-start(bf16[32,4096]{1,0:T(8,128)(2,1)} %collective-permute-done.9.refs_3_), channel_id=1, source_target_pairs={{0,1},{1,0},{2,3},{3,2},{4,5},{5,4},{6,7},{7,6},{8,9},{9,8},{10,11... | collective-permute-start | bytes 786440 | tf_op jit(solution)/shard_map/ppermute | solution.py:38
  63.0 27.3 %all-to-all-start.5 = ((f32[32,8,128]{2,1,0:T(8,128)}), f32[32,8,128]{2,1,0:T(8,128)S(1)}, u32[]{:S(2)}, u32[]{:S(2)}) async-start(f32[32,8,128]{2,1,0:T(8,128)} %broadcast_in_dim.11), calls=%async_computation.5 | async-start | bytes 262144 | tf_op jit(solution)/shard_map/all_to_all | solution.py:71
  66.8 11.6 %collective-permute-start.3 = (bf16[32,4096]{1,0:T(8,128)(2,1)S(1)}, bf16[32,4096]{1,0:T(8,128)(2,1)S(1)}, u32[]{:S(2)}, u32[]{:S(2)}) collective-permute-start(bf16[32,4096]{1,0:T(8,128)(2,1)S(1)} %reshape.100.refs_0_), channel_id=1, source_target_pairs={{0,1},{1,0},{2,3},{3,2},{4,5},{5,4},{6,7},{7,6},{8,9},{9,8},{10,11... | collective-permute-start | bytes 786440 | tf_op jit(solution)/shard_map/ppermute | solution.py:38
  67.1 11.3 %collective-permute-start.4 = (bf16[32,4096]{1,0:T(8,128)(2,1)S(1)}, bf16[32,4096]{1,0:T(8,128)(2,1)S(1)}, u32[]{:S(2)}, u32[]{:S(2)}) collective-permute-start(bf16[32,4096]{1,0:T(8,128)(2,1)S(1)} %collective-permute-done.refs_1_), channel_id=1, source_target_pairs={{0,1},{1,0},{2,3},{3,2},{4,5},{5,4},{6,7},{7,6},{8,9},{9,8},{10,11... | collective-permute-start | bytes 786440 | tf_op jit(solution)/shard_map/ppermute | solution.py:38
  67.4 11.1 %collective-permute-start.5 = (bf16[32,4096]{1,0:T(8,128)(2,1)S(1)}, bf16[32,4096]{1,0:T(8,128)(2,1)S(1)}, u32[]{:S(2)}, u32[]{:S(2)}) collective-permute-start(bf16[32,4096]{1,0:T(8,128)(2,1)S(1)} %collective-permute-done.1.refs_2_), channel_id=1, source_target_pairs={{0,1},{1,0},{2,3},{3,2},{4,5},{5,4},{6,7},{7,6},{8,9},{9,8},{10,11... | collective-permute-start | bytes 786440 | tf_op jit(solution)/shard_map/ppermute | solution.py:38
  67.6 10.8 %collective-permute-start.6 = (bf16[32,4096]{1,0:T(8,128)(2,1)}, bf16[32,4096]{1,0:T(8,128)(2,1)S(1)}, u32[]{:S(2)}, u32[]{:S(2)}) collective-permute-start(bf16[32,4096]{1,0:T(8,128)(2,1)} %collective-permute-done.2.refs_3_), channel_id=1, source_target_pairs={{0,1},{1,0},{2,3},{3,2},{4,5},{5,4},{6,7},{7,6},{8,9},{9,8},{10,11... | collective-permute-start | bytes 786440 | tf_op jit(solution)/shard_map/ppermute | solution.py:38
  90.3 14.1 %all-to-all-start.2 = ((f32[32,8,128]{2,1,0:T(8,128)}), f32[32,8,128]{2,1,0:T(8,128)S(1)}, u32[]{:S(2)}, u32[]{:S(2)}) async-start(f32[32,8,128]{2,1,0:T(8,128)} %second_half.1), calls=%async_computation.2 | async-start | bytes 262144 | tf_op jit(solution)/shard_map/all_to_all | solution.py:71

commit v3 on v0

v3 whole, which is shorter than its diff:
```python
import functools

import jax
import jax.numpy as jnp
import numpy as np
from jax import lax
from jax.experimental import pallas as pl
from jax.experimental.pallas import tpu as pltpu
from jax.sharding import PartitionSpec as P

DOMAINS = 32
SEQS = 16
HIGHEST = lax.Precision.HIGHEST
F32 = jnp.float32
BF16 = jnp.bfloat16
VMEM = pl.BlockSpec(memory_space=pltpu.VMEM)
ANY = pl.BlockSpec(memory_space=pl.ANY)


def axis_sizes(count):
    if count == 32:
        return (4, 2, 2, 2)
    if count == 128:
        return (8, 8, 2)
    return (count, 1)


def strides_of(sizes):
    return [int(np.prod(sizes[i + 1 :])) for i in range(len(sizes))]


def shift(value, sizes, axis, amount):
    size, stride = sizes[axis], strides_of(sizes)[axis]
    pairs = []
    for source in range(int(np.prod(sizes))):
        at = (source // stride) % size
        pairs.append((source, source + ((at + amount) % size - at) * stride))
    return lax.ppermute(value, "dp", pairs)


def coordinate(me, sizes, axis):
    return lax.rem(lax.div(me, strides_of(sizes)[axis]), sizes[axis])


def gather_pieces(rows, sizes, order):
    line = [rows] + [shift(rows, sizes, 0, k) for k in range(1, sizes[0])]
    pieces = [(jnp.concatenate(line, 0), tuple(0 for _ in sizes))]
    for axis in order:
        grown = list(pieces)
        for k in range(1, sizes[axis]):
            for piece, back in pieces:
                moved = tuple(k if i == axis else b for i, b in enumerate(back))
                grown.append((shift(piece, sizes, axis, k), moved))
        pieces = grown
    return [piece for piece, _ in pieces], [back for _, back in pieces]


def gather_stack(value, sizes, order):
    for axis in order:
        moved = [value] + [shift(value, sizes, axis, k) for k in range(1, sizes[axis])]
        value = jnp.stack(moved) if len(moved) > 1 else value[None]
    return value


def slot_order(per_token, sizes):
    rest = int(np.prod(sizes[1:]))
    return per_token.reshape(sizes[0], rest, -1).transpose(1, 0, 2).reshape(-1)


def exchange(blocks, groups=None):
    return lax.all_to_all(
        blocks, "dp", split_axis=0, concat_axis=0, axis_index_groups=groups, tiled=True
    )


def transposed_dot(left, right, precision=None):
    return lax.dot_general(
        left, right, (((1,), (1,)), ((), ())), precision=precision, preferred_element_type=F32
    )


def place_pieces(pieces, backs, sizes, into):
    me = lax.axis_index("dp")
    rows = pieces[0].shape[0]
    for piece, back in zip(pieces, backs):
        slot = 0
        for axis in range(1, len(sizes)):
            at = coordinate(me, sizes, axis) + sizes[axis] - back[axis]
            slot = slot * sizes[axis] + lax.rem(at, sizes[axis])
        into[pl.ds(pl.multiple_of(slot * rows, rows), rows), :] = piece[...]


def stream_products(weights, tokens, sums, buffers, arrived):
    depth, chunk = buffers.shape[0], buffers.shape[3]
    steps = tokens.shape[1] // chunk

    def copy(step, w):
        slot = lax.rem(step, depth)
        columns = pl.ds(pl.multiple_of(step * chunk, chunk), chunk)
        return pltpu.make_async_copy(
            weights[w].at[:, columns], buffers.at[slot, w], arrived.at[slot, w]
        )

    def fetch():
        for step in range(min(depth, steps)):
            for w in range(len(weights)):
                copy(step, w).start()

    def run():
        @pl.loop(0, steps)
        def _(step):
            columns = pl.ds(pl.multiple_of(step * chunk, chunk), chunk)
            for w in range(len(weights)):
                copy(step, w).wait()
                sums[w] += transposed_dot(buffers[lax.rem(step, depth), w], tokens[:, columns])

                @pl.when(step + depth < steps)
                def _():
                    copy(step + depth, w).start()

    return fetch, run


def model_side(proj, tokens, model_cols):
    window = proj.shape[1]
    start = lax.div(lax.axis_index("dp") * model_cols, window) * window
    columns = pl.ds(pl.multiple_of(start, window), window)
    return transposed_dot(proj, tokens[:, columns])


def input_kernel(backs, sizes, model_cols, *refs):
    pieces, refs = refs[: len(backs)], refs[len(backs) :]
    proj, w_gate, w_up, sums, right, tokens, buffers, arrived = refs
    fetch, run = stream_products((w_gate, w_up), tokens, sums, buffers, arrived)
    fetch()
    place_pieces(pieces, backs, sizes, tokens)
    sums[...] = jnp.zeros_like(sums)
    right[...] = model_side(proj[: right.shape[0], :], tokens, model_cols)
    run()


def gradient_kernel(backs, sizes, model_cols, *refs):
    pieces, refs = refs[: len(backs)], refs[len(backs) :]
    forward, right, proj, proj_h, w_down, out, sums, tokens, stacked, buffers, arrived = refs
    fetch, run = stream_products((w_down,), tokens, sums, buffers, arrived)
    fetch()
    place_pieces(pieces, backs, sizes, tokens)
    sums[...] = jnp.zeros_like(sums)
    rank = proj.shape[0] // 3
    last = model_side(proj[2 * rank :, :], tokens, model_cols)
    run()
    hidden_units, count = sums.shape[1:]
    tile = 128 if hidden_units % 128 == 0 else 32

    @pl.loop(0, hidden_units // tile)
    def _(step):
        rows = pl.ds(pl.multiple_of(step * tile, tile), tile)
        grad, gate_value, up_value = sums[0, rows, :], forward[0, rows, :], forward[1, rows, :]
        s = 1.0 / (1.0 + jnp.exp(-gate_value))
        silu = gate_value * s
        stacked[0, rows, :] = (
            grad * up_value * s * (1.0 + gate_value * (1.0 - s))
        ).astype(BF16)
        stacked[1, rows, :] = (grad * silu).astype(BF16)
        stacked[2, rows, :] = (silu * up_value).astype(BF16)

    sides = [
        jnp.dot(proj_h[p * rank : (p + 1) * rank, :], stacked[k], preferred_element_type=F32)
        for k, p in enumerate((1, 2, 0))
    ]
    every = jnp.concatenate(sides + [right[...], last], 0)
    size, each = sizes[0], count // int(np.prod(sizes))
    line = size * each
    source = lax.broadcasted_iota(jnp.int32, (count, count), 0)
    target = lax.broadcasted_iota(jnp.int32, (count, count), 1)
    back = lax.rem(lax.div(source, each), size)
    at = lax.rem(coordinate(lax.axis_index("dp"), sizes, 0) + size - back, size)
    place = lax.div(source, line) * line + at * each + lax.rem(source, each)
    order = (place == target).astype(F32)
    out[...] = jnp.dot(every, order, precision=HIGHEST, preferred_element_type=F32).reshape(
        out.shape
    )


def kernel_options(weights, tokens):
    hidden, width = weights[0].shape
    return dict(
        compiler_params=pltpu.CompilerParams(vmem_limit_bytes=44 * 2**20),
        cost_estimate=pl.CostEstimate(
            flops=2 * len(weights) * hidden * width * tokens,
            bytes_accessed=2 * len(weights) * hidden * width,
            transcendentals=hidden * tokens,
        ),
    )


def stream_scratch(weights, tokens, depth):
    hidden, width = weights[0].shape
    chunk = min(width, 1024)
    return [
        pltpu.VMEM((tokens, width), BF16),
        pltpu.VMEM((depth, len(weights), hidden, chunk), BF16),
        pltpu.SemaphoreType.DMA((depth, len(weights))),
    ]


def input_products(pieces, backs, sizes, model_cols, proj, weights):
    hidden = weights[0].shape[0]
    tokens = pieces[0].shape[0] * len(pieces)
    return pl.pallas_call(
        functools.partial(input_kernel, backs, sizes, model_cols),
        out_shape=(
            jax.ShapeDtypeStruct((2, hidden, tokens), F32),
            jax.ShapeDtypeStruct((proj.shape[0] // 3 * 2, tokens), F32),
        ),
        in_specs=[VMEM] * (len(pieces) + 1) + [ANY] * 2,
        out_specs=(VMEM, VMEM),
        scratch_shapes=stream_scratch(weights, tokens, 2),
        name="input_products",
        **kernel_options(weights, tokens),
    )(*pieces, proj, *weights)


def gradient_products(pieces, backs, sizes, model_cols, forward, right, proj, proj_h, w_down):
    hidden = w_down.shape[0]
    tokens = pieces[0].shape[0] * len(pieces)
    rest = int(np.prod(sizes[1:]))
    scratch = stream_scratch((w_down,), tokens, 4)
    return pl.pallas_call(
        functools.partial(gradient_kernel, backs, sizes, model_cols),
        out_shape=jax.ShapeDtypeStruct((rest, 2 * proj.shape[0] // rest, tokens), F32),
        in_specs=[VMEM] * (len(pieces) + 4) + [ANY],
        out_specs=VMEM,
        scratch_shapes=[pltpu.VMEM((1, hidden, tokens), F32), scratch[0]]
        + [pltpu.VMEM((3, hidden, tokens), BF16)]
        + scratch[1:],
        name="gradient_products",
        **kernel_options((w_down,), tokens),
    )(*pieces, forward, right, proj, proj_h, w_down)


def sum_kernel(values, out):
    total = jnp.sum(values[...], 0)
    out[...] = jnp.broadcast_to(total[None], out.shape)


def sum_copies(values, copies):
    return pl.pallas_call(
        sum_kernel,
        out_shape=jax.ShapeDtypeStruct((copies,) + values.shape[1:], F32),
        in_specs=[VMEM],
        out_specs=VMEM,
        name="sum_copies",
    )(values)


def halves(value):
    high = value.astype(BF16)
    return high, (value - high.astype(F32)).astype(BF16)


def sketch_kernel(sizes, order, vectors, means, ids, sketches, scores, lefts, turned):
    count = int(np.prod(sizes))
    rank = sketches.shape[2]
    tokens = ids.shape[1]
    own_rank = means.shape[2] // rank
    every = vectors[...].reshape(6 * rank, tokens)
    onehot = (ids[...] == lax.broadcasted_iota(jnp.int32, (SEQS, tokens), 0)).astype(F32)
    masks = jnp.concatenate([onehot.astype(BF16)] * 3, 1)
    norm = jnp.zeros((SEQS, 1), F32)
    if own_rank * count > rank:
        lefts[...] = jnp.zeros_like(lefts)
    for k in range(3):
        left = every[k * rank : (k + 1) * rank]
        right = every[(3 + k) * rank : (4 + k) * rank]
        left_high, left_low = halves(left)
        right_high, right_low = halves(right)
        left_three = jnp.concatenate([left_high, left_high, left_low], 1)
        right_three = jnp.concatenate([right_high, right_low, right_high], 1)
        rows = jnp.concatenate([left_three * masks[s : s + 1, :] for s in range(SEQS)], 0)
        sketch = transposed_dot(rows, right_three).reshape(SEQS, rank, rank)
        sketches[:, k] = sketch
        norm += jnp.sum(jnp.sum(sketch * sketch, 1), 1, keepdims=True)

        for i in range(own_rank):
            part = left[i * count : (i + 1) * count]
            lefts[k, : part.shape[0], i * tokens : (i + 1) * tokens] = part
        mean = means[:, k * DOMAINS : (k + 1) * DOMAINS, :].reshape(-1, own_rank * rank)
        result = 0.0
        for part in (right_high, right_low):
            empty = jnp.zeros_like(part)
            wide = jnp.concatenate(
                [
                    jnp.concatenate([part if i == c else empty for c in range(own_rank)], 1)
                    for i in range(own_rank)
                ],
                0,
            )
            result += jnp.dot(mean, wide, preferred_element_type=F32)
        turned[k] = result.reshape(count, DOMAINS, own_rank * tokens)

    me = lax.axis_index("dp")

    def add(device, total):
        place, step = 0, 1
        for axis in order:
            size = sizes[axis]
            back = coordinate(me, sizes, axis) + size - coordinate(device, sizes, axis)
            place += lax.rem(back, size) * step
            step *= size
        for k in range(3):
            total += turned[k, place] * lefts[k, pl.ds(device, 1), :]
        return total

    total = lax.fori_loop(0, count, add, jnp.zeros((DOMAINS, own_rank * tokens), F32))
    total = sum(total[:, i * tokens : (i + 1) * tokens] for i in range(own_rank))
    scores[...] = transposed_dot(onehot, total, HIGHEST) * lax.rsqrt(norm + 1e-06)


def on_device(
    count,
    activations,
    cotangent,
    w_gate,
    w_up,
    w_down,
    proj_model,
    proj_hidden,
    seq_ids,
    targets,
    target_domain,
):
    sizes = axis_sizes(count)
    rank = proj_model.shape[1] // 3
    model_cols = proj_model.shape[0]
    own_rank = -(-rank // count)
    padded = own_rank * count
    tokens = count * activations.shape[0]
    examples = targets.shape[0]
    inner = list(range(1, len(sizes)))
    flipped = inner[:-1][::-1] + inner[-1:]

    in_pieces, in_backs = gather_pieces(activations, sizes, flipped)
    out_pieces, out_backs = gather_pieces(cotangent, sizes, inner)

    cut = jnp.pad(targets, ((0, 0), (0, 0), (0, padded - rank), (0, 0)))
    cut = cut.reshape(examples, 3, own_rank, count, rank).transpose(3, 0, 1, 2, 4)
    entries = 3 * own_rank * rank
    cut = cut.reshape(count, examples, entries)
    tags = jnp.broadcast_to(target_domain.astype(BF16)[None, :, None], (count, examples, 128))
    sent, _ = lax.optimization_barrier((jnp.concatenate([cut, tags], 2), in_pieces[1]))
    held = exchange(sent).reshape(count * examples, -1)
    domains = held[:, -1].astype(F32)
    domain_onehot = (domains[None, :] == jnp.arange(DOMAINS, dtype=F32)[:, None]).astype(BF16)
    domain_sum = jnp.dot(domain_onehot, held[:, :entries], preferred_element_type=F32)
    domain_count = jnp.sum(domain_onehot.astype(F32), 1)
    mean = (domain_sum / domain_count[:, None]).astype(BF16)
    mean = mean.reshape(DOMAINS, 3, own_rank * rank).transpose(1, 0, 2)
    mean_order = [0] + flipped
    means = gather_stack(mean.reshape(3 * DOMAINS, -1), sizes, mean_order)
    means = means.reshape((count,) + means.shape[-2:])

    window = max(model_cols, 128)
    proj_m = proj_model.T
    if window > model_cols:
        at = lax.rem(lax.axis_index("dp"), window // model_cols)
        spots = [
            jnp.where(at == i, proj_m, jnp.zeros_like(proj_m)) for i in range(window // model_cols)
        ]
        proj_m = jnp.concatenate(spots, 1)

    forward, right = input_products(
        in_pieces, in_backs, sizes, model_cols, proj_m, (w_gate, w_up)
    )
    vectors = gradient_products(
        out_pieces, out_backs, sizes, model_cols, forward, right, proj_m, proj_hidden.T, w_down
    )
    first, rest = sizes[0], count // sizes[0]
    planes = [[z * rest + r for r in range(rest)] for z in range(first)]
    lines = [[z * rest + r for z in range(first)] for r in range(rest)]
    vectors = sum_copies(exchange(vectors, planes), first)
    vectors = sum_copies(exchange(vectors, lines), rest)
    vectors = exchange(vectors, planes)

    return pl.pallas_call(
        functools.partial(sketch_kernel, sizes, mean_order),
        out_shape=(
            jax.ShapeDtypeStruct((SEQS, 3, rank, rank), F32),
            jax.ShapeDtypeStruct((SEQS, DOMAINS), F32),
        ),
        in_specs=[VMEM] * 3,
        out_specs=(VMEM, VMEM),
        scratch_shapes=[
            pltpu.VMEM((3, count, own_rank * tokens), F32),
            pltpu.VMEM((3, count, DOMAINS, own_rank * tokens), F32),
        ],
        compiler_params=pltpu.CompilerParams(vmem_limit_bytes=52 * 2**20),
        name="sketches",
    )(vectors, means, slot_order(seq_ids, sizes)[None, :])


def solution(mesh):
    in_specs = (
        P(("groups", "dp"), None),
        P(("groups", "dp"), None),
        P("dp", None),
        P("dp", None),
        P("dp", None),
        P("dp", None),
        P("dp", None),
        P("groups"),
        P(("groups", "dp"), None, None, None),
        P(("groups", "dp")),
    )
    out_specs = (P("groups", None, None, None), P("groups", None))
    return jax.shard_map(
        functools.partial(on_device, mesh.shape["dp"]),
        mesh=mesh,
        in_specs=in_specs,
        out_specs=out_specs,
        check_vma=False,
    )
```

time: 478 us -> 123 us (0.26)
  waiting for transfers between devices: 373 us -> 32.7 us
  matrix products: 38.8 us -> 0.16 us
  starting transfers between devices: 0.34 us -> 35.7 us
  Pallas kernels: 0 us -> 26.9 us
  blocking collectives: 39.3 us -> 19.2 us
  between operations: 13.9 us -> 0.84 us
  local copies, waits for them, and re-layouts: 10.4 us -> 2.84 us
    psum x1 -> x0, waiting for transfers between devices: 133 us -> none  [on_device(): sketches = lax.psum(local_sketch, 'dp')]
    unnamed x5 -> x0, waiting for transfers between devices: 123 us -> none
    all_gather x2 -> x0, waiting for transfers between devices: 116 us -> none  [the longest x1 60.5 us: on_device(): rows_in = lax.all_gather(activations, 'dp', axis=0, tiled=True)]
    psum x1 -> x0, blocking collectives: 39.3 us -> none  [on_device(): total_scores, total_count = lax.psum((folded, domain_count), 'dp')]
    dot_general x11 -> x1, matrix products: 38.8 us -> 0.16 us  [on_device(): jnp.dot(domain_onehot, held[:, :entries], preferred_element_type=F32)]
    ppermute x0 -> x26, starting transfers between devices: none -> 28.3 us  [shift(): return lax.ppermute(value, 'dp', pairs)]
    pallas_call x0 -> x5, Pallas kernels: none -> 26.9 us  [the longest x1 12.1 us: input_products(): pl.pallas_call(functools.partial(input_kernel, backs, sizes, model_cols),...]
    ppermute x0 -> x26, waiting for transfers between devices: none -> 20.8 us  [shift(): return lax.ppermute(value, 'dp', pairs)]
  transfers between devices with their start and end apart: 4 -> 28, of which waited for: 4 -> 11; matrix products, arithmetic and copies ran while one was open for 1% -> 4% of each run, Pallas kernels for 0% -> 19%
where the time goes in v3:
time: 123 us; the launch traced here: 122 us
  starting transfers between devices  35.7 us (29%)
  waiting for transfers between devices  32.7 us (27%)
  Pallas kernels  26.9 us (22%)
  blocking collectives  19.2 us (16%)
  other arithmetic  3.77 us (3%)
  local copies, waits for them, and re-layouts  2.84 us (2%)
    ppermute x26, starting transfers between devices, shift(): return lax.ppermute(value, 'dp', pairs)  28.3 us
    ppermute x26, waiting for transfers between devices, shift(): return lax.ppermute(value, 'dp', pairs)  20.8 us
    all_to_all x2, blocking collectives, exchange(): lax.all_to_all(blocks, 'dp', split_axis=0, concat_axis=0, axis_index_grou...  19.2 us
    pallas_call x1, Pallas kernels, input_products(): pl.pallas_call(functools.partial(input_kernel, backs, sizes, model_cols),...  12.1 us
    all_to_all x2, waiting for transfers between devices, exchange(): lax.all_to_all(blocks, 'dp', split_axis=0, concat_axis=0, axis_index_grou...  11.9 us
    pallas_call x1, Pallas kernels, gradient_products(): pl.pallas_call(functools.partial(gradient_kernel, backs, sizes, model_col...  7.72 us
    all_to_all x2, starting transfers between devices, exchange(): lax.all_to_all(blocks, 'dp', split_axis=0, concat_axis=0, axis_index_grou...  7.33 us
    pallas_call x1, Pallas kernels, on_device(): pl.pallas_call(functools.partial(sketch_kernel, sizes, mean_order), out_s...  3.93 us
  transfers between devices with their start and end apart: 28, of which 11 were waited for; matrix products, arithmetic and copies ran while one was open for 4% of the time, Pallas kernels for 19%

profile of v3, /device:TPU:0, one launch (start us, length us, event | category | flops | bytes accessed | tf_op | source)
XLA Modules:
  0.0 122.1 jit_solution(15820518724059785977)
XLA Ops:
  0.6 3.1 %collective-permute-start.10 = (bf16[4,8192]{1,0:T(4,128)(2,1)}, bf16[4,8192]{1,0:T(4,128)(2,1)S(1)}, u32[]{:S(2)}, u32[]{:S(2)}) collective-permute-start(bf16[4,8192]{1,0:T(4,128)(2,1)} %param.10), channel_id=1, source_target_pairs={{0,8},{1,9},{2,10},{3,11},{4,12},{5,13},{6,14},{7,15},{8,16},{9,17... | collective-permute-start | bytes 196616 | tf_op jit(solution)/shard_map/ppermute | solution.py:38
  3.7 2.6 %collective-permute-start.11 = (bf16[4,8192]{1,0:T(4,128)(2,1)}, bf16[4,8192]{1,0:T(4,128)(2,1)S(1)}, u32[]{:S(2)}, u32[]{:S(2)}) collective-permute-start(bf16[4,8192]{1,0:T(4,128)(2,1)} %param.10), channel_id=1, source_target_pairs={{0,16},{1,17},{2,18},{3,19},{4,20},{5,21},{6,22},{7,23},{8,24},{9,... | collective-permute-start | bytes 196616 | tf_op jit(solution)/shard_map/ppermute | solution.py:38
  6.3 1.3 %collective-permute-start.12 = (bf16[4,8192]{1,0:T(4,128)(2,1)}, bf16[4,8192]{1,0:T(4,128)(2,1)S(1)}, u32[]{:S(2)}, u32[]{:S(2)}) collective-permute-start(bf16[4,8192]{1,0:T(4,128)(2,1)} %param.10), channel_id=1, source_target_pairs={{0,24},{1,25},{2,26},{3,27},{4,28},{5,29},{6,30},{7,31},{8,0},{9,1... | collective-permute-start | bytes 196616 | tf_op jit(solution)/shard_map/ppermute | solution.py:38
  7.6 0.8 collective-permute-done.10
  8.5 2.5 %collective-permute-done.11 = bf16[4,8192]{1,0:T(4,128)(2,1)S(1)} collective-permute-done((bf16[4,8192]{1,0:T(4,128)(2,1)}, bf16[4,8192]{1,0:T(4,128)(2,1)S(1)}, u32[]{:S(2)}, u32[]{:S(2)}) %collective-permute-start.11) | collective-permute-done | bytes 65568 | tf_op jit(solution)/shard_map/ppermute | solution.py:38
  11.0 0.2 collective-permute-done.12
  11.2 1.0 pad_maximum_fusion.3.refs_0_
  12.2 1.6 %collective-permute-start.13 = (bf16[16,8192]{1,0:T(8,128)(2,1)S(1)}, bf16[16,8192]{1,0:T(8,128)(2,1)S(1)}, u32[]{:S(2)}, u32[]{:S(2)}) collective-permute-start(bf16[16,8192]{1,0:T(8,128)(2,1)S(1)} %pad_maximum_fusion.3.refs_0_), channel_id=1, source_target_pairs={{0,2},{1,3},{2,0},{3,1},{4,6},{5,7},{6,4},{7,5},{8,10},{9,11},{10,... | collective-permute-start | bytes 786440 | tf_op jit(solution)/shard_map/ppermute | solution.py:38
  13.8 1.3 %copy.31 = bf16[8,3,2,32,64]{4,2,1,0,3:T(2,128)(2,1)S(1)} copy(bf16[8,3,2,32,64]{4,3,2,1,0:T(8,128)(2,1)} %bitcast.32) | data formatting | bytes 393216 | tf_op jit(solution)/shard_map/reshape | solution.py:347
  15.1 0.3 reshape.35
  15.4 0.7 convert_element_type.22
  16.1 0.7 pad_maximum_fusion.4
  16.9 3.2 %collective-permute-done.13.refs_1_ = bf16[16,8192]{1,0:T(8,128)(2,1)S(1)} collective-permute-done((bf16[16,8192]{1,0:T(8,128)(2,1)S(1)}, bf16[16,8192]{1,0:T(8,128)(2,1)S(1)}, u32[]{:S(2)}, u32[]{:S(2)}) %collective-permute-start.13) | collective-permute-done | bytes 262176 | tf_op jit(solution)/shard_map/ppermute | solution.py:38
  20.1 3.9 %all-to-all-start.3 = ((bf16[32,8,512]{2,1,0:T(8,128)(2,1)}), bf16[32,8,512]{2,1,0:T(8,128)(2,1)S(1)}, u32[]{:S(2)}, u32[]{:S(2)}) async-start(bf16[32,8,512]{2,1,0:T(8,128)(2,1)} %pad_maximum_fusion.4), calls=%async_computation.3 | async-start | bytes 524288 | tf_op jit(solution)/shard_map/all_to_all | solution.py:71
  24.0 1.8 %collective-permute-start = (bf16[4,8192]{1,0:T(4,128)(2,1)}, bf16[4,8192]{1,0:T(4,128)(2,1)S(1)}, u32[]{:S(2)}, u32[]{:S(2)}) collective-permute-start(bf16[4,8192]{1,0:T(4,128)(2,1)} %param.11), channel_id=1, source_target_pairs={{0,8},{1,9},{2,10},{3,11},{4,12},{5,13},{6,14},{7,15},{8,16},{9,17... | collective-permute-start | bytes 196616 | tf_op jit(solution)/shard_map/ppermute | solution.py:38
  25.9 2.4 %collective-permute-start.1 = (bf16[4,8192]{1,0:T(4,128)(2,1)}, bf16[4,8192]{1,0:T(4,128)(2,1)S(1)}, u32[]{:S(2)}, u32[]{:S(2)}) collective-permute-start(bf16[4,8192]{1,0:T(4,128)(2,1)} %param.11), channel_id=1, source_target_pairs={{0,16},{1,17},{2,18},{3,19},{4,20},{5,21},{6,22},{7,23},{8,24},{9,... | collective-permute-start | bytes 196616 | tf_op jit(solution)/shard_map/ppermute | solution.py:38
  28.3 1.4 %collective-permute-start.2 = (bf16[4,8192]{1,0:T(4,128)(2,1)}, bf16[4,8192]{1,0:T(4,128)(2,1)S(1)}, u32[]{:S(2)}, u32[]{:S(2)}) collective-permute-start(bf16[4,8192]{1,0:T(4,128)(2,1)} %param.11), channel_id=1, source_target_pairs={{0,24},{1,25},{2,26},{3,27},{4,28},{5,29},{6,30},{7,31},{8,0},{9,1... | collective-permute-start | bytes 196616 | tf_op jit(solution)/shard_map/ppermute | solution.py:38
  29.7 1.5 %collective-permute-start.14 = (bf16[16,8192]{1,0:T(8,128)(2,1)S(1)}, bf16[16,8192]{1,0:T(8,128)(2,1)S(1)}, u32[]{:S(2)}, u32[]{:S(2)}) collective-permute-start(bf16[16,8192]{1,0:T(8,128)(2,1)S(1)} %pad_maximum_fusion.3.refs_0_), channel_id=1, source_target_pairs={{0,4},{1,5},{2,6},{3,7},{4,0},{5,1},{6,2},{7,3},{8,12},{9,13},{10,... | collective-permute-start | bytes 786440 | tf_op jit(solution)/shard_map/ppermute | solution.py:38
  31.2 6.0 %all-to-all-done.3 = bf16[32,8,512]{2,1,0:T(8,128)(2,1)S(1)} async-done(((bf16[32,8,512]{2,1,0:T(8,128)(2,1)}), bf16[32,8,512]{2,1,0:T(8,128)(2,1)S(1)}, u32[]{:S(2)}, u32[]{:S(2)}) %all-to-all-start.3) | async-done | bytes 262176 | tf_op jit(solution)/shard_map/all_to_all | solution.py:71
  37.5 0.2 fusion
  37.7 0.5 collective-permute-start.21
  38.2 1.0 pad_maximum_fusion.2.refs_0_
  39.2 1.6 %collective-permute-start.3 = (bf16[16,8192]{1,0:T(8,128)(2,1)S(1)}, bf16[16,8192]{1,0:T(8,128)(2,1)S(1)}, u32[]{:S(2)}, u32[]{:S(2)}) collective-permute-start(bf16[16,8192]{1,0:T(8,128)(2,1)S(1)} %pad_maximum_fusion.2.refs_0_), channel_id=1, source_target_pairs={{0,4},{1,5},{2,6},{3,7},{4,0},{5,1},{6,2},{7,3},{8,12},{9,13},{10,... | collective-permute-start | bytes 786440 | tf_op jit(solution)/shard_map/ppermute | solution.py:38
  40.9 2.4 %collective-permute-start.22 = (bf16[96,128]{1,0:T(8,128)(2,1)S(1)}, bf16[96,128]{1,0:T(8,128)(2,1)S(1)}, u32[]{:S(2)}, u32[]{:S(2)}) collective-permute-start(bf16[96,128]{1,0:T(8,128)(2,1)S(1)} %bitcast.38), channel_id=1, source_target_pairs={{0,24},{1,25},{2,26},{3,27},{4,28},{5,29},{6,30},{7,31},{8,0},{9,1... | collective-permute-start | bytes 73736 | tf_op jit(solution)/shard_map/ppermute | solution.py:38
  43.3 1.2 collective-permute-start.15
  44.5 0.3 collective-permute-done.22
  44.8 1.2 collective-permute-start.20
  46.0 4.8 %collective-permute-done.20 = bf16[96,128]{1,0:T(8,128)(2,1)S(1)} collective-permute-done((bf16[96,128]{1,0:T(8,128)(2,1)S(1)}, bf16[96,128]{1,0:T(8,128)(2,1)S(1)}, u32[]{:S(2)}, u32[]{:S(2)}) %collective-permute-start.20) | collective-permute-done | bytes 24608 | tf_op jit(solution)/shard_map/ppermute | solution.py:38
  50.8 1.4 %collective-permute-start.23 = (bf16[4,96,128]{2,1,0:T(8,128)(2,1)S(1)}, bf16[4,96,128]{2,1,0:T(8,128)(2,1)S(1)}, u32[]{:S(2)}, u32[]{:S(2)}) collective-permute-start(bf16[4,96,128]{2,1,0:T(8,128)(2,1)S(1)} %get-tuple-element.13), channel_id=1, source_target_pairs={{0,2},{1,3},{2,0},{3,1},{4,6},{5,7},{6,4},{7,5},{8,10},{9,11},{10,... | collective-permute-start | bytes 294920 | tf_op jit(solution)/shard_map/ppermute | solution.py:38
  52.2 0.7 collective-permute-start.4
  52.9 0.5 collective-permute-start.18
  53.4 1.3 %collective-permute-start.5 = (bf16[16,8192]{1,0:T(8,128)(2,1)S(1)}, bf16[16,8192]{1,0:T(8,128)(2,1)S(1)}, u32[]{:S(2)}, u32[]{:S(2)}) collective-permute-start(bf16[16,8192]{1,0:T(8,128)(2,1)S(1)} %collective-permute-done.3.refs_1_), channel_id=1, source_target_pairs={{0,2},{1,3},{2,0},{3,1},{4,6},{5,7},{6,4},{7,5},{8,10},{9,11},{10,... | collective-permute-start | bytes 786440 | tf_op jit(solution)/shard_map/ppermute | solution.py:38
  54.7 1.1 collective-permute-done.23
  55.9 5.3 %collective-permute-done.4.refs_2_ = bf16[16,8192]{1,0:T(8,128)(2,1)S(1)} collective-permute-done((bf16[16,8192]{1,0:T(8,128)(2,1)S(1)}, bf16[16,8192]{1,0:T(8,128)(2,1)S(1)}, u32[]{:S(2)}, u32[]{:S(2)}) %collective-permute-start.4) | collective-permute-done | bytes 262176 | tf_op jit(solution)/shard_map/ppermute | solution.py:38
  61.2 0.5 collective-permute-start.7
  61.7 2.5 %collective-permute-done.5.refs_3_ = bf16[16,8192]{1,0:T(8,128)(2,1)S(1)} collective-permute-done((bf16[16,8192]{1,0:T(8,128)(2,1)S(1)}, bf16[16,8192]{1,0:T(8,128)(2,1)S(1)}, u32[]{:S(2)}, u32[]{:S(2)}) %collective-permute-start.5) | collective-permute-done | bytes 262176 | tf_op jit(solution)/shard_map/ppermute | solution.py:38
  64.3 0.8 collective-permute-start.24
  65.1 0.9 copy-done
  66.0 12.1 %input_products.1 = (f32[2,896,128]{2,1,0:T(8,128)S(1)}, f32[128,128]{1,0:T(8,128)S(1)}) custom-call(bf16[16,8192]{1,0:T(8,128)(2,1)S(1)} %pad_maximum_fusion.3.refs_0_, bf16[16,8192]{1,0:T(8,128)(2,1)S(1)} %collective-permute-done.13.refs_1_, bf16[16,8192]{1,0:T(8,128)(2,1)S(1)} %collective-permute-done.14.refs_2_, ...), custom_call_target="tpu_custom_call" | custom-call | flops 3758096384 | bytes 29360128 | tf_op jit(solution)/shard_map/input_products/pallas_call | solution.py:210
  78.1 0.3 collective-permute-start.25
  78.5 7.7 %gradient_products.1 = f32[8,48,128]{2,1,0:T(8,128)S(1)} custom-call(bf16[16,8192]{1,0:T(8,128)(2,1)S(1)} %pad_maximum_fusion.2.refs_0_, bf16[16,8192]{1,0:T(8,128)(2,1)S(1)} %collective-permute-done.3.refs_1_, bf16[16,8192]{1,0:T(8,128)(2,1)S(1)} %collective-permute-done.4.refs_2_, bf16[16,8192]{1,0:T(8,128)(2,1)S(1)} %collective-permute-done.5.refs_3_, ...), custom_call_target="tpu_custom_call" | custom-call | flops 1879048192 | bytes 14680064 | tf_op jit(solution)/shard_map/gradient_products/pallas_call | solution.py:229
  86.2 9.4 %all_to_all.20.values = f32[8,48,128]{2,1,0:T(8,128)} all-to-all(f32[8,48,128]{2,1,0:T(8,128)S(1)} %gradient_products.1), channel_id=1, replica_groups={{0,1,2,3,4,5,6,7},{8,9,10,11,12,13,14,15},{16,17,18,19,20,21,22,23},{24..., dimensions={0} | all-to-all | bytes 393216 | tf_op jit(solution)/shard_map/all_to_all | solution.py:71
  95.6 1.6 %sum_copies.2 = f32[4,48,128]{2,1,0:T(8,128)} custom-call(f32[8,48,128]{2,1,0:T(8,128)} %all_to_all.20.values), custom_call_target="tpu_custom_call" | custom-call | tf_op jit(solution)/shard_map/sum_copies/pallas_call | solution.py:248
  97.2 9.8 %all_to_all.21.values = f32[4,48,128]{2,1,0:T(8,128)} all-to-all(f32[4,48,128]{2,1,0:T(8,128)} %sum_copies.2), channel_id=1, replica_groups={{0,8,16,24},{1,9,17,25},{2,10,18,26},{3,11,19,27},{4,12,20,28},{5,13,21..., dimensions={0} | all-to-all | bytes 196608 | tf_op jit(solution)/shard_map/all_to_all | solution.py:71
  107.0 1.6 %sum_copies.3 = f32[8,48,128]{2,1,0:T(8,128)} custom-call(f32[4,48,128]{2,1,0:T(8,128)} %all_to_all.21.values), custom_call_target="tpu_custom_call" | custom-call | tf_op jit(solution)/shard_map/sum_copies/pallas_call | solution.py:248
  108.6 3.4 %all-to-all-start.2 = ((f32[8,48,128]{2,1,0:T(8,128)}), f32[8,48,128]{2,1,0:T(8,128)S(1)}, u32[]{:S(2)}, u32[]{:S(2)}) async-start(f32[8,48,128]{2,1,0:T(8,128)} %sum_copies.3), calls=%async_computation.2 | async-start | bytes 393216 | tf_op jit(solution)/shard_map/all_to_all | solution.py:71
  112.3 5.8 %all-to-all-done.2.vectors = f32[8,48,128]{2,1,0:T(8,128)S(1)} async-done(((f32[8,48,128]{2,1,0:T(8,128)}), f32[8,48,128]{2,1,0:T(8,128)S(1)}, u32[]{:S(2)}, u32[]{:S(2)}) %all-to-all-start.2) | async-done | bytes 196640 | tf_op jit(solution)/shard_map/all_to_all | solution.py:71
  118.1 3.9 %sketches.1 = (f32[16,3,64,64]{3,2,1,0:T(8,128)}, f32[16,32]{1,0:T(8,128)}) custom-call(f32[8,48,128]{2,1,0:T(8,128)S(1)} %all-to-all-done.2.vectors, bf16[32,96,128]{2,1,0:T(8,128)(2,1)S(1)} %bitcast.25, s32[1,128]{1,0:T(1,128)S(1)} %broadcast_in_dim_reshape.3.ids), custom_call_target="tpu_custom_call" | custom-call | tf_op jit(solution)/shard_map/sketches/pallas_call | solution.py:385
  (41 shorter events, 0.9 us)
Async XLA Ops:
  0.6 7.8 %collective-permute-start.10 = (bf16[4,8192]{1,0:T(4,128)(2,1)}, bf16[4,8192]{1,0:T(4,128)(2,1)S(1)}, u32[]{:S(2)}, u32[]{:S(2)}) collective-permute-start(bf16[4,8192]{1,0:T(4,128)(2,1)} %param.10), channel_id=1, source_target_pairs={{0,8},{1,9},{2,10},{3,11},{4,12},{5,13},{6,14},{7,15},{8,16},{9,17... | collective-permute-start | bytes 196616 | tf_op jit(solution)/shard_map/ppermute | solution.py:38
  3.7 7.3 %collective-permute-start.11 = (bf16[4,8192]{1,0:T(4,128)(2,1)}, bf16[4,8192]{1,0:T(4,128)(2,1)S(1)}, u32[]{:S(2)}, u32[]{:S(2)}) collective-permute-start(bf16[4,8192]{1,0:T(4,128)(2,1)} %param.10), channel_id=1, source_target_pairs={{0,16},{1,17},{2,18},{3,19},{4,20},{5,21},{6,22},{7,23},{8,24},{9,... | collective-permute-start | bytes 196616 | tf_op jit(solution)/shard_map/ppermute | solution.py:38
  6.3 4.9 %collective-permute-start.12 = (bf16[4,8192]{1,0:T(4,128)(2,1)}, bf16[4,8192]{1,0:T(4,128)(2,1)S(1)}, u32[]{:S(2)}, u32[]{:S(2)}) collective-permute-start(bf16[4,8192]{1,0:T(4,128)(2,1)} %param.10), channel_id=1, source_target_pairs={{0,24},{1,25},{2,26},{3,27},{4,28},{5,29},{6,30},{7,31},{8,0},{9,1... | collective-permute-start | bytes 196616 | tf_op jit(solution)/shard_map/ppermute | solution.py:38
  12.2 7.9 %collective-permute-start.13 = (bf16[16,8192]{1,0:T(8,128)(2,1)S(1)}, bf16[16,8192]{1,0:T(8,128)(2,1)S(1)}, u32[]{:S(2)}, u32[]{:S(2)}) collective-permute-start(bf16[16,8192]{1,0:T(8,128)(2,1)S(1)} %pad_maximum_fusion.3.refs_0_), channel_id=1, source_target_pairs={{0,2},{1,3},{2,0},{3,1},{4,6},{5,7},{6,4},{7,5},{8,10},{9,11},{10,... | collective-permute-start | bytes 786440 | tf_op jit(solution)/shard_map/ppermute | solution.py:38
  20.1 17.1 %all-to-all-start.3 = ((bf16[32,8,512]{2,1,0:T(8,128)(2,1)}), bf16[32,8,512]{2,1,0:T(8,128)(2,1)S(1)}, u32[]{:S(2)}, u32[]{:S(2)}) async-start(bf16[32,8,512]{2,1,0:T(8,128)(2,1)} %pad_maximum_fusion.4), calls=%async_computation.3 | async-start | bytes 524288 | tf_op jit(solution)/shard_map/all_to_all | solution.py:71
  24.0 13.7 %collective-permute-start = (bf16[4,8192]{1,0:T(4,128)(2,1)}, bf16[4,8192]{1,0:T(4,128)(2,1)S(1)}, u32[]{:S(2)}, u32[]{:S(2)}) collective-permute-start(bf16[4,8192]{1,0:T(4,128)(2,1)} %param.11), channel_id=1, source_target_pairs={{0,8},{1,9},{2,10},{3,11},{4,12},{5,13},{6,14},{7,15},{8,16},{9,17... | collective-permute-start | bytes 196616 | tf_op jit(solution)/shard_map/ppermute | solution.py:38
  25.9 12.4 %collective-permute-start.1 = (bf16[4,8192]{1,0:T(4,128)(2,1)}, bf16[4,8192]{1,0:T(4,128)(2,1)S(1)}, u32[]{:S(2)}, u32[]{:S(2)}) collective-permute-start(bf16[4,8192]{1,0:T(4,128)(2,1)} %param.11), channel_id=1, source_target_pairs={{0,16},{1,17},{2,18},{3,19},{4,20},{5,21},{6,22},{7,23},{8,24},{9,... | collective-permute-start | bytes 196616 | tf_op jit(solution)/shard_map/ppermute | solution.py:38
  28.3 10.0 %collective-permute-start.2 = (bf16[4,8192]{1,0:T(4,128)(2,1)}, bf16[4,8192]{1,0:T(4,128)(2,1)S(1)}, u32[]{:S(2)}, u32[]{:S(2)}) collective-permute-start(bf16[4,8192]{1,0:T(4,128)(2,1)} %param.11), channel_id=1, source_target_pairs={{0,24},{1,25},{2,26},{3,27},{4,28},{5,29},{6,30},{7,31},{8,0},{9,1... | collective-permute-start | bytes 196616 | tf_op jit(solution)/shard_map/ppermute | solution.py:38
  29.7 22.5 %collective-permute-start.14 = (bf16[16,8192]{1,0:T(8,128)(2,1)S(1)}, bf16[16,8192]{1,0:T(8,128)(2,1)S(1)}, u32[]{:S(2)}, u32[]{:S(2)}) collective-permute-start(bf16[16,8192]{1,0:T(8,128)(2,1)S(1)} %pad_maximum_fusion.3.refs_0_), channel_id=1, source_target_pairs={{0,4},{1,5},{2,6},{3,7},{4,0},{5,1},{6,2},{7,3},{8,12},{9,13},{10,... | collective-permute-start | bytes 786440 | tf_op jit(solution)/shard_map/ppermute | solution.py:38
  31.2 21.7 %collective-permute-start.16 = (bf16[16,8192]{1,0:T(8,128)(2,1)S(1)}, bf16[16,8192]{1,0:T(8,128)(2,1)S(1)}, u32[]{:S(2)}, u32[]{:S(2)}) collective-permute-start(bf16[16,8192]{1,0:T(8,128)(2,1)S(1)} %pad_maximum_fusion.3.refs_0_), channel_id=1, source_target_pairs={{0,1},{1,0},{2,3},{3,2},{4,5},{5,4},{6,7},{7,6},{8,9},{9,8},{10,11... | collective-permute-start | bytes 786440 | tf_op jit(solution)/shard_map/ppermute | solution.py:38
  37.7 5.6 %collective-permute-start.21 = (bf16[96,128]{1,0:T(8,128)(2,1)S(1)}, bf16[96,128]{1,0:T(8,128)(2,1)S(1)}, u32[]{:S(2)}, u32[]{:S(2)}) collective-permute-start(bf16[96,128]{1,0:T(8,128)(2,1)S(1)} %bitcast.37), channel_id=1, source_target_pairs={{0,16},{1,17},{2,18},{3,19},{4,20},{5,21},{6,22},{7,23},{8,24},{9,... | collective-permute-start | bytes 73736 | tf_op jit(solution)/shard_map/ppermute | solution.py:38
  39.2 13.6 %collective-permute-start.3 = (bf16[16,8192]{1,0:T(8,128)(2,1)S(1)}, bf16[16,8192]{1,0:T(8,128)(2,1)S(1)}, u32[]{:S(2)}, u32[]{:S(2)}) collective-permute-start(bf16[16,8192]{1,0:T(8,128)(2,1)S(1)} %pad_maximum_fusion.2.refs_0_), channel_id=1, source_target_pairs={{0,4},{1,5},{2,6},{3,7},{4,0},{5,1},{6,2},{7,3},{8,12},{9,13},{10,... | collective-permute-start | bytes 786440 | tf_op jit(solution)/shard_map/ppermute | solution.py:38
  40.9 3.9 %collective-permute-start.22 = (bf16[96,128]{1,0:T(8,128)(2,1)S(1)}, bf16[96,128]{1,0:T(8,128)(2,1)S(1)}, u32[]{:S(2)}, u32[]{:S(2)}) collective-permute-start(bf16[96,128]{1,0:T(8,128)(2,1)S(1)} %bitcast.38), channel_id=1, source_target_pairs={{0,24},{1,25},{2,26},{3,27},{4,28},{5,29},{6,30},{7,31},{8,0},{9,1... | collective-permute-start | bytes 73736 | tf_op jit(solution)/shard_map/ppermute | solution.py:38
  43.3 10.1 %collective-permute-start.15 = (bf16[16,8192]{1,0:T(8,128)(2,1)S(1)}, bf16[16,8192]{1,0:T(8,128)(2,1)S(1)}, u32[]{:S(2)}, u32[]{:S(2)}) collective-permute-start(bf16[16,8192]{1,0:T(8,128)(2,1)S(1)} %collective-permute-done.13.refs_1_), channel_id=1, source_target_pairs={{0,4},{1,5},{2,6},{3,7},{4,0},{5,1},{6,2},{7,3},{8,12},{9,13},{10,... | collective-permute-start | bytes 786440 | tf_op jit(solution)/shard_map/ppermute | solution.py:38
  44.8 5.9 %collective-permute-start.20 = (bf16[96,128]{1,0:T(8,128)(2,1)S(1)}, bf16[96,128]{1,0:T(8,128)(2,1)S(1)}, u32[]{:S(2)}, u32[]{:S(2)}) collective-permute-start(bf16[96,128]{1,0:T(8,128)(2,1)S(1)} %bitcast.39), channel_id=1, source_target_pairs={{0,8},{1,9},{2,10},{3,11},{4,12},{5,13},{6,14},{7,15},{8,16},{9,17... | collective-permute-start | bytes 73736 | tf_op jit(solution)/shard_map/ppermute | solution.py:38
  50.8 5.1 %collective-permute-start.23 = (bf16[4,96,128]{2,1,0:T(8,128)(2,1)S(1)}, bf16[4,96,128]{2,1,0:T(8,128)(2,1)S(1)}, u32[]{:S(2)}, u32[]{:S(2)}) collective-permute-start(bf16[4,96,128]{2,1,0:T(8,128)(2,1)S(1)} %get-tuple-element.13), channel_id=1, source_target_pairs={{0,2},{1,3},{2,0},{3,1},{4,6},{5,7},{6,4},{7,5},{8,10},{9,11},{10,... | collective-permute-start | bytes 294920 | tf_op jit(solution)/shard_map/ppermute | solution.py:38
  52.2 9.0 %collective-permute-start.4 = (bf16[16,8192]{1,0:T(8,128)(2,1)S(1)}, bf16[16,8192]{1,0:T(8,128)(2,1)S(1)}, u32[]{:S(2)}, u32[]{:S(2)}) collective-permute-start(bf16[16,8192]{1,0:T(8,128)(2,1)S(1)} %pad_maximum_fusion.2.refs_0_), channel_id=1, source_target_pairs={{0,2},{1,3},{2,0},{3,1},{4,6},{5,7},{6,4},{7,5},{8,10},{9,11},{10,... | collective-permute-start | bytes 786440 | tf_op jit(solution)/shard_map/ppermute | solution.py:38
  52.9 8.3 %collective-permute-start.17 = (bf16[16,8192]{1,0:T(8,128)(2,1)S(1)}, bf16[16,8192]{1,0:T(8,128)(2,1)S(1)}, u32[]{:S(2)}, u32[]{:S(2)}) collective-permute-start(bf16[16,8192]{1,0:T(8,128)(2,1)S(1)} %collective-permute-done.13.refs_1_), channel_id=1, source_target_pairs={{0,1},{1,0},{2,3},{3,2},{4,5},{5,4},{6,7},{7,6},{8,9},{9,8},{10,11... | collective-permute-start | bytes 786440 | tf_op jit(solution)/shard_map/ppermute | solution.py:38
  52.9 8.8 %collective-permute-start.18 = (bf16[16,8192]{1,0:T(8,128)(2,1)S(1)}, bf16[16,8192]{1,0:T(8,128)(2,1)S(1)}, u32[]{:S(2)}, u32[]{:S(2)}) collective-permute-start(bf16[16,8192]{1,0:T(8,128)(2,1)S(1)} %collective-permute-done.14.refs_2_), channel_id=1, source_target_pairs={{0,1},{1,0},{2,3},{3,2},{4,5},{5,4},{6,7},{7,6},{8,9},{9,8},{10,11... | collective-permute-start | bytes 786440 | tf_op jit(solution)/shard_map/ppermute | solution.py:38
  53.4 10.9 %collective-permute-start.5 = (bf16[16,8192]{1,0:T(8,128)(2,1)S(1)}, bf16[16,8192]{1,0:T(8,128)(2,1)S(1)}, u32[]{:S(2)}, u32[]{:S(2)}) collective-permute-start(bf16[16,8192]{1,0:T(8,128)(2,1)S(1)} %collective-permute-done.3.refs_1_), channel_id=1, source_target_pairs={{0,2},{1,3},{2,0},{3,1},{4,6},{5,7},{6,4},{7,5},{8,10},{9,11},{10,... | collective-permute-start | bytes 786440 | tf_op jit(solution)/shard_map/ppermute | solution.py:38
  55.8 8.4 %collective-permute-start.19 = (bf16[16,8192]{1,0:T(8,128)(2,1)S(1)}, bf16[16,8192]{1,0:T(8,128)(2,1)S(1)}, u32[]{:S(2)}, u32[]{:S(2)}) collective-permute-start(bf16[16,8192]{1,0:T(8,128)(2,1)S(1)} %collective-permute-done.15.refs_3_), channel_id=1, source_target_pairs={{0,1},{1,0},{2,3},{3,2},{4,5},{5,4},{6,7},{7,6},{8,9},{9,8},{10,11... | collective-permute-start | bytes 786440 | tf_op jit(solution)/shard_map/ppermute | solution.py:38
  61.1 17.3 %collective-permute-start.6 = (bf16[16,8192]{1,0:T(8,128)(2,1)S(1)}, bf16[16,8192]{1,0:T(8,128)(2,1)S(1)}, u32[]{:S(2)}, u32[]{:S(2)}) collective-permute-start(bf16[16,8192]{1,0:T(8,128)(2,1)S(1)} %pad_maximum_fusion.2.refs_0_), channel_id=1, source_target_pairs={{0,1},{1,0},{2,3},{3,2},{4,5},{5,4},{6,7},{7,6},{8,9},{9,8},{10,11... | collective-permute-start | bytes 786440 | tf_op jit(solution)/shard_map/ppermute | solution.py:38
  61.2 17.3 %collective-permute-start.7 = (bf16[16,8192]{1,0:T(8,128)(2,1)S(1)}, bf16[16,8192]{1,0:T(8,128)(2,1)S(1)}, u32[]{:S(2)}, u32[]{:S(2)}) collective-permute-start(bf16[16,8192]{1,0:T(8,128)(2,1)S(1)} %collective-permute-done.3.refs_1_), channel_id=1, source_target_pairs={{0,1},{1,0},{2,3},{3,2},{4,5},{5,4},{6,7},{7,6},{8,9},{9,8},{10,11... | collective-permute-start | bytes 786440 | tf_op jit(solution)/shard_map/ppermute | solution.py:38
  61.7 16.8 %collective-permute-start.8 = (bf16[16,8192]{1,0:T(8,128)(2,1)S(1)}, bf16[16,8192]{1,0:T(8,128)(2,1)S(1)}, u32[]{:S(2)}, u32[]{:S(2)}) collective-permute-start(bf16[16,8192]{1,0:T(8,128)(2,1)S(1)} %collective-permute-done.4.refs_2_), channel_id=1, source_target_pairs={{0,1},{1,0},{2,3},{3,2},{4,5},{5,4},{6,7},{7,6},{8,9},{9,8},{10,11... | collective-permute-start | bytes 786440 | tf_op jit(solution)/shard_map/ppermute | solution.py:38
  64.2 14.2 %collective-permute-start.9 = (bf16[16,8192]{1,0:T(8,128)(2,1)S(1)}, bf16[16,8192]{1,0:T(8,128)(2,1)S(1)}, u32[]{:S(2)}, u32[]{:S(2)}) collective-permute-start(bf16[16,8192]{1,0:T(8,128)(2,1)S(1)} %collective-permute-done.5.refs_3_), channel_id=1, source_target_pairs={{0,1},{1,0},{2,3},{3,2},{4,5},{5,4},{6,7},{7,6},{8,9},{9,8},{10,11... | collective-permute-start | bytes 786440 | tf_op jit(solution)/shard_map/ppermute | solution.py:38
  64.3 13.8 %collective-permute-start.24 = (bf16[2,4,96,128]{3,2,1,0:T(8,128)(2,1)S(1)}, bf16[2,4,96,128]{3,2,1,0:T(8,128)(2,1)S(1)}, u32[]{:S(2)}, u32[]{:S(2)}) collective-permute-start(bf16[2,4,96,128]{3,2,1,0:T(8,128)(2,1)S(1)} %get-tuple-element.11), channel_id=1, source_target_pairs={{0,4},{1,5},{2,6},{3,7},{4,0},{5,1},{6,2},{7,3},{8,12},{9,13},{10,... | collective-permute-start | bytes 589832 | tf_op jit(solution)/shard_map/ppermute | solution.py:38
  65.1 0.9 copy-start
  66.0 12.5 %copy-start.1 = (bf16[896,192]{0,1:T(8,128)(2,1)S(1)}, bf16[896,192]{0,1:T(8,128)(2,1)}, u32[]{:S(2)}) copy-start(bf16[896,192]{0,1:T(8,128)(2,1)} %param.16) | copy-start | bytes 1032196
  78.0 33.9 %copy-start.2 = (s32[128]{0:T(128)S(1)}, s32[128]{0:T(128)}, u32[]{:S(2)}) copy-start(s32[128]{0:T(128)} %param.17) | copy-start | bytes 1540
  78.1 34.1 %collective-permute-start.25 = (bf16[2,2,4,96,128]{4,3,2,1,0:T(8,128)(2,1)S(1)}, bf16[2,2,4,96,128]{4,3,2,1,0:T(8,128)(2,1)S(1)}, u32[]{:S(2)}, u32[]{:S(2)}) collective-permute-start(bf16[2,2,4,96,128]{4,3,2,1,0:T(8,128)(2,1)S(1)} %get-tuple-element.9), channel_id=1, source_target_pairs={{0,1},{1,0},{2,3},{3,2},{4,5},{5,4},{6,7},{7,6},{8,9},{9,8},{10,11... | collective-permute-start | bytes 1179656 | tf_op jit(solution)/shard_map/ppermute | solution.py:38
  108.6 9.6 %all-to-all-start.2 = ((f32[8,48,128]{2,1,0:T(8,128)}), f32[8,48,128]{2,1,0:T(8,128)S(1)}, u32[]{:S(2)}, u32[]{:S(2)}) async-start(f32[8,48,128]{2,1,0:T(8,128)} %sum_copies.3), calls=%async_computation.2 | async-start | bytes 393216 | tf_op jit(solution)/shard_map/all_to_all | solution.py:71

commit v4 on v3

v4 whole, which is shorter than its diff:
```python
import functools

import jax
import jax.numpy as jnp
import numpy as np
from jax import lax
from jax.experimental import pallas as pl
from jax.experimental.pallas import tpu as pltpu
from jax.sharding import PartitionSpec as P

DOMAINS = 32
SEQS = 16
HIGHEST = lax.Precision.HIGHEST
F32 = jnp.float32
BF16 = jnp.bfloat16
VMEM = pl.BlockSpec(memory_space=pltpu.VMEM)
ANY = pl.BlockSpec(memory_space=pl.ANY)


def axis_sizes(count):
    if count == 32:
        return (4, 2, 2, 2)
    if count == 128:
        return (8, 8, 2)
    return (count, 1)


def strides_of(sizes):
    return [int(np.prod(sizes[i + 1 :])) for i in range(len(sizes))]


def shift(value, sizes, axis, amount):
    size, stride = sizes[axis], strides_of(sizes)[axis]
    pairs = []
    for source in range(int(np.prod(sizes))):
        at = (source // stride) % size
        pairs.append((source, source + ((at + amount) % size - at) * stride))
    return lax.ppermute(value, "dp", pairs)


def coordinate(me, sizes, axis):
    return lax.rem(lax.div(me, strides_of(sizes)[axis]), sizes[axis])


def gather_pieces(rows, sizes, order):
    line = [rows] + [shift(rows, sizes, 0, k) for k in range(1, sizes[0])]
    pieces = [(jnp.concatenate(line, 0), tuple(0 for _ in sizes))]
    for axis in order:
        grown = list(pieces)
        for k in range(1, sizes[axis]):
            for piece, back in pieces:
                moved = tuple(k if i == axis else b for i, b in enumerate(back))
                grown.append((shift(piece, sizes, axis, k), moved))
        pieces = grown
    return [piece for piece, _ in pieces], [back for _, back in pieces]


def slot_order(per_token, sizes):
    rest = int(np.prod(sizes[1:]))
    return per_token.reshape(sizes[0], rest, -1).transpose(1, 0, 2).reshape(-1)


def exchange(blocks, groups=None):
    return lax.all_to_all(
        blocks, "dp", split_axis=0, concat_axis=0, axis_index_groups=groups, tiled=True
    )


def transposed_dot(left, right, precision=None):
    return lax.dot_general(
        left, right, (((1,), (1,)), ((), ())), precision=precision, preferred_element_type=F32
    )


def place_pieces(pieces, backs, sizes, into):
    me = lax.axis_index("dp")
    rows = pieces[0].shape[0]
    for piece, back in zip(pieces, backs):
        slot = 0
        for axis in range(1, len(sizes)):
            at = coordinate(me, sizes, axis) + sizes[axis] - back[axis]
            slot = slot * sizes[axis] + lax.rem(at, sizes[axis])
        into[pl.ds(pl.multiple_of(slot * rows, rows), rows), :] = piece[...]


def model_side(proj, tokens, model_cols):
    window = proj.shape[1]
    start = lax.div(lax.axis_index("dp") * model_cols, window) * window
    columns = pl.ds(pl.multiple_of(start, window), window)
    return transposed_dot(proj, tokens[:, columns])


def product_kernel(backs, sizes, model_cols, *refs):
    pieces, refs = refs[: len(backs[0])], refs[len(backs[0]) :]
    out_pieces, refs = refs[: len(backs[1])], refs[len(backs[1]) :]
    proj, proj_h, w_gate, w_up, w_down, out, sums, tokens, stacked, buffers, arrived = refs
    weights, sides = (w_gate, w_up, w_down), (0, 0, 1)
    depth, chunk = buffers.shape[0], buffers.shape[3]
    steps = tokens.shape[2] // chunk

    def copy(step, w):
        slot = lax.rem(step, depth)
        columns = pl.ds(pl.multiple_of(step * chunk, chunk), chunk)
        return pltpu.make_async_copy(
            weights[w].at[:, columns], buffers.at[slot, w], arrived.at[slot, w]
        )

    for step in range(min(depth, steps)):
        for w in range(3):
            copy(step, w).start()
    place_pieces(pieces, backs[0], sizes, tokens.at[0])
    place_pieces(out_pieces, backs[1], sizes, tokens.at[1])
    sums[...] = jnp.zeros_like(sums)
    rank = proj.shape[0] // 3
    right = [
        model_side(proj[: 2 * rank, :], tokens.at[0], model_cols),
        model_side(proj[2 * rank :, :], tokens.at[1], model_cols),
    ]

    @pl.loop(0, steps)
    def _(step):
        columns = pl.ds(pl.multiple_of(step * chunk, chunk), chunk)
        for w in range(3):
            copy(step, w).wait()
            sums[w] += transposed_dot(
                buffers[lax.rem(step, depth), w], tokens[sides[w], :, columns]
            )

            @pl.when(step + depth < steps)
            def _():
                copy(step + depth, w).start()

    hidden_units, count = sums.shape[1:]
    tile = 128 if hidden_units % 128 == 0 else 32

    @pl.loop(0, hidden_units // tile)
    def _(step):
        rows = pl.ds(pl.multiple_of(step * tile, tile), tile)
        gate_value, up_value, grad = sums[0, rows, :], sums[1, rows, :], sums[2, rows, :]
        s = 1.0 / (1.0 + jnp.exp(-gate_value))
        silu = gate_value * s
        stacked[0, rows, :] = (
            grad * up_value * s * (1.0 + gate_value * (1.0 - s))
        ).astype(BF16)
        stacked[1, rows, :] = (grad * silu).astype(BF16)
        stacked[2, rows, :] = (silu * up_value).astype(BF16)

    sides = [
        jnp.dot(proj_h[p * rank : (p + 1) * rank, :], stacked[k], preferred_element_type=F32)
        for k, p in enumerate((1, 2, 0))
    ]
    every = jnp.concatenate(sides + right, 0)
    size, each = sizes[0], count // int(np.prod(sizes))
    line = size * each
    source = lax.broadcasted_iota(jnp.int32, (count, count), 0)
    target = lax.broadcasted_iota(jnp.int32, (count, count), 1)
    back = lax.rem(lax.div(source, each), size)
    at = lax.rem(coordinate(lax.axis_index("dp"), sizes, 0) + size - back, size)
    place = lax.div(source, line) * line + at * each + lax.rem(source, each)
    order = (place == target).astype(F32)
    every = jnp.dot(every, order, precision=HIGHEST, preferred_element_type=F32)
    used = every.shape[0] // out.shape[1]
    out[:used] = every.reshape((used,) + out.shape[1:])
    if used < out.shape[0]:
        out[used:] = jnp.zeros_like(out[used:])


def products(in_pieces, out_pieces, backs, sizes, proj, proj_h, w_gate, w_up, w_down):
    hidden, width = w_gate.shape
    count = int(np.prod(sizes))
    tokens = in_pieces[0].shape[0] * len(in_pieces)
    model_cols = width // count
    chunk = min(width, 1024)
    height = 8 * -(-2 * proj.shape[0] // (8 * count))
    return pl.pallas_call(
        functools.partial(product_kernel, backs, sizes, model_cols),
        out_shape=jax.ShapeDtypeStruct((count, height, tokens), F32),
        in_specs=[VMEM] * (len(in_pieces) + len(out_pieces) + 2) + [ANY] * 3,
        out_specs=VMEM,
        scratch_shapes=[
            pltpu.VMEM((3, hidden, tokens), F32),
            pltpu.VMEM((2, tokens, width), BF16),
            pltpu.VMEM((3, hidden, tokens), BF16),
            pltpu.VMEM((2, 3, hidden, chunk), BF16),
            pltpu.SemaphoreType.DMA((2, 3)),
        ],
        compiler_params=pltpu.CompilerParams(vmem_limit_bytes=44 * 2**20),
        cost_estimate=pl.CostEstimate(
            flops=6 * hidden * width * tokens,
            bytes_accessed=6 * hidden * width,
            transcendentals=hidden * tokens,
        ),
        name="products",
    )(*in_pieces, *out_pieces, proj, proj_h, w_gate, w_up, w_down)


def sum_kernel(values, out):
    total = jnp.sum(values[...], 0)
    out[...] = jnp.broadcast_to(total[None], out.shape)


def sum_copies(values):
    return pl.pallas_call(
        sum_kernel,
        out_shape=jax.ShapeDtypeStruct(values.shape, F32),
        in_specs=[VMEM],
        out_specs=VMEM,
        name="sum_copies",
    )(values)


def halves(value):
    high = value.astype(BF16)
    return high, (value - high.astype(F32)).astype(BF16)


def rows_of(vectors, rank):
    height, tokens = vectors.shape[1:]
    return vectors[: 6 * rank // height].reshape(6 * rank, tokens)


def onehot_of(ids, tokens):
    return (ids == lax.broadcasted_iota(jnp.int32, (SEQS, tokens), 0)).astype(F32)


def target_kernel(rank, vectors, ids, targets, domains, out):
    tokens = ids.shape[1]
    examples = targets.shape[0]
    every = rows_of(vectors, rank)
    total = jnp.zeros((examples, tokens), F32)
    for k in range(3):
        left = every[k * rank : (k + 1) * rank]
        target = targets[:, k].reshape(examples * rank, rank)
        turned = sum(
            jnp.dot(target, part, preferred_element_type=F32)
            for part in halves(every[(3 + k) * rank : (4 + k) * rank])
        )
        total += jnp.sum(turned.reshape(examples, rank, tokens) * left[None], 1)
    scores = transposed_dot(total, onehot_of(ids[...], tokens), HIGHEST)
    parts = [scores, domains[...].astype(F32), jnp.ones((examples, 1), F32)]
    rest = out.shape[2] - SEQS - 2
    parts = jnp.concatenate(parts + [jnp.zeros((examples, rest), F32)], 1)
    out[...] = jnp.broadcast_to(parts[None], out.shape)


def sketch_kernel(rank, vectors, ids, sketches, norms):
    tokens = ids.shape[1]
    every = rows_of(vectors, rank)
    masks = jnp.concatenate([onehot_of(ids[...], tokens).astype(BF16)] * 3, 1)
    norm = jnp.zeros((SEQS, 1), F32)
    for k in range(3):
        left_high, left_low = halves(every[k * rank : (k + 1) * rank])
        right_high, right_low = halves(every[(3 + k) * rank : (4 + k) * rank])
        left = jnp.concatenate([left_high, left_high, left_low], 1)
        right = jnp.concatenate([right_high, right_low, right_high], 1)
        rows = jnp.concatenate([left * masks[s : s + 1, :] for s in range(SEQS)], 0)
        sketch = transposed_dot(rows, right).reshape(SEQS, rank, rank)
        sketches[:, k] = sketch
        norm += jnp.sum(jnp.sum(sketch * sketch, 1), 1, keepdims=True)
    norms[...] = jnp.broadcast_to(norm, norms.shape)


def score_kernel(parts, norms, scores):
    every = parts[...].reshape(-1, parts.shape[2])
    domain = lax.broadcasted_iota(jnp.int32, (every.shape[0], DOMAINS), 1).astype(F32)
    onehot = (every[:, SEQS : SEQS + 1] == domain).astype(F32)
    total = lax.dot_general(
        every, onehot, (((0,), (0,)), ((), ())), precision=HIGHEST, preferred_element_type=F32
    )
    mean = total[:SEQS] / total[SEQS + 1 : SEQS + 2]
    scores[...] = mean * lax.rsqrt(norms[:, :DOMAINS] + 1e-06)


def on_device(
    count,
    activations,
    cotangent,
    w_gate,
    w_up,
    w_down,
    proj_model,
    proj_hidden,
    seq_ids,
    targets,
    target_domain,
):
    sizes = axis_sizes(count)
    rank = proj_model.shape[1] // 3
    model_cols = proj_model.shape[0]
    tokens = count * activations.shape[0]
    examples = targets.shape[0]
    inner = list(range(1, len(sizes)))
    flipped = inner[:-1][::-1] + inner[-1:]

    in_pieces, in_backs = gather_pieces(activations, sizes, flipped)
    out_pieces, out_backs = gather_pieces(cotangent, sizes, inner)

    window = max(model_cols, 128)
    proj_m = proj_model.T
    if window > model_cols:
        at = lax.rem(lax.axis_index("dp"), window // model_cols)
        spots = [
            jnp.where(at == i, proj_m, jnp.zeros_like(proj_m)) for i in range(window // model_cols)
        ]
        proj_m = jnp.concatenate(spots, 1)

    vectors = products(
        in_pieces,
        out_pieces,
        (in_backs, out_backs),
        sizes,
        proj_m,
        proj_hidden.T,
        w_gate,
        w_up,
        w_down,
    )
    vectors = exchange(sum_copies(exchange(vectors)))

    ids = slot_order(seq_ids, sizes)[None, :]
    parts = pl.pallas_call(
        functools.partial(target_kernel, rank),
        out_shape=jax.ShapeDtypeStruct((count, examples, 128), F32),
        in_specs=[VMEM] * 4,
        out_specs=VMEM,
        compiler_params=pltpu.CompilerParams(vmem_limit_bytes=32 * 2**20),
        name="target_products",
    )(vectors, ids, targets, target_domain[:, None])
    parts, vectors = lax.optimization_barrier((parts, vectors))
    parts = exchange(parts)
    sketches, norms = pl.pallas_call(
        functools.partial(sketch_kernel, rank),
        out_shape=(
            jax.ShapeDtypeStruct((SEQS, 3, rank, rank), F32),
            jax.ShapeDtypeStruct((SEQS, 128), F32),
        ),
        in_specs=[VMEM] * 2,
        out_specs=(VMEM, VMEM),
        compiler_params=pltpu.CompilerParams(vmem_limit_bytes=40 * 2**20),
        name="sketches",
    )(vectors, ids)
    scores = pl.pallas_call(
        score_kernel,
        out_shape=jax.ShapeDtypeStruct((SEQS, DOMAINS), F32),
        in_specs=[VMEM] * 2,
        out_specs=VMEM,
        name="scores",
    )(parts, norms)
    return sketches, scores


def solution(mesh):
    in_specs = (
        P(("groups", "dp"), None),
        P(("groups", "dp"), None),
        P("dp", None),
        P("dp", None),
        P("dp", None),
        P("dp", None),
        P("dp", None),
        P("groups"),
        P(("groups", "dp"), None, None, None),
        P(("groups", "dp")),
    )
    out_specs = (P("groups", None, None, None), P("groups", None))
    return jax.shard_map(
        functools.partial(on_device, mesh.shape["dp"]),
        mesh=mesh,
        in_specs=in_specs,
        out_specs=out_specs,
        check_vma=False,
    )
```

time: 123 us -> 107 us (0.87)
  starting transfers between devices: 35.7 us -> 26.7 us
  blocking collectives: 19.2 us -> 16.1 us
  Pallas kernels: 26.9 us -> 24.9 us
  other arithmetic: 3.77 us -> 2 us
    ppermute x26 -> x20, starting transfers between devices: 28.3 us -> 21.6 us  [shift(): return lax.ppermute(value, 'dp', pairs)]
    ppermute x26 -> x20, waiting for transfers between devices: 20.8 us -> 16.6 us  [shift(): return lax.ppermute(value, 'dp', pairs)]
    all_to_all x2, waiting for transfers between devices: 11.9 us -> 16 us  [exchange(): lax.all_to_all(blocks, 'dp', split_axis=0, concat_axis=0, axis_index_grou...]
    all_to_all x2 -> x1, blocking collectives: 19.2 us -> 16.1 us  [exchange(): lax.all_to_all(blocks, 'dp', split_axis=0, concat_axis=0, axis_index_grou...]
    all_to_all x2, starting transfers between devices: 7.33 us -> 5.15 us  [exchange(): lax.all_to_all(blocks, 'dp', split_axis=0, concat_axis=0, axis_index_grou...]
    unnamed x7 -> x14, local copies, waits for them, and re-layouts: 0.98 us -> 3.11 us
    pallas_call x5, Pallas kernels: 26.9 us -> 24.9 us  [the longest x1 18.3 us: products(): pl.pallas_call(functools.partial(product_kernel, backs, sizes, model_cols...]
    reshape x3 -> x0, local copies, waits for them, and re-layouts: 1.58 us -> none  [the longest x1 1.3 us: on_device(): cut.reshape(examples, 3, own_rank, count, rank).transpose(3, 0, 1, 2, 4)]
  transfers between devices with their start and end apart: 28 -> 22, of which waited for: 11 -> 10; matrix products, arithmetic and copies ran while one was open for 4% -> 2% of each run, Pallas kernels for 19% -> 2%
where the time goes in v4:
time: 107 us; the launch traced here: 106 us
  waiting for transfers between devices  32.6 us (30%)
  starting transfers between devices  26.7 us (25%)
  Pallas kernels  24.9 us (23%)
  blocking collectives  16.1 us (15%)
  local copies, waits for them, and re-layouts  3.4 us (3%)
  other arithmetic  2 us (2%)
    ppermute x20, starting transfers between devices, shift(): return lax.ppermute(value, 'dp', pairs)  21.6 us
    pallas_call x1, Pallas kernels, products(): pl.pallas_call(functools.partial(product_kernel, backs, sizes, model_cols...  18.3 us
    ppermute x20, waiting for transfers between devices, shift(): return lax.ppermute(value, 'dp', pairs)  16.6 us
    all_to_all x1, blocking collectives, exchange(): lax.all_to_all(blocks, 'dp', split_axis=0, concat_axis=0, axis_index_grou...  16.1 us
    all_to_all x2, waiting for transfers between devices, exchange(): lax.all_to_all(blocks, 'dp', split_axis=0, concat_axis=0, axis_index_grou...  16 us
    all_to_all x2, starting transfers between devices, exchange(): lax.all_to_all(blocks, 'dp', split_axis=0, concat_axis=0, axis_index_grou...  5.15 us
    unnamed x14, local copies, waits for them, and re-layouts  3.11 us
  transfers between devices with their start and end apart: 22, of which 10 were waited for; matrix products, arithmetic and copies ran while one was open for 2% of the time, Pallas kernels for 2%

profile of v4, /device:TPU:0, one launch (start us, length us, event | category | flops | bytes accessed | tf_op | source)
XLA Modules:
  0.0 106.4 jit_solution(14334642587380703075)
XLA Ops:
  0.6 3.1 %collective-permute-start.10 = (bf16[4,8192]{1,0:T(4,128)(2,1)}, bf16[4,8192]{1,0:T(4,128)(2,1)S(1)}, u32[]{:S(2)}, u32[]{:S(2)}) collective-permute-start(bf16[4,8192]{1,0:T(4,128)(2,1)} %param.11), channel_id=1, source_target_pairs={{0,8},{1,9},{2,10},{3,11},{4,12},{5,13},{6,14},{7,15},{8,16},{9,17... | collective-permute-start | bytes 196616 | tf_op jit(solution)/shard_map/ppermute | solution.py:38
  3.7 2.6 %collective-permute-start.11 = (bf16[4,8192]{1,0:T(4,128)(2,1)}, bf16[4,8192]{1,0:T(4,128)(2,1)S(1)}, u32[]{:S(2)}, u32[]{:S(2)}) collective-permute-start(bf16[4,8192]{1,0:T(4,128)(2,1)} %param.11), channel_id=1, source_target_pairs={{0,16},{1,17},{2,18},{3,19},{4,20},{5,21},{6,22},{7,23},{8,24},{9,... | collective-permute-start | bytes 196616 | tf_op jit(solution)/shard_map/ppermute | solution.py:38
  6.3 1.3 %collective-permute-start.12 = (bf16[4,8192]{1,0:T(4,128)(2,1)}, bf16[4,8192]{1,0:T(4,128)(2,1)S(1)}, u32[]{:S(2)}, u32[]{:S(2)}) collective-permute-start(bf16[4,8192]{1,0:T(4,128)(2,1)} %param.11), channel_id=1, source_target_pairs={{0,24},{1,25},{2,26},{3,27},{4,28},{5,29},{6,30},{7,31},{8,0},{9,1... | collective-permute-start | bytes 196616 | tf_op jit(solution)/shard_map/ppermute | solution.py:38
  7.6 0.7 collective-permute-start
  8.3 0.3 collective-permute-start.1
  8.7 0.0 collective-permute-done.10
  8.7 2.8 %collective-permute-start.2 = (bf16[4,8192]{1,0:T(4,128)(2,1)}, bf16[4,8192]{1,0:T(4,128)(2,1)S(1)}, u32[]{:S(2)}, u32[]{:S(2)}) collective-permute-start(bf16[4,8192]{1,0:T(4,128)(2,1)} %param.10), channel_id=1, source_target_pairs={{0,24},{1,25},{2,26},{3,27},{4,28},{5,29},{6,30},{7,31},{8,0},{9,1... | collective-permute-start | bytes 196616 | tf_op jit(solution)/shard_map/ppermute | solution.py:38
  11.5 0.0 collective-permute-done.11
  11.5 1.0 pad_maximum_fusion.1.refs_8_
  12.5 1.6 %collective-permute-start.13 = (bf16[16,8192]{1,0:T(8,128)(2,1)S(1)}, bf16[16,8192]{1,0:T(8,128)(2,1)S(1)}, u32[]{:S(2)}, u32[]{:S(2)}) collective-permute-start(bf16[16,8192]{1,0:T(8,128)(2,1)S(1)} %pad_maximum_fusion.1.refs_8_), channel_id=1, source_target_pairs={{0,4},{1,5},{2,6},{3,7},{4,0},{5,1},{6,2},{7,3},{8,12},{9,13},{10,... | collective-permute-start | bytes 786440 | tf_op jit(solution)/shard_map/ppermute | solution.py:38
  14.1 0.2 collective-permute-done
  14.2 2.4 %collective-permute-done.1 = bf16[4,8192]{1,0:T(4,128)(2,1)S(1)} collective-permute-done((bf16[4,8192]{1,0:T(4,128)(2,1)}, bf16[4,8192]{1,0:T(4,128)(2,1)S(1)}, u32[]{:S(2)}, u32[]{:S(2)}) %collective-permute-start.1) | collective-permute-done | bytes 65568 | tf_op jit(solution)/shard_map/ppermute | solution.py:38
  16.6 0.0 collective-permute-done.2
  16.6 1.0 pad_maximum_fusion.refs_0_
  17.6 1.8 %collective-permute-start.3 = (bf16[16,8192]{1,0:T(8,128)(2,1)S(1)}, bf16[16,8192]{1,0:T(8,128)(2,1)S(1)}, u32[]{:S(2)}, u32[]{:S(2)}) collective-permute-start(bf16[16,8192]{1,0:T(8,128)(2,1)S(1)} %pad_maximum_fusion.refs_0_), channel_id=1, source_target_pairs={{0,2},{1,3},{2,0},{3,1},{4,6},{5,7},{6,4},{7,5},{8,10},{9,11},{10,... | collective-permute-start | bytes 786440 | tf_op jit(solution)/shard_map/ppermute | solution.py:38
  19.4 0.3 collective-permute-start.14
  19.7 1.8 %collective-permute-start.4 = (bf16[16,8192]{1,0:T(8,128)(2,1)S(1)}, bf16[16,8192]{1,0:T(8,128)(2,1)S(1)}, u32[]{:S(2)}, u32[]{:S(2)}) collective-permute-start(bf16[16,8192]{1,0:T(8,128)(2,1)S(1)} %pad_maximum_fusion.refs_0_), channel_id=1, source_target_pairs={{0,4},{1,5},{2,6},{3,7},{4,0},{5,1},{6,2},{7,3},{8,12},{9,13},{10,... | collective-permute-start | bytes 786440 | tf_op jit(solution)/shard_map/ppermute | solution.py:38
  21.5 0.0 collective-permute-start.16
  21.5 0.0 collective-permute-done.13.refs_9_
  21.5 0.5 collective-permute-start.6
  22.0 4.9 %collective-permute-done.3.refs_1_ = bf16[16,8192]{1,0:T(8,128)(2,1)S(1)} collective-permute-done((bf16[16,8192]{1,0:T(8,128)(2,1)S(1)}, bf16[16,8192]{1,0:T(8,128)(2,1)S(1)}, u32[]{:S(2)}, u32[]{:S(2)}) %collective-permute-start.3) | collective-permute-done | bytes 262176 | tf_op jit(solution)/shard_map/ppermute | solution.py:38
  26.9 1.8 %collective-permute-start.15 = (bf16[16,8192]{1,0:T(8,128)(2,1)S(1)}, bf16[16,8192]{1,0:T(8,128)(2,1)S(1)}, u32[]{:S(2)}, u32[]{:S(2)}) collective-permute-start(bf16[16,8192]{1,0:T(8,128)(2,1)S(1)} %collective-permute-done.13.refs_9_), channel_id=1, source_target_pairs={{0,2},{1,3},{2,0},{3,1},{4,6},{5,7},{6,4},{7,5},{8,10},{9,11},{10,... | collective-permute-start | bytes 786440 | tf_op jit(solution)/shard_map/ppermute | solution.py:38
  28.7 3.8 %collective-permute-done.14.refs_10_ = bf16[16,8192]{1,0:T(8,128)(2,1)S(1)} collective-permute-done((bf16[16,8192]{1,0:T(8,128)(2,1)S(1)}, bf16[16,8192]{1,0:T(8,128)(2,1)S(1)}, u32[]{:S(2)}, u32[]{:S(2)}) %collective-permute-start.14) | collective-permute-done | bytes 262176 | tf_op jit(solution)/shard_map/ppermute | solution.py:38
  32.5 1.8 %collective-permute-start.5 = (bf16[16,8192]{1,0:T(8,128)(2,1)S(1)}, bf16[16,8192]{1,0:T(8,128)(2,1)S(1)}, u32[]{:S(2)}, u32[]{:S(2)}) collective-permute-start(bf16[16,8192]{1,0:T(8,128)(2,1)S(1)} %collective-permute-done.3.refs_1_), channel_id=1, source_target_pairs={{0,4},{1,5},{2,6},{3,7},{4,0},{5,1},{6,2},{7,3},{8,12},{9,13},{10,... | collective-permute-start | bytes 786440 | tf_op jit(solution)/shard_map/ppermute | solution.py:38
  34.3 0.5 collective-permute-start.7
  34.9 0.1 collective-permute-start.18
  34.9 2.0 %collective-permute-done.15.refs_11_ = bf16[16,8192]{1,0:T(8,128)(2,1)S(1)} collective-permute-done((bf16[16,8192]{1,0:T(8,128)(2,1)S(1)}, bf16[16,8192]{1,0:T(8,128)(2,1)S(1)}, u32[]{:S(2)}, u32[]{:S(2)}) %collective-permute-start.15) | collective-permute-done | bytes 262176 | tf_op jit(solution)/shard_map/ppermute | solution.py:38
  36.9 1.9 %collective-permute-done.5.refs_3_ = bf16[16,8192]{1,0:T(8,128)(2,1)S(1)} collective-permute-done((bf16[16,8192]{1,0:T(8,128)(2,1)S(1)}, bf16[16,8192]{1,0:T(8,128)(2,1)S(1)}, u32[]{:S(2)}, u32[]{:S(2)}) %collective-permute-start.5) | collective-permute-done | bytes 262176 | tf_op jit(solution)/shard_map/ppermute | solution.py:38
  38.9 0.5 collective-permute-start.9
  39.4 1.0 collective-permute-done.19.refs_15_
  40.4 0.4 collective-permute-done.9.refs_7_
  40.8 1.0 copy-done.1
  41.8 0.9 copy-done.2
  42.7 18.3 %products.1 = f32[32,16,128]{2,1,0:T(8,128)S(1)} custom-call(bf16[16,8192]{1,0:T(8,128)(2,1)S(1)} %pad_maximum_fusion.refs_0_, bf16[16,8192]{1,0:T(8,128)(2,1)S(1)} %collective-permute-done.3.refs_1_, bf16[16,8192]{1,0:T(8,128)(2,1)S(1)} %collective-permute-done.4.refs_2_, bf16[16,8192]{1,0:T(8,128)(2,1)S(1)} %collective-permute-done.5.refs_3_, ...), custom_call_target="tpu_custom_call" | custom-call | flops 5637144576 | bytes 44040192 | tf_op jit(solution)/shard_map/products/pallas_call | solution.py:175
  60.9 16.1 %all_to_all.15.values = f32[32,16,128]{2,1,0:T(8,128)} all-to-all(f32[32,16,128]{2,1,0:T(8,128)S(1)} %products.1), channel_id=1, replica_groups=mesh['groups'=1,'dp'=32] {'dp'}, dimensions={0} | all-to-all | bytes 524288 | tf_op jit(solution)/shard_map/all_to_all | solution.py:64
  77.0 1.7 %sum_copies.1 = f32[32,16,128]{2,1,0:T(8,128)} custom-call(f32[32,16,128]{2,1,0:T(8,128)} %all_to_all.15.values), custom_call_target="tpu_custom_call" | custom-call | tf_op jit(solution)/shard_map/sum_copies/pallas_call | solution.py:203
  78.7 2.6 %all-to-all-start.1 = ((f32[32,16,128]{2,1,0:T(8,128)}), f32[32,16,128]{2,1,0:T(8,128)S(1)}, u32[]{:S(2)}, u32[]{:S(2)}) async-start(f32[32,16,128]{2,1,0:T(8,128)} %sum_copies.1), calls=%async_computation.1 | async-start | bytes 524288 | tf_op jit(solution)/shard_map/all_to_all | solution.py:64
  81.3 0.1 reshape.7
  81.4 0.1 broadcast_in_dim_reshape.3.ids
  81.5 0.1 copy.15.domains
  81.6 10.3 %all-to-all-done.1.vectors = f32[32,16,128]{2,1,0:T(8,128)S(1)} async-done(((f32[32,16,128]{2,1,0:T(8,128)}), f32[32,16,128]{2,1,0:T(8,128)S(1)}, u32[]{:S(2)}, u32[]{:S(2)}) %all-to-all-start.1) | async-done | bytes 262176 | tf_op jit(solution)/shard_map/all_to_all | solution.py:64
  91.9 1.2 %target_products.1 = f32[32,8,128]{2,1,0:T(8,128)} custom-call(f32[32,16,128]{2,1,0:T(8,128)S(1)} %all-to-all-done.1.vectors, s32[1,128]{1,0:T(1,128)S(1)} %broadcast_in_dim_reshape.3.ids, bf16[8,3,64,64]{3,2,1,0:T(8,128)(2,1)S(1)} %copy-done, s32[8,1]{1,0:T(8,128)S(1)} %copy.15.domains), custom_call_target="tpu_custom_call" | custom-call | tf_op jit(solution)/shard_map/target_products/pallas_call | solution.py:321
  93.1 2.6 %all-to-all-start.2 = ((f32[32,8,128]{2,1,0:T(8,128)}), f32[32,8,128]{2,1,0:T(8,128)S(1)}, u32[]{:S(2)}, u32[]{:S(2)}) async-start(f32[32,8,128]{2,1,0:T(8,128)} %target_products.1), calls=%async_computation.2 | async-start | bytes 262144 | tf_op jit(solution)/shard_map/all_to_all | solution.py:64
  95.7 1.9 %sketches.1 = (f32[16,3,64,64]{3,2,1,0:T(8,128)}, f32[16,128]{1,0:T(8,128)S(1)}) custom-call(f32[32,16,128]{2,1,0:T(8,128)S(1)} %all-to-all-done.1.vectors, s32[1,128]{1,0:T(1,128)S(1)} %broadcast_in_dim_reshape.3.ids), custom_call_target="tpu_custom_call" | custom-call | tf_op jit(solution)/shard_map/sketches/pallas_call | solution.py:331
  97.6 0.6 copy-done.3
  98.1 5.8 %all-to-all-done.2.parts = f32[32,8,128]{2,1,0:T(8,128)S(1)} async-done(((f32[32,8,128]{2,1,0:T(8,128)}), f32[32,8,128]{2,1,0:T(8,128)S(1)}, u32[]{:S(2)}, u32[]{:S(2)}) %all-to-all-start.2) | async-done | bytes 131104 | tf_op jit(solution)/shard_map/all_to_all | solution.py:64
  103.9 0.6 copy-done.4
  104.5 1.9 %scores.1 = f32[16,32]{1,0:T(8,128)} custom-call(f32[32,8,128]{2,1,0:T(8,128)} %copy-done.4, f32[16,128]{1,0:T(8,128)} %copy-done.3), custom_call_target="tpu_custom_call" | custom-call | tf_op jit(solution)/shard_map/scores/pallas_call | solution.py:342
  (22 shorter events, 0.1 us)
Async XLA Ops:
  0.6 8.0 %collective-permute-start.10 = (bf16[4,8192]{1,0:T(4,128)(2,1)}, bf16[4,8192]{1,0:T(4,128)(2,1)S(1)}, u32[]{:S(2)}, u32[]{:S(2)}) collective-permute-start(bf16[4,8192]{1,0:T(4,128)(2,1)} %param.11), channel_id=1, source_target_pairs={{0,8},{1,9},{2,10},{3,11},{4,12},{5,13},{6,14},{7,15},{8,16},{9,17... | collective-permute-start | bytes 196616 | tf_op jit(solution)/shard_map/ppermute | solution.py:38
  3.7 7.8 %collective-permute-start.11 = (bf16[4,8192]{1,0:T(4,128)(2,1)}, bf16[4,8192]{1,0:T(4,128)(2,1)S(1)}, u32[]{:S(2)}, u32[]{:S(2)}) collective-permute-start(bf16[4,8192]{1,0:T(4,128)(2,1)} %param.11), channel_id=1, source_target_pairs={{0,16},{1,17},{2,18},{3,19},{4,20},{5,21},{6,22},{7,23},{8,24},{9,... | collective-permute-start | bytes 196616 | tf_op jit(solution)/shard_map/ppermute | solution.py:38
  6.3 5.2 %collective-permute-start.12 = (bf16[4,8192]{1,0:T(4,128)(2,1)}, bf16[4,8192]{1,0:T(4,128)(2,1)S(1)}, u32[]{:S(2)}, u32[]{:S(2)}) collective-permute-start(bf16[4,8192]{1,0:T(4,128)(2,1)} %param.11), channel_id=1, source_target_pairs={{0,24},{1,25},{2,26},{3,27},{4,28},{5,29},{6,30},{7,31},{8,0},{9,1... | collective-permute-start | bytes 196616 | tf_op jit(solution)/shard_map/ppermute | solution.py:38
  7.6 6.6 %collective-permute-start = (bf16[4,8192]{1,0:T(4,128)(2,1)}, bf16[4,8192]{1,0:T(4,128)(2,1)S(1)}, u32[]{:S(2)}, u32[]{:S(2)}) collective-permute-start(bf16[4,8192]{1,0:T(4,128)(2,1)} %param.10), channel_id=1, source_target_pairs={{0,8},{1,9},{2,10},{3,11},{4,12},{5,13},{6,14},{7,15},{8,16},{9,17... | collective-permute-start | bytes 196616 | tf_op jit(solution)/shard_map/ppermute | solution.py:38
  8.3 8.3 %collective-permute-start.1 = (bf16[4,8192]{1,0:T(4,128)(2,1)}, bf16[4,8192]{1,0:T(4,128)(2,1)S(1)}, u32[]{:S(2)}, u32[]{:S(2)}) collective-permute-start(bf16[4,8192]{1,0:T(4,128)(2,1)} %param.10), channel_id=1, source_target_pairs={{0,16},{1,17},{2,18},{3,19},{4,20},{5,21},{6,22},{7,23},{8,24},{9,... | collective-permute-start | bytes 196616 | tf_op jit(solution)/shard_map/ppermute | solution.py:38
  8.7 7.9 %collective-permute-start.2 = (bf16[4,8192]{1,0:T(4,128)(2,1)}, bf16[4,8192]{1,0:T(4,128)(2,1)S(1)}, u32[]{:S(2)}, u32[]{:S(2)}) collective-permute-start(bf16[4,8192]{1,0:T(4,128)(2,1)} %param.10), channel_id=1, source_target_pairs={{0,24},{1,25},{2,26},{3,27},{4,28},{5,29},{6,30},{7,31},{8,0},{9,1... | collective-permute-start | bytes 196616 | tf_op jit(solution)/shard_map/ppermute | solution.py:38
  12.5 9.0 %collective-permute-start.13 = (bf16[16,8192]{1,0:T(8,128)(2,1)S(1)}, bf16[16,8192]{1,0:T(8,128)(2,1)S(1)}, u32[]{:S(2)}, u32[]{:S(2)}) collective-permute-start(bf16[16,8192]{1,0:T(8,128)(2,1)S(1)} %pad_maximum_fusion.1.refs_8_), channel_id=1, source_target_pairs={{0,4},{1,5},{2,6},{3,7},{4,0},{5,1},{6,2},{7,3},{8,12},{9,13},{10,... | collective-permute-start | bytes 786440 | tf_op jit(solution)/shard_map/ppermute | solution.py:38
  17.6 9.3 %collective-permute-start.3 = (bf16[16,8192]{1,0:T(8,128)(2,1)S(1)}, bf16[16,8192]{1,0:T(8,128)(2,1)S(1)}, u32[]{:S(2)}, u32[]{:S(2)}) collective-permute-start(bf16[16,8192]{1,0:T(8,128)(2,1)S(1)} %pad_maximum_fusion.refs_0_), channel_id=1, source_target_pairs={{0,2},{1,3},{2,0},{3,1},{4,6},{5,7},{6,4},{7,5},{8,10},{9,11},{10,... | collective-permute-start | bytes 786440 | tf_op jit(solution)/shard_map/ppermute | solution.py:38
  19.4 13.1 %collective-permute-start.14 = (bf16[16,8192]{1,0:T(8,128)(2,1)S(1)}, bf16[16,8192]{1,0:T(8,128)(2,1)S(1)}, u32[]{:S(2)}, u32[]{:S(2)}) collective-permute-start(bf16[16,8192]{1,0:T(8,128)(2,1)S(1)} %pad_maximum_fusion.1.refs_8_), channel_id=1, source_target_pairs={{0,2},{1,3},{2,0},{3,1},{4,6},{5,7},{6,4},{7,5},{8,10},{9,11},{10,... | collective-permute-start | bytes 786440 | tf_op jit(solution)/shard_map/ppermute | solution.py:38
  19.7 14.6 %collective-permute-start.4 = (bf16[16,8192]{1,0:T(8,128)(2,1)S(1)}, bf16[16,8192]{1,0:T(8,128)(2,1)S(1)}, u32[]{:S(2)}, u32[]{:S(2)}) collective-permute-start(bf16[16,8192]{1,0:T(8,128)(2,1)S(1)} %pad_maximum_fusion.refs_0_), channel_id=1, source_target_pairs={{0,4},{1,5},{2,6},{3,7},{4,0},{5,1},{6,2},{7,3},{8,12},{9,13},{10,... | collective-permute-start | bytes 786440 | tf_op jit(solution)/shard_map/ppermute | solution.py:38
  21.5 12.8 %collective-permute-start.16 = (bf16[16,8192]{1,0:T(8,128)(2,1)S(1)}, bf16[16,8192]{1,0:T(8,128)(2,1)S(1)}, u32[]{:S(2)}, u32[]{:S(2)}) collective-permute-start(bf16[16,8192]{1,0:T(8,128)(2,1)S(1)} %pad_maximum_fusion.1.refs_8_), channel_id=1, source_target_pairs={{0,1},{1,0},{2,3},{3,2},{4,5},{5,4},{6,7},{7,6},{8,9},{9,8},{10,11... | collective-permute-start | bytes 786440 | tf_op jit(solution)/shard_map/ppermute | solution.py:38
  21.5 13.3 %collective-permute-start.6 = (bf16[16,8192]{1,0:T(8,128)(2,1)S(1)}, bf16[16,8192]{1,0:T(8,128)(2,1)S(1)}, u32[]{:S(2)}, u32[]{:S(2)}) collective-permute-start(bf16[16,8192]{1,0:T(8,128)(2,1)S(1)} %pad_maximum_fusion.refs_0_), channel_id=1, source_target_pairs={{0,1},{1,0},{2,3},{3,2},{4,5},{5,4},{6,7},{7,6},{8,9},{9,8},{10,11... | collective-permute-start | bytes 786440 | tf_op jit(solution)/shard_map/ppermute | solution.py:38
  26.9 10.1 %collective-permute-start.15 = (bf16[16,8192]{1,0:T(8,128)(2,1)S(1)}, bf16[16,8192]{1,0:T(8,128)(2,1)S(1)}, u32[]{:S(2)}, u32[]{:S(2)}) collective-permute-start(bf16[16,8192]{1,0:T(8,128)(2,1)S(1)} %collective-permute-done.13.refs_9_), channel_id=1, source_target_pairs={{0,2},{1,3},{2,0},{3,1},{4,6},{5,7},{6,4},{7,5},{8,10},{9,11},{10,... | collective-permute-start | bytes 786440 | tf_op jit(solution)/shard_map/ppermute | solution.py:38
  32.5 6.4 %collective-permute-start.5 = (bf16[16,8192]{1,0:T(8,128)(2,1)S(1)}, bf16[16,8192]{1,0:T(8,128)(2,1)S(1)}, u32[]{:S(2)}, u32[]{:S(2)}) collective-permute-start(bf16[16,8192]{1,0:T(8,128)(2,1)S(1)} %collective-permute-done.3.refs_1_), channel_id=1, source_target_pairs={{0,4},{1,5},{2,6},{3,7},{4,0},{5,1},{6,2},{7,3},{8,12},{9,13},{10,... | collective-permute-start | bytes 786440 | tf_op jit(solution)/shard_map/ppermute | solution.py:38
  34.3 4.5 %collective-permute-start.17 = (bf16[16,8192]{1,0:T(8,128)(2,1)S(1)}, bf16[16,8192]{1,0:T(8,128)(2,1)S(1)}, u32[]{:S(2)}, u32[]{:S(2)}) collective-permute-start(bf16[16,8192]{1,0:T(8,128)(2,1)S(1)} %collective-permute-done.13.refs_9_), channel_id=1, source_target_pairs={{0,1},{1,0},{2,3},{3,2},{4,5},{5,4},{6,7},{7,6},{8,9},{9,8},{10,11... | collective-permute-start | bytes 786440 | tf_op jit(solution)/shard_map/ppermute | solution.py:38
  34.3 5.0 %collective-permute-start.7 = (bf16[16,8192]{1,0:T(8,128)(2,1)S(1)}, bf16[16,8192]{1,0:T(8,128)(2,1)S(1)}, u32[]{:S(2)}, u32[]{:S(2)}) collective-permute-start(bf16[16,8192]{1,0:T(8,128)(2,1)S(1)} %collective-permute-done.3.refs_1_), channel_id=1, source_target_pairs={{0,1},{1,0},{2,3},{3,2},{4,5},{5,4},{6,7},{7,6},{8,9},{9,8},{10,11... | collective-permute-start | bytes 786440 | tf_op jit(solution)/shard_map/ppermute | solution.py:38
  34.9 4.5 %collective-permute-start.18 = (bf16[16,8192]{1,0:T(8,128)(2,1)S(1)}, bf16[16,8192]{1,0:T(8,128)(2,1)S(1)}, u32[]{:S(2)}, u32[]{:S(2)}) collective-permute-start(bf16[16,8192]{1,0:T(8,128)(2,1)S(1)} %collective-permute-done.14.refs_10_), channel_id=1, source_target_pairs={{0,1},{1,0},{2,3},{3,2},{4,5},{5,4},{6,7},{7,6},{8,9},{9,8},{10,11... | collective-permute-start | bytes 786440 | tf_op jit(solution)/shard_map/ppermute | solution.py:38
  36.9 2.5 %collective-permute-start.8 = (bf16[16,8192]{1,0:T(8,128)(2,1)S(1)}, bf16[16,8192]{1,0:T(8,128)(2,1)S(1)}, u32[]{:S(2)}, u32[]{:S(2)}) collective-permute-start(bf16[16,8192]{1,0:T(8,128)(2,1)S(1)} %collective-permute-done.4.refs_2_), channel_id=1, source_target_pairs={{0,1},{1,0},{2,3},{3,2},{4,5},{5,4},{6,7},{7,6},{8,9},{9,8},{10,11... | collective-permute-start | bytes 786440 | tf_op jit(solution)/shard_map/ppermute | solution.py:38
  38.9 1.5 %collective-permute-start.19 = (bf16[16,8192]{1,0:T(8,128)(2,1)S(1)}, bf16[16,8192]{1,0:T(8,128)(2,1)S(1)}, u32[]{:S(2)}, u32[]{:S(2)}) collective-permute-start(bf16[16,8192]{1,0:T(8,128)(2,1)S(1)} %collective-permute-done.15.refs_11_), channel_id=1, source_target_pairs={{0,1},{1,0},{2,3},{3,2},{4,5},{5,4},{6,7},{7,6},{8,9},{9,8},{10,11... | collective-permute-start | bytes 786440 | tf_op jit(solution)/shard_map/ppermute | solution.py:38
  38.9 1.9 %collective-permute-start.9 = (bf16[16,8192]{1,0:T(8,128)(2,1)S(1)}, bf16[16,8192]{1,0:T(8,128)(2,1)S(1)}, u32[]{:S(2)}, u32[]{:S(2)}) collective-permute-start(bf16[16,8192]{1,0:T(8,128)(2,1)S(1)} %collective-permute-done.5.refs_3_), channel_id=1, source_target_pairs={{0,1},{1,0},{2,3},{3,2},{4,5},{5,4},{6,7},{7,6},{8,9},{9,8},{10,11... | collective-permute-start | bytes 786440 | tf_op jit(solution)/shard_map/ppermute | solution.py:38
  40.8 1.0 copy-start.1
  41.8 0.9 copy-start.2
  42.6 38.7 %copy-start.5 = (s32[128]{0:T(128)S(1)}, s32[128]{0:T(128)}, u32[]{:S(2)}) copy-start(s32[128]{0:T(128)} %param.17) | copy-start | bytes 1540
  42.7 38.9 %copy-start.6 = (s32[8]{0:T(128)S(1)}, s32[8]{0:T(128)}, u32[]{:S(2)}) copy-start(s32[8]{0:T(128)} %param.19) | copy-start | bytes 100
  42.7 49.2 %copy-start = (bf16[8,3,64,64]{3,2,1,0:T(8,128)(2,1)S(1)}, bf16[8,3,64,64]{3,2,1,0:T(8,128)(2,1)}, u32[]{:S(2)}) copy-start(bf16[8,3,64,64]{3,2,1,0:T(8,128)(2,1)} %targets.1) | copy-start | bytes 589828
  78.7 13.2 %all-to-all-start.1 = ((f32[32,16,128]{2,1,0:T(8,128)}), f32[32,16,128]{2,1,0:T(8,128)S(1)}, u32[]{:S(2)}, u32[]{:S(2)}) async-start(f32[32,16,128]{2,1,0:T(8,128)} %sum_copies.1), calls=%async_computation.1 | async-start | bytes 524288 | tf_op jit(solution)/shard_map/all_to_all | solution.py:64
  93.1 10.8 %all-to-all-start.2 = ((f32[32,8,128]{2,1,0:T(8,128)}), f32[32,8,128]{2,1,0:T(8,128)S(1)}, u32[]{:S(2)}, u32[]{:S(2)}) async-start(f32[32,8,128]{2,1,0:T(8,128)} %target_products.1), calls=%async_computation.2 | async-start | bytes 262144 | tf_op jit(solution)/shard_map/all_to_all | solution.py:64
  97.6 0.6 copy-start.3
  103.9 0.7 copy-start.4

commit v5 on v4

--- a/solution.py
+++ b/solution.py
@@ -14,7 +14,7 @@
 F32 = jnp.float32
 BF16 = jnp.bfloat16
 VMEM = pl.BlockSpec(memory_space=pltpu.VMEM)
-ANY = pl.BlockSpec(memory_space=pl.ANY)
+HBM = pl.BlockSpec(memory_space=pltpu.HBM)
 
 
 def axis_sizes(count):
@@ -42,17 +42,28 @@
     return lax.rem(lax.div(me, strides_of(sizes)[axis]), sizes[axis])
 
 
-def gather_pieces(rows, sizes, order):
-    line = [rows] + [shift(rows, sizes, 0, k) for k in range(1, sizes[0])]
-    pieces = [(jnp.concatenate(line, 0), tuple(0 for _ in sizes))]
-    for axis in order:
-        grown = list(pieces)
-        for k in range(1, sizes[axis]):
-            for piece, back in pieces:
-                moved = tuple(k if i == axis else b for i, b in enumerate(back))
-                grown.append((shift(piece, sizes, axis, k), moved))
-        pieces = grown
-    return [piece for piece, _ in pieces], [back for _, back in pieces]
+def gather_rows(rows, sizes, order):
+    backs = [tuple(0 for _ in sizes)]
+
+    def moved(axis, amount):
+        return [tuple(amount if i == axis else b for i, b in enumerate(back)) for back in backs]
+
+    def received(piece, axis):
+        return [shift(piece, sizes, axis, k) for k in range(1, sizes[axis])]
+
+    piece = lax.optimization_barrier(jnp.concatenate([rows] + received(rows, 0), 0))
+    for axis in order[:-1]:
+        piece = jnp.concatenate([piece] + received(piece, axis), 0)
+        backs = sum([moved(axis, k) for k in range(1, sizes[axis])], backs)
+    pieces = [(piece, backs)]
+    for axis in order[-1:]:
+        others = zip(received(piece, axis), range(1, sizes[axis]))
+        pieces += [(other, moved(axis, k)) for other, k in others]
+    core = len(sizes) - 1
+    for piece, backs in list(pieces):
+        others = zip(received(piece, core), range(1, sizes[core]))
+        pieces += [(other, moved(core, k)) for other, k in others]
+    return [piece for piece, _ in pieces], [backs for _, backs in pieces]
 
 
 def slot_order(per_token, sizes):
@@ -74,13 +85,15 @@
 
 def place_pieces(pieces, backs, sizes, into):
     me = lax.axis_index("dp")
-    rows = pieces[0].shape[0]
-    for piece, back in zip(pieces, backs):
-        slot = 0
-        for axis in range(1, len(sizes)):
-            at = coordinate(me, sizes, axis) + sizes[axis] - back[axis]
-            slot = slot * sizes[axis] + lax.rem(at, sizes[axis])
-        into[pl.ds(pl.multiple_of(slot * rows, rows), rows), :] = piece[...]
+    for piece, lines in zip(pieces, backs):
+        rows = piece.shape[0] // len(lines)
+        for i, back in enumerate(lines):
+            slot = 0
+            for axis in range(1, len(sizes)):
+                at = coordinate(me, sizes, axis) + sizes[axis] - back[axis]
+                slot = slot * sizes[axis] + lax.rem(at, sizes[axis])
+            start = pl.multiple_of(slot * rows, rows)
+            into[pl.ds(start, rows), :] = piece[i * rows : (i + 1) * rows, :]
 
 
 def model_side(proj, tokens, model_cols):
@@ -93,44 +106,49 @@
 def product_kernel(backs, sizes, model_cols, *refs):
     pieces, refs = refs[: len(backs[0])], refs[len(backs[0]) :]
     out_pieces, refs = refs[: len(backs[1])], refs[len(backs[1]) :]
-    proj, proj_h, w_gate, w_up, w_down, out, sums, tokens, stacked, buffers, arrived = refs
-    weights, sides = (w_gate, w_up, w_down), (0, 0, 1)
-    depth, chunk = buffers.shape[0], buffers.shape[3]
+    proj, *weights, out, sums, tokens, stacked, buffers, arrived = refs
+    sides = (0, 0, 1)
+    depth, _, block, chunk = buffers.shape
+    hidden_units, count = sums.shape[1:]
     steps = tokens.shape[2] // chunk
+    total = steps * (hidden_units // block)
+
+    def places(step):
+        rows = pl.ds(pl.multiple_of(lax.div(step, steps) * block, block), block)
+        return rows, pl.ds(pl.multiple_of(lax.rem(step, steps) * chunk, chunk), chunk)
 
     def copy(step, w):
         slot = lax.rem(step, depth)
-        columns = pl.ds(pl.multiple_of(step * chunk, chunk), chunk)
         return pltpu.make_async_copy(
-            weights[w].at[:, columns], buffers.at[slot, w], arrived.at[slot, w]
+            weights[w].at[places(step)], buffers.at[slot, w], arrived.at[slot, w]
         )
 
-    for step in range(min(depth, steps)):
+    for step in range(min(depth, total)):
         for w in range(3):
             copy(step, w).start()
     place_pieces(pieces, backs[0], sizes, tokens.at[0])
     place_pieces(out_pieces, backs[1], sizes, tokens.at[1])
     sums[...] = jnp.zeros_like(sums)
-    rank = proj.shape[0] // 3
-    right = [
-        model_side(proj[: 2 * rank, :], tokens.at[0], model_cols),
-        model_side(proj[2 * rank :, :], tokens.at[1], model_cols),
-    ]
-
-    @pl.loop(0, steps)
+
+    @pl.loop(0, total)
     def _(step):
-        columns = pl.ds(pl.multiple_of(step * chunk, chunk), chunk)
+        rows, columns = places(step)
         for w in range(3):
             copy(step, w).wait()
-            sums[w] += transposed_dot(
+            sums[w, rows, :] += transposed_dot(
                 buffers[lax.rem(step, depth), w], tokens[sides[w], :, columns]
             )
 
-            @pl.when(step + depth < steps)
+            @pl.when(step + depth < total)
             def _():
                 copy(step + depth, w).start()
 
-    hidden_units, count = sums.shape[1:]
+    rank = proj.shape[0] // 3
+    window = proj.shape[1] - hidden_units
+    right = [
+        model_side(proj[: 2 * rank, :window], tokens.at[0], model_cols),
+        model_side(proj[2 * rank :, :window], tokens.at[1], model_cols),
+    ]
     tile = 128 if hidden_units % 128 == 0 else 32
 
     @pl.loop(0, hidden_units // tile)
@@ -146,7 +164,7 @@
         stacked[2, rows, :] = (silu * up_value).astype(BF16)
 
     sides = [
-        jnp.dot(proj_h[p * rank : (p + 1) * rank, :], stacked[k], preferred_element_type=F32)
+        jnp.dot(proj[p * rank : (p + 1) * rank, window:], stacked[k], preferred_element_type=F32)
         for k, p in enumerate((1, 2, 0))
     ]
     every = jnp.concatenate(sides + right, 0)
@@ -165,23 +183,24 @@
         out[used:] = jnp.zeros_like(out[used:])
 
 
-def products(in_pieces, out_pieces, backs, sizes, proj, proj_h, w_gate, w_up, w_down):
+def products(in_pieces, out_pieces, backs, sizes, proj, w_gate, w_up, w_down):
     hidden, width = w_gate.shape
     count = int(np.prod(sizes))
-    tokens = in_pieces[0].shape[0] * len(in_pieces)
+    tokens = sum(piece.shape[0] for piece in in_pieces)
     model_cols = width // count
-    chunk = min(width, 1024)
+    chunk = min(width, 2048)
+    block = hidden // 2 if hidden % 32 == 0 and hidden > 256 else hidden
     height = 8 * -(-2 * proj.shape[0] // (8 * count))
     return pl.pallas_call(
         functools.partial(product_kernel, backs, sizes, model_cols),
         out_shape=jax.ShapeDtypeStruct((count, height, tokens), F32),
-        in_specs=[VMEM] * (len(in_pieces) + len(out_pieces) + 2) + [ANY] * 3,
+        in_specs=[VMEM] * (len(in_pieces) + len(out_pieces) + 1) + [HBM] * 3,
         out_specs=VMEM,
         scratch_shapes=[
             pltpu.VMEM((3, hidden, tokens), F32),
             pltpu.VMEM((2, tokens, width), BF16),
             pltpu.VMEM((3, hidden, tokens), BF16),
-            pltpu.VMEM((2, 3, hidden, chunk), BF16),
+            pltpu.VMEM((2, 3, block, chunk), BF16),
             pltpu.SemaphoreType.DMA((2, 3)),
         ],
         compiler_params=pltpu.CompilerParams(vmem_limit_bytes=44 * 2**20),
@@ -191,12 +210,19 @@
             transcendentals=hidden * tokens,
         ),
         name="products",
-    )(*in_pieces, *out_pieces, proj, proj_h, w_gate, w_up, w_down)
+    )(*in_pieces, *out_pieces, proj, w_gate, w_up, w_down)
+
+
+def small_kernel(megabytes):
+    return pltpu.CompilerParams(vmem_limit_bytes=megabytes * 2**20)
 
 
 def sum_kernel(values, out):
-    total = jnp.sum(values[...], 0)
-    out[...] = jnp.broadcast_to(total[None], out.shape)
+    total = values[0]
+    for i in range(1, values.shape[0]):
+        total += values[i]
+    for i in range(out.shape[0]):
+        out[i] = total
 
 
 def sum_copies(values):
@@ -205,6 +231,7 @@
         out_shape=jax.ShapeDtypeStruct(values.shape, F32),
         in_specs=[VMEM],
         out_specs=VMEM,
+        compiler_params=small_kernel(8),
         name="sum_copies",
     )(values)
 
@@ -236,11 +263,16 @@
             for part in halves(every[(3 + k) * rank : (4 + k) * rank])
         )
         total += jnp.sum(turned.reshape(examples, rank, tokens) * left[None], 1)
-    scores = transposed_dot(total, onehot_of(ids[...], tokens), HIGHEST)
-    parts = [scores, domains[...].astype(F32), jnp.ones((examples, 1), F32)]
-    rest = out.shape[2] - SEQS - 2
-    parts = jnp.concatenate(parts + [jnp.zeros((examples, rest), F32)], 1)
-    out[...] = jnp.broadcast_to(parts[None], out.shape)
+    domain = lax.broadcasted_iota(jnp.int32, (DOMAINS, examples), 0)
+    domains = (domains[...] == domain).astype(F32)
+    total = jnp.dot(domains, total, precision=HIGHEST, preferred_element_type=F32)
+    scores = transposed_dot(onehot_of(ids[...], tokens), total, HIGHEST)
+    counts = transposed_dot(jnp.ones((SEQS // 2, examples), F32), domains, HIGHEST)
+    rest = out.shape[2] - 3 * DOMAINS
+    parts = [scores[: SEQS // 2], scores[SEQS // 2 :], counts, jnp.zeros((SEQS // 2, rest), F32)]
+    parts = jnp.concatenate(parts, 1)
+    for i in range(out.shape[0]):
+        out[i] = parts
 
 
 def sketch_kernel(rank, vectors, ids, sketches, norms):
@@ -261,14 +293,15 @@
 
 
 def score_kernel(parts, norms, scores):
-    every = parts[...].reshape(-1, parts.shape[2])
-    domain = lax.broadcasted_iota(jnp.int32, (every.shape[0], DOMAINS), 1).astype(F32)
-    onehot = (every[:, SEQS : SEQS + 1] == domain).astype(F32)
-    total = lax.dot_general(
-        every, onehot, (((0,), (0,)), ((), ())), precision=HIGHEST, preferred_element_type=F32
-    )
-    mean = total[:SEQS] / total[SEQS + 1 : SEQS + 2]
-    scores[...] = mean * lax.rsqrt(norms[:, :DOMAINS] + 1e-06)
+    total = parts[0]
+    for i in range(1, parts.shape[0]):
+        total += parts[i]
+    counts = total[:, 2 * DOMAINS : 3 * DOMAINS]
+    half = SEQS // 2
+    for i in range(2):
+        mean = total[:, i * DOMAINS : (i + 1) * DOMAINS] / counts
+        norm = norms[i * half : (i + 1) * half, :DOMAINS]
+        scores[i * half : (i + 1) * half, :] = mean * lax.rsqrt(norm + 1e-06)
 
 
 def on_device(
@@ -288,12 +321,9 @@
     rank = proj_model.shape[1] // 3
     model_cols = proj_model.shape[0]
     tokens = count * activations.shape[0]
-    examples = targets.shape[0]
-    inner = list(range(1, len(sizes)))
-    flipped = inner[:-1][::-1] + inner[-1:]
-
-    in_pieces, in_backs = gather_pieces(activations, sizes, flipped)
-    out_pieces, out_backs = gather_pieces(cotangent, sizes, inner)
+    inner = list(range(1, len(sizes) - 1))
+    in_pieces, in_backs = gather_rows(activations, sizes, inner)
+    out_pieces, out_backs = gather_rows(cotangent, sizes, inner[::-1])
 
     window = max(model_cols, 128)
     proj_m = proj_model.T
@@ -309,8 +339,7 @@
         out_pieces,
         (in_backs, out_backs),
         sizes,
-        proj_m,
-        proj_hidden.T,
+        jnp.concatenate([proj_m, proj_hidden.T], 1),
         w_gate,
         w_up,
         w_down,
@@ -320,12 +349,12 @@
     ids = slot_order(seq_ids, sizes)[None, :]
     parts = pl.pallas_call(
         functools.partial(target_kernel, rank),
-        out_shape=jax.ShapeDtypeStruct((count, examples, 128), F32),
+        out_shape=jax.ShapeDtypeStruct((count, SEQS // 2, 128), F32),
         in_specs=[VMEM] * 4,
         out_specs=VMEM,
-        compiler_params=pltpu.CompilerParams(vmem_limit_bytes=32 * 2**20),
+        compiler_params=small_kernel(16),
         name="target_products",
-    )(vectors, ids, targets, target_domain[:, None])
+    )(vectors, ids, targets, target_domain[None, :])
     parts, vectors = lax.optimization_barrier((parts, vectors))
     parts = exchange(parts)
     sketches, norms = pl.pallas_call(
@@ -336,7 +365,7 @@
         ),
         in_specs=[VMEM] * 2,
         out_specs=(VMEM, VMEM),
-        compiler_params=pltpu.CompilerParams(vmem_limit_bytes=40 * 2**20),
+        compiler_params=small_kernel(24),
         name="sketches",
     )(vectors, ids)
     scores = pl.pallas_call(
@@ -344,6 +373,7 @@
         out_shape=jax.ShapeDtypeStruct((SEQS, DOMAINS), F32),
         in_specs=[VMEM] * 2,
         out_specs=VMEM,
+        compiler_params=small_kernel(4),
         name="scores",
     )(parts, norms)
     return sketches, scores

time: 107 us -> 101 us (0.944)
  starting transfers between devices: 26.7 us -> 22.7 us
  waiting for transfers between devices: 32.6 us -> 35.8 us
  local copies, waits for them, and re-layouts: 3.4 us -> 0.23 us
  blocking collectives: 16.1 us -> 14.3 us
  Pallas kernels: 24.9 us -> 23.3 us
  other arithmetic: 2 us -> 3.1 us
    ppermute x20 -> x14, starting transfers between devices: 21.6 us -> 17.5 us  [shift(): return lax.ppermute(value, 'dp', pairs)]
    unnamed x14 -> x6, local copies, waits for them, and re-layouts: 3.11 us -> 0.02 us
    ppermute x20 -> x14, waiting for transfers between devices: 16.6 us -> 19.2 us  [shift(): return lax.ppermute(value, 'dp', pairs)]
    all_to_all x1, blocking collectives: 16.1 us -> 14.3 us  [exchange(): lax.all_to_all(blocks, 'dp', split_axis=0, concat_axis=0, axis_index_grou...]
    concatenate x2 -> x5, other arithmetic: 2 us -> 3.1 us  [the longest x2 2 us: gather_rows(): jnp.concatenate([rows] + received(rows, 0), 0)]
    pallas_call x1, Pallas kernels: 1.86 us -> 0.77 us  [on_device(): pl.pallas_call(score_kernel, out_shape=jax.ShapeDtypeStruct((SEQS, DOMAIN...]
  transfers between devices with their start and end apart: 22 -> 16, of which waited for: 10 -> 9; matrix products, arithmetic and copies ran while one was open for 2% -> 3% of each run, Pallas kernels for 2% -> 2%
where the time goes in v5:
time: 101 us; the launch traced here: 100 us
  waiting for transfers between devices  35.8 us (35%)
  Pallas kernels  23.3 us (23%)
  starting transfers between devices  22.7 us (22%)
  blocking collectives  14.3 us (14%)
  other arithmetic  3.1 us (3%)
    ppermute x14, waiting for transfers between devices, shift(): return lax.ppermute(value, 'dp', pairs)  19.2 us
    pallas_call x1, Pallas kernels, products(): pl.pallas_call(functools.partial(product_kernel, backs, sizes, model_cols...  18.3 us
    ppermute x14, starting transfers between devices, shift(): return lax.ppermute(value, 'dp', pairs)  17.5 us
    all_to_all x2, waiting for transfers between devices, exchange(): lax.all_to_all(blocks, 'dp', split_axis=0, concat_axis=0, axis_index_grou...  16.7 us
    all_to_all x1, blocking collectives, exchange(): lax.all_to_all(blocks, 'dp', split_axis=0, concat_axis=0, axis_index_grou...  14.3 us
    all_to_all x2, starting transfers between devices, exchange(): lax.all_to_all(blocks, 'dp', split_axis=0, concat_axis=0, axis_index_grou...  5.14 us
  transfers between devices with their start and end apart: 16, of which 9 were waited for; matrix products, arithmetic and copies ran while one was open for 3% of the time, Pallas kernels for 2%

profile of v5, /device:TPU:0, one launch (start us, length us, event | category | flops | bytes accessed | tf_op | source)
XLA Modules:
  0.0 100.2 jit_solution(6805103265667744403)
XLA Ops:
  0.6 3.1 %collective-permute-start.7 = (bf16[4,8192]{1,0:T(4,128)(2,1)}, bf16[4,8192]{1,0:T(4,128)(2,1)S(1)}, u32[]{:S(2)}, u32[]{:S(2)}) collective-permute-start(bf16[4,8192]{1,0:T(4,128)(2,1)} %param.11), channel_id=1, source_target_pairs={{0,8},{1,9},{2,10},{3,11},{4,12},{5,13},{6,14},{7,15},{8,16},{9,17... | collective-permute-start | bytes 196616 | tf_op jit(solution)/shard_map/ppermute | solution.py:38
  3.7 2.6 %collective-permute-start.8 = (bf16[4,8192]{1,0:T(4,128)(2,1)}, bf16[4,8192]{1,0:T(4,128)(2,1)S(1)}, u32[]{:S(2)}, u32[]{:S(2)}) collective-permute-start(bf16[4,8192]{1,0:T(4,128)(2,1)} %param.11), channel_id=1, source_target_pairs={{0,16},{1,17},{2,18},{3,19},{4,20},{5,21},{6,22},{7,23},{8,24},{9,... | collective-permute-start | bytes 196616 | tf_op jit(solution)/shard_map/ppermute | solution.py:38
  6.3 1.3 %collective-permute-start.9 = (bf16[4,8192]{1,0:T(4,128)(2,1)}, bf16[4,8192]{1,0:T(4,128)(2,1)S(1)}, u32[]{:S(2)}, u32[]{:S(2)}) collective-permute-start(bf16[4,8192]{1,0:T(4,128)(2,1)} %param.11), channel_id=1, source_target_pairs={{0,24},{1,25},{2,26},{3,27},{4,28},{5,29},{6,30},{7,31},{8,0},{9,1... | collective-permute-start | bytes 196616 | tf_op jit(solution)/shard_map/ppermute | solution.py:38
  7.6 0.7 collective-permute-start
  8.3 0.3 collective-permute-start.1
  8.7 0.0 collective-permute-done.7
  8.7 2.8 %collective-permute-start.2 = (bf16[4,8192]{1,0:T(4,128)(2,1)}, bf16[4,8192]{1,0:T(4,128)(2,1)S(1)}, u32[]{:S(2)}, u32[]{:S(2)}) collective-permute-start(bf16[4,8192]{1,0:T(4,128)(2,1)} %param.10), channel_id=1, source_target_pairs={{0,24},{1,25},{2,26},{3,27},{4,28},{5,29},{6,30},{7,31},{8,0},{9,1... | collective-permute-start | bytes 196616 | tf_op jit(solution)/shard_map/ppermute | solution.py:38
  11.5 0.0 collective-permute-done.8
  11.5 0.0 collective-permute-done.9
  11.5 1.0 pad_maximum_fusion.4
  12.5 1.6 %collective-permute-start.10 = (bf16[16,8192]{1,0:T(8,128)(2,1)S(1)}, bf16[16,8192]{1,0:T(8,128)(2,1)S(1)}, u32[]{:S(2)}, u32[]{:S(2)}) collective-permute-start(bf16[16,8192]{1,0:T(8,128)(2,1)S(1)} %pad_maximum_fusion.4), channel_id=1, source_target_pairs={{0,2},{1,3},{2,0},{3,1},{4,6},{5,7},{6,4},{7,5},{8,10},{9,11},{10,... | collective-permute-start | bytes 786440 | tf_op jit(solution)/shard_map/ppermute | solution.py:38
  14.0 0.2 collective-permute-done
  14.2 2.4 %collective-permute-done.1 = bf16[4,8192]{1,0:T(4,128)(2,1)S(1)} collective-permute-done((bf16[4,8192]{1,0:T(4,128)(2,1)}, bf16[4,8192]{1,0:T(4,128)(2,1)S(1)}, u32[]{:S(2)}, u32[]{:S(2)}) %collective-permute-start.1) | collective-permute-done | bytes 65568 | tf_op jit(solution)/shard_map/ppermute | solution.py:38
  16.6 0.0 collective-permute-done.2
  16.6 1.0 pad_maximum_fusion.3
  17.6 1.9 %collective-permute-start.3 = (bf16[16,8192]{1,0:T(8,128)(2,1)S(1)}, bf16[16,8192]{1,0:T(8,128)(2,1)S(1)}, u32[]{:S(2)}, u32[]{:S(2)}) collective-permute-start(bf16[16,8192]{1,0:T(8,128)(2,1)S(1)} %pad_maximum_fusion.3), channel_id=1, source_target_pairs={{0,4},{1,5},{2,6},{3,7},{4,0},{5,1},{6,2},{7,3},{8,12},{9,13},{10,... | collective-permute-start | bytes 786440 | tf_op jit(solution)/shard_map/ppermute | solution.py:38
  19.5 0.6 collective-permute-done.10
  20.1 0.9 collective-permute-start.11
  21.0 5.9 %collective-permute-done.3 = bf16[16,8192]{1,0:T(8,128)(2,1)S(1)} collective-permute-done((bf16[16,8192]{1,0:T(8,128)(2,1)S(1)}, bf16[16,8192]{1,0:T(8,128)(2,1)S(1)}, u32[]{:S(2)}, u32[]{:S(2)}) %collective-permute-start.3) | collective-permute-done | bytes 262176 | tf_op jit(solution)/shard_map/ppermute | solution.py:38
  26.9 1.9 %collective-permute-start.4 = (bf16[32,8192]{1,0:T(8,128)(2,1)S(1)}, bf16[32,8192]{1,0:T(8,128)(2,1)S(1)}, u32[]{:S(2)}, u32[]{:S(2)}) collective-permute-start(bf16[32,8192]{1,0:T(8,128)(2,1)S(1)} %pad_maximum_fusion.refs_0_), channel_id=1, source_target_pairs={{0,2},{1,3},{2,0},{3,1},{4,6},{5,7},{6,4},{7,5},{8,10},{9,11},{10,... | collective-permute-start | bytes 1572872 | tf_op jit(solution)/shard_map/ppermute | solution.py:38
  28.8 0.0 collective-permute-start.12
  28.8 0.5 collective-permute-start.5
  29.3 7.6 %collective-permute-done.11.refs_5_ = bf16[32,8192]{1,0:T(8,128)(2,1)S(1)} collective-permute-done((bf16[32,8192]{1,0:T(8,128)(2,1)S(1)}, bf16[32,8192]{1,0:T(8,128)(2,1)S(1)}, u32[]{:S(2)}, u32[]{:S(2)}) %collective-permute-start.11) | collective-permute-done | bytes 524320 | tf_op jit(solution)/shard_map/ppermute | solution.py:38
  36.9 0.0 collective-permute-start.13
  36.9 1.6 %collective-permute-done.4.refs_1_ = bf16[32,8192]{1,0:T(8,128)(2,1)S(1)} collective-permute-done((bf16[32,8192]{1,0:T(8,128)(2,1)S(1)}, bf16[32,8192]{1,0:T(8,128)(2,1)S(1)}, u32[]{:S(2)}, u32[]{:S(2)}) %collective-permute-start.4) | collective-permute-done | bytes 524320 | tf_op jit(solution)/shard_map/ppermute | solution.py:38
  38.6 0.0 collective-permute-start.6
  38.6 1.0 %pad_maximum_fusion.2.refs_8_ = bf16[192,1152]{1,0:T(8,128)(2,1)S(1)} fusion(bf16[192,896]{1,0:T(8,128)(2,1)} %bitcast.5, bf16[192,256]{1,0:T(8,128)(2,1)} %bitcast.6), kind=kLoop, calls=%fused_computation.2 | loop fusion | flops 884736 | bytes 884736 | tf_op jit(solution)/shard_map/concatenate | solution.py:342
  39.6 0.0 copy-start.2
  39.6 0.0 copy-start
  39.6 0.0 copy-start.1
  39.6 0.0 collective-permute-done.12.refs_6_
  39.7 0.0 collective-permute-done.5.refs_2_
  39.7 0.0 collective-permute-done.13.refs_7_
  39.7 0.8 collective-permute-done.6.refs_3_
  40.5 18.3 %products.1 = f32[32,16,128]{2,1,0:T(8,128)S(1)} custom-call(bf16[32,8192]{1,0:T(8,128)(2,1)S(1)} %pad_maximum_fusion.refs_0_, bf16[32,8192]{1,0:T(8,128)(2,1)S(1)} %collective-permute-done.4.refs_1_, bf16[32,8192]{1,0:T(8,128)(2,1)S(1)} %collective-permute-done.5.refs_2_, bf16[32,8192]{1,0:T(8,128)(2,1)S(1)} %collective-permute-done.6.refs_3_, ...), custom_call_target="tpu_custom_call" | custom-call | flops 5637144576 | bytes 44040192 | tf_op jit(solution)/shard_map/products/pallas_call | solution.py:194
  58.8 14.3 %all_to_all.15.values = f32[32,16,128]{2,1,0:T(8,128)S(1)} all-to-all(f32[32,16,128]{2,1,0:T(8,128)S(1)} %products.1), channel_id=1, replica_groups=mesh['groups'=1,'dp'=32] {'dp'}, dimensions={0} | all-to-all | bytes 524288 | tf_op jit(solution)/shard_map/all_to_all | solution.py:75
  73.2 0.8 sum_copies.1
  73.9 2.6 %all-to-all-start.1 = ((f32[32,16,128]{2,1,0:T(8,128)}), f32[32,16,128]{2,1,0:T(8,128)S(1)}, u32[]{:S(2)}, u32[]{:S(2)}) async-start(f32[32,16,128]{2,1,0:T(8,128)} %sum_copies.1), calls=%async_computation.1 | async-start | bytes 524288 | tf_op jit(solution)/shard_map/all_to_all | solution.py:75
  76.5 0.0 copy-done.2
  76.5 0.1 reshape.7
  76.6 0.1 broadcast_in_dim_reshape.3.ids
  76.7 10.4 %all-to-all-done.1.vectors = f32[32,16,128]{2,1,0:T(8,128)S(1)} async-done(((f32[32,16,128]{2,1,0:T(8,128)}), f32[32,16,128]{2,1,0:T(8,128)S(1)}, u32[]{:S(2)}, u32[]{:S(2)}) %all-to-all-start.1) | async-done | bytes 262176 | tf_op jit(solution)/shard_map/all_to_all | solution.py:75
  87.1 0.0 copy-done
  87.1 1.5 %target_products.1 = f32[32,8,128]{2,1,0:T(8,128)} custom-call(f32[32,16,128]{2,1,0:T(8,128)S(1)} %all-to-all-done.1.vectors, s32[1,128]{1,0:T(1,128)S(1)} %broadcast_in_dim_reshape.3.ids, bf16[8,3,64,64]{3,2,1,0:T(8,128)(2,1)S(1)} %copy-done, s32[1,8]{1,0:T(1,128)S(1)} %bitcast.4), custom_call_target="tpu_custom_call" | custom-call | tf_op jit(solution)/shard_map/target_products/pallas_call | solution.py:350
  88.6 2.6 %all-to-all-start.2 = ((f32[32,8,128]{2,1,0:T(8,128)}), f32[32,8,128]{2,1,0:T(8,128)S(1)}, u32[]{:S(2)}, u32[]{:S(2)}) async-start(f32[32,8,128]{2,1,0:T(8,128)} %target_products.1), calls=%async_computation.2 | async-start | bytes 262144 | tf_op jit(solution)/shard_map/all_to_all | solution.py:75
  91.2 1.9 %sketches.1 = (f32[16,3,64,64]{3,2,1,0:T(8,128)}, f32[16,128]{1,0:T(8,128)S(1)}) custom-call(f32[32,16,128]{2,1,0:T(8,128)S(1)} %all-to-all-done.1.vectors, s32[1,128]{1,0:T(1,128)S(1)} %broadcast_in_dim_reshape.3.ids), custom_call_target="tpu_custom_call" | custom-call | tf_op jit(solution)/shard_map/sketches/pallas_call | solution.py:360
  93.1 6.3 %all-to-all-done.2.parts = f32[32,8,128]{2,1,0:T(8,128)S(1)} async-done(((f32[32,8,128]{2,1,0:T(8,128)}), f32[32,8,128]{2,1,0:T(8,128)S(1)}, u32[]{:S(2)}, u32[]{:S(2)}) %all-to-all-start.2) | async-done | bytes 131104 | tf_op jit(solution)/shard_map/all_to_all | solution.py:75
  99.4 0.8 scores.1
  (4 shorter events, 0.1 us)
Async XLA Ops:
  0.6 8.0 %collective-permute-start.7 = (bf16[4,8192]{1,0:T(4,128)(2,1)}, bf16[4,8192]{1,0:T(4,128)(2,1)S(1)}, u32[]{:S(2)}, u32[]{:S(2)}) collective-permute-start(bf16[4,8192]{1,0:T(4,128)(2,1)} %param.11), channel_id=1, source_target_pairs={{0,8},{1,9},{2,10},{3,11},{4,12},{5,13},{6,14},{7,15},{8,16},{9,17... | collective-permute-start | bytes 196616 | tf_op jit(solution)/shard_map/ppermute | solution.py:38
  3.7 7.8 %collective-permute-start.8 = (bf16[4,8192]{1,0:T(4,128)(2,1)}, bf16[4,8192]{1,0:T(4,128)(2,1)S(1)}, u32[]{:S(2)}, u32[]{:S(2)}) collective-permute-start(bf16[4,8192]{1,0:T(4,128)(2,1)} %param.11), channel_id=1, source_target_pairs={{0,16},{1,17},{2,18},{3,19},{4,20},{5,21},{6,22},{7,23},{8,24},{9,... | collective-permute-start | bytes 196616 | tf_op jit(solution)/shard_map/ppermute | solution.py:38
  6.3 5.2 %collective-permute-start.9 = (bf16[4,8192]{1,0:T(4,128)(2,1)}, bf16[4,8192]{1,0:T(4,128)(2,1)S(1)}, u32[]{:S(2)}, u32[]{:S(2)}) collective-permute-start(bf16[4,8192]{1,0:T(4,128)(2,1)} %param.11), channel_id=1, source_target_pairs={{0,24},{1,25},{2,26},{3,27},{4,28},{5,29},{6,30},{7,31},{8,0},{9,1... | collective-permute-start | bytes 196616 | tf_op jit(solution)/shard_map/ppermute | solution.py:38
  7.6 6.6 %collective-permute-start = (bf16[4,8192]{1,0:T(4,128)(2,1)}, bf16[4,8192]{1,0:T(4,128)(2,1)S(1)}, u32[]{:S(2)}, u32[]{:S(2)}) collective-permute-start(bf16[4,8192]{1,0:T(4,128)(2,1)} %param.10), channel_id=1, source_target_pairs={{0,8},{1,9},{2,10},{3,11},{4,12},{5,13},{6,14},{7,15},{8,16},{9,17... | collective-permute-start | bytes 196616 | tf_op jit(solution)/shard_map/ppermute | solution.py:38
  8.3 8.3 %collective-permute-start.1 = (bf16[4,8192]{1,0:T(4,128)(2,1)}, bf16[4,8192]{1,0:T(4,128)(2,1)S(1)}, u32[]{:S(2)}, u32[]{:S(2)}) collective-permute-start(bf16[4,8192]{1,0:T(4,128)(2,1)} %param.10), channel_id=1, source_target_pairs={{0,16},{1,17},{2,18},{3,19},{4,20},{5,21},{6,22},{7,23},{8,24},{9,... | collective-permute-start | bytes 196616 | tf_op jit(solution)/shard_map/ppermute | solution.py:38
  8.7 7.9 %collective-permute-start.2 = (bf16[4,8192]{1,0:T(4,128)(2,1)}, bf16[4,8192]{1,0:T(4,128)(2,1)S(1)}, u32[]{:S(2)}, u32[]{:S(2)}) collective-permute-start(bf16[4,8192]{1,0:T(4,128)(2,1)} %param.10), channel_id=1, source_target_pairs={{0,24},{1,25},{2,26},{3,27},{4,28},{5,29},{6,30},{7,31},{8,0},{9,1... | collective-permute-start | bytes 196616 | tf_op jit(solution)/shard_map/ppermute | solution.py:38
  12.5 7.6 %collective-permute-start.10 = (bf16[16,8192]{1,0:T(8,128)(2,1)S(1)}, bf16[16,8192]{1,0:T(8,128)(2,1)S(1)}, u32[]{:S(2)}, u32[]{:S(2)}) collective-permute-start(bf16[16,8192]{1,0:T(8,128)(2,1)S(1)} %pad_maximum_fusion.4), channel_id=1, source_target_pairs={{0,2},{1,3},{2,0},{3,1},{4,6},{5,7},{6,4},{7,5},{8,10},{9,11},{10,... | collective-permute-start | bytes 786440 | tf_op jit(solution)/shard_map/ppermute | solution.py:38
  17.6 9.3 %collective-permute-start.3 = (bf16[16,8192]{1,0:T(8,128)(2,1)S(1)}, bf16[16,8192]{1,0:T(8,128)(2,1)S(1)}, u32[]{:S(2)}, u32[]{:S(2)}) collective-permute-start(bf16[16,8192]{1,0:T(8,128)(2,1)S(1)} %pad_maximum_fusion.3), channel_id=1, source_target_pairs={{0,4},{1,5},{2,6},{3,7},{4,0},{5,1},{6,2},{7,3},{8,12},{9,13},{10,... | collective-permute-start | bytes 786440 | tf_op jit(solution)/shard_map/ppermute | solution.py:38
  20.1 16.8 %collective-permute-start.11 = (bf16[32,8192]{1,0:T(8,128)(2,1)S(1)}, bf16[32,8192]{1,0:T(8,128)(2,1)S(1)}, u32[]{:S(2)}, u32[]{:S(2)}) collective-permute-start(bf16[32,8192]{1,0:T(8,128)(2,1)S(1)} %pad_maximum_fusion.1.refs_4_), channel_id=1, source_target_pairs={{0,4},{1,5},{2,6},{3,7},{4,0},{5,1},{6,2},{7,3},{8,12},{9,13},{10,... | collective-permute-start | bytes 1572872 | tf_op jit(solution)/shard_map/ppermute | solution.py:38
  26.9 11.7 %collective-permute-start.4 = (bf16[32,8192]{1,0:T(8,128)(2,1)S(1)}, bf16[32,8192]{1,0:T(8,128)(2,1)S(1)}, u32[]{:S(2)}, u32[]{:S(2)}) collective-permute-start(bf16[32,8192]{1,0:T(8,128)(2,1)S(1)} %pad_maximum_fusion.refs_0_), channel_id=1, source_target_pairs={{0,2},{1,3},{2,0},{3,1},{4,6},{5,7},{6,4},{7,5},{8,10},{9,11},{10,... | collective-permute-start | bytes 1572872 | tf_op jit(solution)/shard_map/ppermute | solution.py:38
  28.8 10.9 %collective-permute-start.12 = (bf16[32,8192]{1,0:T(8,128)(2,1)S(1)}, bf16[32,8192]{1,0:T(8,128)(2,1)S(1)}, u32[]{:S(2)}, u32[]{:S(2)}) collective-permute-start(bf16[32,8192]{1,0:T(8,128)(2,1)S(1)} %pad_maximum_fusion.1.refs_4_), channel_id=1, source_target_pairs={{0,1},{1,0},{2,3},{3,2},{4,5},{5,4},{6,7},{7,6},{8,9},{9,8},{10,11... | collective-permute-start | bytes 1572872 | tf_op jit(solution)/shard_map/ppermute | solution.py:38
  28.8 10.9 %collective-permute-start.5 = (bf16[32,8192]{1,0:T(8,128)(2,1)S(1)}, bf16[32,8192]{1,0:T(8,128)(2,1)S(1)}, u32[]{:S(2)}, u32[]{:S(2)}) collective-permute-start(bf16[32,8192]{1,0:T(8,128)(2,1)S(1)} %pad_maximum_fusion.refs_0_), channel_id=1, source_target_pairs={{0,1},{1,0},{2,3},{3,2},{4,5},{5,4},{6,7},{7,6},{8,9},{9,8},{10,11... | collective-permute-start | bytes 1572872 | tf_op jit(solution)/shard_map/ppermute | solution.py:38
  36.9 2.7 %collective-permute-start.13 = (bf16[32,8192]{1,0:T(8,128)(2,1)S(1)}, bf16[32,8192]{1,0:T(8,128)(2,1)S(1)}, u32[]{:S(2)}, u32[]{:S(2)}) collective-permute-start(bf16[32,8192]{1,0:T(8,128)(2,1)S(1)} %collective-permute-done.11.refs_5_), channel_id=1, source_target_pairs={{0,1},{1,0},{2,3},{3,2},{4,5},{5,4},{6,7},{7,6},{8,9},{9,8},{10,11... | collective-permute-start | bytes 1572872 | tf_op jit(solution)/shard_map/ppermute | solution.py:38
  38.6 1.9 %collective-permute-start.6 = (bf16[32,8192]{1,0:T(8,128)(2,1)S(1)}, bf16[32,8192]{1,0:T(8,128)(2,1)S(1)}, u32[]{:S(2)}, u32[]{:S(2)}) collective-permute-start(bf16[32,8192]{1,0:T(8,128)(2,1)S(1)} %collective-permute-done.4.refs_1_), channel_id=1, source_target_pairs={{0,1},{1,0},{2,3},{3,2},{4,5},{5,4},{6,7},{7,6},{8,9},{9,8},{10,11... | collective-permute-start | bytes 1572872 | tf_op jit(solution)/shard_map/ppermute | solution.py:38
  39.6 36.9 %copy-start.2 = (s32[128]{0:T(128)S(1)}, s32[128]{0:T(128)}, u32[]{:S(2)}) copy-start(s32[128]{0:T(128)} %param.17) | copy-start | bytes 1540
  39.6 47.5 %copy-start = (bf16[8,3,64,64]{3,2,1,0:T(8,128)(2,1)S(1)}, bf16[8,3,64,64]{3,2,1,0:T(8,128)(2,1)}, u32[]{:S(2)}) copy-start(bf16[8,3,64,64]{3,2,1,0:T(8,128)(2,1)} %targets.1) | copy-start | bytes 589828
  39.6 47.5 %copy-start.1 = (s32[8]{0:T(128)S(1)}, s32[8]{0:T(128)}, u32[]{:S(2)}) copy-start(s32[8]{0:T(128)} %param.19) | copy-start | bytes 100
  73.9 13.2 %all-to-all-start.1 = ((f32[32,16,128]{2,1,0:T(8,128)}), f32[32,16,128]{2,1,0:T(8,128)S(1)}, u32[]{:S(2)}, u32[]{:S(2)}) async-start(f32[32,16,128]{2,1,0:T(8,128)} %sum_copies.1), calls=%async_computation.1 | async-start | bytes 524288 | tf_op jit(solution)/shard_map/all_to_all | solution.py:75
  88.6 10.8 %all-to-all-start.2 = ((f32[32,8,128]{2,1,0:T(8,128)}), f32[32,8,128]{2,1,0:T(8,128)S(1)}, u32[]{:S(2)}, u32[]{:S(2)}) async-start(f32[32,8,128]{2,1,0:T(8,128)} %target_products.1), calls=%async_computation.2 | async-start | bytes 262144 | tf_op jit(solution)/shard_map/all_to_all | solution.py:75

commit v6 on v5

--- a/solution.py
+++ b/solution.py
@@ -42,28 +42,43 @@
     return lax.rem(lax.div(me, strides_of(sizes)[axis]), sizes[axis])
 
 
-def gather_rows(rows, sizes, order):
+def received(piece, sizes, axis):
+    return [shift(piece, sizes, axis, k) for k in range(1, sizes[axis])]
+
+
+def gather_lines(parts, sizes):
+    rows = parts[0].shape[0]
+    both = lax.optimization_barrier(jnp.concatenate(parts, 0))
+    blocks = [both] + received(both, sizes, 0)
+    lines = [
+        jnp.concatenate([block[i * rows : (i + 1) * rows] for block in blocks], 0)
+        for i in range(len(parts))
+    ]
+    return [lax.optimization_barrier(line) for line in lines]
+
+
+def gather_plane(piece, sizes, order):
     backs = [tuple(0 for _ in sizes)]
 
     def moved(axis, amount):
         return [tuple(amount if i == axis else b for i, b in enumerate(back)) for back in backs]
 
-    def received(piece, axis):
-        return [shift(piece, sizes, axis, k) for k in range(1, sizes[axis])]
-
-    piece = lax.optimization_barrier(jnp.concatenate([rows] + received(rows, 0), 0))
+    first = None
     for axis in order[:-1]:
-        piece = jnp.concatenate([piece] + received(piece, axis), 0)
+        others = received(piece, sizes, axis)
+        first = others[0] if first is None else first
+        piece = jnp.concatenate([piece] + others, 0)
         backs = sum([moved(axis, k) for k in range(1, sizes[axis])], backs)
     pieces = [(piece, backs)]
     for axis in order[-1:]:
-        others = zip(received(piece, axis), range(1, sizes[axis]))
+        others = zip(received(piece, sizes, axis), range(1, sizes[axis]))
         pieces += [(other, moved(axis, k)) for other, k in others]
     core = len(sizes) - 1
     for piece, backs in list(pieces):
-        others = zip(received(piece, core), range(1, sizes[core]))
+        others = zip(received(piece, sizes, core), range(1, sizes[core]))
         pieces += [(other, moved(core, k)) for other, k in others]
-    return [piece for piece, _ in pieces], [backs for _, backs in pieces]
+    first = pieces[0][0] if first is None else first
+    return [piece for piece, _ in pieces], [backs for _, backs in pieces], first
 
 
 def slot_order(per_token, sizes):
@@ -106,8 +121,8 @@
 def product_kernel(backs, sizes, model_cols, *refs):
     pieces, refs = refs[: len(backs[0])], refs[len(backs[0]) :]
     out_pieces, refs = refs[: len(backs[1])], refs[len(backs[1]) :]
-    proj, *weights, out, sums, tokens, stacked, buffers, arrived = refs
-    sides = (0, 0, 1)
+    proj, w_down, *weights, out, sums, tokens, stacked, buffers, arrived = refs
+    streamed = len(weights)
     depth, _, block, chunk = buffers.shape
     hidden_units, count = sums.shape[1:]
     steps = tokens.shape[2] // chunk
@@ -124,7 +139,7 @@
         )
 
     for step in range(min(depth, total)):
-        for w in range(3):
+        for w in range(streamed):
             copy(step, w).start()
     place_pieces(pieces, backs[0], sizes, tokens.at[0])
     place_pieces(out_pieces, backs[1], sizes, tokens.at[1])
@@ -133,10 +148,11 @@
     @pl.loop(0, total)
     def _(step):
         rows, columns = places(step)
-        for w in range(3):
+        sums[2, rows, :] += transposed_dot(w_down[rows, columns], tokens[1, :, columns])
+        for w in range(streamed):
             copy(step, w).wait()
             sums[w, rows, :] += transposed_dot(
-                buffers[lax.rem(step, depth), w], tokens[sides[w], :, columns]
+                buffers[lax.rem(step, depth), w], tokens[0, :, columns]
             )
 
             @pl.when(step + depth < total)
@@ -183,7 +199,42 @@
         out[used:] = jnp.zeros_like(out[used:])
 
 
-def products(in_pieces, out_pieces, backs, sizes, proj, w_gate, w_up, w_down):
+def small_kernel(megabytes):
+    return pltpu.CompilerParams(vmem_limit_bytes=megabytes * 2**20)
+
+
+def near_kernel(proj_m, proj_h, weight, proj, near, arrived):
+    window = proj_m.shape[1]
+    copies = [
+        pltpu.make_async_copy(weight, near, arrived.at[0]),
+        pltpu.make_async_copy(proj_m, proj.at[:, :window], arrived.at[1]),
+        pltpu.make_async_copy(proj_h, proj.at[:, window:], arrived.at[2]),
+    ]
+    for copy in copies:
+        copy.start()
+    for copy in copies:
+        copy.wait()
+
+
+def bring_near(proj_m, proj_h, weight):
+    columns = proj_m.shape[1] + proj_h.shape[1]
+    size = 2 * weight.shape[0] * weight.shape[1]
+    return pl.pallas_call(
+        near_kernel,
+        out_shape=(
+            jax.ShapeDtypeStruct((proj_m.shape[0], columns), BF16),
+            jax.ShapeDtypeStruct(weight.shape, BF16),
+        ),
+        in_specs=[HBM] * 3,
+        out_specs=(VMEM, VMEM),
+        scratch_shapes=[pltpu.SemaphoreType.DMA((3,))],
+        compiler_params=small_kernel(34),
+        cost_estimate=pl.CostEstimate(flops=0, bytes_accessed=2 * size, transcendentals=0),
+        name="bring_near",
+    )(proj_m, proj_h, weight)
+
+
+def products(in_pieces, out_pieces, backs, sizes, proj, w_down, w_gate, w_up):
     hidden, width = w_gate.shape
     count = int(np.prod(sizes))
     tokens = sum(piece.shape[0] for piece in in_pieces)
@@ -194,27 +245,23 @@
     return pl.pallas_call(
         functools.partial(product_kernel, backs, sizes, model_cols),
         out_shape=jax.ShapeDtypeStruct((count, height, tokens), F32),
-        in_specs=[VMEM] * (len(in_pieces) + len(out_pieces) + 1) + [HBM] * 3,
+        in_specs=[VMEM] * (len(in_pieces) + len(out_pieces) + 2) + [HBM] * 2,
         out_specs=VMEM,
         scratch_shapes=[
             pltpu.VMEM((3, hidden, tokens), F32),
             pltpu.VMEM((2, tokens, width), BF16),
             pltpu.VMEM((3, hidden, tokens), BF16),
-            pltpu.VMEM((2, 3, block, chunk), BF16),
-            pltpu.SemaphoreType.DMA((2, 3)),
+            pltpu.VMEM((2, 2, block, chunk), BF16),
+            pltpu.SemaphoreType.DMA((2, 2)),
         ],
-        compiler_params=pltpu.CompilerParams(vmem_limit_bytes=44 * 2**20),
+        compiler_params=pltpu.CompilerParams(vmem_limit_bytes=28 * 2**20),
         cost_estimate=pl.CostEstimate(
             flops=6 * hidden * width * tokens,
             bytes_accessed=6 * hidden * width,
             transcendentals=hidden * tokens,
         ),
         name="products",
-    )(*in_pieces, *out_pieces, proj, w_gate, w_up, w_down)
-
-
-def small_kernel(megabytes):
-    return pltpu.CompilerParams(vmem_limit_bytes=megabytes * 2**20)
+    )(*in_pieces, *out_pieces, proj, w_down, w_gate, w_up)
 
 
 def sum_kernel(values, out):
@@ -322,8 +369,9 @@
     model_cols = proj_model.shape[0]
     tokens = count * activations.shape[0]
     inner = list(range(1, len(sizes) - 1))
-    in_pieces, in_backs = gather_rows(activations, sizes, inner)
-    out_pieces, out_backs = gather_rows(cotangent, sizes, inner[::-1])
+    in_line, out_line = gather_lines([activations, cotangent], sizes)
+    in_pieces, in_backs, in_first = gather_plane(in_line, sizes, inner)
+    out_pieces, out_backs, out_first = gather_plane(out_line, sizes, inner[::-1])
 
     window = max(model_cols, 128)
     proj_m = proj_model.T
@@ -334,15 +382,16 @@
         ]
         proj_m = jnp.concatenate(spots, 1)
 
+    held = lax.optimization_barrier((proj_m, proj_hidden.T, w_down, in_first, out_first))
+    near = bring_near(*held[:3])
     vectors = products(
         in_pieces,
         out_pieces,
         (in_backs, out_backs),
         sizes,
-        jnp.concatenate([proj_m, proj_hidden.T], 1),
+        *near,
         w_gate,
         w_up,
-        w_down,
     )
     vectors = exchange(sum_copies(exchange(vectors)))
 

time: 101 us -> 106 us (1.050)
  Pallas kernels: 23.3 us -> 27.7 us
  starting transfers between devices: 22.7 us -> 19 us
  waiting for transfers between devices: 35.8 us -> 39.4 us
  local copies, waits for them, and re-layouts: 0.23 us -> 2.28 us
  other arithmetic: 3.1 us -> 1.33 us
    pallas_call x0 -> x1, Pallas kernels: none -> 5.2 us  [bring_near(): pl.pallas_call(near_kernel, out_shape=(jax.ShapeDtypeStruct((proj_m.shape...]
    ppermute x14 -> x11, starting transfers between devices: 17.5 us -> 13.8 us  [shift(): return lax.ppermute(value, 'dp', pairs)]
    ppermute x14 -> x11, waiting for transfers between devices: 19.2 us -> 22.7 us  [shift(): return lax.ppermute(value, 'dp', pairs)]
    unnamed x6 -> x10, local copies, waits for them, and re-layouts: 0.02 us -> 1.89 us
    concatenate x5, other arithmetic: 3.1 us -> 1.33 us  [the longest x1 0.94 us: gather_lines(): both = lax.optimization_barrier(jnp.concatenate(parts, 0))]
  transfers between devices with their start and end apart: 16 -> 13, of which waited for: 9 -> 7; matrix products, arithmetic and copies ran while one was open for 3% -> 1% of each run, Pallas kernels for 2% -> 7%
where the time goes in v6:
time: 106 us
  waiting for transfers between devices  39.4 us (37%)
  Pallas kernels  27.7 us (26%)
  starting transfers between devices  19 us (18%)
  blocking collectives  15.2 us (14%)
  local copies, waits for them, and re-layouts  2.28 us (2%)
  other arithmetic  1.33 us (1%)
    ppermute x11, waiting for transfers between devices, shift(): return lax.ppermute(value, 'dp', pairs)  22.7 us
    pallas_call x1, Pallas kernels, products(): pl.pallas_call(functools.partial(product_kernel, backs, sizes, model_cols...  17.6 us
    all_to_all x2, waiting for transfers between devices, exchange(): lax.all_to_all(blocks, 'dp', split_axis=0, concat_axis=0, axis_index_grou...  16.7 us
    all_to_all x1, blocking collectives, exchange(): lax.all_to_all(blocks, 'dp', split_axis=0, concat_axis=0, axis_index_grou...  15.2 us
    ppermute x11, starting transfers between devices, shift(): return lax.ppermute(value, 'dp', pairs)  13.8 us
    pallas_call x1, Pallas kernels, bring_near(): pl.pallas_call(near_kernel, out_shape=(jax.ShapeDtypeStruct((proj_m.shape...  5.2 us
    all_to_all x2, starting transfers between devices, exchange(): lax.all_to_all(blocks, 'dp', split_axis=0, concat_axis=0, axis_index_grou...  5.15 us
  transfers between devices with their start and end apart: 13, of which 7 were waited for; matrix products, arithmetic and copies ran while one was open for 1% of the time, Pallas kernels for 7%

profile of v6, /device:TPU:0, one launch (start us, length us, event | category | flops | bytes accessed | tf_op | source)
XLA Modules:
  0.0 105.7 jit_solution(10435042608610379120)
XLA Ops:
  0.6 0.9 pad_maximum_fusion.4
  1.6 3.1 %collective-permute-start = (bf16[8,8192]{1,0:T(8,128)(2,1)S(1)}, bf16[8,8192]{1,0:T(8,128)(2,1)S(1)}, u32[]{:S(2)}, u32[]{:S(2)}) collective-permute-start(bf16[8,8192]{1,0:T(8,128)(2,1)S(1)} %pad_maximum_fusion.4), channel_id=1, source_target_pairs={{0,8},{1,9},{2,10},{3,11},{4,12},{5,13},{6,14},{7,15},{8,16},{9,17... | collective-permute-start | bytes 393224 | tf_op jit(solution)/shard_map/ppermute | solution.py:38
  4.6 2.6 %collective-permute-start.1 = (bf16[8,8192]{1,0:T(8,128)(2,1)S(1)}, bf16[8,8192]{1,0:T(8,128)(2,1)S(1)}, u32[]{:S(2)}, u32[]{:S(2)}) collective-permute-start(bf16[8,8192]{1,0:T(8,128)(2,1)S(1)} %pad_maximum_fusion.4), channel_id=1, source_target_pairs={{0,16},{1,17},{2,18},{3,19},{4,20},{5,21},{6,22},{7,23},{8,24},{9,... | collective-permute-start | bytes 393224 | tf_op jit(solution)/shard_map/ppermute | solution.py:38
  7.2 1.3 %collective-permute-start.2 = (bf16[8,8192]{1,0:T(8,128)(2,1)S(1)}, bf16[8,8192]{1,0:T(8,128)(2,1)S(1)}, u32[]{:S(2)}, u32[]{:S(2)}) collective-permute-start(bf16[8,8192]{1,0:T(8,128)(2,1)S(1)} %pad_maximum_fusion.4), channel_id=1, source_target_pairs={{0,24},{1,25},{2,26},{3,27},{4,28},{5,29},{6,30},{7,31},{8,0},{9,1... | collective-permute-start | bytes 393224 | tf_op jit(solution)/shard_map/ppermute | solution.py:38
  8.6 2.5 %collective-permute-done = bf16[8,8192]{1,0:T(8,128)(2,1)S(1)} collective-permute-done((bf16[8,8192]{1,0:T(8,128)(2,1)S(1)}, bf16[8,8192]{1,0:T(8,128)(2,1)S(1)}, u32[]{:S(2)}, u32[]{:S(2)}) %collective-permute-start) | collective-permute-done | bytes 131104 | tf_op jit(solution)/shard_map/ppermute | solution.py:38
  11.1 4.7 %collective-permute-done.1 = bf16[8,8192]{1,0:T(8,128)(2,1)S(1)} collective-permute-done((bf16[8,8192]{1,0:T(8,128)(2,1)S(1)}, bf16[8,8192]{1,0:T(8,128)(2,1)S(1)}, u32[]{:S(2)}, u32[]{:S(2)}) %collective-permute-start.1) | collective-permute-done | bytes 131104 | tf_op jit(solution)/shard_map/ppermute | solution.py:38
  15.9 0.0 collective-permute-done.2
  16.0 0.2 pad_maximum_fusion.3
  16.2 1.6 %collective-permute-start.7 = (bf16[16,8192]{1,0:T(8,128)(2,1)S(1)}, bf16[16,8192]{1,0:T(8,128)(2,1)S(1)}, u32[]{:S(2)}, u32[]{:S(2)}) collective-permute-start(bf16[16,8192]{1,0:T(8,128)(2,1)S(1)} %pad_maximum_fusion.3), channel_id=1, source_target_pairs={{0,2},{1,3},{2,0},{3,1},{4,6},{5,7},{6,4},{7,5},{8,10},{9,11},{10,... | collective-permute-start | bytes 786440 | tf_op jit(solution)/shard_map/ppermute | solution.py:38
  17.7 0.2 pad_maximum_fusion.2
  17.9 1.6 %collective-permute-start.3 = (bf16[16,8192]{1,0:T(8,128)(2,1)S(1)}, bf16[16,8192]{1,0:T(8,128)(2,1)S(1)}, u32[]{:S(2)}, u32[]{:S(2)}) collective-permute-start(bf16[16,8192]{1,0:T(8,128)(2,1)S(1)} %pad_maximum_fusion.2), channel_id=1, source_target_pairs={{0,4},{1,5},{2,6},{3,7},{4,0},{5,1},{6,2},{7,3},{8,12},{9,13},{10,... | collective-permute-start | bytes 786440 | tf_op jit(solution)/shard_map/ppermute | solution.py:38
  19.5 4.9 %collective-permute-done.7 = bf16[16,8192]{1,0:T(8,128)(2,1)S(1)} collective-permute-done((bf16[16,8192]{1,0:T(8,128)(2,1)S(1)}, bf16[16,8192]{1,0:T(8,128)(2,1)S(1)}, u32[]{:S(2)}, u32[]{:S(2)}) %collective-permute-start.7) | collective-permute-done | bytes 262176 | tf_op jit(solution)/shard_map/ppermute | solution.py:38
  24.4 1.6 %collective-permute-start.8 = (bf16[32,8192]{1,0:T(8,128)(2,1)S(1)}, bf16[32,8192]{1,0:T(8,128)(2,1)S(1)}, u32[]{:S(2)}, u32[]{:S(2)}) collective-permute-start(bf16[32,8192]{1,0:T(8,128)(2,1)S(1)} %pad_maximum_fusion.1.refs_4_), channel_id=1, source_target_pairs={{0,4},{1,5},{2,6},{3,7},{4,0},{5,1},{6,2},{7,3},{8,12},{9,13},{10,... | collective-permute-start | bytes 1572872 | tf_op jit(solution)/shard_map/ppermute | solution.py:38
  26.0 0.0 collective-permute-done.3
  26.0 1.6 %collective-permute-start.4 = (bf16[32,8192]{1,0:T(8,128)(2,1)S(1)}, bf16[32,8192]{1,0:T(8,128)(2,1)S(1)}, u32[]{:S(2)}, u32[]{:S(2)}) collective-permute-start(bf16[32,8192]{1,0:T(8,128)(2,1)S(1)} %pad_maximum_fusion.refs_0_), channel_id=1, source_target_pairs={{0,2},{1,3},{2,0},{3,1},{4,6},{5,7},{6,4},{7,5},{8,10},{9,11},{10,... | collective-permute-start | bytes 1572872 | tf_op jit(solution)/shard_map/ppermute | solution.py:38
  27.6 0.0 collective-permute-start.9
  27.6 0.5 collective-permute-start.5
  28.1 9.3 %collective-permute-done.8.refs_5_ = bf16[32,8192]{1,0:T(8,128)(2,1)S(1)} collective-permute-done((bf16[32,8192]{1,0:T(8,128)(2,1)S(1)}, bf16[32,8192]{1,0:T(8,128)(2,1)S(1)}, u32[]{:S(2)}, u32[]{:S(2)}) %collective-permute-start.8) | collective-permute-done | bytes 524320 | tf_op jit(solution)/shard_map/ppermute | solution.py:38
  37.4 0.0 collective-permute-start.10
  37.4 1.3 %collective-permute-done.4.refs_1_ = bf16[32,8192]{1,0:T(8,128)(2,1)S(1)} collective-permute-done((bf16[32,8192]{1,0:T(8,128)(2,1)S(1)}, bf16[32,8192]{1,0:T(8,128)(2,1)S(1)}, u32[]{:S(2)}, u32[]{:S(2)}) %collective-permute-start.4) | collective-permute-done | bytes 524320 | tf_op jit(solution)/shard_map/ppermute | solution.py:38
  38.7 0.0 collective-permute-start.6
  38.7 0.0 copy-start.1
  38.7 1.0 copy-done.1
  39.7 0.0 copy-start.2
  39.7 0.9 copy-done.2
  40.6 5.2 %bring_near.1 = (bf16[192,1152]{1,0:T(8,128)(2,1)S(1)}, bf16[896,8192]{1,0:T(8,128)(2,1)S(1)}) custom-call(bf16[192,256]{1,0:T(8,128)(2,1)S(1)} %bitcast.5, bf16[192,896]{1,0:T(8,128)(2,1)S(1)} %bitcast.4, bf16[896,8192]{1,0:T(8,128)(2,1)} %weight), custom_call_target="tpu_custom_call" | custom-call | bytes 29360128 | tf_op jit(solution)/shard_map/bring_near/pallas_call | solution.py:222
  45.8 0.0 collective-permute-done.9.refs_6_
  45.8 0.0 collective-permute-done.5.refs_2_
  45.8 0.0 collective-permute-done.10.refs_7_
  45.8 0.0 collective-permute-done.6.refs_3_
  45.8 0.0 copy-start.4
  45.8 0.0 copy-start
  45.9 0.0 copy-start.3
  45.9 17.6 %products.1 = f32[32,16,128]{2,1,0:T(8,128)S(1)} custom-call(bf16[32,8192]{1,0:T(8,128)(2,1)S(1)} %pad_maximum_fusion.refs_0_, bf16[32,8192]{1,0:T(8,128)(2,1)S(1)} %collective-permute-done.4.refs_1_, bf16[32,8192]{1,0:T(8,128)(2,1)S(1)} %collective-permute-done.5.refs_2_, bf16[32,8192]{1,0:T(8,128)(2,1)S(1)} %collective-permute-done.6.refs_3_, ...), custom_call_target="tpu_custom_call" | custom-call | flops 5637144576 | bytes 44040192 | tf_op jit(solution)/shard_map/products/pallas_call | solution.py:245
  63.4 15.2 %all_to_all.15.values = f32[32,16,128]{2,1,0:T(8,128)S(1)} all-to-all(f32[32,16,128]{2,1,0:T(8,128)S(1)} %products.1), channel_id=1, replica_groups=mesh['groups'=1,'dp'=32] {'dp'}, dimensions={0} | all-to-all | bytes 524288 | tf_op jit(solution)/shard_map/all_to_all | solution.py:90
  78.7 0.8 sum_copies.1
  79.4 2.6 %all-to-all-start.1 = ((f32[32,16,128]{2,1,0:T(8,128)}), f32[32,16,128]{2,1,0:T(8,128)S(1)}, u32[]{:S(2)}, u32[]{:S(2)}) async-start(f32[32,16,128]{2,1,0:T(8,128)} %sum_copies.1), calls=%async_computation.1 | async-start | bytes 524288 | tf_op jit(solution)/shard_map/all_to_all | solution.py:90
  82.0 0.0 copy-done.4
  82.0 0.1 reshape.7
  82.2 0.1 broadcast_in_dim_reshape.3.ids
  82.3 10.4 %all-to-all-done.1.vectors = f32[32,16,128]{2,1,0:T(8,128)S(1)} async-done(((f32[32,16,128]{2,1,0:T(8,128)}), f32[32,16,128]{2,1,0:T(8,128)S(1)}, u32[]{:S(2)}, u32[]{:S(2)}) %all-to-all-start.1) | async-done | bytes 262176 | tf_op jit(solution)/shard_map/all_to_all | solution.py:90
  92.6 0.0 copy-done
  92.6 0.0 copy-done.3
  92.6 1.5 %target_products.1 = f32[32,8,128]{2,1,0:T(8,128)} custom-call(f32[32,16,128]{2,1,0:T(8,128)S(1)} %all-to-all-done.1.vectors, s32[1,128]{1,0:T(1,128)S(1)} %broadcast_in_dim_reshape.3.ids, bf16[8,3,64,64]{3,2,1,0:T(8,128)(2,1)S(1)} %copy-done, s32[1,8]{1,0:T(1,128)S(1)} %bitcast.6), custom_call_target="tpu_custom_call" | custom-call | tf_op jit(solution)/shard_map/target_products/pallas_call | solution.py:399
  94.1 2.6 %all-to-all-start.2 = ((f32[32,8,128]{2,1,0:T(8,128)}), f32[32,8,128]{2,1,0:T(8,128)S(1)}, u32[]{:S(2)}, u32[]{:S(2)}) async-start(f32[32,8,128]{2,1,0:T(8,128)} %target_products.1), calls=%async_computation.2 | async-start | bytes 262144 | tf_op jit(solution)/shard_map/all_to_all | solution.py:90
  96.7 1.9 %sketches.1 = (f32[16,3,64,64]{3,2,1,0:T(8,128)}, f32[16,128]{1,0:T(8,128)S(1)}) custom-call(f32[32,16,128]{2,1,0:T(8,128)S(1)} %all-to-all-done.1.vectors, s32[1,128]{1,0:T(1,128)S(1)} %broadcast_in_dim_reshape.3.ids), custom_call_target="tpu_custom_call" | custom-call | tf_op jit(solution)/shard_map/sketches/pallas_call | solution.py:409
  98.6 6.3 %all-to-all-done.2.parts = f32[32,8,128]{2,1,0:T(8,128)S(1)} async-done(((f32[32,8,128]{2,1,0:T(8,128)}), f32[32,8,128]{2,1,0:T(8,128)S(1)}, u32[]{:S(2)}, u32[]{:S(2)}) %all-to-all-start.2) | async-done | bytes 131104 | tf_op jit(solution)/shard_map/all_to_all | solution.py:90
  105.0 0.8 scores.1
  (7 shorter events, 0.3 us)
Async XLA Ops:
  1.6 9.5 %collective-permute-start = (bf16[8,8192]{1,0:T(8,128)(2,1)S(1)}, bf16[8,8192]{1,0:T(8,128)(2,1)S(1)}, u32[]{:S(2)}, u32[]{:S(2)}) collective-permute-start(bf16[8,8192]{1,0:T(8,128)(2,1)S(1)} %pad_maximum_fusion.4), channel_id=1, source_target_pairs={{0,8},{1,9},{2,10},{3,11},{4,12},{5,13},{6,14},{7,15},{8,16},{9,17... | collective-permute-start | bytes 393224 | tf_op jit(solution)/shard_map/ppermute | solution.py:38
  4.6 11.2 %collective-permute-start.1 = (bf16[8,8192]{1,0:T(8,128)(2,1)S(1)}, bf16[8,8192]{1,0:T(8,128)(2,1)S(1)}, u32[]{:S(2)}, u32[]{:S(2)}) collective-permute-start(bf16[8,8192]{1,0:T(8,128)(2,1)S(1)} %pad_maximum_fusion.4), channel_id=1, source_target_pairs={{0,16},{1,17},{2,18},{3,19},{4,20},{5,21},{6,22},{7,23},{8,24},{9,... | collective-permute-start | bytes 393224 | tf_op jit(solution)/shard_map/ppermute | solution.py:38
  7.2 8.7 %collective-permute-start.2 = (bf16[8,8192]{1,0:T(8,128)(2,1)S(1)}, bf16[8,8192]{1,0:T(8,128)(2,1)S(1)}, u32[]{:S(2)}, u32[]{:S(2)}) collective-permute-start(bf16[8,8192]{1,0:T(8,128)(2,1)S(1)} %pad_maximum_fusion.4), channel_id=1, source_target_pairs={{0,24},{1,25},{2,26},{3,27},{4,28},{5,29},{6,30},{7,31},{8,0},{9,1... | collective-permute-start | bytes 393224 | tf_op jit(solution)/shard_map/ppermute | solution.py:38
  16.2 8.2 %collective-permute-start.7 = (bf16[16,8192]{1,0:T(8,128)(2,1)S(1)}, bf16[16,8192]{1,0:T(8,128)(2,1)S(1)}, u32[]{:S(2)}, u32[]{:S(2)}) collective-permute-start(bf16[16,8192]{1,0:T(8,128)(2,1)S(1)} %pad_maximum_fusion.3), channel_id=1, source_target_pairs={{0,2},{1,3},{2,0},{3,1},{4,6},{5,7},{6,4},{7,5},{8,10},{9,11},{10,... | collective-permute-start | bytes 786440 | tf_op jit(solution)/shard_map/ppermute | solution.py:38
  17.9 8.1 %collective-permute-start.3 = (bf16[16,8192]{1,0:T(8,128)(2,1)S(1)}, bf16[16,8192]{1,0:T(8,128)(2,1)S(1)}, u32[]{:S(2)}, u32[]{:S(2)}) collective-permute-start(bf16[16,8192]{1,0:T(8,128)(2,1)S(1)} %pad_maximum_fusion.2), channel_id=1, source_target_pairs={{0,4},{1,5},{2,6},{3,7},{4,0},{5,1},{6,2},{7,3},{8,12},{9,13},{10,... | collective-permute-start | bytes 786440 | tf_op jit(solution)/shard_map/ppermute | solution.py:38
  24.4 13.0 %collective-permute-start.8 = (bf16[32,8192]{1,0:T(8,128)(2,1)S(1)}, bf16[32,8192]{1,0:T(8,128)(2,1)S(1)}, u32[]{:S(2)}, u32[]{:S(2)}) collective-permute-start(bf16[32,8192]{1,0:T(8,128)(2,1)S(1)} %pad_maximum_fusion.1.refs_4_), channel_id=1, source_target_pairs={{0,4},{1,5},{2,6},{3,7},{4,0},{5,1},{6,2},{7,3},{8,12},{9,13},{10,... | collective-permute-start | bytes 1572872 | tf_op jit(solution)/shard_map/ppermute | solution.py:38
  26.0 12.7 %collective-permute-start.4 = (bf16[32,8192]{1,0:T(8,128)(2,1)S(1)}, bf16[32,8192]{1,0:T(8,128)(2,1)S(1)}, u32[]{:S(2)}, u32[]{:S(2)}) collective-permute-start(bf16[32,8192]{1,0:T(8,128)(2,1)S(1)} %pad_maximum_fusion.refs_0_), channel_id=1, source_target_pairs={{0,2},{1,3},{2,0},{3,1},{4,6},{5,7},{6,4},{7,5},{8,10},{9,11},{10,... | collective-permute-start | bytes 1572872 | tf_op jit(solution)/shard_map/ppermute | solution.py:38
  27.6 18.2 %collective-permute-start.9 = (bf16[32,8192]{1,0:T(8,128)(2,1)S(1)}, bf16[32,8192]{1,0:T(8,128)(2,1)S(1)}, u32[]{:S(2)}, u32[]{:S(2)}) collective-permute-start(bf16[32,8192]{1,0:T(8,128)(2,1)S(1)} %pad_maximum_fusion.1.refs_4_), channel_id=1, source_target_pairs={{0,1},{1,0},{2,3},{3,2},{4,5},{5,4},{6,7},{7,6},{8,9},{9,8},{10,11... | collective-permute-start | bytes 1572872 | tf_op jit(solution)/shard_map/ppermute | solution.py:38
  27.6 18.2 %collective-permute-start.5 = (bf16[32,8192]{1,0:T(8,128)(2,1)S(1)}, bf16[32,8192]{1,0:T(8,128)(2,1)S(1)}, u32[]{:S(2)}, u32[]{:S(2)}) collective-permute-start(bf16[32,8192]{1,0:T(8,128)(2,1)S(1)} %pad_maximum_fusion.refs_0_), channel_id=1, source_target_pairs={{0,1},{1,0},{2,3},{3,2},{4,5},{5,4},{6,7},{7,6},{8,9},{9,8},{10,11... | collective-permute-start | bytes 1572872 | tf_op jit(solution)/shard_map/ppermute | solution.py:38
  37.4 8.5 %collective-permute-start.10 = (bf16[32,8192]{1,0:T(8,128)(2,1)S(1)}, bf16[32,8192]{1,0:T(8,128)(2,1)S(1)}, u32[]{:S(2)}, u32[]{:S(2)}) collective-permute-start(bf16[32,8192]{1,0:T(8,128)(2,1)S(1)} %collective-permute-done.8.refs_5_), channel_id=1, source_target_pairs={{0,1},{1,0},{2,3},{3,2},{4,5},{5,4},{6,7},{7,6},{8,9},{9,8},{10,11... | collective-permute-start | bytes 1572872 | tf_op jit(solution)/shard_map/ppermute | solution.py:38
  38.7 7.1 %collective-permute-start.6 = (bf16[32,8192]{1,0:T(8,128)(2,1)S(1)}, bf16[32,8192]{1,0:T(8,128)(2,1)S(1)}, u32[]{:S(2)}, u32[]{:S(2)}) collective-permute-start(bf16[32,8192]{1,0:T(8,128)(2,1)S(1)} %collective-permute-done.4.refs_1_), channel_id=1, source_target_pairs={{0,1},{1,0},{2,3},{3,2},{4,5},{5,4},{6,7},{7,6},{8,9},{9,8},{10,11... | collective-permute-start | bytes 1572872 | tf_op jit(solution)/shard_map/ppermute | solution.py:38
  38.7 1.0 copy-start.1
  39.7 0.9 copy-start.2
  45.8 36.2 %copy-start.4 = (s32[128]{0:T(128)S(1)}, s32[128]{0:T(128)}, u32[]{:S(2)}) copy-start(s32[128]{0:T(128)} %param.17) | copy-start | bytes 1540
  45.8 46.8 %copy-start = (bf16[8,3,64,64]{3,2,1,0:T(8,128)(2,1)S(1)}, bf16[8,3,64,64]{3,2,1,0:T(8,128)(2,1)}, u32[]{:S(2)}) copy-start(bf16[8,3,64,64]{3,2,1,0:T(8,128)(2,1)} %targets.1) | copy-start | bytes 589828
  45.9 46.8 %copy-start.3 = (s32[8]{0:T(128)S(1)}, s32[8]{0:T(128)}, u32[]{:S(2)}) copy-start(s32[8]{0:T(128)} %param.19) | copy-start | bytes 100
  79.4 13.2 %all-to-all-start.1 = ((f32[32,16,128]{2,1,0:T(8,128)}), f32[32,16,128]{2,1,0:T(8,128)S(1)}, u32[]{:S(2)}, u32[]{:S(2)}) async-start(f32[32,16,128]{2,1,0:T(8,128)} %sum_copies.1), calls=%async_computation.1 | async-start | bytes 524288 | tf_op jit(solution)/shard_map/all_to_all | solution.py:90
  94.1 10.8 %all-to-all-start.2 = ((f32[32,8,128]{2,1,0:T(8,128)}), f32[32,8,128]{2,1,0:T(8,128)S(1)}, u32[]{:S(2)}, u32[]{:S(2)}) async-start(f32[32,8,128]{2,1,0:T(8,128)} %target_products.1), calls=%async_computation.2 | async-start | bytes 262144 | tf_op jit(solution)/shard_map/all_to_all | solution.py:90

commit v7 on v5

--- a/solution.py
+++ b/solution.py
@@ -38,32 +38,72 @@
     return lax.ppermute(value, "dp", pairs)
 
 
+def partner(value, sizes, axis, bit):
+    size, stride = sizes[axis], strides_of(sizes)[axis]
+    pairs = []
+    for source in range(int(np.prod(sizes))):
+        at = (source // stride) % size
+        pairs.append((source, source + ((at ^ bit) - at) * stride))
+    return lax.ppermute(value, "dp", pairs)
+
+
+def spread_axis(value, sizes, axis):
+    if sizes[axis] == 4:
+        far, near = partner(value, sizes, axis, 2), partner(value, sizes, axis, 1)
+        return [value, near, far, partner(far, sizes, axis, 1)]
+    return [value] + [shift(value, sizes, axis, k) for k in range(1, sizes[axis])]
+
+
+def origin(at, distance, size):
+    if size == 4:
+        return lax.bitwise_xor(at, distance)
+    return lax.rem(at + size - distance, size)
+
+
 def coordinate(me, sizes, axis):
     return lax.rem(lax.div(me, strides_of(sizes)[axis]), sizes[axis])
 
 
-def gather_rows(rows, sizes, order):
+def gather_lines(parts, sizes, others):
+    rows = parts[0].shape[0]
+    both = lax.optimization_barrier(jnp.concatenate(parts, 0))
+    blocks = spread_axis(both, sizes, 0)
+    lines = [
+        jnp.concatenate([block[i * rows : (i + 1) * rows] for block in blocks], 0)
+        for i in range(len(parts))
+    ]
+    made = lax.optimization_barrier((*lines, *others))
+    return made[: len(lines)], made[len(lines) :]
+
+
+def gather_stack(value, sizes, order):
+    for axis in order:
+        value = jnp.stack(spread_axis(value, sizes, axis))
+    return value
+
+
+def gather_plane(piece, sizes, order):
     backs = [tuple(0 for _ in sizes)]
 
     def moved(axis, amount):
         return [tuple(amount if i == axis else b for i, b in enumerate(back)) for back in backs]
 
-    def received(piece, axis):
-        return [shift(piece, sizes, axis, k) for k in range(1, sizes[axis])]
-
-    piece = lax.optimization_barrier(jnp.concatenate([rows] + received(rows, 0), 0))
+    first = None
     for axis in order[:-1]:
-        piece = jnp.concatenate([piece] + received(piece, axis), 0)
+        others = spread_axis(piece, sizes, axis)[1:]
+        first = others[0] if first is None else first
+        piece = jnp.concatenate([piece] + others, 0)
         backs = sum([moved(axis, k) for k in range(1, sizes[axis])], backs)
     pieces = [(piece, backs)]
     for axis in order[-1:]:
-        others = zip(received(piece, axis), range(1, sizes[axis]))
+        others = zip(spread_axis(piece, sizes, axis)[1:], range(1, sizes[axis]))
         pieces += [(other, moved(axis, k)) for other, k in others]
     core = len(sizes) - 1
     for piece, backs in list(pieces):
-        others = zip(received(piece, core), range(1, sizes[core]))
+        others = zip(spread_axis(piece, sizes, core)[1:], range(1, sizes[core]))
         pieces += [(other, moved(core, k)) for other, k in others]
-    return [piece for piece, _ in pieces], [backs for _, backs in pieces]
+    first = pieces[0][0] if first is None else first
+    return [piece for piece, _ in pieces], [backs for _, backs in pieces], first
 
 
 def slot_order(per_token, sizes):
@@ -90,8 +130,8 @@
         for i, back in enumerate(lines):
             slot = 0
             for axis in range(1, len(sizes)):
-                at = coordinate(me, sizes, axis) + sizes[axis] - back[axis]
-                slot = slot * sizes[axis] + lax.rem(at, sizes[axis])
+                at = origin(coordinate(me, sizes, axis), back[axis], sizes[axis])
+                slot = slot * sizes[axis] + at
             start = pl.multiple_of(slot * rows, rows)
             into[pl.ds(start, rows), :] = piece[i * rows : (i + 1) * rows, :]
 
@@ -173,7 +213,7 @@
     source = lax.broadcasted_iota(jnp.int32, (count, count), 0)
     target = lax.broadcasted_iota(jnp.int32, (count, count), 1)
     back = lax.rem(lax.div(source, each), size)
-    at = lax.rem(coordinate(lax.axis_index("dp"), sizes, 0) + size - back, size)
+    at = origin(coordinate(lax.axis_index("dp"), sizes, 0), back, size)
     place = lax.div(source, line) * line + at * each + lax.rem(source, each)
     order = (place == target).astype(F32)
     every = jnp.dot(every, order, precision=HIGHEST, preferred_element_type=F32)
@@ -181,6 +221,10 @@
     out[:used] = every.reshape((used,) + out.shape[1:])
     if used < out.shape[0]:
         out[used:] = jnp.zeros_like(out[used:])
+
+
+def small_kernel(megabytes):
+    return pltpu.CompilerParams(vmem_limit_bytes=megabytes * 2**20)
 
 
 def products(in_pieces, out_pieces, backs, sizes, proj, w_gate, w_up, w_down):
@@ -213,10 +257,6 @@
     )(*in_pieces, *out_pieces, proj, w_gate, w_up, w_down)
 
 
-def small_kernel(megabytes):
-    return pltpu.CompilerParams(vmem_limit_bytes=megabytes * 2**20)
-
-
 def sum_kernel(values, out):
     total = values[0]
     for i in range(1, values.shape[0]):
@@ -250,58 +290,63 @@
     return (ids == lax.broadcasted_iota(jnp.int32, (SEQS, tokens), 0)).astype(F32)
 
 
-def target_kernel(rank, vectors, ids, targets, domains, out):
+def sketch_kernel(sizes, order, vectors, means, ids, sketches, scores, lefts, turned):
+    count = int(np.prod(sizes))
+    rank = sketches.shape[2]
     tokens = ids.shape[1]
-    examples = targets.shape[0]
+    own_rank = means.shape[2] // rank
     every = rows_of(vectors, rank)
-    total = jnp.zeros((examples, tokens), F32)
+    onehot = onehot_of(ids[...], tokens)
+    masks = jnp.concatenate([onehot.astype(BF16)] * 3, 1)
+    norm = jnp.zeros((SEQS, 1), F32)
+    if own_rank * count > rank:
+        lefts[...] = jnp.zeros_like(lefts)
     for k in range(3):
         left = every[k * rank : (k + 1) * rank]
-        target = targets[:, k].reshape(examples * rank, rank)
-        turned = sum(
-            jnp.dot(target, part, preferred_element_type=F32)
-            for part in halves(every[(3 + k) * rank : (4 + k) * rank])
-        )
-        total += jnp.sum(turned.reshape(examples, rank, tokens) * left[None], 1)
-    domain = lax.broadcasted_iota(jnp.int32, (DOMAINS, examples), 0)
-    domains = (domains[...] == domain).astype(F32)
-    total = jnp.dot(domains, total, precision=HIGHEST, preferred_element_type=F32)
-    scores = transposed_dot(onehot_of(ids[...], tokens), total, HIGHEST)
-    counts = transposed_dot(jnp.ones((SEQS // 2, examples), F32), domains, HIGHEST)
-    rest = out.shape[2] - 3 * DOMAINS
-    parts = [scores[: SEQS // 2], scores[SEQS // 2 :], counts, jnp.zeros((SEQS // 2, rest), F32)]
-    parts = jnp.concatenate(parts, 1)
-    for i in range(out.shape[0]):
-        out[i] = parts
-
-
-def sketch_kernel(rank, vectors, ids, sketches, norms):
-    tokens = ids.shape[1]
-    every = rows_of(vectors, rank)
-    masks = jnp.concatenate([onehot_of(ids[...], tokens).astype(BF16)] * 3, 1)
-    norm = jnp.zeros((SEQS, 1), F32)
-    for k in range(3):
-        left_high, left_low = halves(every[k * rank : (k + 1) * rank])
-        right_high, right_low = halves(every[(3 + k) * rank : (4 + k) * rank])
-        left = jnp.concatenate([left_high, left_high, left_low], 1)
-        right = jnp.concatenate([right_high, right_low, right_high], 1)
-        rows = jnp.concatenate([left * masks[s : s + 1, :] for s in range(SEQS)], 0)
-        sketch = transposed_dot(rows, right).reshape(SEQS, rank, rank)
+        right = every[(3 + k) * rank : (4 + k) * rank]
+        left_high, left_low = halves(left)
+        right_high, right_low = halves(right)
+        left_three = jnp.concatenate([left_high, left_high, left_low], 1)
+        right_three = jnp.concatenate([right_high, right_low, right_high], 1)
+        rows = jnp.concatenate([left_three * masks[s : s + 1, :] for s in range(SEQS)], 0)
+        sketch = transposed_dot(rows, right_three).reshape(SEQS, rank, rank)
         sketches[:, k] = sketch
         norm += jnp.sum(jnp.sum(sketch * sketch, 1), 1, keepdims=True)
-    norms[...] = jnp.broadcast_to(norm, norms.shape)
-
-
-def score_kernel(parts, norms, scores):
-    total = parts[0]
-    for i in range(1, parts.shape[0]):
-        total += parts[i]
-    counts = total[:, 2 * DOMAINS : 3 * DOMAINS]
-    half = SEQS // 2
-    for i in range(2):
-        mean = total[:, i * DOMAINS : (i + 1) * DOMAINS] / counts
-        norm = norms[i * half : (i + 1) * half, :DOMAINS]
-        scores[i * half : (i + 1) * half, :] = mean * lax.rsqrt(norm + 1e-06)
+
+        for i in range(own_rank):
+            part = left[i * count : (i + 1) * count]
+            lefts[k, : part.shape[0], i * tokens : (i + 1) * tokens] = part
+        mean = means[:, k * DOMAINS : (k + 1) * DOMAINS, :].reshape(-1, own_rank * rank)
+        result = 0.0
+        for part in (right_high, right_low):
+            empty = jnp.zeros_like(part)
+            wide = jnp.concatenate(
+                [
+                    jnp.concatenate([part if i == c else empty for c in range(own_rank)], 1)
+                    for i in range(own_rank)
+                ],
+                0,
+            )
+            result += jnp.dot(mean, wide, preferred_element_type=F32)
+        turned[k] = result.reshape(count, DOMAINS, own_rank * tokens)
+
+    me = lax.axis_index("dp")
+
+    def add(device, total):
+        place, step = 0, 1
+        for axis in order:
+            back = origin(
+                coordinate(me, sizes, axis), coordinate(device, sizes, axis), sizes[axis]
+            )
+            place += back * step
+            step *= sizes[axis]
+        for k in range(3):
+            total += turned[k, place] * lefts[k, pl.ds(device, 1), :]
+        return total
+
+    total = lax.fori_loop(0, count, add, jnp.zeros((DOMAINS, own_rank * tokens), F32))
+    total = sum(total[:, i * tokens : (i + 1) * tokens] for i in range(own_rank))
+    scores[...] = transposed_dot(onehot, total, HIGHEST) * lax.rsqrt(norm + 1e-06)
 
 
 def on_device(
@@ -320,10 +365,11 @@
     sizes = axis_sizes(count)
     rank = proj_model.shape[1] // 3
     model_cols = proj_model.shape[0]
+    own_rank = -(-rank // count)
+    padded = own_rank * count
     tokens = count * activations.shape[0]
+    examples = targets.shape[0]
     inner = list(range(1, len(sizes) - 1))
-    in_pieces, in_backs = gather_rows(activations, sizes, inner)
-    out_pieces, out_backs = gather_rows(cotangent, sizes, inner[::-1])
 
     window = max(model_cols, 128)
     proj_m = proj_model.T
@@ -333,50 +379,52 @@
             jnp.where(at == i, proj_m, jnp.zeros_like(proj_m)) for i in range(window // model_cols)
         ]
         proj_m = jnp.concatenate(spots, 1)
+    proj = jnp.concatenate([proj_m, proj_hidden.T], 1)
+
+    cut = jnp.pad(targets, ((0, 0), (0, 0), (0, padded - rank), (0, 0)))
+    cut = cut.reshape(examples, 3, own_rank, count, rank).transpose(3, 0, 1, 2, 4)
+    entries = 3 * own_rank * rank
+    cut = cut.reshape(count, examples, entries)
+    tags = jnp.broadcast_to(target_domain.astype(BF16)[None, :, None], (count, examples, 128))
+    sent = jnp.concatenate([cut, tags], 2)
+
+    (in_line, out_line), (proj, sent) = gather_lines([activations, cotangent], sizes, [proj, sent])
+    in_pieces, in_backs, in_first = gather_plane(in_line, sizes, inner)
+    out_pieces, out_backs, out_first = gather_plane(out_line, sizes, inner[::-1])
+    sent, _, _ = lax.optimization_barrier((sent, in_first, out_first))
+    held = exchange(sent).reshape(count * examples, -1)
 
     vectors = products(
-        in_pieces,
-        out_pieces,
-        (in_backs, out_backs),
-        sizes,
-        jnp.concatenate([proj_m, proj_hidden.T], 1),
-        w_gate,
-        w_up,
-        w_down,
+        in_pieces, out_pieces, (in_backs, out_backs), sizes, proj, w_gate, w_up, w_down
     )
+    vectors, held = lax.optimization_barrier((vectors, held))
     vectors = exchange(sum_copies(exchange(vectors)))
 
-    ids = slot_order(seq_ids, sizes)[None, :]
-    parts = pl.pallas_call(
-        functools.partial(target_kernel, rank),
-        out_shape=jax.ShapeDtypeStruct((count, SEQS // 2, 128), F32),
-        in_specs=[VMEM] * 4,
-        out_specs=VMEM,
-        compiler_params=small_kernel(16),
-        name="target_products",
-    )(vectors, ids, targets, target_domain[None, :])
-    parts, vectors = lax.optimization_barrier((parts, vectors))
-    parts = exchange(parts)
-    sketches, norms = pl.pallas_call(
-        functools.partial(sketch_kernel, rank),
+    domains = held[:, -1].astype(F32)
+    domain_onehot = (domains[None, :] == jnp.arange(DOMAINS, dtype=F32)[:, None]).astype(BF16)
+    domain_sum = jnp.dot(domain_onehot, held[:, :entries], preferred_element_type=F32)
+    domain_count = jnp.sum(domain_onehot.astype(F32), 1)
+    mean = (domain_sum / domain_count[:, None]).astype(BF16)
+    mean = mean.reshape(DOMAINS, 3, own_rank * rank).transpose(1, 0, 2)
+    mean_order = [0] + inner + [len(sizes) - 1]
+    means = gather_stack(mean.reshape(3 * DOMAINS, -1), sizes, mean_order)
+    means = means.reshape((count,) + means.shape[-2:])
+
+    return pl.pallas_call(
+        functools.partial(sketch_kernel, sizes, mean_order),
         out_shape=(
             jax.ShapeDtypeStruct((SEQS, 3, rank, rank), F32),
-            jax.ShapeDtypeStruct((SEQS, 128), F32),
+            jax.ShapeDtypeStruct((SEQS, DOMAINS), F32),
         ),
-        in_specs=[VMEM] * 2,
+        in_specs=[VMEM] * 3,
         out_specs=(VMEM, VMEM),
-        compiler_params=small_kernel(24),
+        scratch_shapes=[
+            pltpu.VMEM((3, count, own_rank * tokens), F32),
+            pltpu.VMEM((3, count, DOMAINS, own_rank * tokens), F32),
+        ],
+        compiler_params=small_kernel(24 if tokens < 256 else 52),
         name="sketches",
-    )(vectors, ids)
-    scores = pl.pallas_call(
-        score_kernel,
-        out_shape=jax.ShapeDtypeStruct((SEQS, DOMAINS), F32),
-        in_specs=[VMEM] * 2,
-        out_specs=VMEM,
-        compiler_params=small_kernel(4),
-        name="scores",
-    )(parts, norms)
-    return sketches, scores
+    )(vectors, means, slot_order(seq_ids, sizes)[None, :])
 
 
 def solution(mesh):

time: 101 us -> 110 us (1.089)
  blocking collectives: 14.3 us -> 0 us
  starting transfers between devices: 22.7 us -> 37 us
  waiting for transfers between devices: 35.8 us -> 40.5 us
  local copies, waits for them, and re-layouts: 0.23 us -> 2.27 us
  Pallas kernels: 23.3 us -> 24.9 us
    all_to_all x1 -> x0, blocking collectives: 14.3 us -> none  [exchange(): lax.all_to_all(blocks, 'dp', split_axis=0, concat_axis=0, axis_index_grou...]
    ppermute x0 -> x6, starting transfers between devices: none -> 12.3 us  [partner(): return lax.ppermute(value, 'dp', pairs)]
    all_to_all x2 -> x3, starting transfers between devices: 5.14 us -> 15 us  [exchange(): lax.all_to_all(blocks, 'dp', split_axis=0, concat_axis=0, axis_index_grou...]
    ppermute x14 -> x11, starting transfers between devices: 17.5 us -> 9.67 us  [shift(): return lax.ppermute(value, 'dp', pairs)]
    ppermute x0 -> x6, waiting for transfers between devices: none -> 7.53 us  [partner(): return lax.ppermute(value, 'dp', pairs)]
    all_to_all x2 -> x3, waiting for transfers between devices: 16.7 us -> 10.9 us  [exchange(): lax.all_to_all(blocks, 'dp', split_axis=0, concat_axis=0, axis_index_grou...]
    ppermute x14 -> x11, waiting for transfers between devices: 19.2 us -> 22.1 us  [shift(): return lax.ppermute(value, 'dp', pairs)]
    pallas_call x1, Pallas kernels: 18.3 us -> 20.3 us  [products(): pl.pallas_call(functools.partial(product_kernel, backs, sizes, model_cols...]
  transfers between devices with their start and end apart: 16 -> 20, of which waited for: 9 -> 12; matrix products, arithmetic and copies ran while one was open for 3% -> 4% of each run, Pallas kernels for 2% -> 19%
where the time goes in v7:
time: 110 us
  waiting for transfers between devices  40.5 us (37%)
  starting transfers between devices  37 us (34%)
  Pallas kernels  24.9 us (23%)
  other arithmetic  4 us (4%)
  local copies, waits for them, and re-layouts  2.27 us (2%)
    ppermute x11, waiting for transfers between devices, shift(): return lax.ppermute(value, 'dp', pairs)  22.1 us
    pallas_call x1, Pallas kernels, products(): pl.pallas_call(functools.partial(product_kernel, backs, sizes, model_cols...  20.3 us
    all_to_all x3, starting transfers between devices, exchange(): lax.all_to_all(blocks, 'dp', split_axis=0, concat_axis=0, axis_index_grou...  15 us
    ppermute x6, starting transfers between devices, partner(): return lax.ppermute(value, 'dp', pairs)  12.3 us
    all_to_all x3, waiting for transfers between devices, exchange(): lax.all_to_all(blocks, 'dp', split_axis=0, concat_axis=0, axis_index_grou...  10.9 us
    ppermute x11, starting transfers between devices, shift(): return lax.ppermute(value, 'dp', pairs)  9.67 us
    ppermute x6, waiting for transfers between devices, partner(): return lax.ppermute(value, 'dp', pairs)  7.53 us
    pallas_call x1, Pallas kernels, on_device(): pl.pallas_call(functools.partial(sketch_kernel, sizes, mean_order), out_s...  3.87 us
  transfers between devices with their start and end apart: 20, of which 12 were waited for; matrix products, arithmetic and copies ran while one was open for 4% of the time, Pallas kernels for 19%

profile of v7, /device:TPU:0, one launch (start us, length us, event | category | flops | bytes accessed | tf_op | source)
XLA Modules:
  0.0 109.8 jit_solution(9736304578281635773)
XLA Ops:
  0.6 0.9 pad_maximum_fusion.7
  1.6 4.1 %collective-permute-start.1 = (bf16[8,8192]{1,0:T(8,128)(2,1)S(1)}, bf16[8,8192]{1,0:T(8,128)(2,1)S(1)}, u32[]{:S(2)}, u32[]{:S(2)}) collective-permute-start(bf16[8,8192]{1,0:T(8,128)(2,1)S(1)} %pad_maximum_fusion.7), channel_id=1, source_target_pairs={{0,16},{1,17},{2,18},{3,19},{4,20},{5,21},{6,22},{7,23},{8,24},{9,... | collective-permute-start | bytes 393224 | tf_op jit(solution)/shard_map/ppermute | solution.py:47
  5.7 1.6 %collective-permute-start = (bf16[8,8192]{1,0:T(8,128)(2,1)S(1)}, bf16[8,8192]{1,0:T(8,128)(2,1)S(1)}, u32[]{:S(2)}, u32[]{:S(2)}) collective-permute-start(bf16[8,8192]{1,0:T(8,128)(2,1)S(1)} %pad_maximum_fusion.7), channel_id=1, source_target_pairs={{0,8},{1,9},{2,10},{3,11},{4,12},{5,13},{6,14},{7,15},{8,0},{9,1},... | collective-permute-start | bytes 393224 | tf_op jit(solution)/shard_map/ppermute | solution.py:47
  7.3 1.0 pad_maximum_fusion.1.refs_8_
  8.3 1.3 %copy.29 = bf16[8,3,2,32,64]{4,2,1,0,3:T(2,128)(2,1)S(1)} copy(bf16[8,3,2,32,64]{4,3,2,1,0:T(8,128)(2,1)} %bitcast.29) | data formatting | bytes 393216 | tf_op jit(solution)/shard_map/reshape | solution.py:385
  9.6 0.3 reshape.35
  9.9 0.7 convert_element_type.22
  10.6 0.1 broadcast_in_dim.2
  10.7 0.7 pad_maximum_fusion.5
  11.4 0.7 collective-permute-done.1
  12.1 0.6 collective-permute-start.2
  12.8 4.2 %collective-permute-done.2 = bf16[8,8192]{1,0:T(8,128)(2,1)S(1)} collective-permute-done((bf16[8,8192]{1,0:T(8,128)(2,1)S(1)}, bf16[8,8192]{1,0:T(8,128)(2,1)S(1)}, u32[]{:S(2)}, u32[]{:S(2)}) %collective-permute-start.2) | collective-permute-done | bytes 131104 | tf_op jit(solution)/shard_map/ppermute | solution.py:47
  17.1 0.3 pad_maximum_fusion.3
  17.4 1.6 %collective-permute-start.7 = (bf16[16,8192]{1,0:T(8,128)(2,1)S(1)}, bf16[16,8192]{1,0:T(8,128)(2,1)S(1)}, u32[]{:S(2)}, u32[]{:S(2)}) collective-permute-start(bf16[16,8192]{1,0:T(8,128)(2,1)S(1)} %get-tuple-element.10), channel_id=1, source_target_pairs={{0,2},{1,3},{2,0},{3,1},{4,6},{5,7},{6,4},{7,5},{8,10},{9,11},{10,... | collective-permute-start | bytes 786440 | tf_op jit(solution)/shard_map/ppermute | solution.py:38
  19.0 1.6 %collective-permute-start.3 = (bf16[16,8192]{1,0:T(8,128)(2,1)S(1)}, bf16[16,8192]{1,0:T(8,128)(2,1)S(1)}, u32[]{:S(2)}, u32[]{:S(2)}) collective-permute-start(bf16[16,8192]{1,0:T(8,128)(2,1)S(1)} %get-tuple-element.9), channel_id=1, source_target_pairs={{0,4},{1,5},{2,6},{3,7},{4,0},{5,1},{6,2},{7,3},{8,12},{9,13},{10,... | collective-permute-start | bytes 786440 | tf_op jit(solution)/shard_map/ppermute | solution.py:38
  20.7 3.2 %collective-permute-done.7 = bf16[16,8192]{1,0:T(8,128)(2,1)S(1)} collective-permute-done((bf16[16,8192]{1,0:T(8,128)(2,1)S(1)}, bf16[16,8192]{1,0:T(8,128)(2,1)S(1)}, u32[]{:S(2)}, u32[]{:S(2)}) %collective-permute-start.7) | collective-permute-done | bytes 262176 | tf_op jit(solution)/shard_map/ppermute | solution.py:38
  23.9 1.6 %collective-permute-start.8 = (bf16[32,8192]{1,0:T(8,128)(2,1)S(1)}, bf16[32,8192]{1,0:T(8,128)(2,1)S(1)}, u32[]{:S(2)}, u32[]{:S(2)}) collective-permute-start(bf16[32,8192]{1,0:T(8,128)(2,1)S(1)} %constant_dynamic-update-slice_fusion.2.refs_4_), channel_id=1, source_target_pairs={{0,4},{1,5},{2,6},{3,7},{4,0},{5,1},{6,2},{7,3},{8,12},{9,13},{10,... | collective-permute-start | bytes 1572872 | tf_op jit(solution)/shard_map/ppermute | solution.py:38
  25.5 2.4 %collective-permute-done.3 = bf16[16,8192]{1,0:T(8,128)(2,1)S(1)} collective-permute-done((bf16[16,8192]{1,0:T(8,128)(2,1)S(1)}, bf16[16,8192]{1,0:T(8,128)(2,1)S(1)}, u32[]{:S(2)}, u32[]{:S(2)}) %collective-permute-start.3) | collective-permute-done | bytes 262176 | tf_op jit(solution)/shard_map/ppermute | solution.py:38
  27.9 0.1 collective-permute-start.4
  28.0 0.1 collective-permute-start.9
  28.0 0.5 collective-permute-start.5
  28.5 8.2 %collective-permute-done.8.refs_5_ = bf16[32,8192]{1,0:T(8,128)(2,1)S(1)} collective-permute-done((bf16[32,8192]{1,0:T(8,128)(2,1)S(1)}, bf16[32,8192]{1,0:T(8,128)(2,1)S(1)}, u32[]{:S(2)}, u32[]{:S(2)}) %collective-permute-start.8) | collective-permute-done | bytes 524320 | tf_op jit(solution)/shard_map/ppermute | solution.py:38
  36.7 0.4 collective-permute-done.4.refs_1_
  37.1 0.1 collective-permute-start.6
  37.2 6.4 %all-to-all-start = ((bf16[32,8,512]{2,1,0:T(8,128)(2,1)}), bf16[32,8,512]{2,1,0:T(8,128)(2,1)S(1)}, u32[]{:S(2)}, u32[]{:S(2)}) async-start(bf16[32,8,512]{2,1,0:T(8,128)(2,1)} %pad_maximum_fusion.5), calls=%async_computation | async-start | bytes 524288 | tf_op jit(solution)/shard_map/all_to_all | solution.py:115
  43.7 20.3 %products.1 = f32[32,16,128]{2,1,0:T(8,128)} custom-call(bf16[32,8192]{1,0:T(8,128)(2,1)S(1)} %constant_dynamic-update-slice_fusion.refs_0_, bf16[32,8192]{1,0:T(8,128)(2,1)S(1)} %collective-permute-done.4.refs_1_, bf16[32,8192]{1,0:T(8,128)(2,1)} %collective-permute-done.5.refs_2_, bf16[32,8192]{1,0:T(8,128)(2,1)} %collective-permute-done.6.refs_3_, ...), custom_call_target="tpu_custom_call" | custom-call | flops 5637144576 | bytes 44040192 | tf_op jit(solution)/shard_map/products/pallas_call | solution.py:238
  64.1 0.1 copy.24
  64.2 0.1 convert_reduce_fusion
  64.3 0.2 fusion
  64.5 2.7 %collective-permute-start.12 = (bf16[96,128]{1,0:T(8,128)(2,1)S(1)}, bf16[96,128]{1,0:T(8,128)(2,1)S(1)}, u32[]{:S(2)}, u32[]{:S(2)}) collective-permute-start(bf16[96,128]{1,0:T(8,128)(2,1)S(1)} %bitcast.36), channel_id=1, source_target_pairs={{0,16},{1,17},{2,18},{3,19},{4,20},{5,21},{6,22},{7,23},{8,24},{9,... | collective-permute-start | bytes 73736 | tf_op jit(solution)/shard_map/ppermute | solution.py:47
  67.3 1.5 %collective-permute-start.11 = (bf16[96,128]{1,0:T(8,128)(2,1)S(1)}, bf16[96,128]{1,0:T(8,128)(2,1)S(1)}, u32[]{:S(2)}, u32[]{:S(2)}) collective-permute-start(bf16[96,128]{1,0:T(8,128)(2,1)S(1)} %bitcast.37), channel_id=1, source_target_pairs={{0,8},{1,9},{2,10},{3,11},{4,12},{5,13},{6,14},{7,15},{8,0},{9,1},... | collective-permute-start | bytes 73736 | tf_op jit(solution)/shard_map/ppermute | solution.py:47
  68.8 0.5 collective-permute-done.12
  69.3 1.8 %collective-permute-start.13 = (bf16[96,128]{1,0:T(8,128)(2,1)S(1)}, bf16[96,128]{1,0:T(8,128)(2,1)S(1)}, u32[]{:S(2)}, u32[]{:S(2)}) collective-permute-start(bf16[96,128]{1,0:T(8,128)(2,1)S(1)} %collective-permute-done.12), channel_id=1, source_target_pairs={{0,8},{1,9},{2,10},{3,11},{4,12},{5,13},{6,14},{7,15},{8,0},{9,1},... | collective-permute-start | bytes 73736 | tf_op jit(solution)/shard_map/ppermute | solution.py:47
  71.1 0.1 collective-permute-done.11
  71.2 2.0 %collective-permute-done.13 = bf16[96,128]{1,0:T(8,128)(2,1)S(1)} collective-permute-done((bf16[96,128]{1,0:T(8,128)(2,1)S(1)}, bf16[96,128]{1,0:T(8,128)(2,1)S(1)}, u32[]{:S(2)}, u32[]{:S(2)}) %collective-permute-start.13) | collective-permute-done | bytes 24608 | tf_op jit(solution)/shard_map/ppermute | solution.py:47
  73.2 2.2 %collective-permute-start.14 = (bf16[4,96,128]{2,1,0:T(8,128)(2,1)S(1)}, bf16[4,96,128]{2,1,0:T(8,128)(2,1)S(1)}, u32[]{:S(2)}, u32[]{:S(2)}) collective-permute-start(bf16[4,96,128]{2,1,0:T(8,128)(2,1)S(1)} %get-tuple-element.29), channel_id=1, source_target_pairs={{0,4},{1,5},{2,6},{3,7},{4,0},{5,1},{6,2},{7,3},{8,12},{9,13},{10,... | collective-permute-start | bytes 294920 | tf_op jit(solution)/shard_map/ppermute | solution.py:38
  75.4 4.5 %all-to-all-start.1 = ((f32[32,16,128]{2,1,0:T(8,128)}), f32[32,16,128]{2,1,0:T(8,128)S(1)}, u32[]{:S(2)}, u32[]{:S(2)}) async-start(f32[32,16,128]{2,1,0:T(8,128)} %products.1), calls=%async_computation.1 | async-start | bytes 524288 | tf_op jit(solution)/shard_map/all_to_all | solution.py:115
  79.9 1.8 %collective-permute-start.15 = (bf16[2,4,96,128]{3,2,1,0:T(8,128)(2,1)S(1)}, bf16[2,4,96,128]{3,2,1,0:T(8,128)(2,1)S(1)}, u32[]{:S(2)}, u32[]{:S(2)}) collective-permute-start(bf16[2,4,96,128]{3,2,1,0:T(8,128)(2,1)S(1)} %get-tuple-element.19), channel_id=1, source_target_pairs={{0,2},{1,3},{2,0},{3,1},{4,6},{5,7},{6,4},{7,5},{8,10},{9,11},{10,... | collective-permute-start | bytes 589832 | tf_op jit(solution)/shard_map/ppermute | solution.py:38
  81.7 7.9 %collective-permute-done.15 = bf16[2,4,96,128]{3,2,1,0:T(8,128)(2,1)S(1)} collective-permute-done((bf16[2,4,96,128]{3,2,1,0:T(8,128)(2,1)S(1)}, bf16[2,4,96,128]{3,2,1,0:T(8,128)(2,1)S(1)}, u32[]{:S(2)}, u32[]{:S(2)}) %collective-permute-start.15) | collective-permute-done | bytes 196640 | tf_op jit(solution)/shard_map/ppermute | solution.py:38
  89.7 0.1 collective-permute-start.16
  89.8 0.7 all-to-all-done.1.values
  90.4 0.8 sum_copies.1
  91.2 4.1 %all-to-all-start.2 = ((f32[32,16,128]{2,1,0:T(8,128)}), f32[32,16,128]{2,1,0:T(8,128)S(1)}, u32[]{:S(2)}, u32[]{:S(2)}) async-start(f32[32,16,128]{2,1,0:T(8,128)} %sum_copies.1), calls=%async_computation.2 | async-start | bytes 524288 | tf_op jit(solution)/shard_map/all_to_all | solution.py:115
  95.3 0.1 reshape.40
  95.4 0.1 broadcast_in_dim_reshape.3.ids
  95.5 0.1 pad_maximum_fusion
  95.6 10.3 %all-to-all-done.2.vectors = f32[32,16,128]{2,1,0:T(8,128)S(1)} async-done(((f32[32,16,128]{2,1,0:T(8,128)}), f32[32,16,128]{2,1,0:T(8,128)S(1)}, u32[]{:S(2)}, u32[]{:S(2)}) %all-to-all-start.2) | async-done | bytes 262176 | tf_op jit(solution)/shard_map/all_to_all | solution.py:115
  105.9 3.9 %sketches.1 = (f32[16,3,64,64]{3,2,1,0:T(8,128)}, f32[16,32]{1,0:T(8,128)}) custom-call(f32[32,16,128]{2,1,0:T(8,128)S(1)} %all-to-all-done.2.vectors, bf16[32,96,128]{2,1,0:T(8,128)(2,1)S(1)} %bitcast.25, s32[1,128]{1,0:T(1,128)S(1)} %broadcast_in_dim_reshape.3.ids), custom_call_target="tpu_custom_call" | custom-call | tf_op jit(solution)/shard_map/sketches/pallas_call | solution.py:413
  (26 shorter events, 0.4 us)
Async XLA Ops:
  1.6 10.5 %collective-permute-start.1 = (bf16[8,8192]{1,0:T(8,128)(2,1)S(1)}, bf16[8,8192]{1,0:T(8,128)(2,1)S(1)}, u32[]{:S(2)}, u32[]{:S(2)}) collective-permute-start(bf16[8,8192]{1,0:T(8,128)(2,1)S(1)} %pad_maximum_fusion.7), channel_id=1, source_target_pairs={{0,16},{1,17},{2,18},{3,19},{4,20},{5,21},{6,22},{7,23},{8,24},{9,... | collective-permute-start | bytes 393224 | tf_op jit(solution)/shard_map/ppermute | solution.py:47
  5.7 7.1 %collective-permute-start = (bf16[8,8192]{1,0:T(8,128)(2,1)S(1)}, bf16[8,8192]{1,0:T(8,128)(2,1)S(1)}, u32[]{:S(2)}, u32[]{:S(2)}) collective-permute-start(bf16[8,8192]{1,0:T(8,128)(2,1)S(1)} %pad_maximum_fusion.7), channel_id=1, source_target_pairs={{0,8},{1,9},{2,10},{3,11},{4,12},{5,13},{6,14},{7,15},{8,0},{9,1},... | collective-permute-start | bytes 393224 | tf_op jit(solution)/shard_map/ppermute | solution.py:47
  12.1 5.0 %collective-permute-start.2 = (bf16[8,8192]{1,0:T(8,128)(2,1)S(1)}, bf16[8,8192]{1,0:T(8,128)(2,1)S(1)}, u32[]{:S(2)}, u32[]{:S(2)}) collective-permute-start(bf16[8,8192]{1,0:T(8,128)(2,1)S(1)} %collective-permute-done.1), channel_id=1, source_target_pairs={{0,8},{1,9},{2,10},{3,11},{4,12},{5,13},{6,14},{7,15},{8,0},{9,1},... | collective-permute-start | bytes 393224 | tf_op jit(solution)/shard_map/ppermute | solution.py:47
  17.4 6.4 %collective-permute-start.7 = (bf16[16,8192]{1,0:T(8,128)(2,1)S(1)}, bf16[16,8192]{1,0:T(8,128)(2,1)S(1)}, u32[]{:S(2)}, u32[]{:S(2)}) collective-permute-start(bf16[16,8192]{1,0:T(8,128)(2,1)S(1)} %get-tuple-element.10), channel_id=1, source_target_pairs={{0,2},{1,3},{2,0},{3,1},{4,6},{5,7},{6,4},{7,5},{8,10},{9,11},{10,... | collective-permute-start | bytes 786440 | tf_op jit(solution)/shard_map/ppermute | solution.py:38
  19.0 8.8 %collective-permute-start.3 = (bf16[16,8192]{1,0:T(8,128)(2,1)S(1)}, bf16[16,8192]{1,0:T(8,128)(2,1)S(1)}, u32[]{:S(2)}, u32[]{:S(2)}) collective-permute-start(bf16[16,8192]{1,0:T(8,128)(2,1)S(1)} %get-tuple-element.9), channel_id=1, source_target_pairs={{0,4},{1,5},{2,6},{3,7},{4,0},{5,1},{6,2},{7,3},{8,12},{9,13},{10,... | collective-permute-start | bytes 786440 | tf_op jit(solution)/shard_map/ppermute | solution.py:38
  23.9 12.8 %collective-permute-start.8 = (bf16[32,8192]{1,0:T(8,128)(2,1)S(1)}, bf16[32,8192]{1,0:T(8,128)(2,1)S(1)}, u32[]{:S(2)}, u32[]{:S(2)}) collective-permute-start(bf16[32,8192]{1,0:T(8,128)(2,1)S(1)} %constant_dynamic-update-slice_fusion.2.refs_4_), channel_id=1, source_target_pairs={{0,4},{1,5},{2,6},{3,7},{4,0},{5,1},{6,2},{7,3},{8,12},{9,13},{10,... | collective-permute-start | bytes 1572872 | tf_op jit(solution)/shard_map/ppermute | solution.py:38
  27.9 9.2 %collective-permute-start.4 = (bf16[32,8192]{1,0:T(8,128)(2,1)S(1)}, bf16[32,8192]{1,0:T(8,128)(2,1)S(1)}, u32[]{:S(2)}, u32[]{:S(2)}) collective-permute-start(bf16[32,8192]{1,0:T(8,128)(2,1)S(1)} %constant_dynamic-update-slice_fusion.refs_0_), channel_id=1, source_target_pairs={{0,2},{1,3},{2,0},{3,1},{4,6},{5,7},{6,4},{7,5},{8,10},{9,11},{10,... | collective-permute-start | bytes 1572872 | tf_op jit(solution)/shard_map/ppermute | solution.py:38
  28.0 15.7 %collective-permute-start.9 = (bf16[32,8192]{1,0:T(8,128)(2,1)S(1)}, bf16[32,8192]{1,0:T(8,128)(2,1)S(1)}, u32[]{:S(2)}, u32[]{:S(2)}) collective-permute-start(bf16[32,8192]{1,0:T(8,128)(2,1)S(1)} %constant_dynamic-update-slice_fusion.2.refs_4_), channel_id=1, source_target_pairs={{0,1},{1,0},{2,3},{3,2},{4,5},{5,4},{6,7},{7,6},{8,9},{9,8},{10,11... | collective-permute-start | bytes 1572872 | tf_op jit(solution)/shard_map/ppermute | solution.py:38
  28.0 15.7 %collective-permute-start.5 = (bf16[32,8192]{1,0:T(8,128)(2,1)S(1)}, bf16[32,8192]{1,0:T(8,128)(2,1)}, u32[]{:S(2)}, u32[]{:S(2)}) collective-permute-start(bf16[32,8192]{1,0:T(8,128)(2,1)S(1)} %constant_dynamic-update-slice_fusion.refs_0_), channel_id=1, source_target_pairs={{0,1},{1,0},{2,3},{3,2},{4,5},{5,4},{6,7},{7,6},{8,9},{9,8},{10,11... | collective-permute-start | bytes 1572872 | tf_op jit(solution)/shard_map/ppermute | solution.py:38
  36.7 7.0 %collective-permute-start.10 = (bf16[32,8192]{1,0:T(8,128)(2,1)S(1)}, bf16[32,8192]{1,0:T(8,128)(2,1)}, u32[]{:S(2)}, u32[]{:S(2)}) collective-permute-start(bf16[32,8192]{1,0:T(8,128)(2,1)S(1)} %collective-permute-done.8.refs_5_), channel_id=1, source_target_pairs={{0,1},{1,0},{2,3},{3,2},{4,5},{5,4},{6,7},{7,6},{8,9},{9,8},{10,11... | collective-permute-start | bytes 1572872 | tf_op jit(solution)/shard_map/ppermute | solution.py:38
  37.1 6.6 %collective-permute-start.6 = (bf16[32,8192]{1,0:T(8,128)(2,1)S(1)}, bf16[32,8192]{1,0:T(8,128)(2,1)}, u32[]{:S(2)}, u32[]{:S(2)}) collective-permute-start(bf16[32,8192]{1,0:T(8,128)(2,1)S(1)} %collective-permute-done.4.refs_1_), channel_id=1, source_target_pairs={{0,1},{1,0},{2,3},{3,2},{4,5},{5,4},{6,7},{7,6},{8,9},{9,8},{10,11... | collective-permute-start | bytes 1572872 | tf_op jit(solution)/shard_map/ppermute | solution.py:38
  37.2 26.8 %all-to-all-start = ((bf16[32,8,512]{2,1,0:T(8,128)(2,1)}), bf16[32,8,512]{2,1,0:T(8,128)(2,1)S(1)}, u32[]{:S(2)}, u32[]{:S(2)}) async-start(bf16[32,8,512]{2,1,0:T(8,128)(2,1)} %pad_maximum_fusion.5), calls=%async_computation | async-start | bytes 524288 | tf_op jit(solution)/shard_map/all_to_all | solution.py:115
  43.7 51.6 %copy-start = (s32[128]{0:T(128)S(1)}, s32[128]{0:T(128)}, u32[]{:S(2)}) copy-start(s32[128]{0:T(128)} %param.17) | copy-start | bytes 1540
  64.5 4.8 %collective-permute-start.12 = (bf16[96,128]{1,0:T(8,128)(2,1)S(1)}, bf16[96,128]{1,0:T(8,128)(2,1)S(1)}, u32[]{:S(2)}, u32[]{:S(2)}) collective-permute-start(bf16[96,128]{1,0:T(8,128)(2,1)S(1)} %bitcast.36), channel_id=1, source_target_pairs={{0,16},{1,17},{2,18},{3,19},{4,20},{5,21},{6,22},{7,23},{8,24},{9,... | collective-permute-start | bytes 73736 | tf_op jit(solution)/shard_map/ppermute | solution.py:47
  67.3 3.9 %collective-permute-start.11 = (bf16[96,128]{1,0:T(8,128)(2,1)S(1)}, bf16[96,128]{1,0:T(8,128)(2,1)S(1)}, u32[]{:S(2)}, u32[]{:S(2)}) collective-permute-start(bf16[96,128]{1,0:T(8,128)(2,1)S(1)} %bitcast.37), channel_id=1, source_target_pairs={{0,8},{1,9},{2,10},{3,11},{4,12},{5,13},{6,14},{7,15},{8,0},{9,1},... | collective-permute-start | bytes 73736 | tf_op jit(solution)/shard_map/ppermute | solution.py:47
  69.3 3.8 %collective-permute-start.13 = (bf16[96,128]{1,0:T(8,128)(2,1)S(1)}, bf16[96,128]{1,0:T(8,128)(2,1)S(1)}, u32[]{:S(2)}, u32[]{:S(2)}) collective-permute-start(bf16[96,128]{1,0:T(8,128)(2,1)S(1)} %collective-permute-done.12), channel_id=1, source_target_pairs={{0,8},{1,9},{2,10},{3,11},{4,12},{5,13},{6,14},{7,15},{8,0},{9,1},... | collective-permute-start | bytes 73736 | tf_op jit(solution)/shard_map/ppermute | solution.py:47
  73.2 6.7 %collective-permute-start.14 = (bf16[4,96,128]{2,1,0:T(8,128)(2,1)S(1)}, bf16[4,96,128]{2,1,0:T(8,128)(2,1)S(1)}, u32[]{:S(2)}, u32[]{:S(2)}) collective-permute-start(bf16[4,96,128]{2,1,0:T(8,128)(2,1)S(1)} %get-tuple-element.29), channel_id=1, source_target_pairs={{0,4},{1,5},{2,6},{3,7},{4,0},{5,1},{6,2},{7,3},{8,12},{9,13},{10,... | collective-permute-start | bytes 294920 | tf_op jit(solution)/shard_map/ppermute | solution.py:38
  75.4 15.1 %all-to-all-start.1 = ((f32[32,16,128]{2,1,0:T(8,128)}), f32[32,16,128]{2,1,0:T(8,128)S(1)}, u32[]{:S(2)}, u32[]{:S(2)}) async-start(f32[32,16,128]{2,1,0:T(8,128)} %products.1), calls=%async_computation.1 | async-start | bytes 524288 | tf_op jit(solution)/shard_map/all_to_all | solution.py:115
  79.9 9.7 %collective-permute-start.15 = (bf16[2,4,96,128]{3,2,1,0:T(8,128)(2,1)S(1)}, bf16[2,4,96,128]{3,2,1,0:T(8,128)(2,1)S(1)}, u32[]{:S(2)}, u32[]{:S(2)}) collective-permute-start(bf16[2,4,96,128]{3,2,1,0:T(8,128)(2,1)S(1)} %get-tuple-element.19), channel_id=1, source_target_pairs={{0,2},{1,3},{2,0},{3,1},{4,6},{5,7},{6,4},{7,5},{8,10},{9,11},{10,... | collective-permute-start | bytes 589832 | tf_op jit(solution)/shard_map/ppermute | solution.py:38
  89.7 5.8 %collective-permute-start.16 = (bf16[2,2,4,96,128]{4,3,2,1,0:T(8,128)(2,1)S(1)}, bf16[2,2,4,96,128]{4,3,2,1,0:T(8,128)(2,1)S(1)}, u32[]{:S(2)}, u32[]{:S(2)}) collective-permute-start(bf16[2,2,4,96,128]{4,3,2,1,0:T(8,128)(2,1)S(1)} %get-tuple-element.17), channel_id=1, source_target_pairs={{0,1},{1,0},{2,3},{3,2},{4,5},{5,4},{6,7},{7,6},{8,9},{9,8},{10,11... | collective-permute-start | bytes 1179656 | tf_op jit(solution)/shard_map/ppermute | solution.py:38
  91.2 14.7 %all-to-all-start.2 = ((f32[32,16,128]{2,1,0:T(8,128)}), f32[32,16,128]{2,1,0:T(8,128)S(1)}, u32[]{:S(2)}, u32[]{:S(2)}) async-start(f32[32,16,128]{2,1,0:T(8,128)} %sum_copies.1), calls=%async_computation.2 | async-start | bytes 524288 | tf_op jit(solution)/shard_map/all_to_all | solution.py:115

commit v8 on v7

--- a/solution.py
+++ b/solution.py
@@ -391,24 +391,29 @@
     (in_line, out_line), (proj, sent) = gather_lines([activations, cotangent], sizes, [proj, sent])
     in_pieces, in_backs, in_first = gather_plane(in_line, sizes, inner)
     out_pieces, out_backs, out_first = gather_plane(out_line, sizes, inner[::-1])
-    sent, _, _ = lax.optimization_barrier((sent, in_first, out_first))
     held = exchange(sent).reshape(count * examples, -1)
-
-    vectors = products(
-        in_pieces, out_pieces, (in_backs, out_backs), sizes, proj, w_gate, w_up, w_down
-    )
-    vectors, held = lax.optimization_barrier((vectors, held))
-    vectors = exchange(sum_copies(exchange(vectors)))
-
+    held, _, _ = lax.optimization_barrier((held, in_first, out_first))
     domains = held[:, -1].astype(F32)
     domain_onehot = (domains[None, :] == jnp.arange(DOMAINS, dtype=F32)[:, None]).astype(BF16)
     domain_sum = jnp.dot(domain_onehot, held[:, :entries], preferred_element_type=F32)
     domain_count = jnp.sum(domain_onehot.astype(F32), 1)
     mean = (domain_sum / domain_count[:, None]).astype(BF16)
     mean = mean.reshape(DOMAINS, 3, own_rank * rank).transpose(1, 0, 2)
+    means = gather_stack(mean.reshape(3 * DOMAINS, -1), sizes, [0])
+
+    vectors = products(
+        in_pieces, out_pieces, (in_backs, out_backs), sizes, proj, w_gate, w_up, w_down
+    )
+    for axis in inner[:-1]:
+        means = gather_stack(means, sizes, [axis])
+    vectors, means = lax.optimization_barrier((vectors, means))
+    vectors = sum_copies(exchange(vectors))
+    means = gather_stack(means, sizes, inner[-1:])
+    vectors, means = lax.optimization_barrier((vectors, means))
+    vectors = exchange(vectors)
+    means = gather_stack(means, sizes, [len(sizes) - 1])
+    means = means.reshape((count,) + means.shape[-2:])
     mean_order = [0] + inner + [len(sizes) - 1]
-    means = gather_stack(mean.reshape(3 * DOMAINS, -1), sizes, mean_order)
-    means = means.reshape((count,) + means.shape[-2:])
 
     return pl.pallas_call(
         functools.partial(sketch_kernel, sizes, mean_order),

time: 110 us -> 115 us (1.045)
  waiting for transfers between devices: 40.5 us -> 46.7 us
  starting transfers between devices: 37 us -> 34.4 us
    all_to_all x3, waiting for transfers between devices: 10.9 us -> 17.7 us  [exchange(): lax.all_to_all(blocks, 'dp', split_axis=0, concat_axis=0, axis_index_grou...]
    ppermute x11, waiting for transfers between devices: 22.1 us -> 16.8 us  [shift(): return lax.ppermute(value, 'dp', pairs)]
    ppermute x6, waiting for transfers between devices: 7.53 us -> 12.2 us  [partner(): return lax.ppermute(value, 'dp', pairs)]
    all_to_all x3, starting transfers between devices: 15 us -> 12.9 us  [exchange(): lax.all_to_all(blocks, 'dp', split_axis=0, concat_axis=0, axis_index_grou...]
  transfers between devices with their start and end apart: 20 -> 20, of which waited for: 12 -> 12; matrix products, arithmetic and copies ran while one was open for 4% -> 6% of each run, Pallas kernels for 19% -> 0%
where the time goes in v8:
time: 115 us
  waiting for transfers between devices  46.7 us (41%)
  starting transfers between devices  34.4 us (30%)
  Pallas kernels  24.9 us (22%)
  other arithmetic  4.64 us (4%)
  local copies, waits for them, and re-layouts  2.97 us (3%)
    pallas_call x1, Pallas kernels, products(): pl.pallas_call(functools.partial(product_kernel, backs, sizes, model_cols...  20.3 us
    all_to_all x3, waiting for transfers between devices, exchange(): lax.all_to_all(blocks, 'dp', split_axis=0, concat_axis=0, axis_index_grou...  17.7 us
    ppermute x11, waiting for transfers between devices, shift(): return lax.ppermute(value, 'dp', pairs)  16.8 us
    all_to_all x3, starting transfers between devices, exchange(): lax.all_to_all(blocks, 'dp', split_axis=0, concat_axis=0, axis_index_grou...  12.9 us
    ppermute x6, waiting for transfers between devices, partner(): return lax.ppermute(value, 'dp', pairs)  12.2 us
    ppermute x6, starting transfers between devices, partner(): return lax.ppermute(value, 'dp', pairs)  11.5 us
    ppermute x11, starting transfers between devices, shift(): return lax.ppermute(value, 'dp', pairs)  10 us
    pallas_call x1, Pallas kernels, on_device(): pl.pallas_call(functools.partial(sketch_kernel, sizes, mean_order), out_s...  3.87 us
  transfers between devices with their start and end apart: 20, of which 12 were waited for; matrix products, arithmetic and copies ran while one was open for 6% of the time, Pallas kernels for 0%

profile of v8, /device:TPU:0, one launch (start us, length us, event | category | flops | bytes accessed | tf_op | source)
XLA Modules:
  0.0 114.7 jit_solution(5473346668093759445)
XLA Ops:
  0.6 0.9 pad_maximum_fusion.7
  1.6 4.1 %collective-permute-start.1 = (bf16[8,8192]{1,0:T(8,128)(2,1)S(1)}, bf16[8,8192]{1,0:T(8,128)(2,1)S(1)}, u32[]{:S(2)}, u32[]{:S(2)}) collective-permute-start(bf16[8,8192]{1,0:T(8,128)(2,1)S(1)} %pad_maximum_fusion.7), channel_id=1, source_target_pairs={{0,16},{1,17},{2,18},{3,19},{4,20},{5,21},{6,22},{7,23},{8,24},{9,... | collective-permute-start | bytes 393224 | tf_op jit(solution)/shard_map/ppermute | solution.py:47
  5.7 1.6 %collective-permute-start = (bf16[8,8192]{1,0:T(8,128)(2,1)S(1)}, bf16[8,8192]{1,0:T(8,128)(2,1)S(1)}, u32[]{:S(2)}, u32[]{:S(2)}) collective-permute-start(bf16[8,8192]{1,0:T(8,128)(2,1)S(1)} %pad_maximum_fusion.7), channel_id=1, source_target_pairs={{0,8},{1,9},{2,10},{3,11},{4,12},{5,13},{6,14},{7,15},{8,0},{9,1},... | collective-permute-start | bytes 393224 | tf_op jit(solution)/shard_map/ppermute | solution.py:47
  7.3 1.0 pad_maximum_fusion.1.refs_8_
  8.3 1.3 %copy.29 = bf16[8,3,2,32,64]{4,2,1,0,3:T(2,128)(2,1)S(1)} copy(bf16[8,3,2,32,64]{4,3,2,1,0:T(8,128)(2,1)} %bitcast.29) | data formatting | bytes 393216 | tf_op jit(solution)/shard_map/reshape | solution.py:385
  9.6 0.3 reshape.35
  9.9 0.7 convert_element_type.22
  10.6 0.1 broadcast_in_dim.2
  10.7 0.7 pad_maximum_fusion.5
  11.4 0.7 collective-permute-done.1
  12.1 0.6 collective-permute-start.2
  12.8 0.0 collective-permute-done
  12.8 4.2 %collective-permute-done.2 = bf16[8,8192]{1,0:T(8,128)(2,1)S(1)} collective-permute-done((bf16[8,8192]{1,0:T(8,128)(2,1)S(1)}, bf16[8,8192]{1,0:T(8,128)(2,1)S(1)}, u32[]{:S(2)}, u32[]{:S(2)}) %collective-permute-start.2) | collective-permute-done | bytes 131104 | tf_op jit(solution)/shard_map/ppermute | solution.py:47
  17.1 0.3 pad_maximum_fusion.3
  17.4 1.6 %collective-permute-start.7 = (bf16[16,8192]{1,0:T(8,128)(2,1)S(1)}, bf16[16,8192]{1,0:T(8,128)(2,1)S(1)}, u32[]{:S(2)}, u32[]{:S(2)}) collective-permute-start(bf16[16,8192]{1,0:T(8,128)(2,1)S(1)} %get-tuple-element.12), channel_id=1, source_target_pairs={{0,2},{1,3},{2,0},{3,1},{4,6},{5,7},{6,4},{7,5},{8,10},{9,11},{10,... | collective-permute-start | bytes 786440 | tf_op jit(solution)/shard_map/ppermute | solution.py:38
  19.0 1.6 %collective-permute-start.3 = (bf16[16,8192]{1,0:T(8,128)(2,1)S(1)}, bf16[16,8192]{1,0:T(8,128)(2,1)S(1)}, u32[]{:S(2)}, u32[]{:S(2)}) collective-permute-start(bf16[16,8192]{1,0:T(8,128)(2,1)S(1)} %get-tuple-element.11), channel_id=1, source_target_pairs={{0,4},{1,5},{2,6},{3,7},{4,0},{5,1},{6,2},{7,3},{8,12},{9,13},{10,... | collective-permute-start | bytes 786440 | tf_op jit(solution)/shard_map/ppermute | solution.py:38
  20.7 4.2 %all-to-all-start = ((bf16[32,8,512]{2,1,0:T(8,128)(2,1)}), bf16[32,8,512]{2,1,0:T(8,128)(2,1)S(1)}, u32[]{:S(2)}, u32[]{:S(2)}) async-start(bf16[32,8,512]{2,1,0:T(8,128)(2,1)} %pad_maximum_fusion.5), calls=%async_computation | async-start | bytes 524288 | tf_op jit(solution)/shard_map/all_to_all | solution.py:115
  24.9 1.8 %collective-permute-start.8 = (bf16[32,8192]{1,0:T(8,128)(2,1)S(1)}, bf16[32,8192]{1,0:T(8,128)(2,1)S(1)}, u32[]{:S(2)}, u32[]{:S(2)}) collective-permute-start(bf16[32,8192]{1,0:T(8,128)(2,1)S(1)} %constant_dynamic-update-slice_fusion.2.refs_4_), channel_id=1, source_target_pairs={{0,4},{1,5},{2,6},{3,7},{4,0},{5,1},{6,2},{7,3},{8,12},{9,13},{10,... | collective-permute-start | bytes 1572872 | tf_op jit(solution)/shard_map/ppermute | solution.py:38
  26.8 1.5 %collective-permute-start.4 = (bf16[32,8192]{1,0:T(8,128)(2,1)S(1)}, bf16[32,8192]{1,0:T(8,128)(2,1)S(1)}, u32[]{:S(2)}, u32[]{:S(2)}) collective-permute-start(bf16[32,8192]{1,0:T(8,128)(2,1)S(1)} %constant_dynamic-update-slice_fusion.refs_0_), channel_id=1, source_target_pairs={{0,2},{1,3},{2,0},{3,1},{4,6},{5,7},{6,4},{7,5},{8,10},{9,11},{10,... | collective-permute-start | bytes 1572872 | tf_op jit(solution)/shard_map/ppermute | solution.py:38
  28.3 0.5 collective-permute-start.5
  28.8 6.7 %all-to-all-done = bf16[32,8,512]{2,1,0:T(8,128)(2,1)S(1)} async-done(((bf16[32,8,512]{2,1,0:T(8,128)(2,1)}), bf16[32,8,512]{2,1,0:T(8,128)(2,1)S(1)}, u32[]{:S(2)}, u32[]{:S(2)}) %all-to-all-start) | async-done | bytes 262176 | tf_op jit(solution)/shard_map/all_to_all | solution.py:115
  35.5 0.8 copy.24
  36.3 0.7 slice_convert_fusion
  37.0 0.1 convert_reduce_fusion
  37.1 4.7 %collective-permute-done.8.refs_5_ = bf16[32,8192]{1,0:T(8,128)(2,1)S(1)} collective-permute-done((bf16[32,8192]{1,0:T(8,128)(2,1)S(1)}, bf16[32,8192]{1,0:T(8,128)(2,1)S(1)}, u32[]{:S(2)}, u32[]{:S(2)}) %collective-permute-start.8) | collective-permute-done | bytes 524320 | tf_op jit(solution)/shard_map/ppermute | solution.py:38
  41.8 0.6 collective-permute-done.4.refs_1_
  42.4 0.1 fusion
  42.6 2.3 %collective-permute-start.12 = (bf16[96,128]{1,0:T(8,128)(2,1)S(1)}, bf16[96,128]{1,0:T(8,128)(2,1)S(1)}, u32[]{:S(2)}, u32[]{:S(2)}) collective-permute-start(bf16[96,128]{1,0:T(8,128)(2,1)S(1)} %bitcast.35), channel_id=1, source_target_pairs={{0,16},{1,17},{2,18},{3,19},{4,20},{5,21},{6,22},{7,23},{8,24},{9,... | collective-permute-start | bytes 73736 | tf_op jit(solution)/shard_map/ppermute | solution.py:47
  44.9 2.5 %collective-permute-done.12 = bf16[96,128]{1,0:T(8,128)(2,1)S(1)} collective-permute-done((bf16[96,128]{1,0:T(8,128)(2,1)S(1)}, bf16[96,128]{1,0:T(8,128)(2,1)S(1)}, u32[]{:S(2)}, u32[]{:S(2)}) %collective-permute-start.12) | collective-permute-done | bytes 24608 | tf_op jit(solution)/shard_map/ppermute | solution.py:47
  47.4 1.4 %collective-permute-start.11 = (bf16[96,128]{1,0:T(8,128)(2,1)S(1)}, bf16[96,128]{1,0:T(8,128)(2,1)S(1)}, u32[]{:S(2)}, u32[]{:S(2)}) collective-permute-start(bf16[96,128]{1,0:T(8,128)(2,1)S(1)} %bitcast.36), channel_id=1, source_target_pairs={{0,8},{1,9},{2,10},{3,11},{4,12},{5,13},{6,14},{7,15},{8,0},{9,1},... | collective-permute-start | bytes 73736 | tf_op jit(solution)/shard_map/ppermute | solution.py:47
  48.8 2.4 %collective-permute-done.11 = bf16[96,128]{1,0:T(8,128)(2,1)S(1)} collective-permute-done((bf16[96,128]{1,0:T(8,128)(2,1)S(1)}, bf16[96,128]{1,0:T(8,128)(2,1)S(1)}, u32[]{:S(2)}, u32[]{:S(2)}) %collective-permute-start.11) | collective-permute-done | bytes 24608 | tf_op jit(solution)/shard_map/ppermute | solution.py:47
  51.2 1.4 %collective-permute-start.13 = (bf16[96,128]{1,0:T(8,128)(2,1)S(1)}, bf16[96,128]{1,0:T(8,128)(2,1)S(1)}, u32[]{:S(2)}, u32[]{:S(2)}) collective-permute-start(bf16[96,128]{1,0:T(8,128)(2,1)S(1)} %collective-permute-done.12), channel_id=1, source_target_pairs={{0,8},{1,9},{2,10},{3,11},{4,12},{5,13},{6,14},{7,15},{8,0},{9,1},... | collective-permute-start | bytes 73736 | tf_op jit(solution)/shard_map/ppermute | solution.py:47
  52.7 2.4 %collective-permute-done.13 = bf16[96,128]{1,0:T(8,128)(2,1)S(1)} collective-permute-done((bf16[96,128]{1,0:T(8,128)(2,1)S(1)}, bf16[96,128]{1,0:T(8,128)(2,1)S(1)}, u32[]{:S(2)}, u32[]{:S(2)}) %collective-permute-start.13) | collective-permute-done | bytes 24608 | tf_op jit(solution)/shard_map/ppermute | solution.py:47
  55.1 1.1 collective-permute-start.14
  56.2 3.5 %collective-permute-done.14 = bf16[4,96,128]{2,1,0:T(8,128)(2,1)S(1)} collective-permute-done((bf16[4,96,128]{2,1,0:T(8,128)(2,1)S(1)}, bf16[4,96,128]{2,1,0:T(8,128)(2,1)S(1)}, u32[]{:S(2)}, u32[]{:S(2)}) %collective-permute-start.14) | collective-permute-done | bytes 98336 | tf_op jit(solution)/shard_map/ppermute | solution.py:38
  59.8 0.0 copy-start
  59.9 20.3 %products.1 = f32[32,16,128]{2,1,0:T(8,128)} custom-call(bf16[32,8192]{1,0:T(8,128)(2,1)S(1)} %constant_dynamic-update-slice_fusion.refs_0_, bf16[32,8192]{1,0:T(8,128)(2,1)S(1)} %collective-permute-done.4.refs_1_, bf16[32,8192]{1,0:T(8,128)(2,1)} %collective-permute-done.5.refs_2_, bf16[32,8192]{1,0:T(8,128)(2,1)} %collective-permute-done.6.refs_3_, ...), custom_call_target="tpu_custom_call" | custom-call | flops 5637144576 | bytes 44040192 | tf_op jit(solution)/shard_map/products/pallas_call | solution.py:238
  80.2 4.7 %all-to-all-start.1 = ((f32[32,16,128]{2,1,0:T(8,128)}), f32[32,16,128]{2,1,0:T(8,128)S(1)}, u32[]{:S(2)}, u32[]{:S(2)}) async-start(f32[32,16,128]{2,1,0:T(8,128)} %products.1), calls=%async_computation.1 | async-start | bytes 524288 | tf_op jit(solution)/shard_map/all_to_all | solution.py:115
  84.8 1.8 %collective-permute-start.15 = (bf16[2,4,96,128]{3,2,1,0:T(8,128)(2,1)S(1)}, bf16[2,4,96,128]{3,2,1,0:T(8,128)(2,1)S(1)}, u32[]{:S(2)}, u32[]{:S(2)}) collective-permute-start(bf16[2,4,96,128]{3,2,1,0:T(8,128)(2,1)S(1)} %pad_maximum_fusion.6), channel_id=1, source_target_pairs={{0,2},{1,3},{2,0},{3,1},{4,6},{5,7},{6,4},{7,5},{8,10},{9,11},{10,... | collective-permute-start | bytes 589832 | tf_op jit(solution)/shard_map/ppermute | solution.py:38
  86.7 8.0 %collective-permute-done.15 = bf16[2,4,96,128]{3,2,1,0:T(8,128)(2,1)S(1)} collective-permute-done((bf16[2,4,96,128]{3,2,1,0:T(8,128)(2,1)S(1)}, bf16[2,4,96,128]{3,2,1,0:T(8,128)(2,1)S(1)}, u32[]{:S(2)}, u32[]{:S(2)}) %collective-permute-start.15) | collective-permute-done | bytes 196640 | tf_op jit(solution)/shard_map/ppermute | solution.py:38
  94.7 0.8 all-to-all-done.1.values
  95.4 0.8 sum_copies.1
  96.2 4.0 %all-to-all-start.2 = ((f32[32,16,128]{2,1,0:T(8,128)}), f32[32,16,128]{2,1,0:T(8,128)S(1)}, u32[]{:S(2)}, u32[]{:S(2)}) async-start(f32[32,16,128]{2,1,0:T(8,128)} %sum_copies.1), calls=%async_computation.2 | async-start | bytes 524288 | tf_op jit(solution)/shard_map/all_to_all | solution.py:115
  100.2 0.1 reshape.40
  100.3 0.1 broadcast_in_dim_reshape.3.ids
  100.4 0.1 pad_maximum_fusion
  100.5 10.3 %all-to-all-done.2.vectors = f32[32,16,128]{2,1,0:T(8,128)S(1)} async-done(((f32[32,16,128]{2,1,0:T(8,128)}), f32[32,16,128]{2,1,0:T(8,128)S(1)}, u32[]{:S(2)}, u32[]{:S(2)}) %all-to-all-start.2) | async-done | bytes 262176 | tf_op jit(solution)/shard_map/all_to_all | solution.py:115
  110.8 3.9 %sketches.1 = (f32[16,3,64,64]{3,2,1,0:T(8,128)}, f32[16,32]{1,0:T(8,128)}) custom-call(f32[32,16,128]{2,1,0:T(8,128)S(1)} %all-to-all-done.2.vectors, bf16[32,96,128]{2,1,0:T(8,128)(2,1)S(1)} %bitcast.23, s32[1,128]{1,0:T(1,128)S(1)} %broadcast_in_dim_reshape.3.ids), custom_call_target="tpu_custom_call" | custom-call | tf_op jit(solution)/shard_map/sketches/pallas_call | solution.py:418
  (26 shorter events, 0.4 us)
Async XLA Ops:
  1.6 10.5 %collective-permute-start.1 = (bf16[8,8192]{1,0:T(8,128)(2,1)S(1)}, bf16[8,8192]{1,0:T(8,128)(2,1)S(1)}, u32[]{:S(2)}, u32[]{:S(2)}) collective-permute-start(bf16[8,8192]{1,0:T(8,128)(2,1)S(1)} %pad_maximum_fusion.7), channel_id=1, source_target_pairs={{0,16},{1,17},{2,18},{3,19},{4,20},{5,21},{6,22},{7,23},{8,24},{9,... | collective-permute-start | bytes 393224 | tf_op jit(solution)/shard_map/ppermute | solution.py:47
  5.7 7.1 %collective-permute-start = (bf16[8,8192]{1,0:T(8,128)(2,1)S(1)}, bf16[8,8192]{1,0:T(8,128)(2,1)S(1)}, u32[]{:S(2)}, u32[]{:S(2)}) collective-permute-start(bf16[8,8192]{1,0:T(8,128)(2,1)S(1)} %pad_maximum_fusion.7), channel_id=1, source_target_pairs={{0,8},{1,9},{2,10},{3,11},{4,12},{5,13},{6,14},{7,15},{8,0},{9,1},... | collective-permute-start | bytes 393224 | tf_op jit(solution)/shard_map/ppermute | solution.py:47
  12.1 5.0 %collective-permute-start.2 = (bf16[8,8192]{1,0:T(8,128)(2,1)S(1)}, bf16[8,8192]{1,0:T(8,128)(2,1)S(1)}, u32[]{:S(2)}, u32[]{:S(2)}) collective-permute-start(bf16[8,8192]{1,0:T(8,128)(2,1)S(1)} %collective-permute-done.1), channel_id=1, source_target_pairs={{0,8},{1,9},{2,10},{3,11},{4,12},{5,13},{6,14},{7,15},{8,0},{9,1},... | collective-permute-start | bytes 393224 | tf_op jit(solution)/shard_map/ppermute | solution.py:47
  17.4 7.4 %collective-permute-start.7 = (bf16[16,8192]{1,0:T(8,128)(2,1)S(1)}, bf16[16,8192]{1,0:T(8,128)(2,1)S(1)}, u32[]{:S(2)}, u32[]{:S(2)}) collective-permute-start(bf16[16,8192]{1,0:T(8,128)(2,1)S(1)} %get-tuple-element.12), channel_id=1, source_target_pairs={{0,2},{1,3},{2,0},{3,1},{4,6},{5,7},{6,4},{7,5},{8,10},{9,11},{10,... | collective-permute-start | bytes 786440 | tf_op jit(solution)/shard_map/ppermute | solution.py:38
  19.0 7.7 %collective-permute-start.3 = (bf16[16,8192]{1,0:T(8,128)(2,1)S(1)}, bf16[16,8192]{1,0:T(8,128)(2,1)S(1)}, u32[]{:S(2)}, u32[]{:S(2)}) collective-permute-start(bf16[16,8192]{1,0:T(8,128)(2,1)S(1)} %get-tuple-element.11), channel_id=1, source_target_pairs={{0,4},{1,5},{2,6},{3,7},{4,0},{5,1},{6,2},{7,3},{8,12},{9,13},{10,... | collective-permute-start | bytes 786440 | tf_op jit(solution)/shard_map/ppermute | solution.py:38
  20.7 14.8 %all-to-all-start = ((bf16[32,8,512]{2,1,0:T(8,128)(2,1)}), bf16[32,8,512]{2,1,0:T(8,128)(2,1)S(1)}, u32[]{:S(2)}, u32[]{:S(2)}) async-start(bf16[32,8,512]{2,1,0:T(8,128)(2,1)} %pad_maximum_fusion.5), calls=%async_computation | async-start | bytes 524288 | tf_op jit(solution)/shard_map/all_to_all | solution.py:115
  24.9 16.9 %collective-permute-start.8 = (bf16[32,8192]{1,0:T(8,128)(2,1)S(1)}, bf16[32,8192]{1,0:T(8,128)(2,1)S(1)}, u32[]{:S(2)}, u32[]{:S(2)}) collective-permute-start(bf16[32,8192]{1,0:T(8,128)(2,1)S(1)} %constant_dynamic-update-slice_fusion.2.refs_4_), channel_id=1, source_target_pairs={{0,4},{1,5},{2,6},{3,7},{4,0},{5,1},{6,2},{7,3},{8,12},{9,13},{10,... | collective-permute-start | bytes 1572872 | tf_op jit(solution)/shard_map/ppermute | solution.py:38
  26.8 15.7 %collective-permute-start.4 = (bf16[32,8192]{1,0:T(8,128)(2,1)S(1)}, bf16[32,8192]{1,0:T(8,128)(2,1)S(1)}, u32[]{:S(2)}, u32[]{:S(2)}) collective-permute-start(bf16[32,8192]{1,0:T(8,128)(2,1)S(1)} %constant_dynamic-update-slice_fusion.refs_0_), channel_id=1, source_target_pairs={{0,2},{1,3},{2,0},{3,1},{4,6},{5,7},{6,4},{7,5},{8,10},{9,11},{10,... | collective-permute-start | bytes 1572872 | tf_op jit(solution)/shard_map/ppermute | solution.py:38
  28.3 31.5 %collective-permute-start.9 = (bf16[32,8192]{1,0:T(8,128)(2,1)S(1)}, bf16[32,8192]{1,0:T(8,128)(2,1)S(1)}, u32[]{:S(2)}, u32[]{:S(2)}) collective-permute-start(bf16[32,8192]{1,0:T(8,128)(2,1)S(1)} %constant_dynamic-update-slice_fusion.2.refs_4_), channel_id=1, source_target_pairs={{0,1},{1,0},{2,3},{3,2},{4,5},{5,4},{6,7},{7,6},{8,9},{9,8},{10,11... | collective-permute-start | bytes 1572872 | tf_op jit(solution)/shard_map/ppermute | solution.py:38
  28.3 31.5 %collective-permute-start.5 = (bf16[32,8192]{1,0:T(8,128)(2,1)S(1)}, bf16[32,8192]{1,0:T(8,128)(2,1)}, u32[]{:S(2)}, u32[]{:S(2)}) collective-permute-start(bf16[32,8192]{1,0:T(8,128)(2,1)S(1)} %constant_dynamic-update-slice_fusion.refs_0_), channel_id=1, source_target_pairs={{0,1},{1,0},{2,3},{3,2},{4,5},{5,4},{6,7},{7,6},{8,9},{9,8},{10,11... | collective-permute-start | bytes 1572872 | tf_op jit(solution)/shard_map/ppermute | solution.py:38
  41.8 18.1 %collective-permute-start.10 = (bf16[32,8192]{1,0:T(8,128)(2,1)S(1)}, bf16[32,8192]{1,0:T(8,128)(2,1)}, u32[]{:S(2)}, u32[]{:S(2)}) collective-permute-start(bf16[32,8192]{1,0:T(8,128)(2,1)S(1)} %collective-permute-done.8.refs_5_), channel_id=1, source_target_pairs={{0,1},{1,0},{2,3},{3,2},{4,5},{5,4},{6,7},{7,6},{8,9},{9,8},{10,11... | collective-permute-start | bytes 1572872 | tf_op jit(solution)/shard_map/ppermute | solution.py:38
  42.4 17.4 %collective-permute-start.6 = (bf16[32,8192]{1,0:T(8,128)(2,1)S(1)}, bf16[32,8192]{1,0:T(8,128)(2,1)}, u32[]{:S(2)}, u32[]{:S(2)}) collective-permute-start(bf16[32,8192]{1,0:T(8,128)(2,1)S(1)} %collective-permute-done.4.refs_1_), channel_id=1, source_target_pairs={{0,1},{1,0},{2,3},{3,2},{4,5},{5,4},{6,7},{7,6},{8,9},{9,8},{10,11... | collective-permute-start | bytes 1572872 | tf_op jit(solution)/shard_map/ppermute | solution.py:38
  42.6 4.8 %collective-permute-start.12 = (bf16[96,128]{1,0:T(8,128)(2,1)S(1)}, bf16[96,128]{1,0:T(8,128)(2,1)S(1)}, u32[]{:S(2)}, u32[]{:S(2)}) collective-permute-start(bf16[96,128]{1,0:T(8,128)(2,1)S(1)} %bitcast.35), channel_id=1, source_target_pairs={{0,16},{1,17},{2,18},{3,19},{4,20},{5,21},{6,22},{7,23},{8,24},{9,... | collective-permute-start | bytes 73736 | tf_op jit(solution)/shard_map/ppermute | solution.py:47
  47.4 3.8 %collective-permute-start.11 = (bf16[96,128]{1,0:T(8,128)(2,1)S(1)}, bf16[96,128]{1,0:T(8,128)(2,1)S(1)}, u32[]{:S(2)}, u32[]{:S(2)}) collective-permute-start(bf16[96,128]{1,0:T(8,128)(2,1)S(1)} %bitcast.36), channel_id=1, source_target_pairs={{0,8},{1,9},{2,10},{3,11},{4,12},{5,13},{6,14},{7,15},{8,0},{9,1},... | collective-permute-start | bytes 73736 | tf_op jit(solution)/shard_map/ppermute | solution.py:47
  51.2 3.8 %collective-permute-start.13 = (bf16[96,128]{1,0:T(8,128)(2,1)S(1)}, bf16[96,128]{1,0:T(8,128)(2,1)S(1)}, u32[]{:S(2)}, u32[]{:S(2)}) collective-permute-start(bf16[96,128]{1,0:T(8,128)(2,1)S(1)} %collective-permute-done.12), channel_id=1, source_target_pairs={{0,8},{1,9},{2,10},{3,11},{4,12},{5,13},{6,14},{7,15},{8,0},{9,1},... | collective-permute-start | bytes 73736 | tf_op jit(solution)/shard_map/ppermute | solution.py:47
  55.1 4.7 %collective-permute-start.14 = (bf16[4,96,128]{2,1,0:T(8,128)(2,1)S(1)}, bf16[4,96,128]{2,1,0:T(8,128)(2,1)S(1)}, u32[]{:S(2)}, u32[]{:S(2)}) collective-permute-start(bf16[4,96,128]{2,1,0:T(8,128)(2,1)S(1)} %get-tuple-element.29), channel_id=1, source_target_pairs={{0,4},{1,5},{2,6},{3,7},{4,0},{5,1},{6,2},{7,3},{8,12},{9,13},{10,... | collective-permute-start | bytes 294920 | tf_op jit(solution)/shard_map/ppermute | solution.py:38
  59.8 40.4 %copy-start = (s32[128]{0:T(128)S(1)}, s32[128]{0:T(128)}, u32[]{:S(2)}) copy-start(s32[128]{0:T(128)} %param.17) | copy-start | bytes 1540
  80.2 15.3 %all-to-all-start.1 = ((f32[32,16,128]{2,1,0:T(8,128)}), f32[32,16,128]{2,1,0:T(8,128)S(1)}, u32[]{:S(2)}, u32[]{:S(2)}) async-start(f32[32,16,128]{2,1,0:T(8,128)} %products.1), calls=%async_computation.1 | async-start | bytes 524288 | tf_op jit(solution)/shard_map/all_to_all | solution.py:115
  84.8 9.8 %collective-permute-start.15 = (bf16[2,4,96,128]{3,2,1,0:T(8,128)(2,1)S(1)}, bf16[2,4,96,128]{3,2,1,0:T(8,128)(2,1)S(1)}, u32[]{:S(2)}, u32[]{:S(2)}) collective-permute-start(bf16[2,4,96,128]{3,2,1,0:T(8,128)(2,1)S(1)} %pad_maximum_fusion.6), channel_id=1, source_target_pairs={{0,2},{1,3},{2,0},{3,1},{4,6},{5,7},{6,4},{7,5},{8,10},{9,11},{10,... | collective-permute-start | bytes 589832 | tf_op jit(solution)/shard_map/ppermute | solution.py:38
  96.2 4.3 %collective-permute-start.16 = (bf16[2,2,4,96,128]{4,3,2,1,0:T(8,128)(2,1)S(1)}, bf16[2,2,4,96,128]{4,3,2,1,0:T(8,128)(2,1)S(1)}, u32[]{:S(2)}, u32[]{:S(2)}) collective-permute-start(bf16[2,2,4,96,128]{4,3,2,1,0:T(8,128)(2,1)S(1)} %pad_maximum_fusion.2), channel_id=1, source_target_pairs={{0,1},{1,0},{2,3},{3,2},{4,5},{5,4},{6,7},{7,6},{8,9},{9,8},{10,11... | collective-permute-start | bytes 1179656 | tf_op jit(solution)/shard_map/ppermute | solution.py:38
  96.2 14.6 %all-to-all-start.2 = ((f32[32,16,128]{2,1,0:T(8,128)}), f32[32,16,128]{2,1,0:T(8,128)S(1)}, u32[]{:S(2)}, u32[]{:S(2)}) async-start(f32[32,16,128]{2,1,0:T(8,128)} %sum_copies.1), calls=%async_computation.2 | async-start | bytes 524288 | tf_op jit(solution)/shard_map/all_to_all | solution.py:115

commit v9 on v5

--- a/solution.py
+++ b/solution.py
@@ -38,30 +38,61 @@
     return lax.ppermute(value, "dp", pairs)
 
 
+def partner(value, sizes, axis, bit):
+    size, stride = sizes[axis], strides_of(sizes)[axis]
+    pairs = []
+    for source in range(int(np.prod(sizes))):
+        at = (source // stride) % size
+        pairs.append((source, source + ((at ^ bit) - at) * stride))
+    return lax.ppermute(value, "dp", pairs)
+
+
+def spread_axis(value, sizes, axis):
+    if sizes[axis] == 4:
+        far, near = partner(value, sizes, axis, 2), partner(value, sizes, axis, 1)
+        return [value, near, far, partner(far, sizes, axis, 1)]
+    return [value] + [shift(value, sizes, axis, k) for k in range(1, sizes[axis])]
+
+
+def origin(at, distance, size):
+    if size == 4:
+        return lax.bitwise_xor(at, distance)
+    return lax.rem(at + size - distance, size)
+
+
 def coordinate(me, sizes, axis):
     return lax.rem(lax.div(me, strides_of(sizes)[axis]), sizes[axis])
 
 
-def gather_rows(rows, sizes, order):
+def gather_lines(parts, sizes, others):
+    rows = parts[0].shape[0]
+    both = lax.optimization_barrier(jnp.concatenate(parts, 0))
+    blocks = spread_axis(both, sizes, 0)
+    lines = [
+        jnp.concatenate([block[i * rows : (i + 1) * rows] for block in blocks], 0)
+        for i in range(len(parts))
+    ]
+    made = lax.optimization_barrier((*lines, *others))
+    return made[: len(lines)], made[len(lines) :]
+
+
+def gather_plane(piece, sizes, order):
     backs = [tuple(0 for _ in sizes)]
 
     def moved(axis, amount):
         return [tuple(amount if i == axis else b for i, b in enumerate(back)) for back in backs]
 
-    def received(piece, axis):
-        return [shift(piece, sizes, axis, k) for k in range(1, sizes[axis])]
-
-    piece = lax.optimization_barrier(jnp.concatenate([rows] + received(rows, 0), 0))
     for axis in order[:-1]:
-        piece = jnp.concatenate([piece] + received(piece, axis), 0)
+        others = spread_axis(piece, sizes, axis)[1:]
+        piece = jnp.concatenate([piece] + others, 0)
         backs = sum([moved(axis, k) for k in range(1, sizes[axis])], backs)
     pieces = [(piece, backs)]
     for axis in order[-1:]:
-        others = zip(received(piece, axis), range(1, sizes[axis]))
+        others = zip(spread_axis(piece, sizes, axis)[1:], range(1, sizes[axis]))
         pieces += [(other, moved(axis, k)) for other, k in others]
     core = len(sizes) - 1
     for piece, backs in list(pieces):
-        others = zip(received(piece, core), range(1, sizes[core]))
+        others = zip(spread_axis(piece, sizes, core)[1:], range(1, sizes[core]))
         pieces += [(other, moved(core, k)) for other, k in others]
     return [piece for piece, _ in pieces], [backs for _, backs in pieces]
 
@@ -90,8 +121,8 @@
         for i, back in enumerate(lines):
             slot = 0
             for axis in range(1, len(sizes)):
-                at = coordinate(me, sizes, axis) + sizes[axis] - back[axis]
-                slot = slot * sizes[axis] + lax.rem(at, sizes[axis])
+                at = origin(coordinate(me, sizes, axis), back[axis], sizes[axis])
+                slot = slot * sizes[axis] + at
             start = pl.multiple_of(slot * rows, rows)
             into[pl.ds(start, rows), :] = piece[i * rows : (i + 1) * rows, :]
 
@@ -113,6 +144,8 @@
     steps = tokens.shape[2] // chunk
     total = steps * (hidden_units // block)
 
+    part = block // 2 if block % 32 == 0 else block
+
     def places(step):
         rows = pl.ds(pl.multiple_of(lax.div(step, steps) * block, block), block)
         return rows, pl.ds(pl.multiple_of(lax.rem(step, steps) * chunk, chunk), chunk)
@@ -132,12 +165,15 @@
 
     @pl.loop(0, total)
     def _(step):
-        rows, columns = places(step)
+        _, columns = places(step)
+        first = lax.div(step, steps) * block
         for w in range(3):
             copy(step, w).wait()
-            sums[w, rows, :] += transposed_dot(
-                buffers[lax.rem(step, depth), w], tokens[sides[w], :, columns]
-            )
+            for i in range(0, block, part):
+                rows = pl.ds(pl.multiple_of(first + i, part), part)
+                sums[w, rows, :] += transposed_dot(
+                    buffers[lax.rem(step, depth), w, i : i + part, :], tokens[sides[w], :, columns]
+                )
 
             @pl.when(step + depth < total)
             def _():
@@ -173,7 +209,7 @@
     source = lax.broadcasted_iota(jnp.int32, (count, count), 0)
     target = lax.broadcasted_iota(jnp.int32, (count, count), 1)
     back = lax.rem(lax.div(source, each), size)
-    at = lax.rem(coordinate(lax.axis_index("dp"), sizes, 0) + size - back, size)
+    at = origin(coordinate(lax.axis_index("dp"), sizes, 0), back, size)
     place = lax.div(source, line) * line + at * each + lax.rem(source, each)
     order = (place == target).astype(F32)
     every = jnp.dot(every, order, precision=HIGHEST, preferred_element_type=F32)
@@ -181,6 +217,10 @@
     out[:used] = every.reshape((used,) + out.shape[1:])
     if used < out.shape[0]:
         out[used:] = jnp.zeros_like(out[used:])
+
+
+def small_kernel(megabytes):
+    return pltpu.CompilerParams(vmem_limit_bytes=megabytes * 2**20)
 
 
 def products(in_pieces, out_pieces, backs, sizes, proj, w_gate, w_up, w_down):
@@ -203,7 +243,7 @@
             pltpu.VMEM((2, 3, block, chunk), BF16),
             pltpu.SemaphoreType.DMA((2, 3)),
         ],
-        compiler_params=pltpu.CompilerParams(vmem_limit_bytes=44 * 2**20),
+        compiler_params=pltpu.CompilerParams(vmem_limit_bytes=40 * 2**20),
         cost_estimate=pl.CostEstimate(
             flops=6 * hidden * width * tokens,
             bytes_accessed=6 * hidden * width,
@@ -211,10 +251,6 @@
         ),
         name="products",
     )(*in_pieces, *out_pieces, proj, w_gate, w_up, w_down)
-
-
-def small_kernel(megabytes):
-    return pltpu.CompilerParams(vmem_limit_bytes=megabytes * 2**20)
 
 
 def sum_kernel(values, out):
@@ -320,10 +356,7 @@
     sizes = axis_sizes(count)
     rank = proj_model.shape[1] // 3
     model_cols = proj_model.shape[0]
-    tokens = count * activations.shape[0]
     inner = list(range(1, len(sizes) - 1))
-    in_pieces, in_backs = gather_rows(activations, sizes, inner)
-    out_pieces, out_backs = gather_rows(cotangent, sizes, inner[::-1])
 
     window = max(model_cols, 128)
     proj_m = proj_model.T
@@ -333,16 +366,13 @@
             jnp.where(at == i, proj_m, jnp.zeros_like(proj_m)) for i in range(window // model_cols)
         ]
         proj_m = jnp.concatenate(spots, 1)
-
+    proj = jnp.concatenate([proj_m, proj_hidden.T], 1)
+
+    (in_line, out_line), (proj,) = gather_lines([activations, cotangent], sizes, [proj])
+    in_pieces, in_backs = gather_plane(in_line, sizes, inner)
+    out_pieces, out_backs = gather_plane(out_line, sizes, inner[::-1])
     vectors = products(
-        in_pieces,
-        out_pieces,
-        (in_backs, out_backs),
-        sizes,
-        jnp.concatenate([proj_m, proj_hidden.T], 1),
-        w_gate,
-        w_up,
-        w_down,
+        in_pieces, out_pieces, (in_backs, out_backs), sizes, proj, w_gate, w_up, w_down
     )
     vectors = exchange(sum_copies(exchange(vectors)))
 

time: 101 us -> 102 us (level)
  starting transfers between devices: 22.7 us -> 17 us
  waiting for transfers between devices: 35.8 us -> 41 us
  blocking collectives: 14.3 us -> 16.9 us
    ppermute x14 -> x8, starting transfers between devices: 17.5 us -> 5.53 us  [shift(): return lax.ppermute(value, 'dp', pairs)]
    ppermute x0 -> x3, waiting for transfers between devices: none -> 7.99 us  [partner(): return lax.ppermute(value, 'dp', pairs)]
    ppermute x0 -> x3, starting transfers between devices: none -> 6.29 us  [partner(): return lax.ppermute(value, 'dp', pairs)]
    ppermute x14 -> x8, waiting for transfers between devices: 19.2 us -> 16.3 us  [shift(): return lax.ppermute(value, 'dp', pairs)]
    all_to_all x1, blocking collectives: 14.3 us -> 16.9 us  [exchange(): lax.all_to_all(blocks, 'dp', split_axis=0, concat_axis=0, axis_index_grou...]
    concatenate x5 -> x3, other arithmetic: 3.1 us -> 2.29 us  [the longest x1 1.03 us: on_device(): proj = jnp.concatenate([proj_m, proj_hidden.T], 1)]
  transfers between devices with their start and end apart: 16 -> 13, of which waited for: 9 -> 10; matrix products, arithmetic and copies ran while one was open for 3% -> 1% of each run, Pallas kernels for 2% -> 2%
where the time goes in v9:
time: 102 us
  waiting for transfers between devices  41 us (40%)
  Pallas kernels  23.2 us (23%)
  starting transfers between devices  17 us (17%)
  blocking collectives  16.9 us (17%)
  other arithmetic  2.29 us (2%)
    pallas_call x1, Pallas kernels, products(): pl.pallas_call(functools.partial(product_kernel, backs, sizes, model_cols...  18.2 us
    all_to_all x1, blocking collectives, exchange(): lax.all_to_all(blocks, 'dp', split_axis=0, concat_axis=0, axis_index_grou...  16.9 us
    all_to_all x2, waiting for transfers between devices, exchange(): lax.all_to_all(blocks, 'dp', split_axis=0, concat_axis=0, axis_index_grou...  16.7 us
    ppermute x8, waiting for transfers between devices, shift(): return lax.ppermute(value, 'dp', pairs)  16.3 us
    ppermute x3, waiting for transfers between devices, partner(): return lax.ppermute(value, 'dp', pairs)  7.99 us
    ppermute x3, starting transfers between devices, partner(): return lax.ppermute(value, 'dp', pairs)  6.29 us
    ppermute x8, starting transfers between devices, shift(): return lax.ppermute(value, 'dp', pairs)  5.53 us
    all_to_all x2, starting transfers between devices, exchange(): lax.all_to_all(blocks, 'dp', split_axis=0, concat_axis=0, axis_index_grou...  5.15 us
  transfers between devices with their start and end apart: 13, of which 10 were waited for; matrix products, arithmetic and copies ran while one was open for 1% of the time, Pallas kernels for 2%

profile of v9, /device:TPU:0, one launch (start us, length us, event | category | flops | bytes accessed | tf_op | source)
XLA Modules:
  0.0 101.5 jit_solution(5805662535660266746)
XLA Ops:
  0.6 0.9 pad_maximum_fusion.3
  1.6 4.1 %collective-permute-start.1 = (bf16[8,8192]{1,0:T(8,128)(2,1)S(1)}, bf16[8,8192]{1,0:T(8,128)(2,1)S(1)}, u32[]{:S(2)}, u32[]{:S(2)}) collective-permute-start(bf16[8,8192]{1,0:T(8,128)(2,1)S(1)} %pad_maximum_fusion.3), channel_id=1, source_target_pairs={{0,16},{1,17},{2,18},{3,19},{4,20},{5,21},{6,22},{7,23},{8,24},{9,... | collective-permute-start | bytes 393224 | tf_op jit(solution)/shard_map/ppermute | solution.py:47
  5.7 1.6 %collective-permute-start = (bf16[8,8192]{1,0:T(8,128)(2,1)S(1)}, bf16[8,8192]{1,0:T(8,128)(2,1)S(1)}, u32[]{:S(2)}, u32[]{:S(2)}) collective-permute-start(bf16[8,8192]{1,0:T(8,128)(2,1)S(1)} %pad_maximum_fusion.3), channel_id=1, source_target_pairs={{0,8},{1,9},{2,10},{3,11},{4,12},{5,13},{6,14},{7,15},{8,0},{9,1},... | collective-permute-start | bytes 393224 | tf_op jit(solution)/shard_map/ppermute | solution.py:47
  7.3 1.0 %pad_maximum_fusion.refs_8_ = bf16[192,1152]{1,0:T(8,128)(2,1)S(1)} fusion(bf16[192,896]{1,0:T(8,128)(2,1)} %bitcast.5, bf16[192,256]{1,0:T(8,128)(2,1)} %bitcast.6), kind=kLoop, calls=%fused_computation | loop fusion | flops 884736 | bytes 884736 | tf_op jit(solution)/shard_map/concatenate | solution.py:369
  8.3 3.7 %collective-permute-done.1 = bf16[8,8192]{1,0:T(8,128)(2,1)S(1)} collective-permute-done((bf16[8,8192]{1,0:T(8,128)(2,1)S(1)}, bf16[8,8192]{1,0:T(8,128)(2,1)S(1)}, u32[]{:S(2)}, u32[]{:S(2)}) %collective-permute-start.1) | collective-permute-done | bytes 131104 | tf_op jit(solution)/shard_map/ppermute | solution.py:47
  12.1 0.6 collective-permute-start.2
  12.8 0.0 collective-permute-done
  12.8 4.2 %collective-permute-done.2 = bf16[8,8192]{1,0:T(8,128)(2,1)S(1)} collective-permute-done((bf16[8,8192]{1,0:T(8,128)(2,1)S(1)}, bf16[8,8192]{1,0:T(8,128)(2,1)S(1)}, u32[]{:S(2)}, u32[]{:S(2)}) %collective-permute-start.2) | collective-permute-done | bytes 131104 | tf_op jit(solution)/shard_map/ppermute | solution.py:47
  17.1 0.3 pad_maximum_fusion.1
  17.4 1.6 %collective-permute-start.7 = (bf16[16,8192]{1,0:T(8,128)(2,1)S(1)}, bf16[16,8192]{1,0:T(8,128)(2,1)S(1)}, u32[]{:S(2)}, u32[]{:S(2)}) collective-permute-start(bf16[16,8192]{1,0:T(8,128)(2,1)S(1)} %get-tuple-element.10), channel_id=1, source_target_pairs={{0,2},{1,3},{2,0},{3,1},{4,6},{5,7},{6,4},{7,5},{8,10},{9,11},{10,... | collective-permute-start | bytes 786440 | tf_op jit(solution)/shard_map/ppermute | solution.py:38
  19.1 1.6 %collective-permute-start.3 = (bf16[16,8192]{1,0:T(8,128)(2,1)S(1)}, bf16[16,8192]{1,0:T(8,128)(2,1)S(1)}, u32[]{:S(2)}, u32[]{:S(2)}) collective-permute-start(bf16[16,8192]{1,0:T(8,128)(2,1)S(1)} %get-tuple-element.9), channel_id=1, source_target_pairs={{0,4},{1,5},{2,6},{3,7},{4,0},{5,1},{6,2},{7,3},{8,12},{9,13},{10,... | collective-permute-start | bytes 786440 | tf_op jit(solution)/shard_map/ppermute | solution.py:38
  20.7 3.2 %collective-permute-done.7 = bf16[16,8192]{1,0:T(8,128)(2,1)S(1)} collective-permute-done((bf16[16,8192]{1,0:T(8,128)(2,1)S(1)}, bf16[16,8192]{1,0:T(8,128)(2,1)S(1)}, u32[]{:S(2)}, u32[]{:S(2)}) %collective-permute-start.7) | collective-permute-done | bytes 262176 | tf_op jit(solution)/shard_map/ppermute | solution.py:38
  23.9 1.6 %collective-permute-start.8 = (bf16[32,8192]{1,0:T(8,128)(2,1)S(1)}, bf16[32,8192]{1,0:T(8,128)(2,1)S(1)}, u32[]{:S(2)}, u32[]{:S(2)}) collective-permute-start(bf16[32,8192]{1,0:T(8,128)(2,1)S(1)} %constant_dynamic-update-slice_fusion.2.refs_4_), channel_id=1, source_target_pairs={{0,4},{1,5},{2,6},{3,7},{4,0},{5,1},{6,2},{7,3},{8,12},{9,13},{10,... | collective-permute-start | bytes 1572872 | tf_op jit(solution)/shard_map/ppermute | solution.py:38
  25.5 2.4 %collective-permute-done.3 = bf16[16,8192]{1,0:T(8,128)(2,1)S(1)} collective-permute-done((bf16[16,8192]{1,0:T(8,128)(2,1)S(1)}, bf16[16,8192]{1,0:T(8,128)(2,1)S(1)}, u32[]{:S(2)}, u32[]{:S(2)}) %collective-permute-start.3) | collective-permute-done | bytes 262176 | tf_op jit(solution)/shard_map/ppermute | solution.py:38
  27.9 0.0 copy-start.2
  27.9 0.0 copy-start
  27.9 0.0 copy-start.1
  28.0 0.1 collective-permute-start.4
  28.0 0.1 collective-permute-start.9
  28.1 0.5 collective-permute-start.5
  28.6 8.1 %collective-permute-done.8.refs_5_ = bf16[32,8192]{1,0:T(8,128)(2,1)S(1)} collective-permute-done((bf16[32,8192]{1,0:T(8,128)(2,1)S(1)}, bf16[32,8192]{1,0:T(8,128)(2,1)S(1)}, u32[]{:S(2)}, u32[]{:S(2)}) %collective-permute-start.8) | collective-permute-done | bytes 524320 | tf_op jit(solution)/shard_map/ppermute | solution.py:38
  36.8 0.0 collective-permute-start.10
  36.8 0.4 collective-permute-done.4.refs_1_
  37.2 0.1 collective-permute-start.6
  37.3 0.0 collective-permute-done.9.refs_6_
  37.3 0.0 collective-permute-done.5.refs_2_
  37.3 1.4 %collective-permute-done.10.refs_7_ = bf16[32,8192]{1,0:T(8,128)(2,1)S(1)} collective-permute-done((bf16[32,8192]{1,0:T(8,128)(2,1)S(1)}, bf16[32,8192]{1,0:T(8,128)(2,1)S(1)}, u32[]{:S(2)}, u32[]{:S(2)}) %collective-permute-start.10) | collective-permute-done | bytes 524320 | tf_op jit(solution)/shard_map/ppermute | solution.py:38
  38.7 0.7 collective-permute-done.6.refs_3_
  39.4 18.2 %products.1 = f32[32,16,128]{2,1,0:T(8,128)S(1)} custom-call(bf16[32,8192]{1,0:T(8,128)(2,1)S(1)} %constant_dynamic-update-slice_fusion.refs_0_, bf16[32,8192]{1,0:T(8,128)(2,1)S(1)} %collective-permute-done.4.refs_1_, bf16[32,8192]{1,0:T(8,128)(2,1)S(1)} %collective-permute-done.5.refs_2_, bf16[32,8192]{1,0:T(8,128)(2,1)S(1)} %collective-permute-done.6.refs_3_, ...), custom_call_target="tpu_custom_call" | custom-call | flops 5637144576 | bytes 44040192 | tf_op jit(solution)/shard_map/products/pallas_call | solution.py:234
  57.6 16.9 %all_to_all.15.values = f32[32,16,128]{2,1,0:T(8,128)S(1)} all-to-all(f32[32,16,128]{2,1,0:T(8,128)S(1)} %products.1), channel_id=1, replica_groups=mesh['groups'=1,'dp'=32] {'dp'}, dimensions={0} | all-to-all | bytes 524288 | tf_op jit(solution)/shard_map/all_to_all | solution.py:106
  74.5 0.8 sum_copies.1
  75.2 2.6 %all-to-all-start.1 = ((f32[32,16,128]{2,1,0:T(8,128)}), f32[32,16,128]{2,1,0:T(8,128)S(1)}, u32[]{:S(2)}, u32[]{:S(2)}) async-start(f32[32,16,128]{2,1,0:T(8,128)} %sum_copies.1), calls=%async_computation.1 | async-start | bytes 524288 | tf_op jit(solution)/shard_map/all_to_all | solution.py:106
  77.8 0.0 copy-done.2
  77.8 0.1 reshape.7
  78.0 0.1 broadcast_in_dim_reshape.3.ids
  78.1 10.4 %all-to-all-done.1.vectors = f32[32,16,128]{2,1,0:T(8,128)S(1)} async-done(((f32[32,16,128]{2,1,0:T(8,128)}), f32[32,16,128]{2,1,0:T(8,128)S(1)}, u32[]{:S(2)}, u32[]{:S(2)}) %all-to-all-start.1) | async-done | bytes 262176 | tf_op jit(solution)/shard_map/all_to_all | solution.py:106
  88.4 0.0 copy-done
  88.4 0.0 copy-done.1
  88.4 1.5 %target_products.1 = f32[32,8,128]{2,1,0:T(8,128)} custom-call(f32[32,16,128]{2,1,0:T(8,128)S(1)} %all-to-all-done.1.vectors, s32[1,128]{1,0:T(1,128)S(1)} %broadcast_in_dim_reshape.3.ids, bf16[8,3,64,64]{3,2,1,0:T(8,128)(2,1)S(1)} %copy-done, s32[1,8]{1,0:T(1,128)S(1)} %bitcast.4), custom_call_target="tpu_custom_call" | custom-call | tf_op jit(solution)/shard_map/target_products/pallas_call | solution.py:380
  90.0 2.6 %all-to-all-start.2 = ((f32[32,8,128]{2,1,0:T(8,128)}), f32[32,8,128]{2,1,0:T(8,128)S(1)}, u32[]{:S(2)}, u32[]{:S(2)}) async-start(f32[32,8,128]{2,1,0:T(8,128)} %target_products.1), calls=%async_computation.2 | async-start | bytes 262144 | tf_op jit(solution)/shard_map/all_to_all | solution.py:106
  92.5 1.9 %sketches.1 = (f32[16,3,64,64]{3,2,1,0:T(8,128)}, f32[16,128]{1,0:T(8,128)S(1)}) custom-call(f32[32,16,128]{2,1,0:T(8,128)S(1)} %all-to-all-done.1.vectors, s32[1,128]{1,0:T(1,128)S(1)} %broadcast_in_dim_reshape.3.ids), custom_call_target="tpu_custom_call" | custom-call | tf_op jit(solution)/shard_map/sketches/pallas_call | solution.py:390
  94.4 6.3 %all-to-all-done.2.parts = f32[32,8,128]{2,1,0:T(8,128)S(1)} async-done(((f32[32,8,128]{2,1,0:T(8,128)}), f32[32,8,128]{2,1,0:T(8,128)S(1)}, u32[]{:S(2)}, u32[]{:S(2)}) %all-to-all-start.2) | async-done | bytes 131104 | tf_op jit(solution)/shard_map/all_to_all | solution.py:106
  100.8 0.8 scores.1
  (9 shorter events, 0.3 us)
Async XLA Ops:
  1.6 10.5 %collective-permute-start.1 = (bf16[8,8192]{1,0:T(8,128)(2,1)S(1)}, bf16[8,8192]{1,0:T(8,128)(2,1)S(1)}, u32[]{:S(2)}, u32[]{:S(2)}) collective-permute-start(bf16[8,8192]{1,0:T(8,128)(2,1)S(1)} %pad_maximum_fusion.3), channel_id=1, source_target_pairs={{0,16},{1,17},{2,18},{3,19},{4,20},{5,21},{6,22},{7,23},{8,24},{9,... | collective-permute-start | bytes 393224 | tf_op jit(solution)/shard_map/ppermute | solution.py:47
  5.7 7.1 %collective-permute-start = (bf16[8,8192]{1,0:T(8,128)(2,1)S(1)}, bf16[8,8192]{1,0:T(8,128)(2,1)S(1)}, u32[]{:S(2)}, u32[]{:S(2)}) collective-permute-start(bf16[8,8192]{1,0:T(8,128)(2,1)S(1)} %pad_maximum_fusion.3), channel_id=1, source_target_pairs={{0,8},{1,9},{2,10},{3,11},{4,12},{5,13},{6,14},{7,15},{8,0},{9,1},... | collective-permute-start | bytes 393224 | tf_op jit(solution)/shard_map/ppermute | solution.py:47
  12.1 5.0 %collective-permute-start.2 = (bf16[8,8192]{1,0:T(8,128)(2,1)S(1)}, bf16[8,8192]{1,0:T(8,128)(2,1)S(1)}, u32[]{:S(2)}, u32[]{:S(2)}) collective-permute-start(bf16[8,8192]{1,0:T(8,128)(2,1)S(1)} %collective-permute-done.1), channel_id=1, source_target_pairs={{0,8},{1,9},{2,10},{3,11},{4,12},{5,13},{6,14},{7,15},{8,0},{9,1},... | collective-permute-start | bytes 393224 | tf_op jit(solution)/shard_map/ppermute | solution.py:47
  17.4 6.4 %collective-permute-start.7 = (bf16[16,8192]{1,0:T(8,128)(2,1)S(1)}, bf16[16,8192]{1,0:T(8,128)(2,1)S(1)}, u32[]{:S(2)}, u32[]{:S(2)}) collective-permute-start(bf16[16,8192]{1,0:T(8,128)(2,1)S(1)} %get-tuple-element.10), channel_id=1, source_target_pairs={{0,2},{1,3},{2,0},{3,1},{4,6},{5,7},{6,4},{7,5},{8,10},{9,11},{10,... | collective-permute-start | bytes 786440 | tf_op jit(solution)/shard_map/ppermute | solution.py:38
  19.1 8.8 %collective-permute-start.3 = (bf16[16,8192]{1,0:T(8,128)(2,1)S(1)}, bf16[16,8192]{1,0:T(8,128)(2,1)S(1)}, u32[]{:S(2)}, u32[]{:S(2)}) collective-permute-start(bf16[16,8192]{1,0:T(8,128)(2,1)S(1)} %get-tuple-element.9), channel_id=1, source_target_pairs={{0,4},{1,5},{2,6},{3,7},{4,0},{5,1},{6,2},{7,3},{8,12},{9,13},{10,... | collective-permute-start | bytes 786440 | tf_op jit(solution)/shard_map/ppermute | solution.py:38
  23.9 12.8 %collective-permute-start.8 = (bf16[32,8192]{1,0:T(8,128)(2,1)S(1)}, bf16[32,8192]{1,0:T(8,128)(2,1)S(1)}, u32[]{:S(2)}, u32[]{:S(2)}) collective-permute-start(bf16[32,8192]{1,0:T(8,128)(2,1)S(1)} %constant_dynamic-update-slice_fusion.2.refs_4_), channel_id=1, source_target_pairs={{0,4},{1,5},{2,6},{3,7},{4,0},{5,1},{6,2},{7,3},{8,12},{9,13},{10,... | collective-permute-start | bytes 1572872 | tf_op jit(solution)/shard_map/ppermute | solution.py:38
  27.9 49.9 %copy-start.2 = (s32[128]{0:T(128)S(1)}, s32[128]{0:T(128)}, u32[]{:S(2)}) copy-start(s32[128]{0:T(128)} %param.17) | copy-start | bytes 1540
  27.9 60.5 %copy-start = (bf16[8,3,64,64]{3,2,1,0:T(8,128)(2,1)S(1)}, bf16[8,3,64,64]{3,2,1,0:T(8,128)(2,1)}, u32[]{:S(2)}) copy-start(bf16[8,3,64,64]{3,2,1,0:T(8,128)(2,1)} %targets.1) | copy-start | bytes 589828
  27.9 60.5 %copy-start.1 = (s32[8]{0:T(128)S(1)}, s32[8]{0:T(128)}, u32[]{:S(2)}) copy-start(s32[8]{0:T(128)} %param.19) | copy-start | bytes 100
  28.0 9.2 %collective-permute-start.4 = (bf16[32,8192]{1,0:T(8,128)(2,1)S(1)}, bf16[32,8192]{1,0:T(8,128)(2,1)S(1)}, u32[]{:S(2)}, u32[]{:S(2)}) collective-permute-start(bf16[32,8192]{1,0:T(8,128)(2,1)S(1)} %constant_dynamic-update-slice_fusion.refs_0_), channel_id=1, source_target_pairs={{0,2},{1,3},{2,0},{3,1},{4,6},{5,7},{6,4},{7,5},{8,10},{9,11},{10,... | collective-permute-start | bytes 1572872 | tf_op jit(solution)/shard_map/ppermute | solution.py:38
  28.0 9.2 %collective-permute-start.9 = (bf16[32,8192]{1,0:T(8,128)(2,1)S(1)}, bf16[32,8192]{1,0:T(8,128)(2,1)S(1)}, u32[]{:S(2)}, u32[]{:S(2)}) collective-permute-start(bf16[32,8192]{1,0:T(8,128)(2,1)S(1)} %constant_dynamic-update-slice_fusion.2.refs_4_), channel_id=1, source_target_pairs={{0,1},{1,0},{2,3},{3,2},{4,5},{5,4},{6,7},{7,6},{8,9},{9,8},{10,11... | collective-permute-start | bytes 1572872 | tf_op jit(solution)/shard_map/ppermute | solution.py:38
  28.1 9.2 %collective-permute-start.5 = (bf16[32,8192]{1,0:T(8,128)(2,1)S(1)}, bf16[32,8192]{1,0:T(8,128)(2,1)S(1)}, u32[]{:S(2)}, u32[]{:S(2)}) collective-permute-start(bf16[32,8192]{1,0:T(8,128)(2,1)S(1)} %constant_dynamic-update-slice_fusion.refs_0_), channel_id=1, source_target_pairs={{0,1},{1,0},{2,3},{3,2},{4,5},{5,4},{6,7},{7,6},{8,9},{9,8},{10,11... | collective-permute-start | bytes 1572872 | tf_op jit(solution)/shard_map/ppermute | solution.py:38
  36.8 1.9 %collective-permute-start.10 = (bf16[32,8192]{1,0:T(8,128)(2,1)S(1)}, bf16[32,8192]{1,0:T(8,128)(2,1)S(1)}, u32[]{:S(2)}, u32[]{:S(2)}) collective-permute-start(bf16[32,8192]{1,0:T(8,128)(2,1)S(1)} %collective-permute-done.8.refs_5_), channel_id=1, source_target_pairs={{0,1},{1,0},{2,3},{3,2},{4,5},{5,4},{6,7},{7,6},{8,9},{9,8},{10,11... | collective-permute-start | bytes 1572872 | tf_op jit(solution)/shard_map/ppermute | solution.py:38
  37.2 2.2 %collective-permute-start.6 = (bf16[32,8192]{1,0:T(8,128)(2,1)S(1)}, bf16[32,8192]{1,0:T(8,128)(2,1)S(1)}, u32[]{:S(2)}, u32[]{:S(2)}) collective-permute-start(bf16[32,8192]{1,0:T(8,128)(2,1)S(1)} %collective-permute-done.4.refs_1_), channel_id=1, source_target_pairs={{0,1},{1,0},{2,3},{3,2},{4,5},{5,4},{6,7},{7,6},{8,9},{9,8},{10,11... | collective-permute-start | bytes 1572872 | tf_op jit(solution)/shard_map/ppermute | solution.py:38
  75.2 13.2 %all-to-all-start.1 = ((f32[32,16,128]{2,1,0:T(8,128)}), f32[32,16,128]{2,1,0:T(8,128)S(1)}, u32[]{:S(2)}, u32[]{:S(2)}) async-start(f32[32,16,128]{2,1,0:T(8,128)} %sum_copies.1), calls=%async_computation.1 | async-start | bytes 524288 | tf_op jit(solution)/shard_map/all_to_all | solution.py:106
  90.0 10.8 %all-to-all-start.2 = ((f32[32,8,128]{2,1,0:T(8,128)}), f32[32,8,128]{2,1,0:T(8,128)S(1)}, u32[]{:S(2)}, u32[]{:S(2)}) async-start(f32[32,8,128]{2,1,0:T(8,128)} %target_products.1), calls=%async_computation.2 | async-start | bytes 262144 | tf_op jit(solution)/shard_map/all_to_all | solution.py:106

commit v10 on v5

--- a/solution.py
+++ b/solution.py
@@ -42,7 +42,7 @@
     return lax.rem(lax.div(me, strides_of(sizes)[axis]), sizes[axis])
 
 
-def gather_rows(rows, sizes, order):
+def gather_rows(rows, own, made, sizes, order):
     backs = [tuple(0 for _ in sizes)]
 
     def moved(axis, amount):
@@ -51,7 +51,8 @@
     def received(piece, axis):
         return [shift(piece, sizes, axis, k) for k in range(1, sizes[axis])]
 
-    piece = lax.optimization_barrier(jnp.concatenate([rows] + received(rows, 0), 0))
+    piece = jnp.concatenate([own] + received(rows, 0), 0)
+    piece, *made = lax.optimization_barrier((piece, *made))
     for axis in order[:-1]:
         piece = jnp.concatenate([piece] + received(piece, axis), 0)
         backs = sum([moved(axis, k) for k in range(1, sizes[axis])], backs)
@@ -63,7 +64,7 @@
     for piece, backs in list(pieces):
         others = zip(received(piece, core), range(1, sizes[core]))
         pieces += [(other, moved(core, k)) for other, k in others]
-    return [piece for piece, _ in pieces], [backs for _, backs in pieces]
+    return [piece for piece, _ in pieces], [backs for _, backs in pieces], made
 
 
 def slot_order(per_token, sizes):
@@ -190,7 +191,7 @@
     model_cols = width // count
     chunk = min(width, 2048)
     block = hidden // 2 if hidden % 32 == 0 and hidden > 256 else hidden
-    height = 8 * -(-2 * proj.shape[0] // (8 * count))
+    height = 16 * -(-2 * proj.shape[0] // (16 * count))
     return pl.pallas_call(
         functools.partial(product_kernel, backs, sizes, model_cols),
         out_shape=jax.ShapeDtypeStruct((count, height, tokens), F32),
@@ -222,23 +223,18 @@
     for i in range(1, values.shape[0]):
         total += values[i]
     for i in range(out.shape[0]):
-        out[i] = total
+        out[i] = total.astype(BF16)
 
 
 def sum_copies(values):
     return pl.pallas_call(
         sum_kernel,
-        out_shape=jax.ShapeDtypeStruct(values.shape, F32),
+        out_shape=jax.ShapeDtypeStruct(values.shape, BF16),
         in_specs=[VMEM],
         out_specs=VMEM,
         compiler_params=small_kernel(8),
         name="sum_copies",
     )(values)
-
-
-def halves(value):
-    high = value.astype(BF16)
-    return high, (value - high.astype(F32)).astype(BF16)
 
 
 def rows_of(vectors, rank):
@@ -258,11 +254,9 @@
     for k in range(3):
         left = every[k * rank : (k + 1) * rank]
         target = targets[:, k].reshape(examples * rank, rank)
-        turned = sum(
-            jnp.dot(target, part, preferred_element_type=F32)
-            for part in halves(every[(3 + k) * rank : (4 + k) * rank])
-        )
-        total += jnp.sum(turned.reshape(examples, rank, tokens) * left[None], 1)
+        right = every[(3 + k) * rank : (4 + k) * rank]
+        turned = jnp.dot(target, right, preferred_element_type=F32)
+        total += jnp.sum(turned.reshape(examples, rank, tokens) * left.astype(F32)[None], 1)
     domain = lax.broadcasted_iota(jnp.int32, (DOMAINS, examples), 0)
     domains = (domains[...] == domain).astype(F32)
     total = jnp.dot(domains, total, precision=HIGHEST, preferred_element_type=F32)
@@ -278,13 +272,11 @@
 def sketch_kernel(rank, vectors, ids, sketches, norms):
     tokens = ids.shape[1]
     every = rows_of(vectors, rank)
-    masks = jnp.concatenate([onehot_of(ids[...], tokens).astype(BF16)] * 3, 1)
+    masks = onehot_of(ids[...], tokens).astype(BF16)
     norm = jnp.zeros((SEQS, 1), F32)
     for k in range(3):
-        left_high, left_low = halves(every[k * rank : (k + 1) * rank])
-        right_high, right_low = halves(every[(3 + k) * rank : (4 + k) * rank])
-        left = jnp.concatenate([left_high, left_high, left_low], 1)
-        right = jnp.concatenate([right_high, right_low, right_high], 1)
+        left = every[k * rank : (k + 1) * rank]
+        right = every[(3 + k) * rank : (4 + k) * rank]
         rows = jnp.concatenate([left * masks[s : s + 1, :] for s in range(SEQS)], 0)
         sketch = transposed_dot(rows, right).reshape(SEQS, rank, rank)
         sketches[:, k] = sketch
@@ -321,10 +313,6 @@
     rank = proj_model.shape[1] // 3
     model_cols = proj_model.shape[0]
     tokens = count * activations.shape[0]
-    inner = list(range(1, len(sizes) - 1))
-    in_pieces, in_backs = gather_rows(activations, sizes, inner)
-    out_pieces, out_backs = gather_rows(cotangent, sizes, inner[::-1])
-
     window = max(model_cols, 128)
     proj_m = proj_model.T
     if window > model_cols:
@@ -334,15 +322,16 @@
         ]
         proj_m = jnp.concatenate(spots, 1)
 
+    proj = jnp.concatenate([proj_m, proj_hidden.T], 1)
+
+    inner = list(range(1, len(sizes) - 1))
+    each = activations.shape[0]
+    both = lax.optimization_barrier(jnp.concatenate([activations, cotangent], 0))
+    in_pieces, in_backs, (proj,) = gather_rows(activations, both[:each], [proj], sizes, inner)
+    out_pieces, out_backs, _ = gather_rows(cotangent, both[each:], [], sizes, inner[::-1])
+
     vectors = products(
-        in_pieces,
-        out_pieces,
-        (in_backs, out_backs),
-        sizes,
-        jnp.concatenate([proj_m, proj_hidden.T], 1),
-        w_gate,
-        w_up,
-        w_down,
+        in_pieces, out_pieces, (in_backs, out_backs), sizes, proj, w_gate, w_up, w_down
     )
     vectors = exchange(sum_copies(exchange(vectors)))
 

time: 101 us -> 98 us (0.970)
  waiting for transfers between devices: 35.8 us -> 34.5 us
    all_to_all x2, waiting for transfers between devices: 16.7 us -> 14.7 us  [exchange(): lax.all_to_all(blocks, 'dp', split_axis=0, concat_axis=0, axis_index_grou...]
  transfers between devices with their start and end apart: 16 -> 16, of which waited for: 9 -> 10; matrix products, arithmetic and copies ran while one was open for 3% -> 2% of each run, Pallas kernels for 2% -> 2%
where the time goes in v10:
time: 98 us; the launch traced here: 97.7 us
  waiting for transfers between devices  34.5 us (35%)
  starting transfers between devices  22.6 us (23%)
  Pallas kernels  22.6 us (23%)
  blocking collectives  14.5 us (15%)
  other arithmetic  2.32 us (2%)
    ppermute x14, waiting for transfers between devices, shift(): return lax.ppermute(value, 'dp', pairs)  19.8 us
    pallas_call x1, Pallas kernels, products(): pl.pallas_call(functools.partial(product_kernel, backs, sizes, model_cols...  18.3 us
    ppermute x14, starting transfers between devices, shift(): return lax.ppermute(value, 'dp', pairs)  17.5 us
    all_to_all x2, waiting for transfers between devices, exchange(): lax.all_to_all(blocks, 'dp', split_axis=0, concat_axis=0, axis_index_grou...  14.7 us
    all_to_all x1, blocking collectives, exchange(): lax.all_to_all(blocks, 'dp', split_axis=0, concat_axis=0, axis_index_grou...  14.5 us
    all_to_all x2, starting transfers between devices, exchange(): lax.all_to_all(blocks, 'dp', split_axis=0, concat_axis=0, axis_index_grou...  5.14 us
  transfers between devices with their start and end apart: 16, of which 10 were waited for; matrix products, arithmetic and copies ran while one was open for 2% of the time, Pallas kernels for 2%

profile of v10, /device:TPU:0, one launch (start us, length us, event | category | flops | bytes accessed | tf_op | source)
XLA Modules:
  0.0 97.7 jit_solution(499229029595031558)
XLA Ops:
  0.6 3.1 %collective-permute-start = (bf16[4,8192]{1,0:T(4,128)(2,1)}, bf16[4,8192]{1,0:T(4,128)(2,1)S(1)}, u32[]{:S(2)}, u32[]{:S(2)}) collective-permute-start(bf16[4,8192]{1,0:T(4,128)(2,1)} %param.10), channel_id=1, source_target_pairs={{0,8},{1,9},{2,10},{3,11},{4,12},{5,13},{6,14},{7,15},{8,16},{9,17... | collective-permute-start | bytes 196616 | tf_op jit(solution)/shard_map/ppermute | solution.py:38
  3.7 2.6 %collective-permute-start.1 = (bf16[4,8192]{1,0:T(4,128)(2,1)}, bf16[4,8192]{1,0:T(4,128)(2,1)S(1)}, u32[]{:S(2)}, u32[]{:S(2)}) collective-permute-start(bf16[4,8192]{1,0:T(4,128)(2,1)} %param.10), channel_id=1, source_target_pairs={{0,16},{1,17},{2,18},{3,19},{4,20},{5,21},{6,22},{7,23},{8,24},{9,... | collective-permute-start | bytes 196616 | tf_op jit(solution)/shard_map/ppermute | solution.py:38
  6.3 1.3 %collective-permute-start.2 = (bf16[4,8192]{1,0:T(4,128)(2,1)}, bf16[4,8192]{1,0:T(4,128)(2,1)S(1)}, u32[]{:S(2)}, u32[]{:S(2)}) collective-permute-start(bf16[4,8192]{1,0:T(4,128)(2,1)} %param.10), channel_id=1, source_target_pairs={{0,24},{1,25},{2,26},{3,27},{4,28},{5,29},{6,30},{7,31},{8,0},{9,1... | collective-permute-start | bytes 196616 | tf_op jit(solution)/shard_map/ppermute | solution.py:38
  7.6 0.7 collective-permute-start.7
  8.3 0.3 collective-permute-start.8
  8.7 0.9 pad_maximum_fusion.4
  9.7 0.0 collective-permute-done
  9.7 2.9 %collective-permute-start.9 = (bf16[4,8192]{1,0:T(4,128)(2,1)}, bf16[4,8192]{1,0:T(4,128)(2,1)S(1)}, u32[]{:S(2)}, u32[]{:S(2)}) collective-permute-start(bf16[4,8192]{1,0:T(4,128)(2,1)} %param.11), channel_id=1, source_target_pairs={{0,24},{1,25},{2,26},{3,27},{4,28},{5,29},{6,30},{7,31},{8,0},{9,1... | collective-permute-start | bytes 196616 | tf_op jit(solution)/shard_map/ppermute | solution.py:38
  12.6 1.0 %pad_maximum_fusion.1.refs_8_ = bf16[192,1152]{1,0:T(8,128)(2,1)S(1)} fusion(bf16[192,896]{1,0:T(8,128)(2,1)} %bitcast.5, bf16[192,256]{1,0:T(8,128)(2,1)} %bitcast.6), kind=kLoop, calls=%fused_computation.1 | loop fusion | flops 884736 | bytes 884736 | tf_op jit(solution)/shard_map/concatenate | solution.py:325
  13.6 0.0 collective-permute-done.1
  13.6 0.0 collective-permute-done.2
  13.6 0.9 collective-permute-done.7
  14.5 2.2 %collective-permute-done.8 = bf16[4,8192]{1,0:T(4,128)(2,1)S(1)} collective-permute-done((bf16[4,8192]{1,0:T(4,128)(2,1)}, bf16[4,8192]{1,0:T(4,128)(2,1)S(1)}, u32[]{:S(2)}, u32[]{:S(2)}) %collective-permute-start.8) | collective-permute-done | bytes 65568 | tf_op jit(solution)/shard_map/ppermute | solution.py:38
  16.7 0.2 collective-permute-done.9
  16.8 0.3 pad_maximum_fusion.2
  17.1 1.7 %collective-permute-start.3 = (bf16[16,8192]{1,0:T(8,128)(2,1)S(1)}, bf16[16,8192]{1,0:T(8,128)(2,1)S(1)}, u32[]{:S(2)}, u32[]{:S(2)}) collective-permute-start(bf16[16,8192]{1,0:T(8,128)(2,1)S(1)} %get-tuple-element.8), channel_id=1, source_target_pairs={{0,4},{1,5},{2,6},{3,7},{4,0},{5,1},{6,2},{7,3},{8,12},{9,13},{10,... | collective-permute-start | bytes 786440 | tf_op jit(solution)/shard_map/ppermute | solution.py:38
  18.8 1.6 %collective-permute-start.10 = (bf16[16,8192]{1,0:T(8,128)(2,1)S(1)}, bf16[16,8192]{1,0:T(8,128)(2,1)S(1)}, u32[]{:S(2)}, u32[]{:S(2)}) collective-permute-start(bf16[16,8192]{1,0:T(8,128)(2,1)S(1)} %get-tuple-element.17), channel_id=1, source_target_pairs={{0,2},{1,3},{2,0},{3,1},{4,6},{5,7},{6,4},{7,5},{8,10},{9,11},{10,... | collective-permute-start | bytes 786440 | tf_op jit(solution)/shard_map/ppermute | solution.py:38
  20.4 4.7 %collective-permute-done.3 = bf16[16,8192]{1,0:T(8,128)(2,1)S(1)} collective-permute-done((bf16[16,8192]{1,0:T(8,128)(2,1)S(1)}, bf16[16,8192]{1,0:T(8,128)(2,1)S(1)}, u32[]{:S(2)}, u32[]{:S(2)}) %collective-permute-start.3) | collective-permute-done | bytes 262176 | tf_op jit(solution)/shard_map/ppermute | solution.py:38
  25.1 1.2 %collective-permute-start.4 = (bf16[32,8192]{1,0:T(8,128)(2,1)S(1)}, bf16[32,8192]{1,0:T(8,128)(2,1)S(1)}, u32[]{:S(2)}, u32[]{:S(2)}) collective-permute-start(bf16[32,8192]{1,0:T(8,128)(2,1)S(1)} %constant_dynamic-update-slice_fusion.refs_0_), channel_id=1, source_target_pairs={{0,2},{1,3},{2,0},{3,1},{4,6},{5,7},{6,4},{7,5},{8,10},{9,11},{10,... | collective-permute-start | bytes 1572872 | tf_op jit(solution)/shard_map/ppermute | solution.py:38
  26.3 0.0 collective-permute-done.10
  26.4 0.0 copy-start.2
  26.4 0.0 copy-start
  26.4 0.0 copy-start.1
  26.4 1.6 %collective-permute-start.11 = (bf16[32,8192]{1,0:T(8,128)(2,1)S(1)}, bf16[32,8192]{1,0:T(8,128)(2,1)S(1)}, u32[]{:S(2)}, u32[]{:S(2)}) collective-permute-start(bf16[32,8192]{1,0:T(8,128)(2,1)S(1)} %pad_maximum_fusion.refs_4_), channel_id=1, source_target_pairs={{0,4},{1,5},{2,6},{3,7},{4,0},{5,1},{6,2},{7,3},{8,12},{9,13},{10,... | collective-permute-start | bytes 1572872 | tf_op jit(solution)/shard_map/ppermute | solution.py:38
  28.0 0.0 collective-permute-start.5
  28.0 0.5 collective-permute-start.12
  28.5 9.2 %collective-permute-done.4.refs_1_ = bf16[32,8192]{1,0:T(8,128)(2,1)S(1)} collective-permute-done((bf16[32,8192]{1,0:T(8,128)(2,1)S(1)}, bf16[32,8192]{1,0:T(8,128)(2,1)S(1)}, u32[]{:S(2)}, u32[]{:S(2)}) %collective-permute-start.4) | collective-permute-done | bytes 524320 | tf_op jit(solution)/shard_map/ppermute | solution.py:38
  37.7 0.0 collective-permute-start.6
  37.7 0.6 collective-permute-done.11.refs_5_
  38.4 0.0 collective-permute-start.13
  38.4 0.0 collective-permute-done.5.refs_2_
  38.4 0.0 collective-permute-done.12.refs_6_
  38.4 1.3 %collective-permute-done.6.refs_3_ = bf16[32,8192]{1,0:T(8,128)(2,1)S(1)} collective-permute-done((bf16[32,8192]{1,0:T(8,128)(2,1)S(1)}, bf16[32,8192]{1,0:T(8,128)(2,1)S(1)}, u32[]{:S(2)}, u32[]{:S(2)}) %collective-permute-start.6) | collective-permute-done | bytes 524320 | tf_op jit(solution)/shard_map/ppermute | solution.py:38
  39.6 0.7 collective-permute-done.13.refs_7_
  40.4 18.3 %products.1 = f32[32,16,128]{2,1,0:T(8,128)S(1)} custom-call(bf16[32,8192]{1,0:T(8,128)(2,1)S(1)} %constant_dynamic-update-slice_fusion.refs_0_, bf16[32,8192]{1,0:T(8,128)(2,1)S(1)} %collective-permute-done.4.refs_1_, bf16[32,8192]{1,0:T(8,128)(2,1)S(1)} %collective-permute-done.5.refs_2_, bf16[32,8192]{1,0:T(8,128)(2,1)S(1)} %collective-permute-done.6.refs_3_, ...), custom_call_target="tpu_custom_call" | custom-call | flops 5637144576 | bytes 44040192 | tf_op jit(solution)/shard_map/products/pallas_call | solution.py:195
  58.8 14.5 %all_to_all.15.values = f32[32,16,128]{2,1,0:T(8,128)S(1)} all-to-all(f32[32,16,128]{2,1,0:T(8,128)S(1)} %products.1), channel_id=1, replica_groups=mesh['groups'=1,'dp'=32] {'dp'}, dimensions={0} | all-to-all | bytes 524288 | tf_op jit(solution)/shard_map/all_to_all | solution.py:76
  73.3 0.7 sum_copies.1
  74.0 2.6 %all-to-all-start.1 = ((bf16[32,16,128]{2,1,0:T(8,128)(2,1)}), bf16[32,16,128]{2,1,0:T(8,128)(2,1)S(1)}, u32[]{:S(2)}, u32[]{:S(2)}) async-start(bf16[32,16,128]{2,1,0:T(8,128)(2,1)} %sum_copies.1), calls=%async_computation.1 | async-start | bytes 262144 | tf_op jit(solution)/shard_map/all_to_all | solution.py:76
  76.6 0.0 copy-done.2
  76.6 0.1 reshape.7
  76.7 0.1 broadcast_in_dim_reshape.3.ids
  76.8 8.0 %all-to-all-done.1.vectors = bf16[32,16,128]{2,1,0:T(8,128)(2,1)S(1)} async-done(((bf16[32,16,128]{2,1,0:T(8,128)(2,1)}), bf16[32,16,128]{2,1,0:T(8,128)(2,1)S(1)}, u32[]{:S(2)}, u32[]{:S(2)}) %all-to-all-start.1) | async-done | bytes 131104 | tf_op jit(solution)/shard_map/all_to_all | solution.py:76
  84.8 0.0 copy-done
  84.8 1.3 %target_products.1 = f32[32,8,128]{2,1,0:T(8,128)} custom-call(bf16[32,16,128]{2,1,0:T(8,128)(2,1)S(1)} %all-to-all-done.1.vectors, s32[1,128]{1,0:T(1,128)S(1)} %broadcast_in_dim_reshape.3.ids, bf16[8,3,64,64]{3,2,1,0:T(8,128)(2,1)S(1)} %copy-done, s32[1,8]{1,0:T(1,128)S(1)} %bitcast.4), custom_call_target="tpu_custom_call" | custom-call | tf_op jit(solution)/shard_map/target_products/pallas_call | solution.py:339
  86.1 2.6 %all-to-all-start.2 = ((f32[32,8,128]{2,1,0:T(8,128)}), f32[32,8,128]{2,1,0:T(8,128)S(1)}, u32[]{:S(2)}, u32[]{:S(2)}) async-start(f32[32,8,128]{2,1,0:T(8,128)} %target_products.1), calls=%async_computation.2 | async-start | bytes 262144 | tf_op jit(solution)/shard_map/all_to_all | solution.py:76
  88.7 1.5 %sketches.1 = (f32[16,3,64,64]{3,2,1,0:T(8,128)}, f32[16,128]{1,0:T(8,128)S(1)}) custom-call(bf16[32,16,128]{2,1,0:T(8,128)(2,1)S(1)} %all-to-all-done.1.vectors, s32[1,128]{1,0:T(1,128)S(1)} %broadcast_in_dim_reshape.3.ids), custom_call_target="tpu_custom_call" | custom-call | tf_op jit(solution)/shard_map/sketches/pallas_call | solution.py:349
  90.2 6.7 %all-to-all-done.2.parts = f32[32,8,128]{2,1,0:T(8,128)S(1)} async-done(((f32[32,8,128]{2,1,0:T(8,128)}), f32[32,8,128]{2,1,0:T(8,128)S(1)}, u32[]{:S(2)}, u32[]{:S(2)}) %all-to-all-start.2) | async-done | bytes 131104 | tf_op jit(solution)/shard_map/all_to_all | solution.py:76
  96.9 0.8 scores.1
  (6 shorter events, 0.1 us)
Async XLA Ops:
  0.6 9.0 %collective-permute-start = (bf16[4,8192]{1,0:T(4,128)(2,1)}, bf16[4,8192]{1,0:T(4,128)(2,1)S(1)}, u32[]{:S(2)}, u32[]{:S(2)}) collective-permute-start(bf16[4,8192]{1,0:T(4,128)(2,1)} %param.10), channel_id=1, source_target_pairs={{0,8},{1,9},{2,10},{3,11},{4,12},{5,13},{6,14},{7,15},{8,16},{9,17... | collective-permute-start | bytes 196616 | tf_op jit(solution)/shard_map/ppermute | solution.py:38
  3.7 9.9 %collective-permute-start.1 = (bf16[4,8192]{1,0:T(4,128)(2,1)}, bf16[4,8192]{1,0:T(4,128)(2,1)S(1)}, u32[]{:S(2)}, u32[]{:S(2)}) collective-permute-start(bf16[4,8192]{1,0:T(4,128)(2,1)} %param.10), channel_id=1, source_target_pairs={{0,16},{1,17},{2,18},{3,19},{4,20},{5,21},{6,22},{7,23},{8,24},{9,... | collective-permute-start | bytes 196616 | tf_op jit(solution)/shard_map/ppermute | solution.py:38
  6.3 7.3 %collective-permute-start.2 = (bf16[4,8192]{1,0:T(4,128)(2,1)}, bf16[4,8192]{1,0:T(4,128)(2,1)S(1)}, u32[]{:S(2)}, u32[]{:S(2)}) collective-permute-start(bf16[4,8192]{1,0:T(4,128)(2,1)} %param.10), channel_id=1, source_target_pairs={{0,24},{1,25},{2,26},{3,27},{4,28},{5,29},{6,30},{7,31},{8,0},{9,1... | collective-permute-start | bytes 196616 | tf_op jit(solution)/shard_map/ppermute | solution.py:38
  7.6 6.8 %collective-permute-start.7 = (bf16[4,8192]{1,0:T(4,128)(2,1)}, bf16[4,8192]{1,0:T(4,128)(2,1)S(1)}, u32[]{:S(2)}, u32[]{:S(2)}) collective-permute-start(bf16[4,8192]{1,0:T(4,128)(2,1)} %param.11), channel_id=1, source_target_pairs={{0,8},{1,9},{2,10},{3,11},{4,12},{5,13},{6,14},{7,15},{8,16},{9,17... | collective-permute-start | bytes 196616 | tf_op jit(solution)/shard_map/ppermute | solution.py:38
  8.3 8.3 %collective-permute-start.8 = (bf16[4,8192]{1,0:T(4,128)(2,1)}, bf16[4,8192]{1,0:T(4,128)(2,1)S(1)}, u32[]{:S(2)}, u32[]{:S(2)}) collective-permute-start(bf16[4,8192]{1,0:T(4,128)(2,1)} %param.11), channel_id=1, source_target_pairs={{0,16},{1,17},{2,18},{3,19},{4,20},{5,21},{6,22},{7,23},{8,24},{9,... | collective-permute-start | bytes 196616 | tf_op jit(solution)/shard_map/ppermute | solution.py:38
  9.7 7.1 %collective-permute-start.9 = (bf16[4,8192]{1,0:T(4,128)(2,1)}, bf16[4,8192]{1,0:T(4,128)(2,1)S(1)}, u32[]{:S(2)}, u32[]{:S(2)}) collective-permute-start(bf16[4,8192]{1,0:T(4,128)(2,1)} %param.11), channel_id=1, source_target_pairs={{0,24},{1,25},{2,26},{3,27},{4,28},{5,29},{6,30},{7,31},{8,0},{9,1... | collective-permute-start | bytes 196616 | tf_op jit(solution)/shard_map/ppermute | solution.py:38
  17.1 7.9 %collective-permute-start.3 = (bf16[16,8192]{1,0:T(8,128)(2,1)S(1)}, bf16[16,8192]{1,0:T(8,128)(2,1)S(1)}, u32[]{:S(2)}, u32[]{:S(2)}) collective-permute-start(bf16[16,8192]{1,0:T(8,128)(2,1)S(1)} %get-tuple-element.8), channel_id=1, source_target_pairs={{0,4},{1,5},{2,6},{3,7},{4,0},{5,1},{6,2},{7,3},{8,12},{9,13},{10,... | collective-permute-start | bytes 786440 | tf_op jit(solution)/shard_map/ppermute | solution.py:38
  18.8 7.5 %collective-permute-start.10 = (bf16[16,8192]{1,0:T(8,128)(2,1)S(1)}, bf16[16,8192]{1,0:T(8,128)(2,1)S(1)}, u32[]{:S(2)}, u32[]{:S(2)}) collective-permute-start(bf16[16,8192]{1,0:T(8,128)(2,1)S(1)} %get-tuple-element.17), channel_id=1, source_target_pairs={{0,2},{1,3},{2,0},{3,1},{4,6},{5,7},{6,4},{7,5},{8,10},{9,11},{10,... | collective-permute-start | bytes 786440 | tf_op jit(solution)/shard_map/ppermute | solution.py:38
  25.1 12.6 %collective-permute-start.4 = (bf16[32,8192]{1,0:T(8,128)(2,1)S(1)}, bf16[32,8192]{1,0:T(8,128)(2,1)S(1)}, u32[]{:S(2)}, u32[]{:S(2)}) collective-permute-start(bf16[32,8192]{1,0:T(8,128)(2,1)S(1)} %constant_dynamic-update-slice_fusion.refs_0_), channel_id=1, source_target_pairs={{0,2},{1,3},{2,0},{3,1},{4,6},{5,7},{6,4},{7,5},{8,10},{9,11},{10,... | collective-permute-start | bytes 1572872 | tf_op jit(solution)/shard_map/ppermute | solution.py:38
  26.4 50.2 %copy-start.2 = (s32[128]{0:T(128)S(1)}, s32[128]{0:T(128)}, u32[]{:S(2)}) copy-start(s32[128]{0:T(128)} %param.17) | copy-start | bytes 1540
  26.4 58.4 %copy-start = (bf16[8,3,64,64]{3,2,1,0:T(8,128)(2,1)S(1)}, bf16[8,3,64,64]{3,2,1,0:T(8,128)(2,1)}, u32[]{:S(2)}) copy-start(bf16[8,3,64,64]{3,2,1,0:T(8,128)(2,1)} %targets.1) | copy-start | bytes 589828
  26.4 58.4 %copy-start.1 = (s32[8]{0:T(128)S(1)}, s32[8]{0:T(128)}, u32[]{:S(2)}) copy-start(s32[8]{0:T(128)} %param.19) | copy-start | bytes 100
  26.4 12.0 %collective-permute-start.11 = (bf16[32,8192]{1,0:T(8,128)(2,1)S(1)}, bf16[32,8192]{1,0:T(8,128)(2,1)S(1)}, u32[]{:S(2)}, u32[]{:S(2)}) collective-permute-start(bf16[32,8192]{1,0:T(8,128)(2,1)S(1)} %pad_maximum_fusion.refs_4_), channel_id=1, source_target_pairs={{0,4},{1,5},{2,6},{3,7},{4,0},{5,1},{6,2},{7,3},{8,12},{9,13},{10,... | collective-permute-start | bytes 1572872 | tf_op jit(solution)/shard_map/ppermute | solution.py:38
  28.0 10.4 %collective-permute-start.5 = (bf16[32,8192]{1,0:T(8,128)(2,1)S(1)}, bf16[32,8192]{1,0:T(8,128)(2,1)S(1)}, u32[]{:S(2)}, u32[]{:S(2)}) collective-permute-start(bf16[32,8192]{1,0:T(8,128)(2,1)S(1)} %constant_dynamic-update-slice_fusion.refs_0_), channel_id=1, source_target_pairs={{0,1},{1,0},{2,3},{3,2},{4,5},{5,4},{6,7},{7,6},{8,9},{9,8},{10,11... | collective-permute-start | bytes 1572872 | tf_op jit(solution)/shard_map/ppermute | solution.py:38
  28.0 10.4 %collective-permute-start.12 = (bf16[32,8192]{1,0:T(8,128)(2,1)S(1)}, bf16[32,8192]{1,0:T(8,128)(2,1)S(1)}, u32[]{:S(2)}, u32[]{:S(2)}) collective-permute-start(bf16[32,8192]{1,0:T(8,128)(2,1)S(1)} %pad_maximum_fusion.refs_4_), channel_id=1, source_target_pairs={{0,1},{1,0},{2,3},{3,2},{4,5},{5,4},{6,7},{7,6},{8,9},{9,8},{10,11... | collective-permute-start | bytes 1572872 | tf_op jit(solution)/shard_map/ppermute | solution.py:38
  37.7 1.9 %collective-permute-start.6 = (bf16[32,8192]{1,0:T(8,128)(2,1)S(1)}, bf16[32,8192]{1,0:T(8,128)(2,1)S(1)}, u32[]{:S(2)}, u32[]{:S(2)}) collective-permute-start(bf16[32,8192]{1,0:T(8,128)(2,1)S(1)} %collective-permute-done.4.refs_1_), channel_id=1, source_target_pairs={{0,1},{1,0},{2,3},{3,2},{4,5},{5,4},{6,7},{7,6},{8,9},{9,8},{10,11... | collective-permute-start | bytes 1572872 | tf_op jit(solution)/shard_map/ppermute | solution.py:38
  38.4 2.0 %collective-permute-start.13 = (bf16[32,8192]{1,0:T(8,128)(2,1)S(1)}, bf16[32,8192]{1,0:T(8,128)(2,1)S(1)}, u32[]{:S(2)}, u32[]{:S(2)}) collective-permute-start(bf16[32,8192]{1,0:T(8,128)(2,1)S(1)} %collective-permute-done.11.refs_5_), channel_id=1, source_target_pairs={{0,1},{1,0},{2,3},{3,2},{4,5},{5,4},{6,7},{7,6},{8,9},{9,8},{10,11... | collective-permute-start | bytes 1572872 | tf_op jit(solution)/shard_map/ppermute | solution.py:38
  74.0 10.8 %all-to-all-start.1 = ((bf16[32,16,128]{2,1,0:T(8,128)(2,1)}), bf16[32,16,128]{2,1,0:T(8,128)(2,1)S(1)}, u32[]{:S(2)}, u32[]{:S(2)}) async-start(bf16[32,16,128]{2,1,0:T(8,128)(2,1)} %sum_copies.1), calls=%async_computation.1 | async-start | bytes 262144 | tf_op jit(solution)/shard_map/all_to_all | solution.py:76
  86.1 10.8 %all-to-all-start.2 = ((f32[32,8,128]{2,1,0:T(8,128)}), f32[32,8,128]{2,1,0:T(8,128)S(1)}, u32[]{:S(2)}, u32[]{:S(2)}) async-start(f32[32,8,128]{2,1,0:T(8,128)} %target_products.1), calls=%async_computation.2 | async-start | bytes 262144 | tf_op jit(solution)/shard_map/all_to_all | solution.py:76

commit v11 on v10

--- a/solution.py
+++ b/solution.py
@@ -38,6 +38,28 @@
     return lax.ppermute(value, "dp", pairs)
 
 
+def partner(value, sizes, axis, bit):
+    size, stride = sizes[axis], strides_of(sizes)[axis]
+    pairs = []
+    for source in range(int(np.prod(sizes))):
+        at = (source // stride) % size
+        pairs.append((source, source + ((at ^ bit) - at) * stride))
+    return lax.ppermute(value, "dp", pairs)
+
+
+def spread_axis(value, sizes, axis):
+    if sizes[axis] == 4:
+        far, near = partner(value, sizes, axis, 2), partner(value, sizes, axis, 1)
+        return [value, near, far, partner(far, sizes, axis, 1)]
+    return [value] + [shift(value, sizes, axis, k) for k in range(1, sizes[axis])]
+
+
+def origin(at, distance, size):
+    if size == 4:
+        return lax.bitwise_xor(at, distance)
+    return lax.rem(at + size - distance, size)
+
+
 def coordinate(me, sizes, axis):
     return lax.rem(lax.div(me, strides_of(sizes)[axis]), sizes[axis])
 
@@ -48,21 +70,18 @@
     def moved(axis, amount):
         return [tuple(amount if i == axis else b for i, b in enumerate(back)) for back in backs]
 
-    def received(piece, axis):
-        return [shift(piece, sizes, axis, k) for k in range(1, sizes[axis])]
-
-    piece = jnp.concatenate([own] + received(rows, 0), 0)
+    piece = jnp.concatenate([own] + spread_axis(rows, sizes, 0)[1:], 0)
     piece, *made = lax.optimization_barrier((piece, *made))
     for axis in order[:-1]:
-        piece = jnp.concatenate([piece] + received(piece, axis), 0)
+        piece = jnp.concatenate([piece] + spread_axis(piece, sizes, axis)[1:], 0)
         backs = sum([moved(axis, k) for k in range(1, sizes[axis])], backs)
     pieces = [(piece, backs)]
     for axis in order[-1:]:
-        others = zip(received(piece, axis), range(1, sizes[axis]))
+        others = zip(spread_axis(piece, sizes, axis)[1:], range(1, sizes[axis]))
         pieces += [(other, moved(axis, k)) for other, k in others]
     core = len(sizes) - 1
     for piece, backs in list(pieces):
-        others = zip(received(piece, core), range(1, sizes[core]))
+        others = zip(spread_axis(piece, sizes, core)[1:], range(1, sizes[core]))
         pieces += [(other, moved(core, k)) for other, k in others]
     return [piece for piece, _ in pieces], [backs for _, backs in pieces], made
 
@@ -91,8 +110,8 @@
         for i, back in enumerate(lines):
             slot = 0
             for axis in range(1, len(sizes)):
-                at = coordinate(me, sizes, axis) + sizes[axis] - back[axis]
-                slot = slot * sizes[axis] + lax.rem(at, sizes[axis])
+                at = origin(coordinate(me, sizes, axis), back[axis], sizes[axis])
+                slot = slot * sizes[axis] + at
             start = pl.multiple_of(slot * rows, rows)
             into[pl.ds(start, rows), :] = piece[i * rows : (i + 1) * rows, :]
 
@@ -102,6 +121,10 @@
     start = lax.div(lax.axis_index("dp") * model_cols, window) * window
     columns = pl.ds(pl.multiple_of(start, window), window)
     return transposed_dot(proj, tokens[:, columns])
+
+
+def repeated(used, count):
+    return [*range(used // 2, used), *range(used // 2)][: count - used]
 
 
 def product_kernel(backs, sizes, model_cols, *refs):
@@ -174,14 +197,18 @@
     source = lax.broadcasted_iota(jnp.int32, (count, count), 0)
     target = lax.broadcasted_iota(jnp.int32, (count, count), 1)
     back = lax.rem(lax.div(source, each), size)
-    at = lax.rem(coordinate(lax.axis_index("dp"), sizes, 0) + size - back, size)
+    at = origin(coordinate(lax.axis_index("dp"), sizes, 0), back, size)
     place = lax.div(source, line) * line + at * each + lax.rem(source, each)
     order = (place == target).astype(F32)
     every = jnp.dot(every, order, precision=HIGHEST, preferred_element_type=F32)
     used = every.shape[0] // out.shape[1]
-    out[:used] = every.reshape((used,) + out.shape[1:])
-    if used < out.shape[0]:
-        out[used:] = jnp.zeros_like(out[used:])
+    every = every.reshape((used,) + out.shape[1:])
+    out[:used] = every
+    again = repeated(used, out.shape[0])
+    for i, block in enumerate(again):
+        out[used + i] = every[block]
+    if used + len(again) < out.shape[0]:
+        out[used + len(again) :] = jnp.zeros_like(out[used + len(again) :])
 
 
 def products(in_pieces, out_pieces, backs, sizes, proj, w_gate, w_up, w_down):
@@ -218,17 +245,20 @@
     return pltpu.CompilerParams(vmem_limit_bytes=megabytes * 2**20)
 
 
-def sum_kernel(values, out):
+def sum_kernel(used, values, out):
     total = values[0]
     for i in range(1, values.shape[0]):
         total += values[i]
+    rounded = total.astype(BF16)
+    spare = lax.axis_index("dp") >= used
+    rounded = jnp.where(spare, total - rounded.astype(F32), total).astype(BF16)
     for i in range(out.shape[0]):
-        out[i] = total.astype(BF16)
-
-
-def sum_copies(values):
+        out[i] = rounded
+
+
+def sum_copies(values, used):
     return pl.pallas_call(
-        sum_kernel,
+        functools.partial(sum_kernel, used),
         out_shape=jax.ShapeDtypeStruct(values.shape, BF16),
         in_specs=[VMEM],
         out_specs=VMEM,
@@ -237,9 +267,19 @@
     )(values)
 
 
-def rows_of(vectors, rank):
+def sides_of(vectors, rank):
     height, tokens = vectors.shape[1:]
-    return vectors[: 6 * rank // height].reshape(6 * rank, tokens)
+    used = 6 * rank // height
+    every = vectors[:used].reshape(6 * rank, tokens)
+    again = repeated(used, vectors.shape[0])[: used // 2]
+    rest = vectors[used : used + len(again)].reshape(-1, tokens) if again else every[:0]
+    sides = []
+    for k in range(3):
+        rights = [every[(3 + k) * rank : (4 + k) * rank]]
+        if rest.shape[0] >= (k + 1) * rank:
+            rights.append(rest[k * rank : (k + 1) * rank])
+        sides.append((every[k * rank : (k + 1) * rank], rights))
+    return sides
 
 
 def onehot_of(ids, tokens):
@@ -249,13 +289,10 @@
 def target_kernel(rank, vectors, ids, targets, domains, out):
     tokens = ids.shape[1]
     examples = targets.shape[0]
-    every = rows_of(vectors, rank)
     total = jnp.zeros((examples, tokens), F32)
-    for k in range(3):
-        left = every[k * rank : (k + 1) * rank]
+    for k, (left, rights) in enumerate(sides_of(vectors, rank)):
         target = targets[:, k].reshape(examples * rank, rank)
-        right = every[(3 + k) * rank : (4 + k) * rank]
-        turned = jnp.dot(target, right, preferred_element_type=F32)
+        turned = sum(jnp.dot(target, right, preferred_element_type=F32) for right in rights)
         total += jnp.sum(turned.reshape(examples, rank, tokens) * left.astype(F32)[None], 1)
     domain = lax.broadcasted_iota(jnp.int32, (DOMAINS, examples), 0)
     domains = (domains[...] == domain).astype(F32)
@@ -271,14 +308,12 @@
 
 def sketch_kernel(rank, vectors, ids, sketches, norms):
     tokens = ids.shape[1]
-    every = rows_of(vectors, rank)
     masks = onehot_of(ids[...], tokens).astype(BF16)
     norm = jnp.zeros((SEQS, 1), F32)
-    for k in range(3):
-        left = every[k * rank : (k + 1) * rank]
-        right = every[(3 + k) * rank : (4 + k) * rank]
+    for k, (left, rights) in enumerate(sides_of(vectors, rank)):
         rows = jnp.concatenate([left * masks[s : s + 1, :] for s in range(SEQS)], 0)
-        sketch = transposed_dot(rows, right).reshape(SEQS, rank, rank)
+        sketch = sum(transposed_dot(rows, right) for right in rights)
+        sketch = sketch.reshape(SEQS, rank, rank)
         sketches[:, k] = sketch
         norm += jnp.sum(jnp.sum(sketch * sketch, 1), 1, keepdims=True)
     norms[...] = jnp.broadcast_to(norm, norms.shape)
@@ -333,7 +368,8 @@
     vectors = products(
         in_pieces, out_pieces, (in_backs, out_backs), sizes, proj, w_gate, w_up, w_down
     )
-    vectors = exchange(sum_copies(exchange(vectors)))
+    vectors = exchange(vectors)
+    vectors = exchange(sum_copies(vectors, 6 * rank // vectors.shape[1]))
 
     ids = slot_order(seq_ids, sizes)[None, :]
     parts = pl.pallas_call(

time: 98 us -> 97.1 us (level)
  starting transfers between devices: 22.6 us -> 19 us
  waiting for transfers between devices: 34.5 us -> 36.5 us
    ppermute x14 -> x8, starting transfers between devices: 17.5 us -> 5.33 us  [shift(): return lax.ppermute(value, 'dp', pairs)]
    ppermute x0 -> x6, starting transfers between devices: none -> 8.58 us  [partner(): return lax.ppermute(value, 'dp', pairs)]
    ppermute x0 -> x6, waiting for transfers between devices: none -> 5.32 us  [partner(): return lax.ppermute(value, 'dp', pairs)]
    ppermute x14 -> x8, waiting for transfers between devices: 19.8 us -> 16.5 us  [shift(): return lax.ppermute(value, 'dp', pairs)]
  transfers between devices with their start and end apart: 16 -> 16, of which waited for: 10 -> 11; matrix products, arithmetic and copies ran while one was open for 2% -> 2% of each run, Pallas kernels for 2% -> 2%
where the time goes in v11:
time: 97.1 us; the launch traced here: 96.8 us
  waiting for transfers between devices  36.5 us (38%)
  Pallas kernels  22.8 us (23%)
  starting transfers between devices  19 us (20%)
  blocking collectives  15.1 us (16%)
  other arithmetic  2.32 us (2%)
    pallas_call x1, Pallas kernels, products(): pl.pallas_call(functools.partial(product_kernel, backs, sizes, model_cols...  18.3 us
    ppermute x8, waiting for transfers between devices, shift(): return lax.ppermute(value, 'dp', pairs)  16.5 us
    all_to_all x1, blocking collectives, exchange(): lax.all_to_all(blocks, 'dp', split_axis=0, concat_axis=0, axis_index_grou...  15.1 us
    all_to_all x2, waiting for transfers between devices, exchange(): lax.all_to_all(blocks, 'dp', split_axis=0, concat_axis=0, axis_index_grou...  14.6 us
    ppermute x6, starting transfers between devices, partner(): return lax.ppermute(value, 'dp', pairs)  8.58 us
    ppermute x8, starting transfers between devices, shift(): return lax.ppermute(value, 'dp', pairs)  5.33 us
    ppermute x6, waiting for transfers between devices, partner(): return lax.ppermute(value, 'dp', pairs)  5.32 us
    all_to_all x2, starting transfers between devices, exchange(): lax.all_to_all(blocks, 'dp', split_axis=0, concat_axis=0, axis_index_grou...  5.14 us
  transfers between devices with their start and end apart: 16, of which 11 were waited for; matrix products, arithmetic and copies ran while one was open for 2% of the time, Pallas kernels for 2%

profile of v11, /device:TPU:0, one launch (start us, length us, event | category | flops | bytes accessed | tf_op | source)
XLA Modules:
  0.0 96.8 jit_solution(5271985180588073324)
XLA Ops:
  0.6 4.1 %collective-permute-start.1 = (bf16[4,8192]{1,0:T(4,128)(2,1)}, bf16[4,8192]{1,0:T(4,128)(2,1)S(1)}, u32[]{:S(2)}, u32[]{:S(2)}) collective-permute-start(bf16[4,8192]{1,0:T(4,128)(2,1)} %param.10), channel_id=1, source_target_pairs={{0,16},{1,17},{2,18},{3,19},{4,20},{5,21},{6,22},{7,23},{8,24},{9,... | collective-permute-start | bytes 196616 | tf_op jit(solution)/shard_map/ppermute | solution.py:47
  4.7 1.6 %collective-permute-start = (bf16[4,8192]{1,0:T(4,128)(2,1)}, bf16[4,8192]{1,0:T(4,128)(2,1)S(1)}, u32[]{:S(2)}, u32[]{:S(2)}) collective-permute-start(bf16[4,8192]{1,0:T(4,128)(2,1)} %param.10), channel_id=1, source_target_pairs={{0,8},{1,9},{2,10},{3,11},{4,12},{5,13},{6,14},{7,15},{8,0},{9,1},... | collective-permute-start | bytes 196616 | tf_op jit(solution)/shard_map/ppermute | solution.py:47
  6.3 0.3 collective-permute-start.8
  6.6 0.2 collective-permute-start.7
  6.8 0.9 pad_maximum_fusion.4
  7.8 0.2 collective-permute-done.1
  8.0 2.2 %collective-permute-start.2 = (bf16[4,8192]{1,0:T(4,128)(2,1)S(1)}, bf16[4,8192]{1,0:T(4,128)(2,1)S(1)}, u32[]{:S(2)}, u32[]{:S(2)}) collective-permute-start(bf16[4,8192]{1,0:T(4,128)(2,1)S(1)} %collective-permute-done.1), channel_id=1, source_target_pairs={{0,8},{1,9},{2,10},{3,11},{4,12},{5,13},{6,14},{7,15},{8,0},{9,1},... | collective-permute-start | bytes 196616 | tf_op jit(solution)/shard_map/ppermute | solution.py:47
  10.2 2.2 %collective-permute-done.8 = bf16[4,8192]{1,0:T(4,128)(2,1)S(1)} collective-permute-done((bf16[4,8192]{1,0:T(4,128)(2,1)}, bf16[4,8192]{1,0:T(4,128)(2,1)S(1)}, u32[]{:S(2)}, u32[]{:S(2)}) %collective-permute-start.8) | collective-permute-done | bytes 65568 | tf_op jit(solution)/shard_map/ppermute | solution.py:47
  12.3 0.2 collective-permute-start.9
  12.5 1.0 %pad_maximum_fusion.1.refs_8_ = bf16[192,1152]{1,0:T(8,128)(2,1)S(1)} fusion(bf16[192,896]{1,0:T(8,128)(2,1)} %bitcast.5, bf16[192,256]{1,0:T(8,128)(2,1)} %bitcast.6), kind=kLoop, calls=%fused_computation.1 | loop fusion | flops 884736 | bytes 884736 | tf_op jit(solution)/shard_map/concatenate | solution.py:360
  13.6 0.0 collective-permute-done
  13.6 0.0 collective-permute-done.7
  13.6 0.0 collective-permute-done.2
  13.6 3.0 %collective-permute-done.9 = bf16[4,8192]{1,0:T(4,128)(2,1)S(1)} collective-permute-done((bf16[4,8192]{1,0:T(4,128)(2,1)S(1)}, bf16[4,8192]{1,0:T(4,128)(2,1)S(1)}, u32[]{:S(2)}, u32[]{:S(2)}) %collective-permute-start.9) | collective-permute-done | bytes 65568 | tf_op jit(solution)/shard_map/ppermute | solution.py:47
  16.6 0.3 pad_maximum_fusion.2
  16.9 1.6 %collective-permute-start.3 = (bf16[16,8192]{1,0:T(8,128)(2,1)S(1)}, bf16[16,8192]{1,0:T(8,128)(2,1)S(1)}, u32[]{:S(2)}, u32[]{:S(2)}) collective-permute-start(bf16[16,8192]{1,0:T(8,128)(2,1)S(1)} %get-tuple-element.8), channel_id=1, source_target_pairs={{0,4},{1,5},{2,6},{3,7},{4,0},{5,1},{6,2},{7,3},{8,12},{9,13},{10,... | collective-permute-start | bytes 786440 | tf_op jit(solution)/shard_map/ppermute | solution.py:38
  18.5 1.6 %collective-permute-start.10 = (bf16[16,8192]{1,0:T(8,128)(2,1)S(1)}, bf16[16,8192]{1,0:T(8,128)(2,1)S(1)}, u32[]{:S(2)}, u32[]{:S(2)}) collective-permute-start(bf16[16,8192]{1,0:T(8,128)(2,1)S(1)} %get-tuple-element.17), channel_id=1, source_target_pairs={{0,2},{1,3},{2,0},{3,1},{4,6},{5,7},{6,4},{7,5},{8,10},{9,11},{10,... | collective-permute-start | bytes 786440 | tf_op jit(solution)/shard_map/ppermute | solution.py:38
  20.1 3.3 %collective-permute-done.3 = bf16[16,8192]{1,0:T(8,128)(2,1)S(1)} collective-permute-done((bf16[16,8192]{1,0:T(8,128)(2,1)S(1)}, bf16[16,8192]{1,0:T(8,128)(2,1)S(1)}, u32[]{:S(2)}, u32[]{:S(2)}) %collective-permute-start.3) | collective-permute-done | bytes 262176 | tf_op jit(solution)/shard_map/ppermute | solution.py:38
  23.4 1.6 %collective-permute-start.4 = (bf16[32,8192]{1,0:T(8,128)(2,1)S(1)}, bf16[32,8192]{1,0:T(8,128)(2,1)S(1)}, u32[]{:S(2)}, u32[]{:S(2)}) collective-permute-start(bf16[32,8192]{1,0:T(8,128)(2,1)S(1)} %constant_dynamic-update-slice_fusion.refs_0_), channel_id=1, source_target_pairs={{0,2},{1,3},{2,0},{3,1},{4,6},{5,7},{6,4},{7,5},{8,10},{9,11},{10,... | collective-permute-start | bytes 1572872 | tf_op jit(solution)/shard_map/ppermute | solution.py:38
  24.9 2.8 %collective-permute-done.10 = bf16[16,8192]{1,0:T(8,128)(2,1)S(1)} collective-permute-done((bf16[16,8192]{1,0:T(8,128)(2,1)S(1)}, bf16[16,8192]{1,0:T(8,128)(2,1)S(1)}, u32[]{:S(2)}, u32[]{:S(2)}) %collective-permute-start.10) | collective-permute-done | bytes 262176 | tf_op jit(solution)/shard_map/ppermute | solution.py:38
  27.7 0.0 copy-start.2
  27.7 0.0 copy-start
  27.8 0.0 copy-start.1
  27.8 0.1 collective-permute-start.11
  27.8 0.1 collective-permute-start.5
  27.9 0.5 collective-permute-start.12
  28.4 7.8 %collective-permute-done.4.refs_1_ = bf16[32,8192]{1,0:T(8,128)(2,1)S(1)} collective-permute-done((bf16[32,8192]{1,0:T(8,128)(2,1)S(1)}, bf16[32,8192]{1,0:T(8,128)(2,1)S(1)}, u32[]{:S(2)}, u32[]{:S(2)}) %collective-permute-start.4) | collective-permute-done | bytes 524320 | tf_op jit(solution)/shard_map/ppermute | solution.py:38
  36.2 0.0 collective-permute-start.6
  36.2 0.8 collective-permute-done.11.refs_5_
  37.0 0.0 collective-permute-start.13
  37.0 0.0 collective-permute-done.5.refs_2_
  37.0 0.0 collective-permute-done.12.refs_6_
  37.0 1.1 %collective-permute-done.6.refs_3_ = bf16[32,8192]{1,0:T(8,128)(2,1)S(1)} collective-permute-done((bf16[32,8192]{1,0:T(8,128)(2,1)S(1)}, bf16[32,8192]{1,0:T(8,128)(2,1)S(1)}, u32[]{:S(2)}, u32[]{:S(2)}) %collective-permute-start.6) | collective-permute-done | bytes 524320 | tf_op jit(solution)/shard_map/ppermute | solution.py:38
  38.1 0.8 collective-permute-done.13.refs_7_
  38.9 18.3 %products.1 = f32[32,16,128]{2,1,0:T(8,128)S(1)} custom-call(bf16[32,8192]{1,0:T(8,128)(2,1)S(1)} %constant_dynamic-update-slice_fusion.refs_0_, bf16[32,8192]{1,0:T(8,128)(2,1)S(1)} %collective-permute-done.4.refs_1_, bf16[32,8192]{1,0:T(8,128)(2,1)S(1)} %collective-permute-done.5.refs_2_, bf16[32,8192]{1,0:T(8,128)(2,1)S(1)} %collective-permute-done.6.refs_3_, ...), custom_call_target="tpu_custom_call" | custom-call | flops 5637144576 | bytes 44040192 | tf_op jit(solution)/shard_map/products/pallas_call | solution.py:222
  57.2 15.1 %all_to_all.15.values = f32[32,16,128]{2,1,0:T(8,128)S(1)} all-to-all(f32[32,16,128]{2,1,0:T(8,128)S(1)} %products.1), channel_id=1, replica_groups=mesh['groups'=1,'dp'=32] {'dp'}, dimensions={0} | all-to-all | bytes 524288 | tf_op jit(solution)/shard_map/all_to_all | solution.py:95
  72.3 0.7 sum_copies.1
  73.0 2.6 %all-to-all-start.1 = ((bf16[32,16,128]{2,1,0:T(8,128)(2,1)}), bf16[32,16,128]{2,1,0:T(8,128)(2,1)S(1)}, u32[]{:S(2)}, u32[]{:S(2)}) async-start(bf16[32,16,128]{2,1,0:T(8,128)(2,1)} %sum_copies.1), calls=%async_computation.1 | async-start | bytes 262144 | tf_op jit(solution)/shard_map/all_to_all | solution.py:95
  75.6 0.0 copy-done.2
  75.6 0.1 reshape.7
  75.7 0.1 broadcast_in_dim_reshape.3.ids
  75.9 8.0 %all-to-all-done.1.vectors = bf16[32,16,128]{2,1,0:T(8,128)(2,1)S(1)} async-done(((bf16[32,16,128]{2,1,0:T(8,128)(2,1)}), bf16[32,16,128]{2,1,0:T(8,128)(2,1)S(1)}, u32[]{:S(2)}, u32[]{:S(2)}) %all-to-all-start.1) | async-done | bytes 131104 | tf_op jit(solution)/shard_map/all_to_all | solution.py:95
  83.9 0.0 copy-done
  83.9 1.4 %target_products.1 = f32[32,8,128]{2,1,0:T(8,128)} custom-call(bf16[32,16,128]{2,1,0:T(8,128)(2,1)S(1)} %all-to-all-done.1.vectors, s32[1,128]{1,0:T(1,128)S(1)} %broadcast_in_dim_reshape.3.ids, bf16[8,3,64,64]{3,2,1,0:T(8,128)(2,1)S(1)} %copy-done, s32[1,8]{1,0:T(1,128)S(1)} %bitcast.4), custom_call_target="tpu_custom_call" | custom-call | tf_op jit(solution)/shard_map/target_products/pallas_call | solution.py:375
  85.2 2.6 %all-to-all-start.2 = ((f32[32,8,128]{2,1,0:T(8,128)}), f32[32,8,128]{2,1,0:T(8,128)S(1)}, u32[]{:S(2)}, u32[]{:S(2)}) async-start(f32[32,8,128]{2,1,0:T(8,128)} %target_products.1), calls=%async_computation.2 | async-start | bytes 262144 | tf_op jit(solution)/shard_map/all_to_all | solution.py:95
  87.8 1.6 %sketches.1 = (f32[16,3,64,64]{3,2,1,0:T(8,128)}, f32[16,128]{1,0:T(8,128)S(1)}) custom-call(bf16[32,16,128]{2,1,0:T(8,128)(2,1)S(1)} %all-to-all-done.1.vectors, s32[1,128]{1,0:T(1,128)S(1)} %broadcast_in_dim_reshape.3.ids), custom_call_target="tpu_custom_call" | custom-call | tf_op jit(solution)/shard_map/sketches/pallas_call | solution.py:385
  89.4 6.6 %all-to-all-done.2.parts = f32[32,8,128]{2,1,0:T(8,128)S(1)} async-done(((f32[32,8,128]{2,1,0:T(8,128)}), f32[32,8,128]{2,1,0:T(8,128)S(1)}, u32[]{:S(2)}, u32[]{:S(2)}) %all-to-all-start.2) | async-done | bytes 131104 | tf_op jit(solution)/shard_map/all_to_all | solution.py:95
  96.0 0.8 scores.1
  (6 shorter events, 0.1 us)
Async XLA Ops:
  0.6 7.4 %collective-permute-start.1 = (bf16[4,8192]{1,0:T(4,128)(2,1)}, bf16[4,8192]{1,0:T(4,128)(2,1)S(1)}, u32[]{:S(2)}, u32[]{:S(2)}) collective-permute-start(bf16[4,8192]{1,0:T(4,128)(2,1)} %param.10), channel_id=1, source_target_pairs={{0,16},{1,17},{2,18},{3,19},{4,20},{5,21},{6,22},{7,23},{8,24},{9,... | collective-permute-start | bytes 196616 | tf_op jit(solution)/shard_map/ppermute | solution.py:47
  4.7 8.8 %collective-permute-start = (bf16[4,8192]{1,0:T(4,128)(2,1)}, bf16[4,8192]{1,0:T(4,128)(2,1)S(1)}, u32[]{:S(2)}, u32[]{:S(2)}) collective-permute-start(bf16[4,8192]{1,0:T(4,128)(2,1)} %param.10), channel_id=1, source_target_pairs={{0,8},{1,9},{2,10},{3,11},{4,12},{5,13},{6,14},{7,15},{8,0},{9,1},... | collective-permute-start | bytes 196616 | tf_op jit(solution)/shard_map/ppermute | solution.py:47
  6.3 6.0 %collective-permute-start.8 = (bf16[4,8192]{1,0:T(4,128)(2,1)}, bf16[4,8192]{1,0:T(4,128)(2,1)S(1)}, u32[]{:S(2)}, u32[]{:S(2)}) collective-permute-start(bf16[4,8192]{1,0:T(4,128)(2,1)} %param.11), channel_id=1, source_target_pairs={{0,16},{1,17},{2,18},{3,19},{4,20},{5,21},{6,22},{7,23},{8,24},{9,... | collective-permute-start | bytes 196616 | tf_op jit(solution)/shard_map/ppermute | solution.py:47
  6.6 6.9 %collective-permute-start.7 = (bf16[4,8192]{1,0:T(4,128)(2,1)}, bf16[4,8192]{1,0:T(4,128)(2,1)S(1)}, u32[]{:S(2)}, u32[]{:S(2)}) collective-permute-start(bf16[4,8192]{1,0:T(4,128)(2,1)} %param.11), channel_id=1, source_target_pairs={{0,8},{1,9},{2,10},{3,11},{4,12},{5,13},{6,14},{7,15},{8,0},{9,1},... | collective-permute-start | bytes 196616 | tf_op jit(solution)/shard_map/ppermute | solution.py:47
  8.0 5.6 %collective-permute-start.2 = (bf16[4,8192]{1,0:T(4,128)(2,1)S(1)}, bf16[4,8192]{1,0:T(4,128)(2,1)S(1)}, u32[]{:S(2)}, u32[]{:S(2)}) collective-permute-start(bf16[4,8192]{1,0:T(4,128)(2,1)S(1)} %collective-permute-done.1), channel_id=1, source_target_pairs={{0,8},{1,9},{2,10},{3,11},{4,12},{5,13},{6,14},{7,15},{8,0},{9,1},... | collective-permute-start | bytes 196616 | tf_op jit(solution)/shard_map/ppermute | solution.py:47
  12.3 4.3 %collective-permute-start.9 = (bf16[4,8192]{1,0:T(4,128)(2,1)S(1)}, bf16[4,8192]{1,0:T(4,128)(2,1)S(1)}, u32[]{:S(2)}, u32[]{:S(2)}) collective-permute-start(bf16[4,8192]{1,0:T(4,128)(2,1)S(1)} %collective-permute-done.8), channel_id=1, source_target_pairs={{0,8},{1,9},{2,10},{3,11},{4,12},{5,13},{6,14},{7,15},{8,0},{9,1},... | collective-permute-start | bytes 196616 | tf_op jit(solution)/shard_map/ppermute | solution.py:47
  16.9 6.4 %collective-permute-start.3 = (bf16[16,8192]{1,0:T(8,128)(2,1)S(1)}, bf16[16,8192]{1,0:T(8,128)(2,1)S(1)}, u32[]{:S(2)}, u32[]{:S(2)}) collective-permute-start(bf16[16,8192]{1,0:T(8,128)(2,1)S(1)} %get-tuple-element.8), channel_id=1, source_target_pairs={{0,4},{1,5},{2,6},{3,7},{4,0},{5,1},{6,2},{7,3},{8,12},{9,13},{10,... | collective-permute-start | bytes 786440 | tf_op jit(solution)/shard_map/ppermute | solution.py:38
  18.5 9.2 %collective-permute-start.10 = (bf16[16,8192]{1,0:T(8,128)(2,1)S(1)}, bf16[16,8192]{1,0:T(8,128)(2,1)S(1)}, u32[]{:S(2)}, u32[]{:S(2)}) collective-permute-start(bf16[16,8192]{1,0:T(8,128)(2,1)S(1)} %get-tuple-element.17), channel_id=1, source_target_pairs={{0,2},{1,3},{2,0},{3,1},{4,6},{5,7},{6,4},{7,5},{8,10},{9,11},{10,... | collective-permute-start | bytes 786440 | tf_op jit(solution)/shard_map/ppermute | solution.py:38
  23.4 12.8 %collective-permute-start.4 = (bf16[32,8192]{1,0:T(8,128)(2,1)S(1)}, bf16[32,8192]{1,0:T(8,128)(2,1)S(1)}, u32[]{:S(2)}, u32[]{:S(2)}) collective-permute-start(bf16[32,8192]{1,0:T(8,128)(2,1)S(1)} %constant_dynamic-update-slice_fusion.refs_0_), channel_id=1, source_target_pairs={{0,2},{1,3},{2,0},{3,1},{4,6},{5,7},{6,4},{7,5},{8,10},{9,11},{10,... | collective-permute-start | bytes 1572872 | tf_op jit(solution)/shard_map/ppermute | solution.py:38
  27.7 47.9 %copy-start.2 = (s32[128]{0:T(128)S(1)}, s32[128]{0:T(128)}, u32[]{:S(2)}) copy-start(s32[128]{0:T(128)} %param.17) | copy-start | bytes 1540
  27.7 56.1 %copy-start = (bf16[8,3,64,64]{3,2,1,0:T(8,128)(2,1)S(1)}, bf16[8,3,64,64]{3,2,1,0:T(8,128)(2,1)}, u32[]{:S(2)}) copy-start(bf16[8,3,64,64]{3,2,1,0:T(8,128)(2,1)} %targets.1) | copy-start | bytes 589828
  27.8 56.1 %copy-start.1 = (s32[8]{0:T(128)S(1)}, s32[8]{0:T(128)}, u32[]{:S(2)}) copy-start(s32[8]{0:T(128)} %param.19) | copy-start | bytes 100
  27.8 9.2 %collective-permute-start.11 = (bf16[32,8192]{1,0:T(8,128)(2,1)S(1)}, bf16[32,8192]{1,0:T(8,128)(2,1)S(1)}, u32[]{:S(2)}, u32[]{:S(2)}) collective-permute-start(bf16[32,8192]{1,0:T(8,128)(2,1)S(1)} %pad_maximum_fusion.refs_4_), channel_id=1, source_target_pairs={{0,4},{1,5},{2,6},{3,7},{4,0},{5,1},{6,2},{7,3},{8,12},{9,13},{10,... | collective-permute-start | bytes 1572872 | tf_op jit(solution)/shard_map/ppermute | solution.py:38
  27.8 9.2 %collective-permute-start.5 = (bf16[32,8192]{1,0:T(8,128)(2,1)S(1)}, bf16[32,8192]{1,0:T(8,128)(2,1)S(1)}, u32[]{:S(2)}, u32[]{:S(2)}) collective-permute-start(bf16[32,8192]{1,0:T(8,128)(2,1)S(1)} %constant_dynamic-update-slice_fusion.refs_0_), channel_id=1, source_target_pairs={{0,1},{1,0},{2,3},{3,2},{4,5},{5,4},{6,7},{7,6},{8,9},{9,8},{10,11... | collective-permute-start | bytes 1572872 | tf_op jit(solution)/shard_map/ppermute | solution.py:38
  27.9 9.1 %collective-permute-start.12 = (bf16[32,8192]{1,0:T(8,128)(2,1)S(1)}, bf16[32,8192]{1,0:T(8,128)(2,1)S(1)}, u32[]{:S(2)}, u32[]{:S(2)}) collective-permute-start(bf16[32,8192]{1,0:T(8,128)(2,1)S(1)} %pad_maximum_fusion.refs_4_), channel_id=1, source_target_pairs={{0,1},{1,0},{2,3},{3,2},{4,5},{5,4},{6,7},{7,6},{8,9},{9,8},{10,11... | collective-permute-start | bytes 1572872 | tf_op jit(solution)/shard_map/ppermute | solution.py:38
  36.2 1.9 %collective-permute-start.6 = (bf16[32,8192]{1,0:T(8,128)(2,1)S(1)}, bf16[32,8192]{1,0:T(8,128)(2,1)S(1)}, u32[]{:S(2)}, u32[]{:S(2)}) collective-permute-start(bf16[32,8192]{1,0:T(8,128)(2,1)S(1)} %collective-permute-done.4.refs_1_), channel_id=1, source_target_pairs={{0,1},{1,0},{2,3},{3,2},{4,5},{5,4},{6,7},{7,6},{8,9},{9,8},{10,11... | collective-permute-start | bytes 1572872 | tf_op jit(solution)/shard_map/ppermute | solution.py:38
  37.0 1.9 %collective-permute-start.13 = (bf16[32,8192]{1,0:T(8,128)(2,1)S(1)}, bf16[32,8192]{1,0:T(8,128)(2,1)S(1)}, u32[]{:S(2)}, u32[]{:S(2)}) collective-permute-start(bf16[32,8192]{1,0:T(8,128)(2,1)S(1)} %collective-permute-done.11.refs_5_), channel_id=1, source_target_pairs={{0,1},{1,0},{2,3},{3,2},{4,5},{5,4},{6,7},{7,6},{8,9},{9,8},{10,11... | collective-permute-start | bytes 1572872 | tf_op jit(solution)/shard_map/ppermute | solution.py:38
  73.0 10.8 %all-to-all-start.1 = ((bf16[32,16,128]{2,1,0:T(8,128)(2,1)}), bf16[32,16,128]{2,1,0:T(8,128)(2,1)S(1)}, u32[]{:S(2)}, u32[]{:S(2)}) async-start(bf16[32,16,128]{2,1,0:T(8,128)(2,1)} %sum_copies.1), calls=%async_computation.1 | async-start | bytes 262144 | tf_op jit(solution)/shard_map/all_to_all | solution.py:95
  85.2 10.8 %all-to-all-start.2 = ((f32[32,8,128]{2,1,0:T(8,128)}), f32[32,8,128]{2,1,0:T(8,128)S(1)}, u32[]{:S(2)}, u32[]{:S(2)}) async-start(f32[32,8,128]{2,1,0:T(8,128)} %target_products.1), calls=%async_computation.2 | async-start | bytes 262144 | tf_op jit(solution)/shard_map/all_to_all | solution.py:95

commit v12 on v11

--- a/solution.py
+++ b/solution.py
@@ -216,7 +216,7 @@
     count = int(np.prod(sizes))
     tokens = sum(piece.shape[0] for piece in in_pieces)
     model_cols = width // count
-    chunk = min(width, 2048)
+    chunk = min(width, 1024)
     block = hidden // 2 if hidden % 32 == 0 and hidden > 256 else hidden
     height = 16 * -(-2 * proj.shape[0] // (16 * count))
     return pl.pallas_call(
@@ -228,8 +228,8 @@
             pltpu.VMEM((3, hidden, tokens), F32),
             pltpu.VMEM((2, tokens, width), BF16),
             pltpu.VMEM((3, hidden, tokens), BF16),
-            pltpu.VMEM((2, 3, block, chunk), BF16),
-            pltpu.SemaphoreType.DMA((2, 3)),
+            pltpu.VMEM((4, 3, block, chunk), BF16),
+            pltpu.SemaphoreType.DMA((4, 3)),
         ],
         compiler_params=pltpu.CompilerParams(vmem_limit_bytes=44 * 2**20),
         cost_estimate=pl.CostEstimate(
@@ -296,9 +296,9 @@
         total += jnp.sum(turned.reshape(examples, rank, tokens) * left.astype(F32)[None], 1)
     domain = lax.broadcasted_iota(jnp.int32, (DOMAINS, examples), 0)
     domains = (domains[...] == domain).astype(F32)
-    total = jnp.dot(domains, total, precision=HIGHEST, preferred_element_type=F32)
+    total = sum(domains[:, e : e + 1] * total[e : e + 1, :] for e in range(examples))
     scores = transposed_dot(onehot_of(ids[...], tokens), total, HIGHEST)
-    counts = transposed_dot(jnp.ones((SEQS // 2, examples), F32), domains, HIGHEST)
+    counts = transposed_dot(jnp.ones((SEQS // 2, examples), BF16), domains.astype(BF16))
     rest = out.shape[2] - 3 * DOMAINS
     parts = [scores[: SEQS // 2], scores[SEQS // 2 :], counts, jnp.zeros((SEQS // 2, rest), F32)]
     parts = jnp.concatenate(parts, 1)

time: 97.1 us -> 100 us (1.030)
  Pallas kernels: 22.8 us -> 26.2 us
    pallas_call x1, Pallas kernels: 18.3 us -> 21.8 us  [products(): pl.pallas_call(functools.partial(product_kernel, backs, sizes, model_cols...]
where the time goes in v12:
time: 100 us
  waiting for transfers between devices  36.5 us (36%)
  Pallas kernels  26.2 us (26%)
  starting transfers between devices  19 us (19%)
  blocking collectives  15.1 us (15%)
  other arithmetic  2.32 us (2%)
    pallas_call x1, Pallas kernels, products(): pl.pallas_call(functools.partial(product_kernel, backs, sizes, model_cols...  21.8 us
    ppermute x8, waiting for transfers between devices, shift(): return lax.ppermute(value, 'dp', pairs)  16.5 us
    all_to_all x1, blocking collectives, exchange(): lax.all_to_all(blocks, 'dp', split_axis=0, concat_axis=0, axis_index_grou...  15.1 us
    all_to_all x2, waiting for transfers between devices, exchange(): lax.all_to_all(blocks, 'dp', split_axis=0, concat_axis=0, axis_index_grou...  14.6 us
    ppermute x6, starting transfers between devices, partner(): return lax.ppermute(value, 'dp', pairs)  8.58 us
    ppermute x8, starting transfers between devices, shift(): return lax.ppermute(value, 'dp', pairs)  5.33 us
    ppermute x6, waiting for transfers between devices, partner(): return lax.ppermute(value, 'dp', pairs)  5.32 us
    all_to_all x2, starting transfers between devices, exchange(): lax.all_to_all(blocks, 'dp', split_axis=0, concat_axis=0, axis_index_grou...  5.14 us
  transfers between devices with their start and end apart: 16, of which 11 were waited for; matrix products, arithmetic and copies ran while one was open for 2% of the time, Pallas kernels for 2%

profile of v12, /device:TPU:0, one launch (start us, length us, event | category | flops | bytes accessed | tf_op | source)
XLA Modules:
  0.0 100.2 jit_solution(15963587567208474829)
XLA Ops:
  0.6 4.1 %collective-permute-start.1 = (bf16[4,8192]{1,0:T(4,128)(2,1)}, bf16[4,8192]{1,0:T(4,128)(2,1)S(1)}, u32[]{:S(2)}, u32[]{:S(2)}) collective-permute-start(bf16[4,8192]{1,0:T(4,128)(2,1)} %param.10), channel_id=1, source_target_pairs={{0,16},{1,17},{2,18},{3,19},{4,20},{5,21},{6,22},{7,23},{8,24},{9,... | collective-permute-start | bytes 196616 | tf_op jit(solution)/shard_map/ppermute | solution.py:47
  4.7 1.6 %collective-permute-start = (bf16[4,8192]{1,0:T(4,128)(2,1)}, bf16[4,8192]{1,0:T(4,128)(2,1)S(1)}, u32[]{:S(2)}, u32[]{:S(2)}) collective-permute-start(bf16[4,8192]{1,0:T(4,128)(2,1)} %param.10), channel_id=1, source_target_pairs={{0,8},{1,9},{2,10},{3,11},{4,12},{5,13},{6,14},{7,15},{8,0},{9,1},... | collective-permute-start | bytes 196616 | tf_op jit(solution)/shard_map/ppermute | solution.py:47
  6.3 0.3 collective-permute-start.8
  6.6 0.2 collective-permute-start.7
  6.8 0.9 pad_maximum_fusion.4
  7.8 0.2 collective-permute-done.1
  8.0 2.2 %collective-permute-start.2 = (bf16[4,8192]{1,0:T(4,128)(2,1)S(1)}, bf16[4,8192]{1,0:T(4,128)(2,1)S(1)}, u32[]{:S(2)}, u32[]{:S(2)}) collective-permute-start(bf16[4,8192]{1,0:T(4,128)(2,1)S(1)} %collective-permute-done.1), channel_id=1, source_target_pairs={{0,8},{1,9},{2,10},{3,11},{4,12},{5,13},{6,14},{7,15},{8,0},{9,1},... | collective-permute-start | bytes 196616 | tf_op jit(solution)/shard_map/ppermute | solution.py:47
  10.2 2.2 %collective-permute-done.8 = bf16[4,8192]{1,0:T(4,128)(2,1)S(1)} collective-permute-done((bf16[4,8192]{1,0:T(4,128)(2,1)}, bf16[4,8192]{1,0:T(4,128)(2,1)S(1)}, u32[]{:S(2)}, u32[]{:S(2)}) %collective-permute-start.8) | collective-permute-done | bytes 65568 | tf_op jit(solution)/shard_map/ppermute | solution.py:47
  12.3 0.2 collective-permute-start.9
  12.5 1.0 %pad_maximum_fusion.1.refs_8_ = bf16[192,1152]{1,0:T(8,128)(2,1)S(1)} fusion(bf16[192,896]{1,0:T(8,128)(2,1)} %bitcast.5, bf16[192,256]{1,0:T(8,128)(2,1)} %bitcast.6), kind=kLoop, calls=%fused_computation.1 | loop fusion | flops 884736 | bytes 884736 | tf_op jit(solution)/shard_map/concatenate | solution.py:360
  13.6 0.0 collective-permute-done
  13.6 0.0 collective-permute-done.7
  13.6 0.0 collective-permute-done.2
  13.6 3.0 %collective-permute-done.9 = bf16[4,8192]{1,0:T(4,128)(2,1)S(1)} collective-permute-done((bf16[4,8192]{1,0:T(4,128)(2,1)S(1)}, bf16[4,8192]{1,0:T(4,128)(2,1)S(1)}, u32[]{:S(2)}, u32[]{:S(2)}) %collective-permute-start.9) | collective-permute-done | bytes 65568 | tf_op jit(solution)/shard_map/ppermute | solution.py:47
  16.6 0.3 pad_maximum_fusion.2
  16.9 1.6 %collective-permute-start.3 = (bf16[16,8192]{1,0:T(8,128)(2,1)S(1)}, bf16[16,8192]{1,0:T(8,128)(2,1)S(1)}, u32[]{:S(2)}, u32[]{:S(2)}) collective-permute-start(bf16[16,8192]{1,0:T(8,128)(2,1)S(1)} %get-tuple-element.8), channel_id=1, source_target_pairs={{0,4},{1,5},{2,6},{3,7},{4,0},{5,1},{6,2},{7,3},{8,12},{9,13},{10,... | collective-permute-start | bytes 786440 | tf_op jit(solution)/shard_map/ppermute | solution.py:38
  18.5 1.6 %collective-permute-start.10 = (bf16[16,8192]{1,0:T(8,128)(2,1)S(1)}, bf16[16,8192]{1,0:T(8,128)(2,1)S(1)}, u32[]{:S(2)}, u32[]{:S(2)}) collective-permute-start(bf16[16,8192]{1,0:T(8,128)(2,1)S(1)} %get-tuple-element.17), channel_id=1, source_target_pairs={{0,2},{1,3},{2,0},{3,1},{4,6},{5,7},{6,4},{7,5},{8,10},{9,11},{10,... | collective-permute-start | bytes 786440 | tf_op jit(solution)/shard_map/ppermute | solution.py:38
  20.1 3.3 %collective-permute-done.3 = bf16[16,8192]{1,0:T(8,128)(2,1)S(1)} collective-permute-done((bf16[16,8192]{1,0:T(8,128)(2,1)S(1)}, bf16[16,8192]{1,0:T(8,128)(2,1)S(1)}, u32[]{:S(2)}, u32[]{:S(2)}) %collective-permute-start.3) | collective-permute-done | bytes 262176 | tf_op jit(solution)/shard_map/ppermute | solution.py:38
  23.4 1.6 %collective-permute-start.4 = (bf16[32,8192]{1,0:T(8,128)(2,1)S(1)}, bf16[32,8192]{1,0:T(8,128)(2,1)S(1)}, u32[]{:S(2)}, u32[]{:S(2)}) collective-permute-start(bf16[32,8192]{1,0:T(8,128)(2,1)S(1)} %constant_dynamic-update-slice_fusion.refs_0_), channel_id=1, source_target_pairs={{0,2},{1,3},{2,0},{3,1},{4,6},{5,7},{6,4},{7,5},{8,10},{9,11},{10,... | collective-permute-start | bytes 1572872 | tf_op jit(solution)/shard_map/ppermute | solution.py:38
  24.9 2.8 %collective-permute-done.10 = bf16[16,8192]{1,0:T(8,128)(2,1)S(1)} collective-permute-done((bf16[16,8192]{1,0:T(8,128)(2,1)S(1)}, bf16[16,8192]{1,0:T(8,128)(2,1)S(1)}, u32[]{:S(2)}, u32[]{:S(2)}) %collective-permute-start.10) | collective-permute-done | bytes 262176 | tf_op jit(solution)/shard_map/ppermute | solution.py:38
  27.7 0.0 copy-start.2
  27.7 0.0 copy-start
  27.8 0.0 copy-start.1
  27.8 0.1 collective-permute-start.11
  27.8 0.1 collective-permute-start.5
  27.9 0.5 collective-permute-start.12
  28.4 7.8 %collective-permute-done.4.refs_1_ = bf16[32,8192]{1,0:T(8,128)(2,1)S(1)} collective-permute-done((bf16[32,8192]{1,0:T(8,128)(2,1)S(1)}, bf16[32,8192]{1,0:T(8,128)(2,1)S(1)}, u32[]{:S(2)}, u32[]{:S(2)}) %collective-permute-start.4) | collective-permute-done | bytes 524320 | tf_op jit(solution)/shard_map/ppermute | solution.py:38
  36.2 0.0 collective-permute-start.6
  36.2 0.8 collective-permute-done.11.refs_5_
  37.0 0.0 collective-permute-start.13
  37.0 0.0 collective-permute-done.5.refs_2_
  37.0 0.0 collective-permute-done.12.refs_6_
  37.0 1.1 %collective-permute-done.6.refs_3_ = bf16[32,8192]{1,0:T(8,128)(2,1)S(1)} collective-permute-done((bf16[32,8192]{1,0:T(8,128)(2,1)S(1)}, bf16[32,8192]{1,0:T(8,128)(2,1)S(1)}, u32[]{:S(2)}, u32[]{:S(2)}) %collective-permute-start.6) | collective-permute-done | bytes 524320 | tf_op jit(solution)/shard_map/ppermute | solution.py:38
  38.1 0.8 collective-permute-done.13.refs_7_
  38.9 21.8 %products.1 = f32[32,16,128]{2,1,0:T(8,128)S(1)} custom-call(bf16[32,8192]{1,0:T(8,128)(2,1)S(1)} %constant_dynamic-update-slice_fusion.refs_0_, bf16[32,8192]{1,0:T(8,128)(2,1)S(1)} %collective-permute-done.4.refs_1_, bf16[32,8192]{1,0:T(8,128)(2,1)S(1)} %collective-permute-done.5.refs_2_, bf16[32,8192]{1,0:T(8,128)(2,1)S(1)} %collective-permute-done.6.refs_3_, ...), custom_call_target="tpu_custom_call" | custom-call | flops 5637144576 | bytes 44040192 | tf_op jit(solution)/shard_map/products/pallas_call | solution.py:222
  60.8 15.1 %all_to_all.15.values = f32[32,16,128]{2,1,0:T(8,128)S(1)} all-to-all(f32[32,16,128]{2,1,0:T(8,128)S(1)} %products.1), channel_id=1, replica_groups=mesh['groups'=1,'dp'=32] {'dp'}, dimensions={0} | all-to-all | bytes 524288 | tf_op jit(solution)/shard_map/all_to_all | solution.py:95
  75.8 0.7 sum_copies.1
  76.5 2.6 %all-to-all-start.1 = ((bf16[32,16,128]{2,1,0:T(8,128)(2,1)}), bf16[32,16,128]{2,1,0:T(8,128)(2,1)S(1)}, u32[]{:S(2)}, u32[]{:S(2)}) async-start(bf16[32,16,128]{2,1,0:T(8,128)(2,1)} %sum_copies.1), calls=%async_computation.1 | async-start | bytes 262144 | tf_op jit(solution)/shard_map/all_to_all | solution.py:95
  79.1 0.0 copy-done.2
  79.1 0.1 reshape.7
  79.2 0.1 broadcast_in_dim_reshape.3.ids
  79.3 8.0 %all-to-all-done.1.vectors = bf16[32,16,128]{2,1,0:T(8,128)(2,1)S(1)} async-done(((bf16[32,16,128]{2,1,0:T(8,128)(2,1)}), bf16[32,16,128]{2,1,0:T(8,128)(2,1)S(1)}, u32[]{:S(2)}, u32[]{:S(2)}) %all-to-all-start.1) | async-done | bytes 131104 | tf_op jit(solution)/shard_map/all_to_all | solution.py:95
  87.3 0.0 copy-done
  87.3 1.2 %target_products.1 = f32[32,8,128]{2,1,0:T(8,128)} custom-call(bf16[32,16,128]{2,1,0:T(8,128)(2,1)S(1)} %all-to-all-done.1.vectors, s32[1,128]{1,0:T(1,128)S(1)} %broadcast_in_dim_reshape.3.ids, bf16[8,3,64,64]{3,2,1,0:T(8,128)(2,1)S(1)} %copy-done, s32[1,8]{1,0:T(1,128)S(1)} %bitcast.4), custom_call_target="tpu_custom_call" | custom-call | tf_op jit(solution)/shard_map/target_products/pallas_call | solution.py:375
  88.6 2.6 %all-to-all-start.2 = ((f32[32,8,128]{2,1,0:T(8,128)}), f32[32,8,128]{2,1,0:T(8,128)S(1)}, u32[]{:S(2)}, u32[]{:S(2)}) async-start(f32[32,8,128]{2,1,0:T(8,128)} %target_products.1), calls=%async_computation.2 | async-start | bytes 262144 | tf_op jit(solution)/shard_map/all_to_all | solution.py:95
  91.2 1.6 %sketches.1 = (f32[16,3,64,64]{3,2,1,0:T(8,128)}, f32[16,128]{1,0:T(8,128)S(1)}) custom-call(bf16[32,16,128]{2,1,0:T(8,128)(2,1)S(1)} %all-to-all-done.1.vectors, s32[1,128]{1,0:T(1,128)S(1)} %broadcast_in_dim_reshape.3.ids), custom_call_target="tpu_custom_call" | custom-call | tf_op jit(solution)/shard_map/sketches/pallas_call | solution.py:385
  92.8 6.6 %all-to-all-done.2.parts = f32[32,8,128]{2,1,0:T(8,128)S(1)} async-done(((f32[32,8,128]{2,1,0:T(8,128)}), f32[32,8,128]{2,1,0:T(8,128)S(1)}, u32[]{:S(2)}, u32[]{:S(2)}) %all-to-all-start.2) | async-done | bytes 131104 | tf_op jit(solution)/shard_map/all_to_all | solution.py:95
  99.4 0.8 scores.1
  (6 shorter events, 0.1 us)
Async XLA Ops:
  0.6 7.4 %collective-permute-start.1 = (bf16[4,8192]{1,0:T(4,128)(2,1)}, bf16[4,8192]{1,0:T(4,128)(2,1)S(1)}, u32[]{:S(2)}, u32[]{:S(2)}) collective-permute-start(bf16[4,8192]{1,0:T(4,128)(2,1)} %param.10), channel_id=1, source_target_pairs={{0,16},{1,17},{2,18},{3,19},{4,20},{5,21},{6,22},{7,23},{8,24},{9,... | collective-permute-start | bytes 196616 | tf_op jit(solution)/shard_map/ppermute | solution.py:47
  4.7 8.8 %collective-permute-start = (bf16[4,8192]{1,0:T(4,128)(2,1)}, bf16[4,8192]{1,0:T(4,128)(2,1)S(1)}, u32[]{:S(2)}, u32[]{:S(2)}) collective-permute-start(bf16[4,8192]{1,0:T(4,128)(2,1)} %param.10), channel_id=1, source_target_pairs={{0,8},{1,9},{2,10},{3,11},{4,12},{5,13},{6,14},{7,15},{8,0},{9,1},... | collective-permute-start | bytes 196616 | tf_op jit(solution)/shard_map/ppermute | solution.py:47
  6.3 6.0 %collective-permute-start.8 = (bf16[4,8192]{1,0:T(4,128)(2,1)}, bf16[4,8192]{1,0:T(4,128)(2,1)S(1)}, u32[]{:S(2)}, u32[]{:S(2)}) collective-permute-start(bf16[4,8192]{1,0:T(4,128)(2,1)} %param.11), channel_id=1, source_target_pairs={{0,16},{1,17},{2,18},{3,19},{4,20},{5,21},{6,22},{7,23},{8,24},{9,... | collective-permute-start | bytes 196616 | tf_op jit(solution)/shard_map/ppermute | solution.py:47
  6.6 6.9 %collective-permute-start.7 = (bf16[4,8192]{1,0:T(4,128)(2,1)}, bf16[4,8192]{1,0:T(4,128)(2,1)S(1)}, u32[]{:S(2)}, u32[]{:S(2)}) collective-permute-start(bf16[4,8192]{1,0:T(4,128)(2,1)} %param.11), channel_id=1, source_target_pairs={{0,8},{1,9},{2,10},{3,11},{4,12},{5,13},{6,14},{7,15},{8,0},{9,1},... | collective-permute-start | bytes 196616 | tf_op jit(solution)/shard_map/ppermute | solution.py:47
  8.0 5.6 %collective-permute-start.2 = (bf16[4,8192]{1,0:T(4,128)(2,1)S(1)}, bf16[4,8192]{1,0:T(4,128)(2,1)S(1)}, u32[]{:S(2)}, u32[]{:S(2)}) collective-permute-start(bf16[4,8192]{1,0:T(4,128)(2,1)S(1)} %collective-permute-done.1), channel_id=1, source_target_pairs={{0,8},{1,9},{2,10},{3,11},{4,12},{5,13},{6,14},{7,15},{8,0},{9,1},... | collective-permute-start | bytes 196616 | tf_op jit(solution)/shard_map/ppermute | solution.py:47
  12.3 4.3 %collective-permute-start.9 = (bf16[4,8192]{1,0:T(4,128)(2,1)S(1)}, bf16[4,8192]{1,0:T(4,128)(2,1)S(1)}, u32[]{:S(2)}, u32[]{:S(2)}) collective-permute-start(bf16[4,8192]{1,0:T(4,128)(2,1)S(1)} %collective-permute-done.8), channel_id=1, source_target_pairs={{0,8},{1,9},{2,10},{3,11},{4,12},{5,13},{6,14},{7,15},{8,0},{9,1},... | collective-permute-start | bytes 196616 | tf_op jit(solution)/shard_map/ppermute | solution.py:47
  16.9 6.4 %collective-permute-start.3 = (bf16[16,8192]{1,0:T(8,128)(2,1)S(1)}, bf16[16,8192]{1,0:T(8,128)(2,1)S(1)}, u32[]{:S(2)}, u32[]{:S(2)}) collective-permute-start(bf16[16,8192]{1,0:T(8,128)(2,1)S(1)} %get-tuple-element.8), channel_id=1, source_target_pairs={{0,4},{1,5},{2,6},{3,7},{4,0},{5,1},{6,2},{7,3},{8,12},{9,13},{10,... | collective-permute-start | bytes 786440 | tf_op jit(solution)/shard_map/ppermute | solution.py:38
  18.5 9.2 %collective-permute-start.10 = (bf16[16,8192]{1,0:T(8,128)(2,1)S(1)}, bf16[16,8192]{1,0:T(8,128)(2,1)S(1)}, u32[]{:S(2)}, u32[]{:S(2)}) collective-permute-start(bf16[16,8192]{1,0:T(8,128)(2,1)S(1)} %get-tuple-element.17), channel_id=1, source_target_pairs={{0,2},{1,3},{2,0},{3,1},{4,6},{5,7},{6,4},{7,5},{8,10},{9,11},{10,... | collective-permute-start | bytes 786440 | tf_op jit(solution)/shard_map/ppermute | solution.py:38
  23.4 12.8 %collective-permute-start.4 = (bf16[32,8192]{1,0:T(8,128)(2,1)S(1)}, bf16[32,8192]{1,0:T(8,128)(2,1)S(1)}, u32[]{:S(2)}, u32[]{:S(2)}) collective-permute-start(bf16[32,8192]{1,0:T(8,128)(2,1)S(1)} %constant_dynamic-update-slice_fusion.refs_0_), channel_id=1, source_target_pairs={{0,2},{1,3},{2,0},{3,1},{4,6},{5,7},{6,4},{7,5},{8,10},{9,11},{10,... | collective-permute-start | bytes 1572872 | tf_op jit(solution)/shard_map/ppermute | solution.py:38
  27.7 51.4 %copy-start.2 = (s32[128]{0:T(128)S(1)}, s32[128]{0:T(128)}, u32[]{:S(2)}) copy-start(s32[128]{0:T(128)} %param.17) | copy-start | bytes 1540
  27.7 59.6 %copy-start = (bf16[8,3,64,64]{3,2,1,0:T(8,128)(2,1)S(1)}, bf16[8,3,64,64]{3,2,1,0:T(8,128)(2,1)}, u32[]{:S(2)}) copy-start(bf16[8,3,64,64]{3,2,1,0:T(8,128)(2,1)} %targets.1) | copy-start | bytes 589828
  27.8 59.6 %copy-start.1 = (s32[8]{0:T(128)S(1)}, s32[8]{0:T(128)}, u32[]{:S(2)}) copy-start(s32[8]{0:T(128)} %param.19) | copy-start | bytes 100
  27.8 9.2 %collective-permute-start.11 = (bf16[32,8192]{1,0:T(8,128)(2,1)S(1)}, bf16[32,8192]{1,0:T(8,128)(2,1)S(1)}, u32[]{:S(2)}, u32[]{:S(2)}) collective-permute-start(bf16[32,8192]{1,0:T(8,128)(2,1)S(1)} %pad_maximum_fusion.refs_4_), channel_id=1, source_target_pairs={{0,4},{1,5},{2,6},{3,7},{4,0},{5,1},{6,2},{7,3},{8,12},{9,13},{10,... | collective-permute-start | bytes 1572872 | tf_op jit(solution)/shard_map/ppermute | solution.py:38
  27.8 9.2 %collective-permute-start.5 = (bf16[32,8192]{1,0:T(8,128)(2,1)S(1)}, bf16[32,8192]{1,0:T(8,128)(2,1)S(1)}, u32[]{:S(2)}, u32[]{:S(2)}) collective-permute-start(bf16[32,8192]{1,0:T(8,128)(2,1)S(1)} %constant_dynamic-update-slice_fusion.refs_0_), channel_id=1, source_target_pairs={{0,1},{1,0},{2,3},{3,2},{4,5},{5,4},{6,7},{7,6},{8,9},{9,8},{10,11... | collective-permute-start | bytes 1572872 | tf_op jit(solution)/shard_map/ppermute | solution.py:38
  27.9 9.1 %collective-permute-start.12 = (bf16[32,8192]{1,0:T(8,128)(2,1)S(1)}, bf16[32,8192]{1,0:T(8,128)(2,1)S(1)}, u32[]{:S(2)}, u32[]{:S(2)}) collective-permute-start(bf16[32,8192]{1,0:T(8,128)(2,1)S(1)} %pad_maximum_fusion.refs_4_), channel_id=1, source_target_pairs={{0,1},{1,0},{2,3},{3,2},{4,5},{5,4},{6,7},{7,6},{8,9},{9,8},{10,11... | collective-permute-start | bytes 1572872 | tf_op jit(solution)/shard_map/ppermute | solution.py:38
  36.2 1.9 %collective-permute-start.6 = (bf16[32,8192]{1,0:T(8,128)(2,1)S(1)}, bf16[32,8192]{1,0:T(8,128)(2,1)S(1)}, u32[]{:S(2)}, u32[]{:S(2)}) collective-permute-start(bf16[32,8192]{1,0:T(8,128)(2,1)S(1)} %collective-permute-done.4.refs_1_), channel_id=1, source_target_pairs={{0,1},{1,0},{2,3},{3,2},{4,5},{5,4},{6,7},{7,6},{8,9},{9,8},{10,11... | collective-permute-start | bytes 1572872 | tf_op jit(solution)/shard_map/ppermute | solution.py:38
  37.0 1.9 %collective-permute-start.13 = (bf16[32,8192]{1,0:T(8,128)(2,1)S(1)}, bf16[32,8192]{1,0:T(8,128)(2,1)S(1)}, u32[]{:S(2)}, u32[]{:S(2)}) collective-permute-start(bf16[32,8192]{1,0:T(8,128)(2,1)S(1)} %collective-permute-done.11.refs_5_), channel_id=1, source_target_pairs={{0,1},{1,0},{2,3},{3,2},{4,5},{5,4},{6,7},{7,6},{8,9},{9,8},{10,11... | collective-permute-start | bytes 1572872 | tf_op jit(solution)/shard_map/ppermute | solution.py:38
  76.5 10.8 %all-to-all-start.1 = ((bf16[32,16,128]{2,1,0:T(8,128)(2,1)}), bf16[32,16,128]{2,1,0:T(8,128)(2,1)S(1)}, u32[]{:S(2)}, u32[]{:S(2)}) async-start(bf16[32,16,128]{2,1,0:T(8,128)(2,1)} %sum_copies.1), calls=%async_computation.1 | async-start | bytes 262144 | tf_op jit(solution)/shard_map/all_to_all | solution.py:95
  88.6 10.8 %all-to-all-start.2 = ((f32[32,8,128]{2,1,0:T(8,128)}), f32[32,8,128]{2,1,0:T(8,128)S(1)}, u32[]{:S(2)}, u32[]{:S(2)}) async-start(f32[32,8,128]{2,1,0:T(8,128)} %target_products.1), calls=%async_computation.2 | async-start | bytes 262144 | tf_op jit(solution)/shard_map/all_to_all | solution.py:95

commit v13 on v12

--- a/solution.py
+++ b/solution.py
@@ -154,18 +154,30 @@
     place_pieces(out_pieces, backs[1], sizes, tokens.at[1])
     sums[...] = jnp.zeros_like(sums)
 
-    @pl.loop(0, total)
+    def add(step, w):
+        rows, columns = places(step)
+        sums[w, rows, :] += transposed_dot(
+            buffers[lax.rem(step, depth), w], tokens[sides[w], :, columns]
+        )
+
+    def refill(step):
+        @pl.when(step + depth < total)
+        def _():
+            for w in range(3):
+                copy(step + depth, w).start()
+
+    for w in range(3):
+        copy(0, w).wait()
+        add(0, w)
+    refill(0)
+
+    @pl.loop(1, total)
     def _(step):
-        rows, columns = places(step)
         for w in range(3):
             copy(step, w).wait()
-            sums[w, rows, :] += transposed_dot(
-                buffers[lax.rem(step, depth), w], tokens[sides[w], :, columns]
-            )
-
-            @pl.when(step + depth < total)
-            def _():
-                copy(step + depth, w).start()
+        for w in range(3):
+            add(step, w)
+        refill(step)
 
     rank = proj.shape[0] // 3
     window = proj.shape[1] - hidden_units
@@ -216,7 +228,7 @@
     count = int(np.prod(sizes))
     tokens = sum(piece.shape[0] for piece in in_pieces)
     model_cols = width // count
-    chunk = min(width, 1024)
+    chunk = min(width, 2048)
     block = hidden // 2 if hidden % 32 == 0 and hidden > 256 else hidden
     height = 16 * -(-2 * proj.shape[0] // (16 * count))
     return pl.pallas_call(
@@ -228,8 +240,8 @@
             pltpu.VMEM((3, hidden, tokens), F32),
             pltpu.VMEM((2, tokens, width), BF16),
             pltpu.VMEM((3, hidden, tokens), BF16),
-            pltpu.VMEM((4, 3, block, chunk), BF16),
-            pltpu.SemaphoreType.DMA((4, 3)),
+            pltpu.VMEM((3, 3, block, chunk), BF16),
+            pltpu.SemaphoreType.DMA((3, 3)),
         ],
         compiler_params=pltpu.CompilerParams(vmem_limit_bytes=44 * 2**20),
         cost_estimate=pl.CostEstimate(

time: 100 us -> 95.5 us (0.955)
  Pallas kernels: 26.2 us -> 21.2 us
    pallas_call x1, Pallas kernels: 21.8 us -> 16.9 us  [products(): pl.pallas_call(functools.partial(product_kernel, backs, sizes, model_cols...]
where the time goes in v13:
time: 95.5 us; the launch traced here: 95.2 us
  waiting for transfers between devices  36.5 us (38%)
  Pallas kernels  21.2 us (22%)
  starting transfers between devices  19 us (20%)
  blocking collectives  15.1 us (16%)
  other arithmetic  2.32 us (2%)
    pallas_call x1, Pallas kernels, products(): pl.pallas_call(functools.partial(product_kernel, backs, sizes, model_cols...  16.9 us
    ppermute x8, waiting for transfers between devices, shift(): return lax.ppermute(value, 'dp', pairs)  16.5 us
    all_to_all x1, blocking collectives, exchange(): lax.all_to_all(blocks, 'dp', split_axis=0, concat_axis=0, axis_index_grou...  15.1 us
    all_to_all x2, waiting for transfers between devices, exchange(): lax.all_to_all(blocks, 'dp', split_axis=0, concat_axis=0, axis_index_grou...  14.6 us
    ppermute x6, starting transfers between devices, partner(): return lax.ppermute(value, 'dp', pairs)  8.58 us
    ppermute x8, starting transfers between devices, shift(): return lax.ppermute(value, 'dp', pairs)  5.33 us
    ppermute x6, waiting for transfers between devices, partner(): return lax.ppermute(value, 'dp', pairs)  5.32 us
    all_to_all x2, starting transfers between devices, exchange(): lax.all_to_all(blocks, 'dp', split_axis=0, concat_axis=0, axis_index_grou...  5.14 us
  transfers between devices with their start and end apart: 16, of which 11 were waited for; matrix products, arithmetic and copies ran while one was open for 2% of the time, Pallas kernels for 2%

profile of v13, /device:TPU:0, one launch (start us, length us, event | category | flops | bytes accessed | tf_op | source)
XLA Modules:
  0.0 95.2 jit_solution(15292256735751848497)
XLA Ops:
  0.6 4.1 %collective-permute-start.1 = (bf16[4,8192]{1,0:T(4,128)(2,1)}, bf16[4,8192]{1,0:T(4,128)(2,1)S(1)}, u32[]{:S(2)}, u32[]{:S(2)}) collective-permute-start(bf16[4,8192]{1,0:T(4,128)(2,1)} %param.10), channel_id=1, source_target_pairs={{0,16},{1,17},{2,18},{3,19},{4,20},{5,21},{6,22},{7,23},{8,24},{9,... | collective-permute-start | bytes 196616 | tf_op jit(solution)/shard_map/ppermute | solution.py:47
  4.7 1.6 %collective-permute-start = (bf16[4,8192]{1,0:T(4,128)(2,1)}, bf16[4,8192]{1,0:T(4,128)(2,1)S(1)}, u32[]{:S(2)}, u32[]{:S(2)}) collective-permute-start(bf16[4,8192]{1,0:T(4,128)(2,1)} %param.10), channel_id=1, source_target_pairs={{0,8},{1,9},{2,10},{3,11},{4,12},{5,13},{6,14},{7,15},{8,0},{9,1},... | collective-permute-start | bytes 196616 | tf_op jit(solution)/shard_map/ppermute | solution.py:47
  6.3 0.3 collective-permute-start.8
  6.6 0.2 collective-permute-start.7
  6.8 0.9 pad_maximum_fusion.4
  7.8 0.2 collective-permute-done.1
  8.0 2.2 %collective-permute-start.2 = (bf16[4,8192]{1,0:T(4,128)(2,1)S(1)}, bf16[4,8192]{1,0:T(4,128)(2,1)S(1)}, u32[]{:S(2)}, u32[]{:S(2)}) collective-permute-start(bf16[4,8192]{1,0:T(4,128)(2,1)S(1)} %collective-permute-done.1), channel_id=1, source_target_pairs={{0,8},{1,9},{2,10},{3,11},{4,12},{5,13},{6,14},{7,15},{8,0},{9,1},... | collective-permute-start | bytes 196616 | tf_op jit(solution)/shard_map/ppermute | solution.py:47
  10.2 2.2 %collective-permute-done.8 = bf16[4,8192]{1,0:T(4,128)(2,1)S(1)} collective-permute-done((bf16[4,8192]{1,0:T(4,128)(2,1)}, bf16[4,8192]{1,0:T(4,128)(2,1)S(1)}, u32[]{:S(2)}, u32[]{:S(2)}) %collective-permute-start.8) | collective-permute-done | bytes 65568 | tf_op jit(solution)/shard_map/ppermute | solution.py:47
  12.3 0.2 collective-permute-start.9
  12.5 1.0 %pad_maximum_fusion.1.refs_8_ = bf16[192,1152]{1,0:T(8,128)(2,1)S(1)} fusion(bf16[192,896]{1,0:T(8,128)(2,1)} %bitcast.5, bf16[192,256]{1,0:T(8,128)(2,1)} %bitcast.6), kind=kLoop, calls=%fused_computation.1 | loop fusion | flops 884736 | bytes 884736 | tf_op jit(solution)/shard_map/concatenate | solution.py:372
  13.6 0.0 collective-permute-done
  13.6 0.0 collective-permute-done.7
  13.6 0.0 collective-permute-done.2
  13.6 3.0 %collective-permute-done.9 = bf16[4,8192]{1,0:T(4,128)(2,1)S(1)} collective-permute-done((bf16[4,8192]{1,0:T(4,128)(2,1)S(1)}, bf16[4,8192]{1,0:T(4,128)(2,1)S(1)}, u32[]{:S(2)}, u32[]{:S(2)}) %collective-permute-start.9) | collective-permute-done | bytes 65568 | tf_op jit(solution)/shard_map/ppermute | solution.py:47
  16.6 0.3 pad_maximum_fusion.2
  16.9 1.6 %collective-permute-start.3 = (bf16[16,8192]{1,0:T(8,128)(2,1)S(1)}, bf16[16,8192]{1,0:T(8,128)(2,1)S(1)}, u32[]{:S(2)}, u32[]{:S(2)}) collective-permute-start(bf16[16,8192]{1,0:T(8,128)(2,1)S(1)} %get-tuple-element.8), channel_id=1, source_target_pairs={{0,4},{1,5},{2,6},{3,7},{4,0},{5,1},{6,2},{7,3},{8,12},{9,13},{10,... | collective-permute-start | bytes 786440 | tf_op jit(solution)/shard_map/ppermute | solution.py:38
  18.5 1.6 %collective-permute-start.10 = (bf16[16,8192]{1,0:T(8,128)(2,1)S(1)}, bf16[16,8192]{1,0:T(8,128)(2,1)S(1)}, u32[]{:S(2)}, u32[]{:S(2)}) collective-permute-start(bf16[16,8192]{1,0:T(8,128)(2,1)S(1)} %get-tuple-element.17), channel_id=1, source_target_pairs={{0,2},{1,3},{2,0},{3,1},{4,6},{5,7},{6,4},{7,5},{8,10},{9,11},{10,... | collective-permute-start | bytes 786440 | tf_op jit(solution)/shard_map/ppermute | solution.py:38
  20.1 3.3 %collective-permute-done.3 = bf16[16,8192]{1,0:T(8,128)(2,1)S(1)} collective-permute-done((bf16[16,8192]{1,0:T(8,128)(2,1)S(1)}, bf16[16,8192]{1,0:T(8,128)(2,1)S(1)}, u32[]{:S(2)}, u32[]{:S(2)}) %collective-permute-start.3) | collective-permute-done | bytes 262176 | tf_op jit(solution)/shard_map/ppermute | solution.py:38
  23.4 1.6 %collective-permute-start.4 = (bf16[32,8192]{1,0:T(8,128)(2,1)S(1)}, bf16[32,8192]{1,0:T(8,128)(2,1)S(1)}, u32[]{:S(2)}, u32[]{:S(2)}) collective-permute-start(bf16[32,8192]{1,0:T(8,128)(2,1)S(1)} %constant_dynamic-update-slice_fusion.refs_0_), channel_id=1, source_target_pairs={{0,2},{1,3},{2,0},{3,1},{4,6},{5,7},{6,4},{7,5},{8,10},{9,11},{10,... | collective-permute-start | bytes 1572872 | tf_op jit(solution)/shard_map/ppermute | solution.py:38
  24.9 2.8 %collective-permute-done.10 = bf16[16,8192]{1,0:T(8,128)(2,1)S(1)} collective-permute-done((bf16[16,8192]{1,0:T(8,128)(2,1)S(1)}, bf16[16,8192]{1,0:T(8,128)(2,1)S(1)}, u32[]{:S(2)}, u32[]{:S(2)}) %collective-permute-start.10) | collective-permute-done | bytes 262176 | tf_op jit(solution)/shard_map/ppermute | solution.py:38
  27.7 0.0 copy-start.2
  27.7 0.0 copy-start
  27.8 0.0 copy-start.1
  27.8 0.1 collective-permute-start.11
  27.8 0.1 collective-permute-start.5
  27.9 0.5 collective-permute-start.12
  28.4 7.8 %collective-permute-done.4.refs_1_ = bf16[32,8192]{1,0:T(8,128)(2,1)S(1)} collective-permute-done((bf16[32,8192]{1,0:T(8,128)(2,1)S(1)}, bf16[32,8192]{1,0:T(8,128)(2,1)S(1)}, u32[]{:S(2)}, u32[]{:S(2)}) %collective-permute-start.4) | collective-permute-done | bytes 524320 | tf_op jit(solution)/shard_map/ppermute | solution.py:38
  36.2 0.0 collective-permute-start.6
  36.2 0.8 collective-permute-done.11.refs_5_
  37.0 0.0 collective-permute-start.13
  37.0 0.0 collective-permute-done.5.refs_2_
  37.0 0.0 collective-permute-done.12.refs_6_
  37.0 1.1 %collective-permute-done.6.refs_3_ = bf16[32,8192]{1,0:T(8,128)(2,1)S(1)} collective-permute-done((bf16[32,8192]{1,0:T(8,128)(2,1)S(1)}, bf16[32,8192]{1,0:T(8,128)(2,1)S(1)}, u32[]{:S(2)}, u32[]{:S(2)}) %collective-permute-start.6) | collective-permute-done | bytes 524320 | tf_op jit(solution)/shard_map/ppermute | solution.py:38
  38.1 0.8 collective-permute-done.13.refs_7_
  38.9 16.9 %products.1 = f32[32,16,128]{2,1,0:T(8,128)S(1)} custom-call(bf16[32,8192]{1,0:T(8,128)(2,1)S(1)} %constant_dynamic-update-slice_fusion.refs_0_, bf16[32,8192]{1,0:T(8,128)(2,1)S(1)} %collective-permute-done.4.refs_1_, bf16[32,8192]{1,0:T(8,128)(2,1)S(1)} %collective-permute-done.5.refs_2_, bf16[32,8192]{1,0:T(8,128)(2,1)S(1)} %collective-permute-done.6.refs_3_, ...), custom_call_target="tpu_custom_call" | custom-call | flops 5637144576 | bytes 44040192 | tf_op jit(solution)/shard_map/products/pallas_call | solution.py:234
  55.8 15.1 %all_to_all.15.values = f32[32,16,128]{2,1,0:T(8,128)S(1)} all-to-all(f32[32,16,128]{2,1,0:T(8,128)S(1)} %products.1), channel_id=1, replica_groups=mesh['groups'=1,'dp'=32] {'dp'}, dimensions={0} | all-to-all | bytes 524288 | tf_op jit(solution)/shard_map/all_to_all | solution.py:95
  70.9 0.7 sum_copies.1
  71.6 2.6 %all-to-all-start.1 = ((bf16[32,16,128]{2,1,0:T(8,128)(2,1)}), bf16[32,16,128]{2,1,0:T(8,128)(2,1)S(1)}, u32[]{:S(2)}, u32[]{:S(2)}) async-start(bf16[32,16,128]{2,1,0:T(8,128)(2,1)} %sum_copies.1), calls=%async_computation.1 | async-start | bytes 262144 | tf_op jit(solution)/shard_map/all_to_all | solution.py:95
  74.2 0.0 copy-done.2
  74.2 0.1 reshape.7
  74.3 0.1 broadcast_in_dim_reshape.3.ids
  74.4 8.0 %all-to-all-done.1.vectors = bf16[32,16,128]{2,1,0:T(8,128)(2,1)S(1)} async-done(((bf16[32,16,128]{2,1,0:T(8,128)(2,1)}), bf16[32,16,128]{2,1,0:T(8,128)(2,1)S(1)}, u32[]{:S(2)}, u32[]{:S(2)}) %all-to-all-start.1) | async-done | bytes 131104 | tf_op jit(solution)/shard_map/all_to_all | solution.py:95
  82.4 0.0 copy-done.1
  82.4 1.3 %target_products.1 = f32[32,8,128]{2,1,0:T(8,128)} custom-call(bf16[32,16,128]{2,1,0:T(8,128)(2,1)S(1)} %all-to-all-done.1.vectors, s32[1,128]{1,0:T(1,128)S(1)} %broadcast_in_dim_reshape.3.ids, bf16[8,3,64,64]{3,2,1,0:T(8,128)(2,1)S(1)} %copy-done, s32[1,8]{1,0:T(1,128)S(1)} %bitcast.4), custom_call_target="tpu_custom_call" | custom-call | tf_op jit(solution)/shard_map/target_products/pallas_call | solution.py:387
  83.7 2.6 %all-to-all-start.2 = ((f32[32,8,128]{2,1,0:T(8,128)}), f32[32,8,128]{2,1,0:T(8,128)S(1)}, u32[]{:S(2)}, u32[]{:S(2)}) async-start(f32[32,8,128]{2,1,0:T(8,128)} %target_products.1), calls=%async_computation.2 | async-start | bytes 262144 | tf_op jit(solution)/shard_map/all_to_all | solution.py:95
  86.2 1.6 %sketches.1 = (f32[16,3,64,64]{3,2,1,0:T(8,128)}, f32[16,128]{1,0:T(8,128)S(1)}) custom-call(bf16[32,16,128]{2,1,0:T(8,128)(2,1)S(1)} %all-to-all-done.1.vectors, s32[1,128]{1,0:T(1,128)S(1)} %broadcast_in_dim_reshape.3.ids), custom_call_target="tpu_custom_call" | custom-call | tf_op jit(solution)/shard_map/sketches/pallas_call | solution.py:397
  87.9 6.6 %all-to-all-done.2.parts = f32[32,8,128]{2,1,0:T(8,128)S(1)} async-done(((f32[32,8,128]{2,1,0:T(8,128)}), f32[32,8,128]{2,1,0:T(8,128)S(1)}, u32[]{:S(2)}, u32[]{:S(2)}) %all-to-all-start.2) | async-done | bytes 131104 | tf_op jit(solution)/shard_map/all_to_all | solution.py:95
  94.5 0.8 scores.1
  (6 shorter events, 0.1 us)
Async XLA Ops:
  0.6 7.4 %collective-permute-start.1 = (bf16[4,8192]{1,0:T(4,128)(2,1)}, bf16[4,8192]{1,0:T(4,128)(2,1)S(1)}, u32[]{:S(2)}, u32[]{:S(2)}) collective-permute-start(bf16[4,8192]{1,0:T(4,128)(2,1)} %param.10), channel_id=1, source_target_pairs={{0,16},{1,17},{2,18},{3,19},{4,20},{5,21},{6,22},{7,23},{8,24},{9,... | collective-permute-start | bytes 196616 | tf_op jit(solution)/shard_map/ppermute | solution.py:47
  4.7 8.8 %collective-permute-start = (bf16[4,8192]{1,0:T(4,128)(2,1)}, bf16[4,8192]{1,0:T(4,128)(2,1)S(1)}, u32[]{:S(2)}, u32[]{:S(2)}) collective-permute-start(bf16[4,8192]{1,0:T(4,128)(2,1)} %param.10), channel_id=1, source_target_pairs={{0,8},{1,9},{2,10},{3,11},{4,12},{5,13},{6,14},{7,15},{8,0},{9,1},... | collective-permute-start | bytes 196616 | tf_op jit(solution)/shard_map/ppermute | solution.py:47
  6.3 6.0 %collective-permute-start.8 = (bf16[4,8192]{1,0:T(4,128)(2,1)}, bf16[4,8192]{1,0:T(4,128)(2,1)S(1)}, u32[]{:S(2)}, u32[]{:S(2)}) collective-permute-start(bf16[4,8192]{1,0:T(4,128)(2,1)} %param.11), channel_id=1, source_target_pairs={{0,16},{1,17},{2,18},{3,19},{4,20},{5,21},{6,22},{7,23},{8,24},{9,... | collective-permute-start | bytes 196616 | tf_op jit(solution)/shard_map/ppermute | solution.py:47
  6.6 6.9 %collective-permute-start.7 = (bf16[4,8192]{1,0:T(4,128)(2,1)}, bf16[4,8192]{1,0:T(4,128)(2,1)S(1)}, u32[]{:S(2)}, u32[]{:S(2)}) collective-permute-start(bf16[4,8192]{1,0:T(4,128)(2,1)} %param.11), channel_id=1, source_target_pairs={{0,8},{1,9},{2,10},{3,11},{4,12},{5,13},{6,14},{7,15},{8,0},{9,1},... | collective-permute-start | bytes 196616 | tf_op jit(solution)/shard_map/ppermute | solution.py:47
  8.0 5.6 %collective-permute-start.2 = (bf16[4,8192]{1,0:T(4,128)(2,1)S(1)}, bf16[4,8192]{1,0:T(4,128)(2,1)S(1)}, u32[]{:S(2)}, u32[]{:S(2)}) collective-permute-start(bf16[4,8192]{1,0:T(4,128)(2,1)S(1)} %collective-permute-done.1), channel_id=1, source_target_pairs={{0,8},{1,9},{2,10},{3,11},{4,12},{5,13},{6,14},{7,15},{8,0},{9,1},... | collective-permute-start | bytes 196616 | tf_op jit(solution)/shard_map/ppermute | solution.py:47
  12.3 4.3 %collective-permute-start.9 = (bf16[4,8192]{1,0:T(4,128)(2,1)S(1)}, bf16[4,8192]{1,0:T(4,128)(2,1)S(1)}, u32[]{:S(2)}, u32[]{:S(2)}) collective-permute-start(bf16[4,8192]{1,0:T(4,128)(2,1)S(1)} %collective-permute-done.8), channel_id=1, source_target_pairs={{0,8},{1,9},{2,10},{3,11},{4,12},{5,13},{6,14},{7,15},{8,0},{9,1},... | collective-permute-start | bytes 196616 | tf_op jit(solution)/shard_map/ppermute | solution.py:47
  16.9 6.4 %collective-permute-start.3 = (bf16[16,8192]{1,0:T(8,128)(2,1)S(1)}, bf16[16,8192]{1,0:T(8,128)(2,1)S(1)}, u32[]{:S(2)}, u32[]{:S(2)}) collective-permute-start(bf16[16,8192]{1,0:T(8,128)(2,1)S(1)} %get-tuple-element.8), channel_id=1, source_target_pairs={{0,4},{1,5},{2,6},{3,7},{4,0},{5,1},{6,2},{7,3},{8,12},{9,13},{10,... | collective-permute-start | bytes 786440 | tf_op jit(solution)/shard_map/ppermute | solution.py:38
  18.5 9.2 %collective-permute-start.10 = (bf16[16,8192]{1,0:T(8,128)(2,1)S(1)}, bf16[16,8192]{1,0:T(8,128)(2,1)S(1)}, u32[]{:S(2)}, u32[]{:S(2)}) collective-permute-start(bf16[16,8192]{1,0:T(8,128)(2,1)S(1)} %get-tuple-element.17), channel_id=1, source_target_pairs={{0,2},{1,3},{2,0},{3,1},{4,6},{5,7},{6,4},{7,5},{8,10},{9,11},{10,... | collective-permute-start | bytes 786440 | tf_op jit(solution)/shard_map/ppermute | solution.py:38
  23.4 12.8 %collective-permute-start.4 = (bf16[32,8192]{1,0:T(8,128)(2,1)S(1)}, bf16[32,8192]{1,0:T(8,128)(2,1)S(1)}, u32[]{:S(2)}, u32[]{:S(2)}) collective-permute-start(bf16[32,8192]{1,0:T(8,128)(2,1)S(1)} %constant_dynamic-update-slice_fusion.refs_0_), channel_id=1, source_target_pairs={{0,2},{1,3},{2,0},{3,1},{4,6},{5,7},{6,4},{7,5},{8,10},{9,11},{10,... | collective-permute-start | bytes 1572872 | tf_op jit(solution)/shard_map/ppermute | solution.py:38
  27.7 46.4 %copy-start.2 = (s32[128]{0:T(128)S(1)}, s32[128]{0:T(128)}, u32[]{:S(2)}) copy-start(s32[128]{0:T(128)} %param.17) | copy-start | bytes 1540
  27.7 54.7 %copy-start = (bf16[8,3,64,64]{3,2,1,0:T(8,128)(2,1)S(1)}, bf16[8,3,64,64]{3,2,1,0:T(8,128)(2,1)}, u32[]{:S(2)}) copy-start(bf16[8,3,64,64]{3,2,1,0:T(8,128)(2,1)} %targets.1) | copy-start | bytes 589828
  27.8 54.7 %copy-start.1 = (s32[8]{0:T(128)S(1)}, s32[8]{0:T(128)}, u32[]{:S(2)}) copy-start(s32[8]{0:T(128)} %param.19) | copy-start | bytes 100
  27.8 9.2 %collective-permute-start.11 = (bf16[32,8192]{1,0:T(8,128)(2,1)S(1)}, bf16[32,8192]{1,0:T(8,128)(2,1)S(1)}, u32[]{:S(2)}, u32[]{:S(2)}) collective-permute-start(bf16[32,8192]{1,0:T(8,128)(2,1)S(1)} %pad_maximum_fusion.refs_4_), channel_id=1, source_target_pairs={{0,4},{1,5},{2,6},{3,7},{4,0},{5,1},{6,2},{7,3},{8,12},{9,13},{10,... | collective-permute-start | bytes 1572872 | tf_op jit(solution)/shard_map/ppermute | solution.py:38
  27.8 9.2 %collective-permute-start.5 = (bf16[32,8192]{1,0:T(8,128)(2,1)S(1)}, bf16[32,8192]{1,0:T(8,128)(2,1)S(1)}, u32[]{:S(2)}, u32[]{:S(2)}) collective-permute-start(bf16[32,8192]{1,0:T(8,128)(2,1)S(1)} %constant_dynamic-update-slice_fusion.refs_0_), channel_id=1, source_target_pairs={{0,1},{1,0},{2,3},{3,2},{4,5},{5,4},{6,7},{7,6},{8,9},{9,8},{10,11... | collective-permute-start | bytes 1572872 | tf_op jit(solution)/shard_map/ppermute | solution.py:38
  27.9 9.1 %collective-permute-start.12 = (bf16[32,8192]{1,0:T(8,128)(2,1)S(1)}, bf16[32,8192]{1,0:T(8,128)(2,1)S(1)}, u32[]{:S(2)}, u32[]{:S(2)}) collective-permute-start(bf16[32,8192]{1,0:T(8,128)(2,1)S(1)} %pad_maximum_fusion.refs_4_), channel_id=1, source_target_pairs={{0,1},{1,0},{2,3},{3,2},{4,5},{5,4},{6,7},{7,6},{8,9},{9,8},{10,11... | collective-permute-start | bytes 1572872 | tf_op jit(solution)/shard_map/ppermute | solution.py:38
  36.2 1.9 %collective-permute-start.6 = (bf16[32,8192]{1,0:T(8,128)(2,1)S(1)}, bf16[32,8192]{1,0:T(8,128)(2,1)S(1)}, u32[]{:S(2)}, u32[]{:S(2)}) collective-permute-start(bf16[32,8192]{1,0:T(8,128)(2,1)S(1)} %collective-permute-done.4.refs_1_), channel_id=1, source_target_pairs={{0,1},{1,0},{2,3},{3,2},{4,5},{5,4},{6,7},{7,6},{8,9},{9,8},{10,11... | collective-permute-start | bytes 1572872 | tf_op jit(solution)/shard_map/ppermute | solution.py:38
  37.0 1.9 %collective-permute-start.13 = (bf16[32,8192]{1,0:T(8,128)(2,1)S(1)}, bf16[32,8192]{1,0:T(8,128)(2,1)S(1)}, u32[]{:S(2)}, u32[]{:S(2)}) collective-permute-start(bf16[32,8192]{1,0:T(8,128)(2,1)S(1)} %collective-permute-done.11.refs_5_), channel_id=1, source_target_pairs={{0,1},{1,0},{2,3},{3,2},{4,5},{5,4},{6,7},{7,6},{8,9},{9,8},{10,11... | collective-permute-start | bytes 1572872 | tf_op jit(solution)/shard_map/ppermute | solution.py:38
  71.6 10.8 %all-to-all-start.1 = ((bf16[32,16,128]{2,1,0:T(8,128)(2,1)}), bf16[32,16,128]{2,1,0:T(8,128)(2,1)S(1)}, u32[]{:S(2)}, u32[]{:S(2)}) async-start(bf16[32,16,128]{2,1,0:T(8,128)(2,1)} %sum_copies.1), calls=%async_computation.1 | async-start | bytes 262144 | tf_op jit(solution)/shard_map/all_to_all | solution.py:95
  83.7 10.8 %all-to-all-start.2 = ((f32[32,8,128]{2,1,0:T(8,128)}), f32[32,8,128]{2,1,0:T(8,128)S(1)}, u32[]{:S(2)}, u32[]{:S(2)}) async-start(f32[32,8,128]{2,1,0:T(8,128)} %target_products.1), calls=%async_computation.2 | async-start | bytes 262144 | tf_op jit(solution)/shard_map/all_to_all | solution.py:95

commit v14 on v13

--- a/solution.py
+++ b/solution.py
@@ -166,6 +166,12 @@
             for w in range(3):
                 copy(step + depth, w).start()
 
+    def add_both(step):
+        rows, columns = places(step)
+        pair = buffers[lax.rem(step, depth), :2].reshape(2 * block, chunk)
+        part = transposed_dot(pair, tokens[0, :, columns])
+        sums[:2, rows, :] += part.reshape(2, block, count)
+
     for w in range(3):
         copy(0, w).wait()
         add(0, w)
@@ -175,8 +181,8 @@
     def _(step):
         for w in range(3):
             copy(step, w).wait()
-        for w in range(3):
-            add(step, w)
+        add_both(step)
+        add(step, 2)
         refill(step)
 
     rank = proj.shape[0] // 3

time: 95.5 us -> 95.5 us (level)
  no operation moved by 1% of the time
where the time goes in v14:
time: 95.5 us; the launch traced here: 95.2 us
  waiting for transfers between devices  36.5 us (38%)
  Pallas kernels  21.2 us (22%)
  starting transfers between devices  19 us (20%)
  blocking collectives  15.1 us (16%)
  other arithmetic  2.32 us (2%)
    pallas_call x1, Pallas kernels, products(): pl.pallas_call(functools.partial(product_kernel, backs, sizes, model_cols...  16.9 us
    ppermute x8, waiting for transfers between devices, shift(): return lax.ppermute(value, 'dp', pairs)  16.5 us
    all_to_all x1, blocking collectives, exchange(): lax.all_to_all(blocks, 'dp', split_axis=0, concat_axis=0, axis_index_grou...  15.1 us
    all_to_all x2, waiting for transfers between devices, exchange(): lax.all_to_all(blocks, 'dp', split_axis=0, concat_axis=0, axis_index_grou...  14.6 us
    ppermute x6, starting transfers between devices, partner(): return lax.ppermute(value, 'dp', pairs)  8.58 us
    ppermute x8, starting transfers between devices, shift(): return lax.ppermute(value, 'dp', pairs)  5.33 us
    ppermute x6, waiting for transfers between devices, partner(): return lax.ppermute(value, 'dp', pairs)  5.32 us
    all_to_all x2, starting transfers between devices, exchange(): lax.all_to_all(blocks, 'dp', split_axis=0, concat_axis=0, axis_index_grou...  5.14 us
  transfers between devices with their start and end apart: 16, of which 11 were waited for; matrix products, arithmetic and copies ran while one was open for 2% of the time, Pallas kernels for 2%

profile of v14, /device:TPU:0, one launch (start us, length us, event | category | flops | bytes accessed | tf_op | source)
XLA Modules:
  0.0 95.2 jit_solution(16115978830486386122)
XLA Ops:
  0.6 4.1 %collective-permute-start.1 = (bf16[4,8192]{1,0:T(4,128)(2,1)}, bf16[4,8192]{1,0:T(4,128)(2,1)S(1)}, u32[]{:S(2)}, u32[]{:S(2)}) collective-permute-start(bf16[4,8192]{1,0:T(4,128)(2,1)} %param.10), channel_id=1, source_target_pairs={{0,16},{1,17},{2,18},{3,19},{4,20},{5,21},{6,22},{7,23},{8,24},{9,... | collective-permute-start | bytes 196616 | tf_op jit(solution)/shard_map/ppermute | solution.py:47
  4.7 1.6 %collective-permute-start = (bf16[4,8192]{1,0:T(4,128)(2,1)}, bf16[4,8192]{1,0:T(4,128)(2,1)S(1)}, u32[]{:S(2)}, u32[]{:S(2)}) collective-permute-start(bf16[4,8192]{1,0:T(4,128)(2,1)} %param.10), channel_id=1, source_target_pairs={{0,8},{1,9},{2,10},{3,11},{4,12},{5,13},{6,14},{7,15},{8,0},{9,1},... | collective-permute-start | bytes 196616 | tf_op jit(solution)/shard_map/ppermute | solution.py:47
  6.3 0.3 collective-permute-start.8
  6.6 0.2 collective-permute-start.7
  6.8 0.9 pad_maximum_fusion.4
  7.8 0.2 collective-permute-done.1
  8.0 2.2 %collective-permute-start.2 = (bf16[4,8192]{1,0:T(4,128)(2,1)S(1)}, bf16[4,8192]{1,0:T(4,128)(2,1)S(1)}, u32[]{:S(2)}, u32[]{:S(2)}) collective-permute-start(bf16[4,8192]{1,0:T(4,128)(2,1)S(1)} %collective-permute-done.1), channel_id=1, source_target_pairs={{0,8},{1,9},{2,10},{3,11},{4,12},{5,13},{6,14},{7,15},{8,0},{9,1},... | collective-permute-start | bytes 196616 | tf_op jit(solution)/shard_map/ppermute | solution.py:47
  10.2 2.2 %collective-permute-done.8 = bf16[4,8192]{1,0:T(4,128)(2,1)S(1)} collective-permute-done((bf16[4,8192]{1,0:T(4,128)(2,1)}, bf16[4,8192]{1,0:T(4,128)(2,1)S(1)}, u32[]{:S(2)}, u32[]{:S(2)}) %collective-permute-start.8) | collective-permute-done | bytes 65568 | tf_op jit(solution)/shard_map/ppermute | solution.py:47
  12.3 0.2 collective-permute-start.9
  12.5 1.0 %pad_maximum_fusion.1.refs_8_ = bf16[192,1152]{1,0:T(8,128)(2,1)S(1)} fusion(bf16[192,896]{1,0:T(8,128)(2,1)} %bitcast.5, bf16[192,256]{1,0:T(8,128)(2,1)} %bitcast.6), kind=kLoop, calls=%fused_computation.1 | loop fusion | flops 884736 | bytes 884736 | tf_op jit(solution)/shard_map/concatenate | solution.py:378
  13.6 0.0 collective-permute-done
  13.6 0.0 collective-permute-done.7
  13.6 0.0 collective-permute-done.2
  13.6 3.0 %collective-permute-done.9 = bf16[4,8192]{1,0:T(4,128)(2,1)S(1)} collective-permute-done((bf16[4,8192]{1,0:T(4,128)(2,1)S(1)}, bf16[4,8192]{1,0:T(4,128)(2,1)S(1)}, u32[]{:S(2)}, u32[]{:S(2)}) %collective-permute-start.9) | collective-permute-done | bytes 65568 | tf_op jit(solution)/shard_map/ppermute | solution.py:47
  16.6 0.3 pad_maximum_fusion.2
  16.9 1.6 %collective-permute-start.3 = (bf16[16,8192]{1,0:T(8,128)(2,1)S(1)}, bf16[16,8192]{1,0:T(8,128)(2,1)S(1)}, u32[]{:S(2)}, u32[]{:S(2)}) collective-permute-start(bf16[16,8192]{1,0:T(8,128)(2,1)S(1)} %get-tuple-element.8), channel_id=1, source_target_pairs={{0,4},{1,5},{2,6},{3,7},{4,0},{5,1},{6,2},{7,3},{8,12},{9,13},{10,... | collective-permute-start | bytes 786440 | tf_op jit(solution)/shard_map/ppermute | solution.py:38
  18.5 1.6 %collective-permute-start.10 = (bf16[16,8192]{1,0:T(8,128)(2,1)S(1)}, bf16[16,8192]{1,0:T(8,128)(2,1)S(1)}, u32[]{:S(2)}, u32[]{:S(2)}) collective-permute-start(bf16[16,8192]{1,0:T(8,128)(2,1)S(1)} %get-tuple-element.17), channel_id=1, source_target_pairs={{0,2},{1,3},{2,0},{3,1},{4,6},{5,7},{6,4},{7,5},{8,10},{9,11},{10,... | collective-permute-start | bytes 786440 | tf_op jit(solution)/shard_map/ppermute | solution.py:38
  20.1 3.3 %collective-permute-done.3 = bf16[16,8192]{1,0:T(8,128)(2,1)S(1)} collective-permute-done((bf16[16,8192]{1,0:T(8,128)(2,1)S(1)}, bf16[16,8192]{1,0:T(8,128)(2,1)S(1)}, u32[]{:S(2)}, u32[]{:S(2)}) %collective-permute-start.3) | collective-permute-done | bytes 262176 | tf_op jit(solution)/shard_map/ppermute | solution.py:38
  23.4 1.6 %collective-permute-start.4 = (bf16[32,8192]{1,0:T(8,128)(2,1)S(1)}, bf16[32,8192]{1,0:T(8,128)(2,1)S(1)}, u32[]{:S(2)}, u32[]{:S(2)}) collective-permute-start(bf16[32,8192]{1,0:T(8,128)(2,1)S(1)} %constant_dynamic-update-slice_fusion.refs_0_), channel_id=1, source_target_pairs={{0,2},{1,3},{2,0},{3,1},{4,6},{5,7},{6,4},{7,5},{8,10},{9,11},{10,... | collective-permute-start | bytes 1572872 | tf_op jit(solution)/shard_map/ppermute | solution.py:38
  24.9 2.8 %collective-permute-done.10 = bf16[16,8192]{1,0:T(8,128)(2,1)S(1)} collective-permute-done((bf16[16,8192]{1,0:T(8,128)(2,1)S(1)}, bf16[16,8192]{1,0:T(8,128)(2,1)S(1)}, u32[]{:S(2)}, u32[]{:S(2)}) %collective-permute-start.10) | collective-permute-done | bytes 262176 | tf_op jit(solution)/shard_map/ppermute | solution.py:38
  27.7 0.0 copy-start.2
  27.7 0.0 copy-start
  27.8 0.0 copy-start.1
  27.8 0.1 collective-permute-start.11
  27.8 0.1 collective-permute-start.5
  27.9 0.5 collective-permute-start.12
  28.4 7.8 %collective-permute-done.4.refs_1_ = bf16[32,8192]{1,0:T(8,128)(2,1)S(1)} collective-permute-done((bf16[32,8192]{1,0:T(8,128)(2,1)S(1)}, bf16[32,8192]{1,0:T(8,128)(2,1)S(1)}, u32[]{:S(2)}, u32[]{:S(2)}) %collective-permute-start.4) | collective-permute-done | bytes 524320 | tf_op jit(solution)/shard_map/ppermute | solution.py:38
  36.2 0.0 collective-permute-start.6
  36.2 0.8 collective-permute-done.11.refs_5_
  37.0 0.0 collective-permute-start.13
  37.0 0.0 collective-permute-done.5.refs_2_
  37.0 0.0 collective-permute-done.12.refs_6_
  37.0 1.1 %collective-permute-done.6.refs_3_ = bf16[32,8192]{1,0:T(8,128)(2,1)S(1)} collective-permute-done((bf16[32,8192]{1,0:T(8,128)(2,1)S(1)}, bf16[32,8192]{1,0:T(8,128)(2,1)S(1)}, u32[]{:S(2)}, u32[]{:S(2)}) %collective-permute-start.6) | collective-permute-done | bytes 524320 | tf_op jit(solution)/shard_map/ppermute | solution.py:38
  38.1 0.8 collective-permute-done.13.refs_7_
  38.9 16.9 %products.1 = f32[32,16,128]{2,1,0:T(8,128)S(1)} custom-call(bf16[32,8192]{1,0:T(8,128)(2,1)S(1)} %constant_dynamic-update-slice_fusion.refs_0_, bf16[32,8192]{1,0:T(8,128)(2,1)S(1)} %collective-permute-done.4.refs_1_, bf16[32,8192]{1,0:T(8,128)(2,1)S(1)} %collective-permute-done.5.refs_2_, bf16[32,8192]{1,0:T(8,128)(2,1)S(1)} %collective-permute-done.6.refs_3_, ...), custom_call_target="tpu_custom_call" | custom-call | flops 5637144576 | bytes 44040192 | tf_op jit(solution)/shard_map/products/pallas_call | solution.py:240
  55.8 15.1 %all_to_all.15.values = f32[32,16,128]{2,1,0:T(8,128)S(1)} all-to-all(f32[32,16,128]{2,1,0:T(8,128)S(1)} %products.1), channel_id=1, replica_groups=mesh['groups'=1,'dp'=32] {'dp'}, dimensions={0} | all-to-all | bytes 524288 | tf_op jit(solution)/shard_map/all_to_all | solution.py:95
  70.9 0.7 sum_copies.1
  71.6 2.6 %all-to-all-start.1 = ((bf16[32,16,128]{2,1,0:T(8,128)(2,1)}), bf16[32,16,128]{2,1,0:T(8,128)(2,1)S(1)}, u32[]{:S(2)}, u32[]{:S(2)}) async-start(bf16[32,16,128]{2,1,0:T(8,128)(2,1)} %sum_copies.1), calls=%async_computation.1 | async-start | bytes 262144 | tf_op jit(solution)/shard_map/all_to_all | solution.py:95
  74.2 0.0 copy-done.2
  74.2 0.1 reshape.7
  74.3 0.1 broadcast_in_dim_reshape.3.ids
  74.4 8.0 %all-to-all-done.1.vectors = bf16[32,16,128]{2,1,0:T(8,128)(2,1)S(1)} async-done(((bf16[32,16,128]{2,1,0:T(8,128)(2,1)}), bf16[32,16,128]{2,1,0:T(8,128)(2,1)S(1)}, u32[]{:S(2)}, u32[]{:S(2)}) %all-to-all-start.1) | async-done | bytes 131104 | tf_op jit(solution)/shard_map/all_to_all | solution.py:95
  82.4 0.0 copy-done
  82.4 1.3 %target_products.1 = f32[32,8,128]{2,1,0:T(8,128)} custom-call(bf16[32,16,128]{2,1,0:T(8,128)(2,1)S(1)} %all-to-all-done.1.vectors, s32[1,128]{1,0:T(1,128)S(1)} %broadcast_in_dim_reshape.3.ids, bf16[8,3,64,64]{3,2,1,0:T(8,128)(2,1)S(1)} %copy-done, s32[1,8]{1,0:T(1,128)S(1)} %bitcast.4), custom_call_target="tpu_custom_call" | custom-call | tf_op jit(solution)/shard_map/target_products/pallas_call | solution.py:393
  83.7 2.6 %all-to-all-start.2 = ((f32[32,8,128]{2,1,0:T(8,128)}), f32[32,8,128]{2,1,0:T(8,128)S(1)}, u32[]{:S(2)}, u32[]{:S(2)}) async-start(f32[32,8,128]{2,1,0:T(8,128)} %target_products.1), calls=%async_computation.2 | async-start | bytes 262144 | tf_op jit(solution)/shard_map/all_to_all | solution.py:95
  86.2 1.6 %sketches.1 = (f32[16,3,64,64]{3,2,1,0:T(8,128)}, f32[16,128]{1,0:T(8,128)S(1)}) custom-call(bf16[32,16,128]{2,1,0:T(8,128)(2,1)S(1)} %all-to-all-done.1.vectors, s32[1,128]{1,0:T(1,128)S(1)} %broadcast_in_dim_reshape.3.ids), custom_call_target="tpu_custom_call" | custom-call | tf_op jit(solution)/shard_map/sketches/pallas_call | solution.py:403
  87.9 6.6 %all-to-all-done.2.parts = f32[32,8,128]{2,1,0:T(8,128)S(1)} async-done(((f32[32,8,128]{2,1,0:T(8,128)}), f32[32,8,128]{2,1,0:T(8,128)S(1)}, u32[]{:S(2)}, u32[]{:S(2)}) %all-to-all-start.2) | async-done | bytes 131104 | tf_op jit(solution)/shard_map/all_to_all | solution.py:95
  94.5 0.8 scores.1
  (6 shorter events, 0.1 us)
Async XLA Ops:
  0.6 7.4 %collective-permute-start.1 = (bf16[4,8192]{1,0:T(4,128)(2,1)}, bf16[4,8192]{1,0:T(4,128)(2,1)S(1)}, u32[]{:S(2)}, u32[]{:S(2)}) collective-permute-start(bf16[4,8192]{1,0:T(4,128)(2,1)} %param.10), channel_id=1, source_target_pairs={{0,16},{1,17},{2,18},{3,19},{4,20},{5,21},{6,22},{7,23},{8,24},{9,... | collective-permute-start | bytes 196616 | tf_op jit(solution)/shard_map/ppermute | solution.py:47
  4.7 8.8 %collective-permute-start = (bf16[4,8192]{1,0:T(4,128)(2,1)}, bf16[4,8192]{1,0:T(4,128)(2,1)S(1)}, u32[]{:S(2)}, u32[]{:S(2)}) collective-permute-start(bf16[4,8192]{1,0:T(4,128)(2,1)} %param.10), channel_id=1, source_target_pairs={{0,8},{1,9},{2,10},{3,11},{4,12},{5,13},{6,14},{7,15},{8,0},{9,1},... | collective-permute-start | bytes 196616 | tf_op jit(solution)/shard_map/ppermute | solution.py:47
  6.3 6.0 %collective-permute-start.8 = (bf16[4,8192]{1,0:T(4,128)(2,1)}, bf16[4,8192]{1,0:T(4,128)(2,1)S(1)}, u32[]{:S(2)}, u32[]{:S(2)}) collective-permute-start(bf16[4,8192]{1,0:T(4,128)(2,1)} %param.11), channel_id=1, source_target_pairs={{0,16},{1,17},{2,18},{3,19},{4,20},{5,21},{6,22},{7,23},{8,24},{9,... | collective-permute-start | bytes 196616 | tf_op jit(solution)/shard_map/ppermute | solution.py:47
  6.6 6.9 %collective-permute-start.7 = (bf16[4,8192]{1,0:T(4,128)(2,1)}, bf16[4,8192]{1,0:T(4,128)(2,1)S(1)}, u32[]{:S(2)}, u32[]{:S(2)}) collective-permute-start(bf16[4,8192]{1,0:T(4,128)(2,1)} %param.11), channel_id=1, source_target_pairs={{0,8},{1,9},{2,10},{3,11},{4,12},{5,13},{6,14},{7,15},{8,0},{9,1},... | collective-permute-start | bytes 196616 | tf_op jit(solution)/shard_map/ppermute | solution.py:47
  8.0 5.6 %collective-permute-start.2 = (bf16[4,8192]{1,0:T(4,128)(2,1)S(1)}, bf16[4,8192]{1,0:T(4,128)(2,1)S(1)}, u32[]{:S(2)}, u32[]{:S(2)}) collective-permute-start(bf16[4,8192]{1,0:T(4,128)(2,1)S(1)} %collective-permute-done.1), channel_id=1, source_target_pairs={{0,8},{1,9},{2,10},{3,11},{4,12},{5,13},{6,14},{7,15},{8,0},{9,1},... | collective-permute-start | bytes 196616 | tf_op jit(solution)/shard_map/ppermute | solution.py:47
  12.3 4.3 %collective-permute-start.9 = (bf16[4,8192]{1,0:T(4,128)(2,1)S(1)}, bf16[4,8192]{1,0:T(4,128)(2,1)S(1)}, u32[]{:S(2)}, u32[]{:S(2)}) collective-permute-start(bf16[4,8192]{1,0:T(4,128)(2,1)S(1)} %collective-permute-done.8), channel_id=1, source_target_pairs={{0,8},{1,9},{2,10},{3,11},{4,12},{5,13},{6,14},{7,15},{8,0},{9,1},... | collective-permute-start | bytes 196616 | tf_op jit(solution)/shard_map/ppermute | solution.py:47
  16.9 6.4 %collective-permute-start.3 = (bf16[16,8192]{1,0:T(8,128)(2,1)S(1)}, bf16[16,8192]{1,0:T(8,128)(2,1)S(1)}, u32[]{:S(2)}, u32[]{:S(2)}) collective-permute-start(bf16[16,8192]{1,0:T(8,128)(2,1)S(1)} %get-tuple-element.8), channel_id=1, source_target_pairs={{0,4},{1,5},{2,6},{3,7},{4,0},{5,1},{6,2},{7,3},{8,12},{9,13},{10,... | collective-permute-start | bytes 786440 | tf_op jit(solution)/shard_map/ppermute | solution.py:38
  18.5 9.2 %collective-permute-start.10 = (bf16[16,8192]{1,0:T(8,128)(2,1)S(1)}, bf16[16,8192]{1,0:T(8,128)(2,1)S(1)}, u32[]{:S(2)}, u32[]{:S(2)}) collective-permute-start(bf16[16,8192]{1,0:T(8,128)(2,1)S(1)} %get-tuple-element.17), channel_id=1, source_target_pairs={{0,2},{1,3},{2,0},{3,1},{4,6},{5,7},{6,4},{7,5},{8,10},{9,11},{10,... | collective-permute-start | bytes 786440 | tf_op jit(solution)/shard_map/ppermute | solution.py:38
  23.4 12.8 %collective-permute-start.4 = (bf16[32,8192]{1,0:T(8,128)(2,1)S(1)}, bf16[32,8192]{1,0:T(8,128)(2,1)S(1)}, u32[]{:S(2)}, u32[]{:S(2)}) collective-permute-start(bf16[32,8192]{1,0:T(8,128)(2,1)S(1)} %constant_dynamic-update-slice_fusion.refs_0_), channel_id=1, source_target_pairs={{0,2},{1,3},{2,0},{3,1},{4,6},{5,7},{6,4},{7,5},{8,10},{9,11},{10,... | collective-permute-start | bytes 1572872 | tf_op jit(solution)/shard_map/ppermute | solution.py:38
  27.7 46.5 %copy-start.2 = (s32[128]{0:T(128)S(1)}, s32[128]{0:T(128)}, u32[]{:S(2)}) copy-start(s32[128]{0:T(128)} %param.17) | copy-start | bytes 1540
  27.7 54.7 %copy-start = (bf16[8,3,64,64]{3,2,1,0:T(8,128)(2,1)S(1)}, bf16[8,3,64,64]{3,2,1,0:T(8,128)(2,1)}, u32[]{:S(2)}) copy-start(bf16[8,3,64,64]{3,2,1,0:T(8,128)(2,1)} %targets.1) | copy-start | bytes 589828
  27.8 54.7 %copy-start.1 = (s32[8]{0:T(128)S(1)}, s32[8]{0:T(128)}, u32[]{:S(2)}) copy-start(s32[8]{0:T(128)} %param.19) | copy-start | bytes 100
  27.8 9.2 %collective-permute-start.11 = (bf16[32,8192]{1,0:T(8,128)(2,1)S(1)}, bf16[32,8192]{1,0:T(8,128)(2,1)S(1)}, u32[]{:S(2)}, u32[]{:S(2)}) collective-permute-start(bf16[32,8192]{1,0:T(8,128)(2,1)S(1)} %pad_maximum_fusion.refs_4_), channel_id=1, source_target_pairs={{0,4},{1,5},{2,6},{3,7},{4,0},{5,1},{6,2},{7,3},{8,12},{9,13},{10,... | collective-permute-start | bytes 1572872 | tf_op jit(solution)/shard_map/ppermute | solution.py:38
  27.8 9.2 %collective-permute-start.5 = (bf16[32,8192]{1,0:T(8,128)(2,1)S(1)}, bf16[32,8192]{1,0:T(8,128)(2,1)S(1)}, u32[]{:S(2)}, u32[]{:S(2)}) collective-permute-start(bf16[32,8192]{1,0:T(8,128)(2,1)S(1)} %constant_dynamic-update-slice_fusion.refs_0_), channel_id=1, source_target_pairs={{0,1},{1,0},{2,3},{3,2},{4,5},{5,4},{6,7},{7,6},{8,9},{9,8},{10,11... | collective-permute-start | bytes 1572872 | tf_op jit(solution)/shard_map/ppermute | solution.py:38
  27.9 9.1 %collective-permute-start.12 = (bf16[32,8192]{1,0:T(8,128)(2,1)S(1)}, bf16[32,8192]{1,0:T(8,128)(2,1)S(1)}, u32[]{:S(2)}, u32[]{:S(2)}) collective-permute-start(bf16[32,8192]{1,0:T(8,128)(2,1)S(1)} %pad_maximum_fusion.refs_4_), channel_id=1, source_target_pairs={{0,1},{1,0},{2,3},{3,2},{4,5},{5,4},{6,7},{7,6},{8,9},{9,8},{10,11... | collective-permute-start | bytes 1572872 | tf_op jit(solution)/shard_map/ppermute | solution.py:38
  36.2 1.9 %collective-permute-start.6 = (bf16[32,8192]{1,0:T(8,128)(2,1)S(1)}, bf16[32,8192]{1,0:T(8,128)(2,1)S(1)}, u32[]{:S(2)}, u32[]{:S(2)}) collective-permute-start(bf16[32,8192]{1,0:T(8,128)(2,1)S(1)} %collective-permute-done.4.refs_1_), channel_id=1, source_target_pairs={{0,1},{1,0},{2,3},{3,2},{4,5},{5,4},{6,7},{7,6},{8,9},{9,8},{10,11... | collective-permute-start | bytes 1572872 | tf_op jit(solution)/shard_map/ppermute | solution.py:38
  37.0 1.9 %collective-permute-start.13 = (bf16[32,8192]{1,0:T(8,128)(2,1)S(1)}, bf16[32,8192]{1,0:T(8,128)(2,1)S(1)}, u32[]{:S(2)}, u32[]{:S(2)}) collective-permute-start(bf16[32,8192]{1,0:T(8,128)(2,1)S(1)} %collective-permute-done.11.refs_5_), channel_id=1, source_target_pairs={{0,1},{1,0},{2,3},{3,2},{4,5},{5,4},{6,7},{7,6},{8,9},{9,8},{10,11... | collective-permute-start | bytes 1572872 | tf_op jit(solution)/shard_map/ppermute | solution.py:38
  71.6 10.8 %all-to-all-start.1 = ((bf16[32,16,128]{2,1,0:T(8,128)(2,1)}), bf16[32,16,128]{2,1,0:T(8,128)(2,1)S(1)}, u32[]{:S(2)}, u32[]{:S(2)}) async-start(bf16[32,16,128]{2,1,0:T(8,128)(2,1)} %sum_copies.1), calls=%async_computation.1 | async-start | bytes 262144 | tf_op jit(solution)/shard_map/all_to_all | solution.py:95
  83.7 10.8 %all-to-all-start.2 = ((f32[32,8,128]{2,1,0:T(8,128)}), f32[32,8,128]{2,1,0:T(8,128)S(1)}, u32[]{:S(2)}, u32[]{:S(2)}) async-start(f32[32,8,128]{2,1,0:T(8,128)} %target_products.1), calls=%async_computation.2 | async-start | bytes 262144 | tf_op jit(solution)/shard_map/all_to_all | solution.py:95
